TPU v7x, 32 devices: a whole 2x2x4 slice. The times are simulated.
32 devices in a mesh: au: 4 (over y, x), vert: 8 (over z, core).
Axes of the slice: x: 2, y: 2, z: 4, core: 2. Of those that a mesh axis runs over, the one named last changes fastest.
Arguments:
- visibilities: bfloat16 [768, 2, 2048], P(('au', 'vert')), may hold values from -6 to 6
- baseline_offsets: float32 [768, 2, 128], P(('au', 'vert')), may hold values from -8 to 8
- channel_scale: float32 [16], replicated, may hold values from 0.8 to 1.25
- screen_depth: float32 [768], P(('au', 'vert')), may hold values from -300 to 300
- stations: int32 [768, 2], P(('au', 'vert')), may hold values from 0 to 511
- corners: int32 [768, 2], P(('au', 'vert')), may hold values from 0 to 8191, as said below
- beam_terms: bfloat16 [512, 2, 1024], P(('au', 'vert')), may hold values from -5 to 5
Outputs:
- gridded: float32 [8192, 2, 8192], P('au', None, 'vert')
- dirty_image: float32 [8192, 2, 8192], P(('au', 'vert'))
Inputs may be any that keep to these rules, and one draw needn't show every extreme that they name: Subgrid s belongs to block d = floor(s / 24); with d = r * 8 + c, corners[s, 0] lies in [r * 2048, (r + 1) * 2048) and the columns corners[s, 1] to corners[s, 1] + 31 lie inside one column tile of 1024 columns. At most 6 subgrids of one block lie in one column tile; for every r one column tile holds exactly 6 subgrids of every block of that r.
All inputs are finite; a program needn't handle non-finite values.
Results may differ from a plain program's by a relative error of at most 0.039.
Values may be sent and summed in bfloat16 or wider, within the bound.
No kernel may reach another device: no remote copies, remote signals or barrier semaphores. Data moves between devices by JAX's collectives and lax.ppermute only.
A program may use at most 128 MiB of HBM per device.

v0:
```python
import functools
import math

import jax
import jax.numpy as jnp
from jax import lax
from jax.experimental import pallas as pl
from jax.experimental.pallas import tpu as pltpu
from jax.sharding import PartitionSpec as P

G = 8192
SUB = 32
HALF = SUB // 2
PACK = 4 * SUB
LANES = 128
FINE = G // SUB
CHUNK = 768
MASK_VALUES = 1 << 22
field_view = 0.1
bf16 = jnp.bfloat16
f32 = jnp.float32
VMEM_BYTES = 58 * 1024 * 1024


def cmul(a, b):
    return (a[0] * b[0] - a[1] * b[1], a[0] * b[1] + a[1] * b[0])


def conj(a):
    return (a[0], -a[1])


def sky_kernel(vis_ref, offset_ref, scale_ref, out_ref, cos_ref, sin_ref):
    count, _, vis_count = vis_ref.shape
    times = offset_ref.shape[1]
    step = math.gcd(vis_count, 256)
    row = lax.broadcasted_iota(jnp.int32, (8, step), 0)
    bits = [(row >> bit) % 2 == 1 for bit in range(3)]

    offsets = offset_ref[...]
    parts = []
    for _ in range(3):
        parts.append(offsets.astype(bf16))
        offsets = offsets - parts[-1].astype(f32)
    for start in range(0, vis_count, 512):
        width = min(512, vis_count - start)
        at = pl.ds(start, width)
        time = lax.broadcasted_iota(jnp.int32, (times, width), 0)
        place = lax.broadcasted_iota(jnp.int32, (times, width), 1) + start
        one = (place // (vis_count // times) == time).astype(f32).astype(bf16)
        shifts = sum(jnp.dot(part, one, preferred_element_type=f32) for part in parts)
        half = (math.pi / SUB) * (shifts * scale_ref[:, at])
        square = half * half
        sine, cosine = 1.0, 1.0
        for term in (12, 10, 8, 6, 4, 2):
            sine = 1.0 - square * (1.0 / (term * (term + 1))) * sine
            cosine = 1.0 - square * (1.0 / (term * (term - 1))) * cosine
        sine = sine * half
        cos_ref[:, at] = 1.0 - 2.0 * sine * sine
        sin_ref[:, at] = 2.0 * sine * cosine

    def powers(c, s, extra):
        z = (jnp.broadcast_to(c, (8, step)), jnp.broadcast_to(s, (8, step)))
        low = (jnp.where(bits[0], z[0], 1.0), jnp.where(bits[0], z[1], 0.0))
        power = z
        for bit in (1, 2):
            power = (power[0] * power[0] - power[1] * power[1], 2.0 * power[0] * power[1])
            more = cmul(low, power)
            low = (jnp.where(bits[bit], more[0], low[0]), jnp.where(bits[bit], more[1], low[1]))
        eight = (power[0] * power[0] - power[1] * power[1], 2.0 * power[0] * power[1])
        sixteen = (eight[0] * eight[0] - eight[1] * eight[1], 2.0 * eight[0] * eight[1])
        if extra is not None:
            low = cmul(low, extra)
        blocks = [cmul(low, conj(sixteen)), cmul(low, conj(eight)), low, cmul(low, eight)]
        return jnp.concatenate([block[part] for part in range(2) for block in blocks], axis=0).astype(bf16)

    def one_subgrid(s):
        both = jnp.zeros((2 * SUB, 2 * SUB), f32)
        for start in range(0, vis_count, step):
            at = pl.ds(start, step)
            vis = tuple(
                jnp.broadcast_to(vis_ref[s, part : part + 1, at].astype(f32), (8, step))
                for part in range(2)
            )
            u_row, v_row = pl.ds(2 * s, 1), pl.ds(2 * s + 1, 1)
            left = powers(cos_ref[u_row, at], sin_ref[u_row, at], vis)
            right = powers(cos_ref[v_row, at], sin_ref[v_row, at], None)
            both += lax.dot_general(
                left, right, (((1,), (1,)), ((), ())), preferred_element_type=f32
            )
        real = both[:SUB, :SUB] - both[SUB:, SUB:]
        image = both[:SUB, SUB:] + both[SUB:, :SUB]
        out_ref[s] = jnp.concatenate(
            [real[:HALF], image[:HALF], real[HALF:], image[HALF:]], axis=1
        )

    def some(i, carry):
        for k in range(math.gcd(count, 2)):
            one_subgrid(i * math.gcd(count, 2) + k)
        return carry

    lax.fori_loop(0, count // math.gcd(count, 2), some, 0)


def sky_sums(visibilities, offsets, scale_row, first, count, interpret=False):
    vis_count = visibilities.shape[2]
    times = offsets.shape[1]
    at = first // count
    return pl.pallas_call(
        sky_kernel,
        grid=(1,),
        in_specs=[
            pl.BlockSpec((count, 2, vis_count), lambda i: (at, 0, 0)),
            pl.BlockSpec((2 * count, times), lambda i: (at, 0)),
            pl.BlockSpec((1, vis_count), lambda i: (0, 0)),
        ],
        out_specs=pl.BlockSpec((count, HALF, PACK), lambda i: (0, 0, 0)),
        out_shape=jax.ShapeDtypeStruct((count, HALF, PACK), f32),
        scratch_shapes=[pltpu.VMEM((2 * count, vis_count), f32)] * 2,
        compiler_params=pltpu.CompilerParams(vmem_limit_bytes=VMEM_BYTES),
        cost_estimate=pl.CostEstimate(
            flops=0, bytes_accessed=count * 2_500_000, transcendentals=0
        ),
        name="sky_sums",
        interpret=interpret,
    )(visibilities, offsets, scale_row)


def correct_kernel(stations_ref, *refs, pieces, skies):
    table_refs, refs = refs[:pieces], refs[pieces:]
    sky_refs, refs = refs[:skies], refs[skies:]
    factor_ref, right_ref, left_ref, out_ref, table_ref, mid_ref = refs
    count = factor_ref.shape[0]
    lane = lax.broadcasted_iota(jnp.int32, (HALF, PACK), 1)
    imag = (lane // SUB) % 2 == 1
    sign = jnp.where(imag, 1.0, -1.0)

    def up(x):
        return pltpu.roll(x, SUB, 1)

    def down(x):
        return pltpu.roll(x, PACK - SUB, 1)

    def product(a, b):
        swapped = jnp.where(imag, up(a), down(a))
        return a * jnp.where(imag, up(b), b) + sign * swapped * jnp.where(imag, b, down(b))

    held = 0
    for piece in table_refs:
        table_ref[held : held + piece.shape[0]] = piece[...]
        held += piece.shape[0]
    for s in range(count):
        first = table_ref[stations_ref[2 * s]].astype(f32)
        second = table_ref[stations_ref[2 * s + 1]].astype(f32)
        pair = product(first, -sign * second)
        per = count // skies
        sky = product(sky_refs[s // per][s % per], factor_ref[s])
        mid_ref[HALF * s : HALF * (s + 1), :] = product(sky, pair).astype(bf16)
    mid = jnp.dot(mid_ref[...], right_ref[...], preferred_element_type=f32).astype(bf16)
    for s in range(count):
        rows = mid[HALF * s : HALF * (s + 1)]
        tall = jnp.concatenate([rows[:, : 2 * SUB], rows[:, 2 * SUB :]], axis=0)
        four = jnp.dot(left_ref[...], tall, preferred_element_type=f32)
        real = four[:SUB, :SUB] - four[SUB:, SUB:]
        image = four[:SUB, SUB:] + four[SUB:, :SUB]
        out_ref[s] = jnp.concatenate(
            [real[:HALF], image[:HALF], real[HALF:], image[HALF:]], axis=1
        ).astype(bf16)


def corrected_subgrids(stations, tables, skies, factor, interpret=False):
    count = factor.shape[0]
    centred = jnp.arange(SUB, dtype=jnp.int32) - HALF
    index = jnp.arange(SUB, dtype=jnp.int32)
    angle = 2.0 * math.pi / SUB * (centred[:, None] * centred[None, :] % SUB).astype(f32)
    cols_re, cols_im = jnp.cos(angle) / SUB, -jnp.sin(angle) / SUB
    block = jnp.concatenate(
        [
            jnp.concatenate([cols_re.T, cols_im.T], axis=1),
            jnp.concatenate([-cols_im.T, cols_re.T], axis=1),
        ],
        axis=0,
    )
    right = jnp.kron(jnp.eye(2, dtype=f32), block).astype(bf16)
    angle = 2.0 * math.pi / SUB * ((index - HALF)[:, None] * centred[None, :] % SUB).astype(f32)
    left = jnp.concatenate([jnp.cos(angle) / SUB, -jnp.sin(angle) / SUB], axis=0).astype(bf16)
    rows = sum(piece.shape[0] for piece in tables)
    operands = [*tables, *skies, factor, right, left]

    def whole(operand):
        return pl.BlockSpec(operand.shape, lambda i, *_: (0,) * operand.ndim)

    return pl.pallas_call(
        functools.partial(correct_kernel, pieces=len(tables), skies=len(skies)),
        grid_spec=pltpu.PrefetchScalarGridSpec(
            num_scalar_prefetch=1,
            grid=(1,),
            in_specs=[whole(operand) for operand in operands],
            out_specs=pl.BlockSpec((count, HALF, PACK), lambda i, *_: (0, 0, 0)),
            scratch_shapes=[
                pltpu.VMEM((rows, HALF, PACK), bf16),
                pltpu.VMEM((HALF * count, PACK), bf16),
            ],
        ),
        out_shape=jax.ShapeDtypeStruct((count, HALF, PACK), bf16),
        compiler_params=pltpu.CompilerParams(vmem_limit_bytes=VMEM_BYTES),
        cost_estimate=pl.CostEstimate(flops=0, bytes_accessed=16_000_000, transcendentals=0),
        name="correct",
        interpret=interpret,
    )(stations.reshape(-1), *operands)


def add_subgrids(uv_refs, list_ref, row_ref, col_ref, held_ref, total_ref, lanes):
    first = 0
    for piece in uv_refs:
        held_ref[first : first + piece.shape[0]] = piece[...]
        first += piece.shape[0]
    lane = lax.broadcasted_iota(jnp.int32, (8, LANES), 1)
    row = lax.broadcasted_iota(jnp.int32, (8, LANES), 0)

    def one(entry, carry):
        s = list_ref[entry + 1]
        row_at, col_at = row_ref[s], col_ref[s]
        packed = held_ref[pl.ds(pl.multiple_of(s * HALF, HALF), HALF), :].astype(f32)
        tile = col_at // LANES
        offset = col_at % LANES
        shift = row_at % SUB
        base = row_at - shift

        def place(over):
            inside = lane < offset + SUB - LANES
            if not over:
                inside = (lane >= offset) & (lane < offset + SUB)
            for h in range(2):
                for part in range(2):
                    from_lane = (2 * h + part) * SUB
                    moved = pltpu.roll(packed, lax.rem(offset - from_lane + LANES, LANES), 1)
                    for group in range(2):
                        values = moved[8 * group : 8 * (group + 1)]
                        first_row = HALF * h + 8 * group
                        late = row + first_row >= shift
                        for wrapped in range(2):
                            keep = jnp.logical_and(inside, late if wrapped == 0 else ~late)
                            start = (base + SUB * wrapped + first_row) * lanes
                            start = start + 2 * (tile + over) + part
                            at = pl.ds(start, 8, stride=lanes)
                            total_ref[at, :] = total_ref[at, :] + jnp.where(keep, values, 0.0)

        place(0)

        @pl.when(offset + SUB > LANES)
        def _():
            place(1)

        return carry

    lax.fori_loop(0, list_ref[0], one, 0)


def tile_kernel(block_ref, list_ref, row_ref, col_ref, *refs, pieces, tile_rows, lanes):
    del block_ref
    uv_refs = refs[:pieces]
    out_ref, held_ref, total_ref, sems = refs[pieces:]
    rows_all = total_ref.shape[0]
    zero_rows = math.gcd(rows_all, 1024)

    def clear(i, carry):
        at = pl.ds(pl.multiple_of(i * zero_rows, zero_rows), zero_rows)
        total_ref[at, :] = jnp.zeros((zero_rows, LANES), f32)
        return carry

    lax.fori_loop(0, rows_all // zero_rows, clear, 0)
    add_subgrids(uv_refs, list_ref, row_ref, col_ref, held_ref, total_ref, lanes)
    pieces = sems.shape[0]
    size = tile_rows * lanes // pieces
    copies = [
        pltpu.make_async_copy(
            total_ref.at[pl.ds(i * size, size), :], out_ref.at[pl.ds(i * size, size), :], sems.at[i]
        )
        for i in range(pieces)
    ]
    for copy in copies:
        copy.start()
    for copy in copies:
        copy.wait()


def spill_kernel(block_ref, list_ref, row_ref, col_ref, *refs, pieces, lanes):
    del block_ref
    uv_refs = refs[:pieces]
    _, out_ref, held_ref, total_ref, sem = refs[pieces:]
    size = SUB * lanes
    kept = total_ref.at[pl.ds(size, size), :]
    copy = pltpu.make_async_copy(out_ref.at[pl.ds(0, size), :], kept, sem)
    copy.start()
    copy.wait()
    add_subgrids(uv_refs, list_ref, row_ref, col_ref, held_ref, total_ref, lanes)
    copy = pltpu.make_async_copy(kept, out_ref.at[pl.ds(0, size), :], sem)
    copy.start()
    copy.wait()


def listed(valid):
    count = valid.shape[0]
    index = jnp.arange(count, dtype=jnp.int32)
    before = jnp.sum((index[None, :] < index[:, None]) & valid[None, :], axis=1, dtype=jnp.int32)
    rank = jnp.where(valid, before, -1)
    entries = jnp.sum(
        jnp.where(rank[None, :] == index[:, None], index[None, :], 0), axis=1, dtype=jnp.int32
    )
    return jnp.concatenate([jnp.sum(valid, dtype=jnp.int32)[None], entries])


def tile_places(corners, au_index, vert_index, au_count, vert_count, spilled):
    tile_rows, tile_cols = G // au_count, G // vert_count
    col_at = corners[1] - vert_index * tile_cols
    valid = (col_at >= 0) & (col_at < tile_cols)
    row_at = corners[0] - au_index * tile_rows
    if spilled:
        row_at = (row_at + SUB + G) % G
        valid = valid & (row_at < SUB)
    return listed(valid), row_at, col_at


def uv_tile_own(uv, block, places, au_count, vert_count, interpret=False):
    count = places[1].shape[0]
    tile_rows, tile_cols = G // au_count, G // vert_count
    lanes = 2 * tile_cols // LANES
    rows = count * HALF // len(uv)
    return pl.pallas_call(
        functools.partial(tile_kernel, pieces=len(uv), tile_rows=tile_rows, lanes=lanes),
        grid_spec=pltpu.PrefetchScalarGridSpec(
            num_scalar_prefetch=4,
            grid=(1,),
            in_specs=[pl.BlockSpec((rows, PACK), lambda i, block, *_: (block[0], 0))] * len(uv),
            out_specs=pl.BlockSpec(memory_space=pl.ANY),
            scratch_shapes=[
                pltpu.VMEM((count * HALF, PACK), bf16),
                pltpu.VMEM(((tile_rows + 2 * SUB) * lanes, LANES), f32),
                pltpu.SemaphoreType.DMA((4,)),
            ],
        ),
        out_shape=jax.ShapeDtypeStruct((tile_rows * lanes, LANES), f32),
        compiler_params=pltpu.CompilerParams(vmem_limit_bytes=VMEM_BYTES),
        cost_estimate=pl.CostEstimate(
            flops=0, bytes_accessed=20 * tile_rows * tile_cols, transcendentals=0
        ),
        name="uv_tile",
        interpret=interpret,
    )(block.reshape(1), *places, *[piece.reshape(-1, PACK) for piece in uv])


def uv_tile_spill(tile, uv, block, places, au_count, vert_count, interpret=False):
    count = places[1].shape[0]
    tile_rows, tile_cols = G // au_count, G // vert_count
    lanes = 2 * tile_cols // LANES
    rows = count * HALF // len(uv)
    result = pl.pallas_call(
        functools.partial(spill_kernel, pieces=len(uv), lanes=lanes),
        grid_spec=pltpu.PrefetchScalarGridSpec(
            num_scalar_prefetch=4,
            grid=(1,),
            in_specs=[pl.BlockSpec((rows, PACK), lambda i, block, *_: (block[0], 0))] * len(uv)
            + [pl.BlockSpec(memory_space=pl.ANY)],
            out_specs=pl.BlockSpec(memory_space=pl.ANY),
            scratch_shapes=[
                pltpu.VMEM((count * HALF, PACK), bf16),
                pltpu.VMEM((3 * SUB * lanes, LANES), f32),
                pltpu.SemaphoreType.DMA(()),
            ],
        ),
        out_shape=jax.ShapeDtypeStruct(tile.shape, f32),
        input_output_aliases={4 + len(uv): 0},
        compiler_params=pltpu.CompilerParams(vmem_limit_bytes=VMEM_BYTES),
        cost_estimate=pl.CostEstimate(flops=0, bytes_accessed=8_000_000, transcendentals=0),
        name="uv_spill",
        interpret=interpret,
    )(block.reshape(1), *places, *[piece.reshape(-1, PACK) for piece in uv], tile)
    result = result.reshape(tile_rows, tile_cols // LANES, 2, LANES)
    return jnp.transpose(result, (0, 2, 1, 3)).reshape(tile_rows, 2, tile_cols)


def short_transform(values):
    count = len(values)
    if count == 1:
        return values
    even = short_transform(values[0::2])
    odd = short_transform(values[1::2])
    low, high = [], []
    for k in range(count // 2):
        re, im = odd[k]
        if k == 0:
            turned = (re, im)
        elif 4 * k == count:
            turned = (-im, re)
        elif 8 * k == count:
            root = math.sqrt(0.5)
            turned = ((re - im) * root, (re + im) * root)
        elif 8 * k == 3 * count:
            root = math.sqrt(0.5)
            turned = ((re + im) * -root, (re - im) * root)
        else:
            c, s = math.cos(2 * math.pi * k / count), math.sin(2 * math.pi * k / count)
            turned = (re * c - im * s, re * s + im * c)
        low.append((even[k][0] + turned[0], even[k][1] + turned[1]))
        high.append((even[k][0] - turned[0], even[k][1] - turned[1]))
    return low + high


def image_kernel(
    *refs, pieces, chunks, row_block
):
    uv_refs, refs = refs[:pieces], refs[pieces:]
    corner_ref, phase_ref, columns_ref, unit_ref, count_ref, twist_ref = refs[:6]
    out_ref, uv_wide, here, after, shifts, total = refs[6:]
    step = pl.program_id(0)
    size = uv_wide.shape[0] // HALF
    image_rows = phase_ref.shape[1]

    @pl.when(step < chunks * HALF)
    def _():
        pair = lax.rem(step, HALF)
        chunk = step // HALF

        @pl.when(pair == 0)
        def _():
            held = 0
            for piece in uv_refs:
                uv_wide[held : held + piece.shape[0]] = piece[...].astype(f32)
                held += piece.shape[0]
            corner = corner_ref[...]
            coarse, shift = corner // SUB, corner % SUB

            def looked_up(index, length, table):
                place = lax.broadcasted_iota(jnp.int32, (length, size), 0)
                one = (place == index).astype(f32).astype(bf16)
                return lax.dot_general(
                    one, table, (((0,), (0,)), ((), ())), preferred_element_type=f32
                )

            here[...] = looked_up(coarse, FINE, unit_ref[...]).astype(bf16)
            after[...] = looked_up(lax.rem(coarse + 1, FINE), FINE, unit_ref[...]).astype(bf16)
            shifts[...] = looked_up(shift, SUB, count_ref[...])

        rows = uv_wide[pl.ds(pair, size, stride=HALF), :].astype(bf16)
        spread = lax.dot_general(
            columns_ref[...], rows, (((1,), (1,)), ((), ())), preferred_element_type=f32
        )
        for h in range(2):
            index = pair + HALF * h
            start = 2 * image_rows * h
            part = (spread[start : start + image_rows], spread[start + image_rows : start + 2 * image_rows])
            turned = cmul(part, (phase_ref[0], phase_ref[1]))
            left = jnp.concatenate([turned[0].astype(bf16), turned[1].astype(bf16)], axis=1)
            late = shifts[:, :1] > index.astype(f32)
            table = jnp.where(late, after[...], here[...])
            right = jnp.concatenate(
                [table, jnp.concatenate([-table[:, FINE:], table[:, :FINE]], axis=1)], axis=0
            )
            sums = jnp.dot(left, right, preferred_element_type=f32)
            twist = twist_ref[pl.ds(index, 1), :]
            done = cmul((sums[:, :FINE], sums[:, FINE:]), (twist[:, :FINE], twist[:, FINE:]))

            if chunks == 1:
                total[index, 0] = done[0]
                total[index, 1] = done[1]
            else:
                @pl.when(chunk == 0)
                def _():
                    total[index, 0] = done[0]
                    total[index, 1] = done[1]

                @pl.when(chunk > 0)
                def _():
                    total[index, 0] += done[0]
                    total[index, 1] += done[1]

    @pl.when(step >= chunks * HALF)
    def _():
        first = (step - chunks * HALF) * row_block
        wide = 2 * G // LANES

        def eight_rows(group, carry):
            at = pl.ds(pl.multiple_of(first + 8 * group, 8), 8)
            for tile in range(FINE // LANES):
                lanes = pl.ds(tile * LANES, LANES)
                values = [(total[n, 0, at, lanes], total[n, 1, at, lanes]) for n in range(SUB)]
                for k, value in enumerate(short_transform(values)):
                    for part in range(2):
                        column = 2 * (k * (FINE // LANES) + tile) + part
                        out_ref[pl.ds(group * 8 * wide + column, 8, stride=wide), :] = value[part]
            return carry

        lax.fori_loop(0, row_block // 8, eight_rows, 0)


def image_rows_of(uv, corners_all, first_row, image_rows, interpret=False):
    total = corners_all[0].shape[0]
    size = math.gcd(total, CHUNK) if len(uv) == 1 else total
    chunks = total // size
    row_block = math.gcd(image_rows, 32)
    outs = image_rows // row_block
    wide = 2 * G // LANES
    rows = first_row + jnp.arange(image_rows, dtype=jnp.int32)
    turn = 2.0 * math.pi / G
    angle = turn * (rows[:, None] * corners_all[1][None, :] % G).astype(f32)
    phase = jnp.stack([jnp.cos(angle), jnp.sin(angle)])
    angle = turn * (rows[:, None] * jnp.arange(SUB, dtype=jnp.int32)[None, :] % G).astype(f32)
    re, im = jnp.cos(angle), jnp.sin(angle)
    block = jnp.concatenate(
        [jnp.concatenate([re, -im], axis=1), jnp.concatenate([im, re], axis=1)], axis=0
    )
    columns = jnp.kron(jnp.eye(2, dtype=f32), block).astype(bf16)
    fine = jnp.arange(FINE, dtype=jnp.int32)
    angle = 2.0 * math.pi / FINE * (fine[:, None] * fine[None, :] % FINE).astype(f32)
    unit = jnp.concatenate([jnp.cos(angle), jnp.sin(angle)], axis=1).astype(bf16)
    angle = turn * (jnp.arange(SUB, dtype=jnp.int32)[:, None] * fine[None, :]).astype(f32)
    scale = 1.0 / (SUB * math.sqrt(total))
    twist = jnp.concatenate([jnp.cos(angle), jnp.sin(angle)], axis=1) * scale
    counts = jnp.broadcast_to(jnp.arange(SUB, dtype=f32)[:, None], (SUB, LANES)).astype(bf16)
    last = chunks - 1

    def chunk_of(i):
        return jnp.minimum(i // HALF, last)

    result = pl.pallas_call(
        functools.partial(image_kernel, pieces=len(uv), chunks=chunks, row_block=row_block),
        grid=(chunks * HALF + outs,),
        in_specs=[
            *[pl.BlockSpec((size * HALF // len(uv), PACK), lambda i: (chunk_of(i), 0))] * len(uv),
            pl.BlockSpec((1, size), lambda i: (0, chunk_of(i))),
            pl.BlockSpec((2, image_rows, size), lambda i: (0, 0, chunk_of(i))),
            pl.BlockSpec(columns.shape, lambda i: (0, 0)),
            pl.BlockSpec(unit.shape, lambda i: (0, 0)),
            pl.BlockSpec(counts.shape, lambda i: (0, 0)),
            pl.BlockSpec(twist.shape, lambda i: (0, 0)),
        ],
        out_specs=pl.BlockSpec(
            (row_block * wide, LANES), lambda i: (jnp.maximum(i - chunks * HALF, 0), 0)
        ),
        out_shape=jax.ShapeDtypeStruct((image_rows * wide, LANES), f32),
        scratch_shapes=[
            pltpu.VMEM((size * HALF, PACK), f32),
            pltpu.VMEM((size, 2 * FINE), bf16),
            pltpu.VMEM((size, 2 * FINE), bf16),
            pltpu.VMEM((size, LANES), f32),
            pltpu.VMEM((SUB, 2, image_rows, FINE), f32),
        ],
        compiler_params=pltpu.CompilerParams(vmem_limit_bytes=VMEM_BYTES),
        name="image",
        interpret=interpret,
    )(
        *[piece.reshape(-1, PACK) for piece in uv], corners_all[0].reshape(1, total),
        phase, columns, unit, counts, twist,
    )
    result = result.reshape(image_rows, G // LANES, 2, LANES)
    return jnp.transpose(result, (0, 2, 1, 3)).reshape(image_rows, 2, G)


def packed_beams(beam_terms):
    count = beam_terms.shape[0]
    parts = beam_terms.reshape(count, 2, 2, HALF, SUB)
    return jnp.transpose(parts, (0, 3, 2, 1, 4)).reshape(count, HALF, PACK)


def pixel_factor(screen_depth, shift, vis_count):
    lane = jnp.arange(PACK, dtype=jnp.int32)
    col = lane % SUB
    imag = (lane // SUB) % 2
    row = jnp.arange(HALF, dtype=jnp.int32)[:, None] + (lane // (2 * SUB) * HALF)[None, :]

    def taper(x):
        return 1.0 - ((2.0 * x.astype(f32) + 1.0 - SUB) / SUB) ** 2

    def angle_sq(x):
        return ((x - HALF).astype(f32) * (field_view / SUB)) ** 2

    weight = taper(row) * taper(col) / math.sqrt(vis_count)
    turns = shift[:, None, None] * (row - HALF) % SUB
    angle = (
        -math.pi * screen_depth[:, None, None] * (angle_sq(row) + angle_sq(col))
        + 2.0 * math.pi / SUB * turns.astype(f32)
        - 0.5 * math.pi * imag.astype(f32)
    )
    return jnp.cos(angle) * weight


def from_partner(value, axis, mask):
    count = lax.axis_size(axis)
    return lax.ppermute(value, axis, [(i, i ^ mask) for i in range(count)])


def z_line(own):
    vert_count = lax.axis_size("vert")
    line = [own] + [from_partner(own, "vert", 2 * mask) for mask in range(1, vert_count // 2)]
    return jnp.concatenate(line, axis=0)


def au_lines(line):
    return [line] + [from_partner(line, "au", mask) for mask in range(1, lax.axis_size("au"))]


def with_core(lines):
    return [piece for line in lines for piece in (line, from_partner(line, "vert", 1))]


def whole_gather(own):
    return [lax.all_gather(own, ("au", "vert"), axis=0, tiled=True)]


def gathered_place(owner, by_mask):
    if not by_mask:
        return owner
    vert_count = lax.axis_size("vert")
    au_mask = (owner // vert_count) ^ lax.axis_index("au")
    vert_mask = (owner % vert_count) ^ lax.axis_index("vert")
    return au_mask * vert_count + vert_mask % 2 * (vert_count // 2) + vert_mask // 2


def coded_corners(corners):
    digits = jnp.stack([corners[:, 0] // 128, corners[:, 0] % 128, corners[:, 1] // 128, corners[:, 1] % 128])
    flat = digits.astype(f32).astype(bf16).reshape(-1)
    return jnp.pad(flat, (0, HALF * PACK - flat.shape[0])).reshape(1, HALF, PACK)


def decoded_corners(blocks, count):
    digits = blocks.reshape(blocks.shape[0], HALF * PACK).astype(jnp.int32)
    high_row, low_row, high_col, low_col = [
        digits[:, i * count : (i + 1) * count].reshape(-1) for i in range(4)
    ]
    return (high_row * 128 + low_row, high_col * 128 + low_col)


def on_device(
    visibilities, baseline_offsets, channel_scale, screen_depth, stations, corners, beam_terms
):
    au_count = lax.axis_size("au")
    vert_count = lax.axis_size("vert")
    au_index, vert_index = lax.axis_index("au"), lax.axis_index("vert")
    image_rows = G // (au_count * vert_count)
    count, _, vis_count = visibilities.shape
    own_stations = beam_terms.shape[0]
    held = au_count * vert_count * count * HALF * PACK
    by_mask = held <= MASK_VALUES

    sent = jnp.concatenate([packed_beams(beam_terms), coded_corners(corners)], axis=0)
    offsets = baseline_offsets.reshape(2 * count, -1)
    scale_row = jnp.tile(channel_scale, baseline_offsets.shape[2]).reshape(1, vis_count)
    part = math.gcd(count, 8)
    skies = [sky_sums(visibilities, offsets, scale_row, 0, part)]
    if by_mask:
        line = z_line(sent)
        line, offsets, skies[0] = lax.optimization_barrier((line, offsets, skies[0]))
    for s in range(part, count, part):
        skies.append(sky_sums(visibilities, offsets, scale_row, s, part))
    factor = pixel_factor(screen_depth, corners[:, 0] % SUB, vis_count)
    if by_mask:
        lines = au_lines(line)
        lines, skies = lax.optimization_barrier((lines, skies))
        tables = with_core(lines)
    else:
        tables = whole_gather(sent)
    coded = [
        piece.reshape(-1, own_stations + 1, HALF, PACK)[:, own_stations] for piece in tables
    ]
    corners_all = decoded_corners(jnp.concatenate(coded, axis=0), count)
    owners = stations // own_stations
    station_rows = gathered_place(owners, by_mask) * (own_stations + 1) + stations % own_stations
    uv_own = corrected_subgrids(station_rows, tables, skies, factor)

    per_row = vert_count * count

    def row_place(index):
        return gathered_place(index * vert_count + vert_index, by_mask) // vert_count

    def places_of(place, spilled):
        chosen = [lax.dynamic_slice_in_dim(x, place * per_row, per_row) for x in corners_all]
        return tile_places(chosen, au_index, vert_index, au_count, vert_count, spilled)

    own_place = row_place(au_index)
    before_place = row_place(lax.rem(au_index + au_count - 1, au_count))
    own_list, spill_list = places_of(own_place, False), places_of(before_place, True)
    if by_mask:
        lines = au_lines(z_line(uv_own))
        own_row = with_core(lines[:1])
        tile = uv_tile_own(own_row, own_place, own_list, au_count, vert_count)
        lines, own_row, tile = lax.optimization_barrier((lines, own_row, tile))
        uv = own_row + with_core(lines[1:])
        before = [
            lax.select_n(before_place, *uv[core::2]) if au_count > 2 else uv[core + 2]
            for core in range(2)
        ]
        before_block = jnp.zeros((), jnp.int32)
    else:
        uv = before = whole_gather(uv_own)
        tile = uv_tile_own(uv, own_place, own_list, au_count, vert_count)
        before_block = before_place
    gridded = uv_tile_spill(tile, before, before_block, spill_list, au_count, vert_count)
    first_row = (au_index * vert_count + vert_index) * image_rows
    dirty_image = image_rows_of(uv, corners_all, first_row, image_rows)
    return (gridded, dirty_image)


def solution(mesh):
    return jax.shard_map(
        on_device,
        mesh=mesh,
        in_specs=(
            P(("au", "vert"), None, None),
            P(("au", "vert"), None, None),
            P(),
            P(("au", "vert")),
            P(("au", "vert"), None),
            P(("au", "vert"), None),
            P(("au", "vert"), None, None),
        ),
        out_specs=(P("au", None, "vert"), P(("au", "vert"), None, None)),
        check_vma=False,
    )
```

profile of v0, /device:TPU:0, one launch (start us, length us, event | category | flops | bytes accessed | tf_op | source)
XLA Modules:
  0.0 144.6 jit_solution(12221808882381866576)
XLA Ops:
  0.7 1.1 reshape.711
  1.7 0.2 copy.44
  2.0 0.2 reshape.712
  2.2 0.8 and_select_fusion.15
  3.1 3.1 %collective-permute-start = (bf16[17,16,128]{2,1,0:T(8,128)(2,1)S(1)}, bf16[17,16,128]{2,1,0:T(8,128)(2,1)S(1)}, u32[]{:S(2)}, u32[]{:S(2)}) collective-permute-start(bf16[17,16,128]{2,1,0:T(8,128)(2,1)S(1)} %pad_maximum_fusion.3), channel_id=1, source_target_pairs={{0,2},{1,3},{2,0},{3,1},{4,6},{5,7},{6,4},{7,5},{8,10},{9,11},{10,... | collective-permute-start | bytes 208904 | tf_op jit(solution)/shard_map/ppermute | solution.py:590
  6.2 2.6 %collective-permute-start.1 = (bf16[17,16,128]{2,1,0:T(8,128)(2,1)S(1)}, bf16[17,16,128]{2,1,0:T(8,128)(2,1)S(1)}, u32[]{:S(2)}, u32[]{:S(2)}) collective-permute-start(bf16[17,16,128]{2,1,0:T(8,128)(2,1)S(1)} %pad_maximum_fusion.3), channel_id=1, source_target_pairs={{0,4},{1,5},{2,6},{3,7},{4,0},{5,1},{6,2},{7,3},{8,12},{9,13},{10,... | collective-permute-start | bytes 208904 | tf_op jit(solution)/shard_map/ppermute | solution.py:590
  8.8 0.7 and_select_fusion.2
  9.5 1.1 sine_convert_fusion
  10.6 0.1 fusion.23
  10.8 0.7 reshape_tile.3.scale_ref
  11.5 0.2 fusion.37
  11.8 0.1 fusion.33
  12.0 0.2 multiply_convert_fusion
  12.3 0.1 multiply_convert_fusion.1
  12.4 0.6 pad_maximum_fusion.4.refs_13_
  13.0 0.7 pad_maximum_fusion.2.refs_11_
  13.7 0.6 maximum_multiply_fusion.refs_13_
  14.4 5.2 %sky_sums.3.refs_8_ = f32[8,16,128]{2,1,0:T(8,128)} custom-call(bf16[24,2,2048]{2,1,0:T(2,128)(2,1)} %vis_ref.5, f32[48,128]{1,0:T(8,128)} %bitcast.145, f32[1,2048]{1,0:T(1,128)} %reshape_tile.3.scale_ref), custom_call_target="tpu_custom_call" | custom-call | bytes 20000000 | tf_op jit(solution)/shard_map/sky_sums/pallas_call | solution.py:109
  19.7 1.8 %collective-permute-start.3 = (bf16[68,16,128]{2,1,0:T(8,128)(2,1)S(1)}, bf16[68,16,128]{2,1,0:T(8,128)(2,1)S(1)}, u32[]{:S(2)}, u32[]{:S(2)}) collective-permute-start(bf16[68,16,128]{2,1,0:T(8,128)(2,1)S(1)} %constant_dynamic-update-slice_fusion.refs_0_), channel_id=1, source_target_pairs={{0,8},{8,0},{16,24},{24,16},{1,9},{9,1},{17,25},{25,17},{2,10},{10... | collective-permute-start | bytes 835592 | tf_op jit(solution)/shard_map/ppermute | solution.py:590
  21.5 1.5 %collective-permute-start.4 = (bf16[68,16,128]{2,1,0:T(8,128)(2,1)S(1)}, bf16[68,16,128]{2,1,0:T(8,128)(2,1)S(1)}, u32[]{:S(2)}, u32[]{:S(2)}) collective-permute-start(bf16[68,16,128]{2,1,0:T(8,128)(2,1)S(1)} %constant_dynamic-update-slice_fusion.refs_0_), channel_id=1, source_target_pairs={{0,16},{8,24},{16,0},{24,8},{1,17},{9,25},{17,1},{25,9},{2,18},{10... | collective-permute-start | bytes 835592 | tf_op jit(solution)/shard_map/ppermute | solution.py:590
  23.0 0.3 collective-permute-start.5
  23.4 0.7 reshape.723.stations_ref
  24.1 0.7 convert_element_type.150.refs_12_
  24.8 0.9 copy.24.refs_10_
  25.7 1.5 %fusion.16.refs_11_ = f32[24,16,128]{2,1,0:T(8,128)} fusion(f32[16,128]{1,0:T(8,128)S(1)} %get-tuple-element.64, f32[128]{0:T(128)S(1)} %fusion.47, s32[16,128]{1,0:T(8,128)S(1)} %fusion.36, s32[24]{0:T(128)S(1)} %and_select_fusion.2, f32[16,128]{1,0:T(8,128)S(1)} %get-tuple-element.63, f32[24]{0:T(128)S(1)} %broadcast_multiply_fusion), kind=kLoop, calls=%fused_computation.38 | loop fusion | flops 884736 | bytes 221888 | tf_op jit(solution)/shard_map/mul | solution.py:585
  27.2 5.2 %sky_sums.4.refs_9_ = f32[8,16,128]{2,1,0:T(8,128)} custom-call(bf16[24,2,2048]{2,1,0:T(2,128)(2,1)} %vis_ref.5, f32[48,128]{1,0:T(8,128)} %bitcast.146, f32[1,2048]{1,0:T(1,128)} %reshape_tile.3.scale_ref), custom_call_target="tpu_custom_call" | custom-call | bytes 20000000 | tf_op jit(solution)/shard_map/sky_sums/pallas_call | solution.py:109
  32.4 5.4 %sky_sums.5.refs_10_ = f32[8,16,128]{2,1,0:T(8,128)} custom-call(bf16[24,2,2048]{2,1,0:T(2,128)(2,1)} %vis_ref.5, f32[48,128]{1,0:T(8,128)} %bitcast.147, f32[1,2048]{1,0:T(1,128)} %reshape_tile.3.scale_ref), custom_call_target="tpu_custom_call" | custom-call | bytes 20000000 | tf_op jit(solution)/shard_map/sky_sums/pallas_call | solution.py:109
  37.9 0.5 collective-permute-start.7
  38.4 0.4 collective-permute-start.9
  38.9 0.5 collective-permute-done.6.refs_1_
  39.4 0.4 collective-permute-done.7.refs_3_
  39.8 0.4 collective-permute-done.8.refs_5_
  40.2 0.4 collective-permute-done.9.refs_7_
  40.6 0.3 copy-done.16
  40.9 0.7 copy-done.17
  41.6 6.7 %correct.1 = bf16[24,16,128]{2,1,0:T(8,128)(2,1)} custom-call(s32[48]{0:T(128)} %reshape.723.stations_ref, bf16[68,16,128]{2,1,0:T(8,128)(2,1)} %copy-done.9, bf16[68,16,128]{2,1,0:T(8,128)(2,1)} %copy-done.14, bf16[68,16,128]{2,1,0:T(8,128)(2,1)} %copy-done.11, bf16[68,16,128]{2,1,0:T(8,128)(2,1)} %copy-done.15, bf16[68,16,128]{2,1,0:T(8,128)(2,1)} %copy-done.12, ...), custom_call_target="tpu_custom_call" | custom-call | bytes 16000000 | tf_op jit(solution)/shard_map/correct/pallas_call | solution.py:193
  48.3 3.8 %collective-permute-start.12 = (bf16[24,16,128]{2,1,0:T(8,128)(2,1)}, bf16[24,16,128]{2,1,0:T(8,128)(2,1)S(1)}, u32[]{:S(2)}, u32[]{:S(2)}) collective-permute-start(bf16[24,16,128]{2,1,0:T(8,128)(2,1)} %correct.1), channel_id=1, source_target_pairs={{0,6},{1,7},{2,4},{3,5},{4,2},{5,3},{6,0},{7,1},{8,14},{9,15},{10,... | collective-permute-start | bytes 294920 | tf_op jit(solution)/shard_map/ppermute | solution.py:590
  52.1 0.6 collective-permute-start.10
  52.7 0.7 slice_bitcast_fusion.6
  53.4 0.7 slice_bitcast_fusion.4
  54.2 0.7 slice_bitcast_fusion.2
  54.9 0.7 slice_bitcast_fusion
  55.6 0.1 concatenate.75
  56.1 3.1 %fusion.4 = (f32[1,256,768]{2,1,0:T(8,128)S(1)}, f32[1,256,768]{2,1,0:T(8,128)S(1)}) fusion(s32[768]{0:T(1024)S(1)} %add.360, s32[256]{0:T(256)S(1)} %iota_add_fusion.1), kind=kLoop, calls=%fused_computation.15 | loop fusion | flops 2752512 | bytes 1576960 | tf_op jit(solution)/shard_map/cos | solution.py:507
  59.2 1.4 convert_reduce_fusion.3
  60.6 0.1 convert_reduce_fusion
  60.7 0.1 select_reduce_fusion
  60.8 0.1 convert_reduce_fusion.1
  61.0 1.7 %collective-permute-start.13 = (bf16[96,16,128]{2,1,0:T(8,128)(2,1)S(1)}, bf16[96,16,128]{2,1,0:T(8,128)(2,1)S(1)}, u32[]{:S(2)}, u32[]{:S(2)}) collective-permute-start(bf16[96,16,128]{2,1,0:T(8,128)(2,1)S(1)} %pad_maximum_fusion.1), channel_id=1, source_target_pairs={{0,8},{8,0},{16,24},{24,16},{1,9},{9,1},{17,25},{25,17},{2,10},{10... | collective-permute-start | bytes 1179656 | tf_op jit(solution)/shard_map/ppermute | solution.py:590
  62.8 1.5 %collective-permute-start.14 = (bf16[96,16,128]{2,1,0:T(8,128)(2,1)S(1)}, bf16[96,16,128]{2,1,0:T(8,128)(2,1)S(1)}, u32[]{:S(2)}, u32[]{:S(2)}) collective-permute-start(bf16[96,16,128]{2,1,0:T(8,128)(2,1)S(1)} %pad_maximum_fusion.1), channel_id=1, source_target_pairs={{0,16},{8,24},{16,0},{24,8},{1,17},{9,25},{17,1},{25,9},{2,18},{10... | collective-permute-start | bytes 1179656 | tf_op jit(solution)/shard_map/ppermute | solution.py:590
  64.3 0.3 collective-permute-start.15
  64.6 1.3 pad_add_fusion.1.list_ref
  65.9 1.3 pad_maximum_fusion.refs_9_
  67.2 0.7 copy-done.1
  67.9 14.8 %uv_tile.1.refs_2_ = f32[32768,128]{1,0:T(8,128)} custom-call(s32[1]{0:T(128)} %bitcast.15.block_ref, s32[193]{0:T(256)} %pad_add_fusion.1.list_ref, s32[192]{0:T(256)} %get-tuple-element.49.row_ref, s32[192]{0:T(256)} %get-tuple-element.52.col_ref, bf16[1536,128]{1,0:T(8,128)(2,1)} %bitcast.122, bf16[1536,128]{1,0:T(8,128)(2,1)} %bitcast.124), custom_call_target="tpu_custom_call" | custom-call | bytes 41943040 | tf_op jit(solution)/shard_map/uv_tile/pallas_call | solution.py:330
  82.9 0.5 collective-permute-start.19
  83.4 0.1 select_reduce_fusion.1
  83.5 0.7 add.395.refs_8_
  84.2 1.3 pad_add_fusion.list_ref
  85.5 0.8 select_select_fusion.1
  86.4 1.0 select_select_fusion
  87.4 3.7 %uv_spill.1 = f32[32768,128]{1,0:T(8,128)} custom-call(s32[1]{0:T(128)} %constant.323.clone.1.block_ref, s32[193]{0:T(256)} %pad_add_fusion.list_ref, s32[192]{0:T(256)} %get-tuple-element.40.row_ref, s32[192]{0:T(256)} %get-tuple-element.39.col_ref, bf16[1536,128]{1,0:T(8,128)(2,1)} %bitcast.126, ...), custom_call_target="tpu_custom_call", output_to_operand_aliasing={{}: (6, {})} | custom-call | bytes 8000000 | tf_op jit(solution)/shard_map/uv_spill/pallas_call | solution.py:358
  91.1 0.7 broadcast_in_dim.35.refs_12_
  91.8 52.6 %image.1 = f32[32768,128]{1,0:T(8,128)} custom-call(bf16[1536,128]{1,0:T(8,128)(2,1)} %bitcast.123, bf16[1536,128]{1,0:T(8,128)(2,1)} %bitcast.125, bf16[1536,128]{1,0:T(8,128)(2,1)} %bitcast.128, bf16[1536,128]{1,0:T(8,128)(2,1)} %bitcast.133, bf16[1536,128]{1,0:T(8,128)(2,1)} %bitcast.129, bf16[1536,128]{1,0:T(8,128)(2,1)} %bitcast.131, ...), custom_call_target="tpu_custom_call" | custom-call | tf_op jit(solution)/shard_map/image/pallas_call | solution.py:526
  (108 shorter events, 1.4 us)
Async XLA Ops:
  0.6 10.1 %copy-start.19 = (f32[16]{0:T(128)S(1)}, f32[16]{0:T(128)}, u32[]{:S(2)}) copy-start(f32[16]{0:T(128)} %param.9) | copy-start | bytes 196
  0.6 10.8 %copy-start.18 = (s32[24,2]{0,1:T(2,128)S(1)}, s32[24,2]{0,1:T(2,128)}, u32[]{:S(2)}) copy-start(s32[24,2]{0,1:T(2,128)} %param.11) | copy-start | bytes 580
  0.7 10.9 %copy-start.20 = (f32[24]{0:T(128)S(1)}, f32[24]{0:T(128)}, u32[]{:S(2)}) copy-start(f32[24]{0:T(128)} %param.10) | copy-start | bytes 292
  3.1 16.6 %collective-permute-start = (bf16[17,16,128]{2,1,0:T(8,128)(2,1)S(1)}, bf16[17,16,128]{2,1,0:T(8,128)(2,1)S(1)}, u32[]{:S(2)}, u32[]{:S(2)}) collective-permute-start(bf16[17,16,128]{2,1,0:T(8,128)(2,1)S(1)} %pad_maximum_fusion.3), channel_id=1, source_target_pairs={{0,2},{1,3},{2,0},{3,1},{4,6},{5,7},{6,4},{7,5},{8,10},{9,11},{10,... | collective-permute-start | bytes 208904 | tf_op jit(solution)/shard_map/ppermute | solution.py:590
  6.2 13.5 %collective-permute-start.1 = (bf16[17,16,128]{2,1,0:T(8,128)(2,1)S(1)}, bf16[17,16,128]{2,1,0:T(8,128)(2,1)S(1)}, u32[]{:S(2)}, u32[]{:S(2)}) collective-permute-start(bf16[17,16,128]{2,1,0:T(8,128)(2,1)S(1)} %pad_maximum_fusion.3), channel_id=1, source_target_pairs={{0,4},{1,5},{2,6},{3,7},{4,0},{5,1},{6,2},{7,3},{8,12},{9,13},{10,... | collective-permute-start | bytes 208904 | tf_op jit(solution)/shard_map/ppermute | solution.py:590
  8.7 10.9 %collective-permute-start.2 = (bf16[17,16,128]{2,1,0:T(8,128)(2,1)S(1)}, bf16[17,16,128]{2,1,0:T(8,128)(2,1)S(1)}, u32[]{:S(2)}, u32[]{:S(2)}) collective-permute-start(bf16[17,16,128]{2,1,0:T(8,128)(2,1)S(1)} %pad_maximum_fusion.3), channel_id=1, source_target_pairs={{0,6},{1,7},{2,4},{3,5},{4,2},{5,3},{6,0},{7,1},{8,14},{9,15},{10,... | collective-permute-start | bytes 208904 | tf_op jit(solution)/shard_map/ppermute | solution.py:590
  19.7 20.9 %copy-start.9 = (bf16[68,16,128]{2,1,0:T(8,128)(2,1)}, bf16[68,16,128]{2,1,0:T(8,128)(2,1)S(1)}, u32[]{:S(2)}) copy-start(bf16[68,16,128]{2,1,0:T(8,128)(2,1)S(1)} %constant_dynamic-update-slice_fusion.refs_0_) | copy-start | bytes 835588
  19.7 18.0 %collective-permute-start.3 = (bf16[68,16,128]{2,1,0:T(8,128)(2,1)S(1)}, bf16[68,16,128]{2,1,0:T(8,128)(2,1)S(1)}, u32[]{:S(2)}, u32[]{:S(2)}) collective-permute-start(bf16[68,16,128]{2,1,0:T(8,128)(2,1)S(1)} %constant_dynamic-update-slice_fusion.refs_0_), channel_id=1, source_target_pairs={{0,8},{8,0},{16,24},{24,16},{1,9},{9,1},{17,25},{25,17},{2,10},{10... | collective-permute-start | bytes 835592 | tf_op jit(solution)/shard_map/ppermute | solution.py:590
  21.5 16.3 %collective-permute-start.4 = (bf16[68,16,128]{2,1,0:T(8,128)(2,1)S(1)}, bf16[68,16,128]{2,1,0:T(8,128)(2,1)S(1)}, u32[]{:S(2)}, u32[]{:S(2)}) collective-permute-start(bf16[68,16,128]{2,1,0:T(8,128)(2,1)S(1)} %constant_dynamic-update-slice_fusion.refs_0_), channel_id=1, source_target_pairs={{0,16},{8,24},{16,0},{24,8},{1,17},{9,25},{17,1},{25,9},{2,18},{10... | collective-permute-start | bytes 835592 | tf_op jit(solution)/shard_map/ppermute | solution.py:590
  23.0 14.7 %collective-permute-start.5 = (bf16[68,16,128]{2,1,0:T(8,128)(2,1)S(1)}, bf16[68,16,128]{2,1,0:T(8,128)(2,1)S(1)}, u32[]{:S(2)}, u32[]{:S(2)}) collective-permute-start(bf16[68,16,128]{2,1,0:T(8,128)(2,1)S(1)} %constant_dynamic-update-slice_fusion.refs_0_), channel_id=1, source_target_pairs={{0,24},{8,16},{16,8},{24,0},{1,25},{9,17},{17,9},{25,1},{2,26},{10... | collective-permute-start | bytes 835592 | tf_op jit(solution)/shard_map/ppermute | solution.py:590
  37.7 2.9 %copy-start.11 = (bf16[68,16,128]{2,1,0:T(8,128)(2,1)}, bf16[68,16,128]{2,1,0:T(8,128)(2,1)S(1)}, u32[]{:S(2)}) copy-start(bf16[68,16,128]{2,1,0:T(8,128)(2,1)S(1)} %collective-permute-done.3.refs_2_) | copy-start | bytes 835588
  37.7 2.9 %copy-start.12 = (bf16[68,16,128]{2,1,0:T(8,128)(2,1)}, bf16[68,16,128]{2,1,0:T(8,128)(2,1)S(1)}, u32[]{:S(2)}) copy-start(bf16[68,16,128]{2,1,0:T(8,128)(2,1)S(1)} %collective-permute-done.4.refs_4_) | copy-start | bytes 835588
  37.8 2.8 %copy-start.13 = (bf16[68,16,128]{2,1,0:T(8,128)(2,1)}, bf16[68,16,128]{2,1,0:T(8,128)(2,1)S(1)}, u32[]{:S(2)}) copy-start(bf16[68,16,128]{2,1,0:T(8,128)(2,1)S(1)} %collective-permute-done.5.refs_6_) | copy-start | bytes 835588
  37.8 1.6 %collective-permute-start.6 = (bf16[68,16,128]{2,1,0:T(8,128)(2,1)S(1)}, bf16[68,16,128]{2,1,0:T(8,128)(2,1)S(1)}, u32[]{:S(2)}, u32[]{:S(2)}) collective-permute-start(bf16[68,16,128]{2,1,0:T(8,128)(2,1)S(1)} %constant_dynamic-update-slice_fusion.refs_0_), channel_id=1, source_target_pairs={{0,1},{1,0},{2,3},{3,2},{4,5},{5,4},{6,7},{7,6},{8,9},{9,8},{10,11... | collective-permute-start | bytes 835592 | tf_op jit(solution)/shard_map/ppermute | solution.py:590
  37.9 1.9 %collective-permute-start.7 = (bf16[68,16,128]{2,1,0:T(8,128)(2,1)S(1)}, bf16[68,16,128]{2,1,0:T(8,128)(2,1)S(1)}, u32[]{:S(2)}, u32[]{:S(2)}) collective-permute-start(bf16[68,16,128]{2,1,0:T(8,128)(2,1)S(1)} %collective-permute-done.3.refs_2_), channel_id=1, source_target_pairs={{0,1},{1,0},{2,3},{3,2},{4,5},{5,4},{6,7},{7,6},{8,9},{9,8},{10,11... | collective-permute-start | bytes 835592 | tf_op jit(solution)/shard_map/ppermute | solution.py:590
  38.3 1.8 %collective-permute-start.8 = (bf16[68,16,128]{2,1,0:T(8,128)(2,1)S(1)}, bf16[68,16,128]{2,1,0:T(8,128)(2,1)S(1)}, u32[]{:S(2)}, u32[]{:S(2)}) collective-permute-start(bf16[68,16,128]{2,1,0:T(8,128)(2,1)S(1)} %collective-permute-done.4.refs_4_), channel_id=1, source_target_pairs={{0,1},{1,0},{2,3},{3,2},{4,5},{5,4},{6,7},{7,6},{8,9},{9,8},{10,11... | collective-permute-start | bytes 835592 | tf_op jit(solution)/shard_map/ppermute | solution.py:590
  38.4 2.2 %collective-permute-start.9 = (bf16[68,16,128]{2,1,0:T(8,128)(2,1)S(1)}, bf16[68,16,128]{2,1,0:T(8,128)(2,1)S(1)}, u32[]{:S(2)}, u32[]{:S(2)}) collective-permute-start(bf16[68,16,128]{2,1,0:T(8,128)(2,1)S(1)} %collective-permute-done.5.refs_6_), channel_id=1, source_target_pairs={{0,1},{1,0},{2,3},{3,2},{4,5},{5,4},{6,7},{7,6},{8,9},{9,8},{10,11... | collective-permute-start | bytes 835592 | tf_op jit(solution)/shard_map/ppermute | solution.py:590
  39.4 1.2 copy-start.14
  39.8 0.8 copy-start.15
  40.2 0.7 copy-start.16
  40.9 0.7 copy-start.17
  48.2 12.7 %copy-start.10 = (bf16[24,16,128]{2,1,0:T(8,128)(2,1)S(1)}, bf16[24,16,128]{2,1,0:T(8,128)(2,1)}, u32[]{:S(2)}) copy-start(bf16[24,16,128]{2,1,0:T(8,128)(2,1)} %correct.1) | copy-start | bytes 294916
  48.3 12.7 %collective-permute-start.12 = (bf16[24,16,128]{2,1,0:T(8,128)(2,1)}, bf16[24,16,128]{2,1,0:T(8,128)(2,1)S(1)}, u32[]{:S(2)}, u32[]{:S(2)}) collective-permute-start(bf16[24,16,128]{2,1,0:T(8,128)(2,1)} %correct.1), channel_id=1, source_target_pairs={{0,6},{1,7},{2,4},{3,5},{4,2},{5,3},{6,0},{7,1},{8,14},{9,15},{10,... | collective-permute-start | bytes 294920 | tf_op jit(solution)/shard_map/ppermute | solution.py:590
  52.1 8.9 %collective-permute-start.11 = (bf16[24,16,128]{2,1,0:T(8,128)(2,1)}, bf16[24,16,128]{2,1,0:T(8,128)(2,1)S(1)}, u32[]{:S(2)}, u32[]{:S(2)}) collective-permute-start(bf16[24,16,128]{2,1,0:T(8,128)(2,1)} %correct.1), channel_id=1, source_target_pairs={{0,4},{1,5},{2,6},{3,7},{4,0},{5,1},{6,2},{7,3},{8,12},{9,13},{10,... | collective-permute-start | bytes 294920 | tf_op jit(solution)/shard_map/ppermute | solution.py:590
  52.1 8.9 %collective-permute-start.10 = (bf16[24,16,128]{2,1,0:T(8,128)(2,1)}, bf16[24,16,128]{2,1,0:T(8,128)(2,1)S(1)}, u32[]{:S(2)}, u32[]{:S(2)}) collective-permute-start(bf16[24,16,128]{2,1,0:T(8,128)(2,1)} %correct.1), channel_id=1, source_target_pairs={{0,2},{1,3},{2,0},{3,1},{4,6},{5,7},{6,4},{7,5},{8,10},{9,11},{10,... | collective-permute-start | bytes 294920 | tf_op jit(solution)/shard_map/ppermute | solution.py:590
  61.0 6.2 %copy-start = (bf16[96,16,128]{2,1,0:T(8,128)(2,1)}, bf16[96,16,128]{2,1,0:T(8,128)(2,1)S(1)}, u32[]{:S(2)}) copy-start(bf16[96,16,128]{2,1,0:T(8,128)(2,1)S(1)} %pad_maximum_fusion.1) | copy-start | bytes 1179652
  61.0 21.7 %collective-permute-start.13 = (bf16[96,16,128]{2,1,0:T(8,128)(2,1)S(1)}, bf16[96,16,128]{2,1,0:T(8,128)(2,1)S(1)}, u32[]{:S(2)}, u32[]{:S(2)}) collective-permute-start(bf16[96,16,128]{2,1,0:T(8,128)(2,1)S(1)} %pad_maximum_fusion.1), channel_id=1, source_target_pairs={{0,8},{8,0},{16,24},{24,16},{1,9},{9,1},{17,25},{25,17},{2,10},{10... | collective-permute-start | bytes 1179656 | tf_op jit(solution)/shard_map/ppermute | solution.py:590
  62.8 20.0 %collective-permute-start.14 = (bf16[96,16,128]{2,1,0:T(8,128)(2,1)S(1)}, bf16[96,16,128]{2,1,0:T(8,128)(2,1)S(1)}, u32[]{:S(2)}, u32[]{:S(2)}) collective-permute-start(bf16[96,16,128]{2,1,0:T(8,128)(2,1)S(1)} %pad_maximum_fusion.1), channel_id=1, source_target_pairs={{0,16},{8,24},{16,0},{24,8},{1,17},{9,25},{17,1},{25,9},{2,18},{10... | collective-permute-start | bytes 1179656 | tf_op jit(solution)/shard_map/ppermute | solution.py:590
  64.3 18.5 %collective-permute-start.15 = (bf16[96,16,128]{2,1,0:T(8,128)(2,1)S(1)}, bf16[96,16,128]{2,1,0:T(8,128)(2,1)S(1)}, u32[]{:S(2)}, u32[]{:S(2)}) collective-permute-start(bf16[96,16,128]{2,1,0:T(8,128)(2,1)S(1)} %pad_maximum_fusion.1), channel_id=1, source_target_pairs={{0,24},{8,16},{16,8},{24,0},{1,25},{9,17},{17,9},{25,1},{2,26},{10... | collective-permute-start | bytes 1179656 | tf_op jit(solution)/shard_map/ppermute | solution.py:590
  64.6 2.6 %collective-permute-start.16 = (bf16[96,16,128]{2,1,0:T(8,128)(2,1)S(1)}, bf16[96,16,128]{2,1,0:T(8,128)(2,1)S(1)}, u32[]{:S(2)}, u32[]{:S(2)}) collective-permute-start(bf16[96,16,128]{2,1,0:T(8,128)(2,1)S(1)} %pad_maximum_fusion.1), channel_id=1, source_target_pairs={{0,1},{1,0},{2,3},{3,2},{4,5},{5,4},{6,7},{7,6},{8,9},{9,8},{10,11... | collective-permute-start | bytes 1179656 | tf_op jit(solution)/shard_map/ppermute | solution.py:590
  67.2 0.7 copy-start.1
  82.7 3.7 %copy-start.2 = (bf16[96,16,128]{2,1,0:T(8,128)(2,1)S(1)}, bf16[96,16,128]{2,1,0:T(8,128)(2,1)}, u32[]{:S(2)}) copy-start(bf16[96,16,128]{2,1,0:T(8,128)(2,1)} %copy-done.1) | copy-start | bytes 1179652
  82.7 4.7 %copy-start.3 = (bf16[96,16,128]{2,1,0:T(8,128)(2,1)}, bf16[96,16,128]{2,1,0:T(8,128)(2,1)S(1)}, u32[]{:S(2)}) copy-start(bf16[96,16,128]{2,1,0:T(8,128)(2,1)S(1)} %collective-permute-done.13) | copy-start | bytes 1179652
  82.7 4.6 %copy-start.4 = (bf16[96,16,128]{2,1,0:T(8,128)(2,1)}, bf16[96,16,128]{2,1,0:T(8,128)(2,1)S(1)}, u32[]{:S(2)}) copy-start(bf16[96,16,128]{2,1,0:T(8,128)(2,1)S(1)} %collective-permute-done.14) | copy-start | bytes 1179652
  82.8 4.6 %copy-start.5 = (bf16[96,16,128]{2,1,0:T(8,128)(2,1)}, bf16[96,16,128]{2,1,0:T(8,128)(2,1)S(1)}, u32[]{:S(2)}) copy-start(bf16[96,16,128]{2,1,0:T(8,128)(2,1)S(1)} %collective-permute-done.15) | copy-start | bytes 1179652
  82.8 3.6 %collective-permute-start.18 = (bf16[96,16,128]{2,1,0:T(8,128)(2,1)S(1)}, bf16[96,16,128]{2,1,0:T(8,128)(2,1)S(1)}, u32[]{:S(2)}, u32[]{:S(2)}) collective-permute-start(bf16[96,16,128]{2,1,0:T(8,128)(2,1)S(1)} %collective-permute-done.14), channel_id=1, source_target_pairs={{0,1},{1,0},{2,3},{3,2},{4,5},{5,4},{6,7},{7,6},{8,9},{9,8},{10,11... | collective-permute-start | bytes 1179656 | tf_op jit(solution)/shard_map/ppermute | solution.py:590
  82.9 3.5 %collective-permute-start.19 = (bf16[96,16,128]{2,1,0:T(8,128)(2,1)S(1)}, bf16[96,16,128]{2,1,0:T(8,128)(2,1)S(1)}, u32[]{:S(2)}, u32[]{:S(2)}) collective-permute-start(bf16[96,16,128]{2,1,0:T(8,128)(2,1)S(1)} %collective-permute-done.15), channel_id=1, source_target_pairs={{0,1},{1,0},{2,3},{3,2},{4,5},{5,4},{6,7},{7,6},{8,9},{9,8},{10,11... | collective-permute-start | bytes 1179656 | tf_op jit(solution)/shard_map/ppermute | solution.py:590
  83.4 3.0 %collective-permute-start.17 = (bf16[96,16,128]{2,1,0:T(8,128)(2,1)S(1)}, bf16[96,16,128]{2,1,0:T(8,128)(2,1)S(1)}, u32[]{:S(2)}, u32[]{:S(2)}) collective-permute-start(bf16[96,16,128]{2,1,0:T(8,128)(2,1)S(1)} %collective-permute-done.13), channel_id=1, source_target_pairs={{0,1},{1,0},{2,3},{3,2},{4,5},{5,4},{6,7},{7,6},{8,9},{9,8},{10,11... | collective-permute-start | bytes 1179656 | tf_op jit(solution)/shard_map/ppermute | solution.py:590
  86.4 4.7 %copy-start.6 = (bf16[96,16,128]{2,1,0:T(8,128)(2,1)}, bf16[96,16,128]{2,1,0:T(8,128)(2,1)S(1)}, u32[]{:S(2)}) copy-start(bf16[96,16,128]{2,1,0:T(8,128)(2,1)S(1)} %collective-permute-done.18) | copy-start | bytes 1179652
  86.4 4.7 %copy-start.7 = (bf16[96,16,128]{2,1,0:T(8,128)(2,1)}, bf16[96,16,128]{2,1,0:T(8,128)(2,1)S(1)}, u32[]{:S(2)}) copy-start(bf16[96,16,128]{2,1,0:T(8,128)(2,1)S(1)} %collective-permute-done.19) | copy-start | bytes 1179652
  86.4 4.7 %copy-start.8 = (bf16[96,16,128]{2,1,0:T(8,128)(2,1)}, bf16[96,16,128]{2,1,0:T(8,128)(2,1)S(1)}, u32[]{:S(2)}) copy-start(bf16[96,16,128]{2,1,0:T(8,128)(2,1)S(1)} %collective-permute-done.17) | copy-start | bytes 1179652
where the time goes:
time: 146 us; the launch traced here: 145 us
  Pallas kernels  93.5 us (64%)
  starting transfers between devices  19 us (13%)
  other arithmetic  17.9 us (12%)
  local copies, waits for them, and re-layouts  11.2 us (8%)
  waiting for transfers between devices  1.69 us (1%)
    pallas_call x1, Pallas kernels, image_rows_of(): pl.pallas_call(functools.partial(image_kernel, pieces=len(uv), chunks=chu...  52.6 us
    ppermute x20, starting transfers between devices, from_partner(): return lax.ppermute(value, axis, [(i, i ^ mask) for i in range(count)])  19 us
    pallas_call x3, Pallas kernels, sky_sums(): pl.pallas_call(sky_kernel, grid=(1,), in_specs=[pl.BlockSpec((count, 2, v...  15.8 us
    pallas_call x1, Pallas kernels, uv_tile_own(): pl.pallas_call(functools.partial(tile_kernel, pieces=len(uv), tile_rows=t...  14.8 us
    pallas_call x1, Pallas kernels, corrected_subgrids(): pl.pallas_call(functools.partial(correct_kernel, pieces=len(tables), skie...  6.66 us
    unnamed x63, local copies, waits for them, and re-layouts  4.83 us
    pallas_call x1, Pallas kernels, uv_tile_spill(): pl.pallas_call(functools.partial(spill_kernel, pieces=len(uv), lanes=lane...  3.69 us
    cos x1, other arithmetic, image_rows_of(): phase = jnp.stack([jnp.cos(angle), jnp.sin(angle)])  3.13 us
  transfers between devices with their start and end apart: 20, of which 4 were waited for; matrix products, arithmetic and copies ran while one was open for 16% of the time, Pallas kernels for 21%

commit v1 on v0

--- a/solution.py
+++ b/solution.py
@@ -407,77 +407,87 @@
     return low + high
 
 
-def image_kernel(
-    *refs, pieces, chunks, row_block
-):
+def image_kernel(*refs, pieces, chunks, row_block):
     uv_refs, refs = refs[:pieces], refs[pieces:]
     corner_ref, phase_ref, columns_ref, unit_ref, count_ref, twist_ref = refs[:6]
-    out_ref, uv_wide, here, after, shifts, total = refs[6:]
+    out_ref, uv_wide, here, after, shifts, left_even, left_odd, total = refs[6:]
     step = pl.program_id(0)
     size = uv_wide.shape[0] // HALF
     image_rows = phase_ref.shape[1]
 
-    @pl.when(step < chunks * HALF)
+    def products(pair, h, left):
+        rows = uv_wide[pl.ds(pair, size, stride=HALF), :].astype(bf16)
+        at = pl.ds(2 * image_rows * h, 2 * image_rows)
+        spread = lax.dot_general(
+            columns_ref[at, :], rows, (((1,), (1,)), ((), ())), preferred_element_type=f32
+        ).astype(bf16)
+        turned = cmul((spread[:image_rows], spread[image_rows:]), (phase_ref[0], phase_ref[1]))
+        left[h, :image_rows] = turned[0]
+        left[h, image_rows:] = turned[1]
+
+    def sums(pair, h, left, first):
+        index = pair + HALF * h
+        late = shifts[...] > index.astype(f32)
+        table = jnp.concatenate(
+            [
+                jnp.where(late, after[:, t : t + LANES], here[:, t : t + LANES])
+                for t in range(0, 2 * FINE, LANES)
+            ],
+            axis=1,
+        )
+        four = jnp.dot(left[h], table, preferred_element_type=f32)
+        got = (
+            four[:image_rows, :FINE] - four[image_rows:, FINE:],
+            four[:image_rows, FINE:] + four[image_rows:, :FINE],
+        )
+        twist = twist_ref[pl.ds(index, 1), :]
+        done = cmul(got, (twist[:, :FINE], twist[:, FINE:]))
+        for part in range(2):
+            total[index, part] = done[part] if first else total[index, part] + done[part]
+
+    def chunk(first):
+        held = 0
+        for piece in uv_refs:
+            uv_wide[held : held + piece.shape[0]] = piece[...].astype(f32)
+            held += piece.shape[0]
+        corner = corner_ref[...]
+        coarse, shift = corner // SUB, corner % SUB
+
+        def looked_up(index, length, table):
+            place = lax.broadcasted_iota(jnp.int32, (length, size), 0)
+            one = (place == index).astype(f32).astype(bf16)
+            return lax.dot_general(one, table, (((0,), (0,)), ((), ())), preferred_element_type=f32)
+
+        here[...] = looked_up(coarse, FINE, unit_ref[...]).astype(bf16)
+        after[...] = looked_up(lax.rem(coarse + 1, FINE), FINE, unit_ref[...]).astype(bf16)
+        shifts[...] = looked_up(shift, SUB, count_ref[...])
+        for h in range(2):
+            products(0, h, left_even)
+
+        def two_pairs(i, carry):
+            for h in range(2):
+                products(2 * i + 1, h, left_odd)
+                sums(2 * i, h, left_even, first)
+            for h in range(2):
+                products(jnp.minimum(2 * i + 2, HALF - 1), h, left_even)
+                sums(2 * i + 1, h, left_odd, first)
+            return carry
+
+        lax.fori_loop(0, HALF // 2, two_pairs, 0)
+
+    @pl.when(step == 0)
     def _():
-        pair = lax.rem(step, HALF)
-        chunk = step // HALF
-
-        @pl.when(pair == 0)
+        chunk(True)
+
+    if chunks > 1:
+
+        @pl.when((step > 0) & (step < chunks))
         def _():
-            held = 0
-            for piece in uv_refs:
-                uv_wide[held : held + piece.shape[0]] = piece[...].astype(f32)
-                held += piece.shape[0]
-            corner = corner_ref[...]
-            coarse, shift = corner // SUB, corner % SUB
-
-            def looked_up(index, length, table):
-                place = lax.broadcasted_iota(jnp.int32, (length, size), 0)
-                one = (place == index).astype(f32).astype(bf16)
-                return lax.dot_general(
-                    one, table, (((0,), (0,)), ((), ())), preferred_element_type=f32
-                )
-
-            here[...] = looked_up(coarse, FINE, unit_ref[...]).astype(bf16)
-            after[...] = looked_up(lax.rem(coarse + 1, FINE), FINE, unit_ref[...]).astype(bf16)
-            shifts[...] = looked_up(shift, SUB, count_ref[...])
-
-        rows = uv_wide[pl.ds(pair, size, stride=HALF), :].astype(bf16)
-        spread = lax.dot_general(
-            columns_ref[...], rows, (((1,), (1,)), ((), ())), preferred_element_type=f32
-        )
-        for h in range(2):
-            index = pair + HALF * h
-            start = 2 * image_rows * h
-            part = (spread[start : start + image_rows], spread[start + image_rows : start + 2 * image_rows])
-            turned = cmul(part, (phase_ref[0], phase_ref[1]))
-            left = jnp.concatenate([turned[0].astype(bf16), turned[1].astype(bf16)], axis=1)
-            late = shifts[:, :1] > index.astype(f32)
-            table = jnp.where(late, after[...], here[...])
-            right = jnp.concatenate(
-                [table, jnp.concatenate([-table[:, FINE:], table[:, :FINE]], axis=1)], axis=0
-            )
-            sums = jnp.dot(left, right, preferred_element_type=f32)
-            twist = twist_ref[pl.ds(index, 1), :]
-            done = cmul((sums[:, :FINE], sums[:, FINE:]), (twist[:, :FINE], twist[:, FINE:]))
-
-            if chunks == 1:
-                total[index, 0] = done[0]
-                total[index, 1] = done[1]
-            else:
-                @pl.when(chunk == 0)
-                def _():
-                    total[index, 0] = done[0]
-                    total[index, 1] = done[1]
-
-                @pl.when(chunk > 0)
-                def _():
-                    total[index, 0] += done[0]
-                    total[index, 1] += done[1]
-
-    @pl.when(step >= chunks * HALF)
+            chunk(False)
+
+    @pl.when(step >= chunks)
     def _():
-        first = (step - chunks * HALF) * row_block
+        first = (step - chunks) * row_block
         wide = 2 * G // LANES
 
         def eight_rows(group, carry):
@@ -504,7 +514,7 @@
     rows = first_row + jnp.arange(image_rows, dtype=jnp.int32)
     turn = 2.0 * math.pi / G
     angle = turn * (rows[:, None] * corners_all[1][None, :] % G).astype(f32)
-    phase = jnp.stack([jnp.cos(angle), jnp.sin(angle)])
+    phase = jnp.stack([jnp.cos(angle), jnp.sin(angle)]).astype(bf16)
     angle = turn * (rows[:, None] * jnp.arange(SUB, dtype=jnp.int32)[None, :] % G).astype(f32)
     re, im = jnp.cos(angle), jnp.sin(angle)
     block = jnp.concatenate(
@@ -521,11 +531,11 @@
     last = chunks - 1
 
     def chunk_of(i):
-        return jnp.minimum(i // HALF, last)
+        return jnp.minimum(i, last)
 
     result = pl.pallas_call(
         functools.partial(image_kernel, pieces=len(uv), chunks=chunks, row_block=row_block),
-        grid=(chunks * HALF + outs,),
+        grid=(chunks + outs,),
         in_specs=[
             *[pl.BlockSpec((size * HALF // len(uv), PACK), lambda i: (chunk_of(i), 0))] * len(uv),
             pl.BlockSpec((1, size), lambda i: (0, chunk_of(i))),
@@ -536,7 +546,7 @@
             pl.BlockSpec(twist.shape, lambda i: (0, 0)),
         ],
         out_specs=pl.BlockSpec(
-            (row_block * wide, LANES), lambda i: (jnp.maximum(i - chunks * HALF, 0), 0)
+            (row_block * wide, LANES), lambda i: (jnp.maximum(i - chunks, 0), 0)
         ),
         out_shape=jax.ShapeDtypeStruct((image_rows * wide, LANES), f32),
         scratch_shapes=[
@@ -544,6 +554,8 @@
             pltpu.VMEM((size, 2 * FINE), bf16),
             pltpu.VMEM((size, 2 * FINE), bf16),
             pltpu.VMEM((size, LANES), f32),
+            pltpu.VMEM((2, 2 * image_rows, size), bf16),
+            pltpu.VMEM((2, 2 * image_rows, size), bf16),
             pltpu.VMEM((SUB, 2, image_rows, FINE), f32),
         ],
         compiler_params=pltpu.CompilerParams(vmem_limit_bytes=VMEM_BYTES),

time: 146 us -> 139 us (0.952)
  Pallas kernels: 93.5 us -> 81.4 us
  waiting for transfers between devices: 1.69 us -> 4.29 us
  other arithmetic: 17.9 us -> 20.1 us
    pallas_call x1, Pallas kernels: 52.6 us -> 44.4 us  [image_rows_of(): pl.pallas_call(functools.partial(image_kernel, pieces=len(uv), chunks=chu...]
    pallas_call x1, Pallas kernels: 14.8 us -> 11.1 us  [uv_tile_own(): pl.pallas_call(functools.partial(tile_kernel, pieces=len(uv), tile_rows=t...]
    another operation x3 -> x4, other arithmetic: 2.54 us -> 5.68 us  [the longest x1 1.28 us: image_rows_of(): phase = jnp.stack([jnp.cos(angle), jnp.sin(angle)])]
    cos x1 -> x0, other arithmetic: 3.13 us -> none  [image_rows_of(): phase = jnp.stack([jnp.cos(angle), jnp.sin(angle)])]
    ppermute x20, waiting for transfers between devices: 1.69 us -> 4.29 us  [from_partner(): return lax.ppermute(value, axis, [(i, i ^ mask) for i in range(count)])]
    unnamed x63 -> x53, local copies, waits for them, and re-layouts: 4.83 us -> 4.84 us
  transfers between devices with their start and end apart: 20 -> 20, of which waited for: 4 -> 5; matrix products, arithmetic and copies ran while one was open for 16% -> 18% of each run, Pallas kernels for 21% -> 19%
where the time goes in v1:
time: 139 us; the launch traced here: 138 us
  Pallas kernels  81.4 us (59%)
  other arithmetic  20.1 us (14%)
  starting transfers between devices  18.9 us (14%)
  local copies, waits for them, and re-layouts  11.8 us (8%)
  waiting for transfers between devices  4.29 us (3%)
    pallas_call x1, Pallas kernels, image_rows_of(): pl.pallas_call(functools.partial(image_kernel, pieces=len(uv), chunks=chu...  44.4 us
    ppermute x20, starting transfers between devices, from_partner(): return lax.ppermute(value, axis, [(i, i ^ mask) for i in range(count)])  18.9 us
    pallas_call x3, Pallas kernels, sky_sums(): pl.pallas_call(sky_kernel, grid=(1,), in_specs=[pl.BlockSpec((count, 2, v...  15.6 us
    pallas_call x1, Pallas kernels, uv_tile_own(): pl.pallas_call(functools.partial(tile_kernel, pieces=len(uv), tile_rows=t...  11.1 us
    pallas_call x1, Pallas kernels, corrected_subgrids(): pl.pallas_call(functools.partial(correct_kernel, pieces=len(tables), skie...  6.66 us
    unnamed x53, local copies, waits for them, and re-layouts  4.84 us
    another operation x3, other arithmetic  4.72 us
    ppermute x20, waiting for transfers between devices, from_partner(): return lax.ppermute(value, axis, [(i, i ^ mask) for i in range(count)])  4.29 us
  transfers between devices with their start and end apart: 20, of which 5 were waited for; matrix products, arithmetic and copies ran while one was open for 18% of the time, Pallas kernels for 19%

profile of v1, /device:TPU:0, one launch (start us, length us, event | category | flops | bytes accessed | tf_op | source)
XLA Modules:
  0.0 137.8 jit_solution(4539440335765096327)
XLA Ops:
  0.6 1.0 reshape.711
  1.7 0.2 copy.44
  1.9 0.2 reshape.712
  2.1 0.8 and_select_fusion.15
  3.0 3.1 %collective-permute-start = (bf16[17,16,128]{2,1,0:T(8,128)(2,1)S(1)}, bf16[17,16,128]{2,1,0:T(8,128)(2,1)S(1)}, u32[]{:S(2)}, u32[]{:S(2)}) collective-permute-start(bf16[17,16,128]{2,1,0:T(8,128)(2,1)S(1)} %pad_maximum_fusion.3), channel_id=1, source_target_pairs={{0,2},{1,3},{2,0},{3,1},{4,6},{5,7},{6,4},{7,5},{8,10},{9,11},{10,... | collective-permute-start | bytes 208904 | tf_op jit(solution)/shard_map/ppermute | solution.py:602
  6.1 2.6 %collective-permute-start.1 = (bf16[17,16,128]{2,1,0:T(8,128)(2,1)S(1)}, bf16[17,16,128]{2,1,0:T(8,128)(2,1)S(1)}, u32[]{:S(2)}, u32[]{:S(2)}) collective-permute-start(bf16[17,16,128]{2,1,0:T(8,128)(2,1)S(1)} %pad_maximum_fusion.3), channel_id=1, source_target_pairs={{0,4},{1,5},{2,6},{3,7},{4,0},{5,1},{6,2},{7,3},{8,12},{9,13},{10,... | collective-permute-start | bytes 208904 | tf_op jit(solution)/shard_map/ppermute | solution.py:602
  8.7 0.7 and_select_fusion.2
  9.4 1.1 sine_convert_fusion.1
  10.5 0.1 fusion.21
  10.7 0.7 tile.2
  11.4 0.7 reshape_tile.3.scale_ref
  12.0 0.7 fusion.41
  12.8 0.7 broadcast_multiply_fusion
  13.4 0.2 fusion.35
  13.7 0.1 fusion.31
  13.9 0.2 multiply_convert_fusion
  14.3 0.6 pad_maximum_fusion.4.refs_13_
  14.9 0.7 pad_maximum_fusion.2.refs_11_
  15.7 0.6 maximum_multiply_fusion.refs_13_
  16.3 5.2 %sky_sums.3.refs_8_ = f32[8,16,128]{2,1,0:T(8,128)} custom-call(bf16[24,2,2048]{2,1,0:T(2,128)(2,1)} %vis_ref.5, f32[48,128]{1,0:T(8,128)} %bitcast.145, f32[1,2048]{1,0:T(1,128)} %reshape_tile.3.scale_ref), custom_call_target="tpu_custom_call" | custom-call | bytes 20000000 | tf_op jit(solution)/shard_map/sky_sums/pallas_call | solution.py:109
  21.6 1.8 %collective-permute-start.3 = (bf16[68,16,128]{2,1,0:T(8,128)(2,1)S(1)}, bf16[68,16,128]{2,1,0:T(8,128)(2,1)S(1)}, u32[]{:S(2)}, u32[]{:S(2)}) collective-permute-start(bf16[68,16,128]{2,1,0:T(8,128)(2,1)S(1)} %constant_dynamic-update-slice_fusion.refs_0_), channel_id=1, source_target_pairs={{0,8},{8,0},{16,24},{24,16},{1,9},{9,1},{17,25},{25,17},{2,10},{10... | collective-permute-start | bytes 835592 | tf_op jit(solution)/shard_map/ppermute | solution.py:602
  23.4 1.5 %collective-permute-start.4 = (bf16[68,16,128]{2,1,0:T(8,128)(2,1)S(1)}, bf16[68,16,128]{2,1,0:T(8,128)(2,1)S(1)}, u32[]{:S(2)}, u32[]{:S(2)}) collective-permute-start(bf16[68,16,128]{2,1,0:T(8,128)(2,1)S(1)} %constant_dynamic-update-slice_fusion.refs_0_), channel_id=1, source_target_pairs={{0,16},{8,24},{16,0},{24,8},{1,17},{9,25},{17,1},{25,9},{2,18},{10... | collective-permute-start | bytes 835592 | tf_op jit(solution)/shard_map/ppermute | solution.py:602
  24.9 0.3 collective-permute-start.5
  25.2 0.7 reshape.723.stations_ref
  25.9 0.7 convert_element_type.151.refs_12_
  26.6 0.9 copy.24.refs_10_
  27.5 1.5 %fusion.14.refs_11_ = f32[24,16,128]{2,1,0:T(8,128)} fusion(f32[16,128]{1,0:T(8,128)S(1)} %get-tuple-element.64, f32[128]{0:T(128)S(1)} %fusion.45, s32[16,128]{1,0:T(8,128)S(1)} %fusion.34, s32[24]{0:T(128)S(1)} %and_select_fusion.2, f32[16,128]{1,0:T(8,128)S(1)} %get-tuple-element.63, f32[24]{0:T(128)S(1)} %broadcast_multiply_fusion), kind=kLoop, calls=%fused_computation.38 | loop fusion | flops 884736 | bytes 221888 | tf_op jit(solution)/shard_map/mul | solution.py:597
  29.0 5.2 %sky_sums.4.refs_9_ = f32[8,16,128]{2,1,0:T(8,128)} custom-call(bf16[24,2,2048]{2,1,0:T(2,128)(2,1)} %vis_ref.5, f32[48,128]{1,0:T(8,128)} %bitcast.146, f32[1,2048]{1,0:T(1,128)} %reshape_tile.3.scale_ref), custom_call_target="tpu_custom_call" | custom-call | bytes 20000000 | tf_op jit(solution)/shard_map/sky_sums/pallas_call | solution.py:109
  34.2 5.2 %sky_sums.5.refs_10_ = f32[8,16,128]{2,1,0:T(8,128)} custom-call(bf16[24,2,2048]{2,1,0:T(2,128)(2,1)} %vis_ref.5, f32[48,128]{1,0:T(8,128)} %bitcast.147, f32[1,2048]{1,0:T(1,128)} %reshape_tile.3.scale_ref), custom_call_target="tpu_custom_call" | custom-call | bytes 20000000 | tf_op jit(solution)/shard_map/sky_sums/pallas_call | solution.py:109
  39.6 0.5 collective-permute-start.7
  40.1 0.4 collective-permute-start.9
  40.6 0.5 collective-permute-done.6.refs_1_
  41.1 0.4 collective-permute-done.7.refs_3_
  41.5 0.4 collective-permute-done.8.refs_5_
  41.9 0.4 collective-permute-done.9.refs_7_
  42.3 0.3 copy-done.14
  42.6 0.7 copy-done.15
  43.3 6.7 %correct.1 = bf16[24,16,128]{2,1,0:T(8,128)(2,1)} custom-call(s32[48]{0:T(128)} %reshape.723.stations_ref, bf16[68,16,128]{2,1,0:T(8,128)(2,1)} %copy-done.8, bf16[68,16,128]{2,1,0:T(8,128)(2,1)} %copy-done.12, bf16[68,16,128]{2,1,0:T(8,128)(2,1)} %copy-done.9, bf16[68,16,128]{2,1,0:T(8,128)(2,1)} %copy-done.13, bf16[68,16,128]{2,1,0:T(8,128)(2,1)} %copy-done.10, ...), custom_call_target="tpu_custom_call" | custom-call | bytes 16000000 | tf_op jit(solution)/shard_map/correct/pallas_call | solution.py:193
  50.0 3.8 %collective-permute-start.12 = (bf16[24,16,128]{2,1,0:T(8,128)(2,1)}, bf16[24,16,128]{2,1,0:T(8,128)(2,1)S(1)}, u32[]{:S(2)}, u32[]{:S(2)}) collective-permute-start(bf16[24,16,128]{2,1,0:T(8,128)(2,1)} %correct.1), channel_id=1, source_target_pairs={{0,6},{1,7},{2,4},{3,5},{4,2},{5,3},{6,0},{7,1},{8,14},{9,15},{10,... | collective-permute-start | bytes 294920 | tf_op jit(solution)/shard_map/ppermute | solution.py:602
  53.8 0.6 collective-permute-start.10
  54.4 0.7 slice_bitcast_fusion.6
  55.1 0.7 slice_bitcast_fusion.4
  55.9 0.7 slice_bitcast_fusion.2
  56.6 0.7 slice_bitcast_fusion
  57.3 0.1 concatenate.75
  57.8 3.5 %cosine_convert_fusion = (bf16[1,256,768]{2,1,0:T(8,128)(2,1)S(1)}, bf16[1,256,768]{2,1,0:T(8,128)(2,1)S(1)}) fusion(s32[768]{0:T(1024)S(1)} %add.360, s32[256]{0:T(256)S(1)} %iota_add_fusion.1), kind=kLoop, calls=%fused_computation.10 | loop fusion | flops 3145728 | bytes 790528 | tf_op jit(solution)/shard_map/convert.2
  61.2 1.4 convert_reduce_fusion.3
  63.0 0.9 pad_maximum_fusion.1
  64.0 1.8 %collective-permute-start.13 = (bf16[96,16,128]{2,1,0:T(8,128)(2,1)S(1)}, bf16[96,16,128]{2,1,0:T(8,128)(2,1)S(1)}, u32[]{:S(2)}, u32[]{:S(2)}) collective-permute-start(bf16[96,16,128]{2,1,0:T(8,128)(2,1)S(1)} %pad_maximum_fusion.1), channel_id=1, source_target_pairs={{0,8},{8,0},{16,24},{24,16},{1,9},{9,1},{17,25},{25,17},{2,10},{10... | collective-permute-start | bytes 1179656 | tf_op jit(solution)/shard_map/ppermute | solution.py:602
  65.7 1.5 %collective-permute-start.14 = (bf16[96,16,128]{2,1,0:T(8,128)(2,1)S(1)}, bf16[96,16,128]{2,1,0:T(8,128)(2,1)S(1)}, u32[]{:S(2)}, u32[]{:S(2)}) collective-permute-start(bf16[96,16,128]{2,1,0:T(8,128)(2,1)S(1)} %pad_maximum_fusion.1), channel_id=1, source_target_pairs={{0,16},{8,24},{16,0},{24,8},{1,17},{9,25},{17,1},{25,9},{2,18},{10... | collective-permute-start | bytes 1179656 | tf_op jit(solution)/shard_map/ppermute | solution.py:602
  67.2 0.3 collective-permute-start.15
  67.5 1.3 pad_add_fusion.1.list_ref
  68.8 1.0 pad_maximum_fusion.refs_9_
  69.8 0.7 copy-done.1
  70.5 11.1 %uv_tile.1.refs_2_ = f32[32768,128]{1,0:T(8,128)} custom-call(s32[1]{0:T(128)} %bitcast.15.block_ref, s32[193]{0:T(256)} %pad_add_fusion.1.list_ref, s32[192]{0:T(256)} %get-tuple-element.49.row_ref, s32[192]{0:T(256)} %get-tuple-element.52.col_ref, bf16[1536,128]{1,0:T(8,128)(2,1)} %bitcast.122, bf16[1536,128]{1,0:T(8,128)(2,1)} %bitcast.124), custom_call_target="tpu_custom_call" | custom-call | bytes 41943040 | tf_op jit(solution)/shard_map/uv_tile/pallas_call | solution.py:330
  81.7 2.6 %collective-permute-done.14 = bf16[96,16,128]{2,1,0:T(8,128)(2,1)S(1)} collective-permute-done((bf16[96,16,128]{2,1,0:T(8,128)(2,1)S(1)}, bf16[96,16,128]{2,1,0:T(8,128)(2,1)S(1)}, u32[]{:S(2)}, u32[]{:S(2)}) %collective-permute-start.14) | collective-permute-done | bytes 393248 | tf_op jit(solution)/shard_map/ppermute | solution.py:602
  84.3 0.5 collective-permute-start.19
  85.0 0.7 add.395.refs_8_
  85.7 1.3 pad_add_fusion.list_ref
  87.0 0.8 select_select_fusion.1
  87.9 1.0 select_select_fusion
  88.9 3.7 %uv_spill.1 = f32[32768,128]{1,0:T(8,128)} custom-call(s32[1]{0:T(128)} %constant.323.clone.1.block_ref, s32[193]{0:T(256)} %pad_add_fusion.list_ref, s32[192]{0:T(256)} %get-tuple-element.40.row_ref, s32[192]{0:T(256)} %get-tuple-element.39.col_ref, bf16[1536,128]{1,0:T(8,128)(2,1)} %bitcast.126, ...), custom_call_target="tpu_custom_call", output_to_operand_aliasing={{}: (6, {})} | custom-call | bytes 8000000 | tf_op jit(solution)/shard_map/uv_spill/pallas_call | solution.py:358
  92.6 0.7 broadcast_in_dim.35.refs_12_
  93.2 44.4 %image.1 = f32[32768,128]{1,0:T(8,128)} custom-call(bf16[1536,128]{1,0:T(8,128)(2,1)} %bitcast.123, bf16[1536,128]{1,0:T(8,128)(2,1)} %bitcast.125, bf16[1536,128]{1,0:T(8,128)(2,1)} %bitcast.128, bf16[1536,128]{1,0:T(8,128)(2,1)} %bitcast.133, bf16[1536,128]{1,0:T(8,128)(2,1)} %bitcast.129, bf16[1536,128]{1,0:T(8,128)(2,1)} %bitcast.131, ...), custom_call_target="tpu_custom_call" | custom-call | tf_op jit(solution)/shard_map/image/pallas_call | solution.py:536
  (98 shorter events, 1.9 us)
Async XLA Ops:
  3.0 18.5 %collective-permute-start = (bf16[17,16,128]{2,1,0:T(8,128)(2,1)S(1)}, bf16[17,16,128]{2,1,0:T(8,128)(2,1)S(1)}, u32[]{:S(2)}, u32[]{:S(2)}) collective-permute-start(bf16[17,16,128]{2,1,0:T(8,128)(2,1)S(1)} %pad_maximum_fusion.3), channel_id=1, source_target_pairs={{0,2},{1,3},{2,0},{3,1},{4,6},{5,7},{6,4},{7,5},{8,10},{9,11},{10,... | collective-permute-start | bytes 208904 | tf_op jit(solution)/shard_map/ppermute | solution.py:602
  6.1 15.4 %collective-permute-start.1 = (bf16[17,16,128]{2,1,0:T(8,128)(2,1)S(1)}, bf16[17,16,128]{2,1,0:T(8,128)(2,1)S(1)}, u32[]{:S(2)}, u32[]{:S(2)}) collective-permute-start(bf16[17,16,128]{2,1,0:T(8,128)(2,1)S(1)} %pad_maximum_fusion.3), channel_id=1, source_target_pairs={{0,4},{1,5},{2,6},{3,7},{4,0},{5,1},{6,2},{7,3},{8,12},{9,13},{10,... | collective-permute-start | bytes 208904 | tf_op jit(solution)/shard_map/ppermute | solution.py:602
  8.7 12.9 %collective-permute-start.2 = (bf16[17,16,128]{2,1,0:T(8,128)(2,1)S(1)}, bf16[17,16,128]{2,1,0:T(8,128)(2,1)S(1)}, u32[]{:S(2)}, u32[]{:S(2)}) collective-permute-start(bf16[17,16,128]{2,1,0:T(8,128)(2,1)S(1)} %pad_maximum_fusion.3), channel_id=1, source_target_pairs={{0,6},{1,7},{2,4},{3,5},{4,2},{5,3},{6,0},{7,1},{8,14},{9,15},{10,... | collective-permute-start | bytes 208904 | tf_op jit(solution)/shard_map/ppermute | solution.py:602
  21.6 20.7 %copy-start.8 = (bf16[68,16,128]{2,1,0:T(8,128)(2,1)}, bf16[68,16,128]{2,1,0:T(8,128)(2,1)S(1)}, u32[]{:S(2)}) copy-start(bf16[68,16,128]{2,1,0:T(8,128)(2,1)S(1)} %constant_dynamic-update-slice_fusion.refs_0_) | copy-start | bytes 835588
  21.6 17.9 %collective-permute-start.3 = (bf16[68,16,128]{2,1,0:T(8,128)(2,1)S(1)}, bf16[68,16,128]{2,1,0:T(8,128)(2,1)S(1)}, u32[]{:S(2)}, u32[]{:S(2)}) collective-permute-start(bf16[68,16,128]{2,1,0:T(8,128)(2,1)S(1)} %constant_dynamic-update-slice_fusion.refs_0_), channel_id=1, source_target_pairs={{0,8},{8,0},{16,24},{24,16},{1,9},{9,1},{17,25},{25,17},{2,10},{10... | collective-permute-start | bytes 835592 | tf_op jit(solution)/shard_map/ppermute | solution.py:602
  23.4 16.1 %collective-permute-start.4 = (bf16[68,16,128]{2,1,0:T(8,128)(2,1)S(1)}, bf16[68,16,128]{2,1,0:T(8,128)(2,1)S(1)}, u32[]{:S(2)}, u32[]{:S(2)}) collective-permute-start(bf16[68,16,128]{2,1,0:T(8,128)(2,1)S(1)} %constant_dynamic-update-slice_fusion.refs_0_), channel_id=1, source_target_pairs={{0,16},{8,24},{16,0},{24,8},{1,17},{9,25},{17,1},{25,9},{2,18},{10... | collective-permute-start | bytes 835592 | tf_op jit(solution)/shard_map/ppermute | solution.py:602
  24.9 14.6 %collective-permute-start.5 = (bf16[68,16,128]{2,1,0:T(8,128)(2,1)S(1)}, bf16[68,16,128]{2,1,0:T(8,128)(2,1)S(1)}, u32[]{:S(2)}, u32[]{:S(2)}) collective-permute-start(bf16[68,16,128]{2,1,0:T(8,128)(2,1)S(1)} %constant_dynamic-update-slice_fusion.refs_0_), channel_id=1, source_target_pairs={{0,24},{8,16},{16,8},{24,0},{1,25},{9,17},{17,9},{25,1},{2,26},{10... | collective-permute-start | bytes 835592 | tf_op jit(solution)/shard_map/ppermute | solution.py:602
  39.4 2.9 %copy-start.9 = (bf16[68,16,128]{2,1,0:T(8,128)(2,1)}, bf16[68,16,128]{2,1,0:T(8,128)(2,1)S(1)}, u32[]{:S(2)}) copy-start(bf16[68,16,128]{2,1,0:T(8,128)(2,1)S(1)} %collective-permute-done.3.refs_2_) | copy-start | bytes 835588
  39.4 2.9 %copy-start.10 = (bf16[68,16,128]{2,1,0:T(8,128)(2,1)}, bf16[68,16,128]{2,1,0:T(8,128)(2,1)S(1)}, u32[]{:S(2)}) copy-start(bf16[68,16,128]{2,1,0:T(8,128)(2,1)S(1)} %collective-permute-done.4.refs_4_) | copy-start | bytes 835588
  39.5 2.8 %copy-start.11 = (bf16[68,16,128]{2,1,0:T(8,128)(2,1)}, bf16[68,16,128]{2,1,0:T(8,128)(2,1)S(1)}, u32[]{:S(2)}) copy-start(bf16[68,16,128]{2,1,0:T(8,128)(2,1)S(1)} %collective-permute-done.5.refs_6_) | copy-start | bytes 835588
  39.5 1.6 %collective-permute-start.6 = (bf16[68,16,128]{2,1,0:T(8,128)(2,1)S(1)}, bf16[68,16,128]{2,1,0:T(8,128)(2,1)S(1)}, u32[]{:S(2)}, u32[]{:S(2)}) collective-permute-start(bf16[68,16,128]{2,1,0:T(8,128)(2,1)S(1)} %constant_dynamic-update-slice_fusion.refs_0_), channel_id=1, source_target_pairs={{0,1},{1,0},{2,3},{3,2},{4,5},{5,4},{6,7},{7,6},{8,9},{9,8},{10,11... | collective-permute-start | bytes 835592 | tf_op jit(solution)/shard_map/ppermute | solution.py:602
  39.6 1.9 %collective-permute-start.7 = (bf16[68,16,128]{2,1,0:T(8,128)(2,1)S(1)}, bf16[68,16,128]{2,1,0:T(8,128)(2,1)S(1)}, u32[]{:S(2)}, u32[]{:S(2)}) collective-permute-start(bf16[68,16,128]{2,1,0:T(8,128)(2,1)S(1)} %collective-permute-done.3.refs_2_), channel_id=1, source_target_pairs={{0,1},{1,0},{2,3},{3,2},{4,5},{5,4},{6,7},{7,6},{8,9},{9,8},{10,11... | collective-permute-start | bytes 835592 | tf_op jit(solution)/shard_map/ppermute | solution.py:602
  40.1 1.8 %collective-permute-start.8 = (bf16[68,16,128]{2,1,0:T(8,128)(2,1)S(1)}, bf16[68,16,128]{2,1,0:T(8,128)(2,1)S(1)}, u32[]{:S(2)}, u32[]{:S(2)}) collective-permute-start(bf16[68,16,128]{2,1,0:T(8,128)(2,1)S(1)} %collective-permute-done.4.refs_4_), channel_id=1, source_target_pairs={{0,1},{1,0},{2,3},{3,2},{4,5},{5,4},{6,7},{7,6},{8,9},{9,8},{10,11... | collective-permute-start | bytes 835592 | tf_op jit(solution)/shard_map/ppermute | solution.py:602
  40.1 2.2 %collective-permute-start.9 = (bf16[68,16,128]{2,1,0:T(8,128)(2,1)S(1)}, bf16[68,16,128]{2,1,0:T(8,128)(2,1)S(1)}, u32[]{:S(2)}, u32[]{:S(2)}) collective-permute-start(bf16[68,16,128]{2,1,0:T(8,128)(2,1)S(1)} %collective-permute-done.5.refs_6_), channel_id=1, source_target_pairs={{0,1},{1,0},{2,3},{3,2},{4,5},{5,4},{6,7},{7,6},{8,9},{9,8},{10,11... | collective-permute-start | bytes 835592 | tf_op jit(solution)/shard_map/ppermute | solution.py:602
  41.1 1.2 copy-start.12
  41.5 0.8 copy-start.13
  41.9 0.7 copy-start.14
  42.6 0.7 copy-start.15
  50.0 13.0 %collective-permute-start.12 = (bf16[24,16,128]{2,1,0:T(8,128)(2,1)}, bf16[24,16,128]{2,1,0:T(8,128)(2,1)S(1)}, u32[]{:S(2)}, u32[]{:S(2)}) collective-permute-start(bf16[24,16,128]{2,1,0:T(8,128)(2,1)} %correct.1), channel_id=1, source_target_pairs={{0,6},{1,7},{2,4},{3,5},{4,2},{5,3},{6,0},{7,1},{8,14},{9,15},{10,... | collective-permute-start | bytes 294920 | tf_op jit(solution)/shard_map/ppermute | solution.py:602
  53.8 9.2 %collective-permute-start.11 = (bf16[24,16,128]{2,1,0:T(8,128)(2,1)}, bf16[24,16,128]{2,1,0:T(8,128)(2,1)S(1)}, u32[]{:S(2)}, u32[]{:S(2)}) collective-permute-start(bf16[24,16,128]{2,1,0:T(8,128)(2,1)} %correct.1), channel_id=1, source_target_pairs={{0,4},{1,5},{2,6},{3,7},{4,0},{5,1},{6,2},{7,3},{8,12},{9,13},{10,... | collective-permute-start | bytes 294920 | tf_op jit(solution)/shard_map/ppermute | solution.py:602
  53.8 9.2 %collective-permute-start.10 = (bf16[24,16,128]{2,1,0:T(8,128)(2,1)}, bf16[24,16,128]{2,1,0:T(8,128)(2,1)S(1)}, u32[]{:S(2)}, u32[]{:S(2)}) collective-permute-start(bf16[24,16,128]{2,1,0:T(8,128)(2,1)} %correct.1), channel_id=1, source_target_pairs={{0,2},{1,3},{2,0},{3,1},{4,6},{5,7},{6,4},{7,5},{8,10},{9,11},{10,... | collective-permute-start | bytes 294920 | tf_op jit(solution)/shard_map/ppermute | solution.py:602
  64.0 5.8 %copy-start = (bf16[96,16,128]{2,1,0:T(8,128)(2,1)}, bf16[96,16,128]{2,1,0:T(8,128)(2,1)S(1)}, u32[]{:S(2)}) copy-start(bf16[96,16,128]{2,1,0:T(8,128)(2,1)S(1)} %pad_maximum_fusion.1) | copy-start | bytes 1179652
  64.0 17.7 %collective-permute-start.13 = (bf16[96,16,128]{2,1,0:T(8,128)(2,1)S(1)}, bf16[96,16,128]{2,1,0:T(8,128)(2,1)S(1)}, u32[]{:S(2)}, u32[]{:S(2)}) collective-permute-start(bf16[96,16,128]{2,1,0:T(8,128)(2,1)S(1)} %pad_maximum_fusion.1), channel_id=1, source_target_pairs={{0,8},{8,0},{16,24},{24,16},{1,9},{9,1},{17,25},{25,17},{2,10},{10... | collective-permute-start | bytes 1179656 | tf_op jit(solution)/shard_map/ppermute | solution.py:602
  65.7 18.5 %collective-permute-start.14 = (bf16[96,16,128]{2,1,0:T(8,128)(2,1)S(1)}, bf16[96,16,128]{2,1,0:T(8,128)(2,1)S(1)}, u32[]{:S(2)}, u32[]{:S(2)}) collective-permute-start(bf16[96,16,128]{2,1,0:T(8,128)(2,1)S(1)} %pad_maximum_fusion.1), channel_id=1, source_target_pairs={{0,16},{8,24},{16,0},{24,8},{1,17},{9,25},{17,1},{25,9},{2,18},{10... | collective-permute-start | bytes 1179656 | tf_op jit(solution)/shard_map/ppermute | solution.py:602
  67.2 17.0 %collective-permute-start.15 = (bf16[96,16,128]{2,1,0:T(8,128)(2,1)S(1)}, bf16[96,16,128]{2,1,0:T(8,128)(2,1)S(1)}, u32[]{:S(2)}, u32[]{:S(2)}) collective-permute-start(bf16[96,16,128]{2,1,0:T(8,128)(2,1)S(1)} %pad_maximum_fusion.1), channel_id=1, source_target_pairs={{0,24},{8,16},{16,8},{24,0},{1,25},{9,17},{17,9},{25,1},{2,26},{10... | collective-permute-start | bytes 1179656 | tf_op jit(solution)/shard_map/ppermute | solution.py:602
  67.5 2.3 %collective-permute-start.16 = (bf16[96,16,128]{2,1,0:T(8,128)(2,1)S(1)}, bf16[96,16,128]{2,1,0:T(8,128)(2,1)S(1)}, u32[]{:S(2)}, u32[]{:S(2)}) collective-permute-start(bf16[96,16,128]{2,1,0:T(8,128)(2,1)S(1)} %pad_maximum_fusion.1), channel_id=1, source_target_pairs={{0,1},{1,0},{2,3},{3,2},{4,5},{5,4},{6,7},{7,6},{8,9},{9,8},{10,11... | collective-permute-start | bytes 1179656 | tf_op jit(solution)/shard_map/ppermute | solution.py:602
  69.8 0.7 copy-start.1
  81.6 10.9 %copy-start.2 = (bf16[96,16,128]{2,1,0:T(8,128)(2,1)}, bf16[96,16,128]{2,1,0:T(8,128)(2,1)S(1)}, u32[]{:S(2)}) copy-start(bf16[96,16,128]{2,1,0:T(8,128)(2,1)S(1)} %collective-permute-done.13) | copy-start | bytes 1179652
  84.3 8.3 %copy-start.3 = (bf16[96,16,128]{2,1,0:T(8,128)(2,1)}, bf16[96,16,128]{2,1,0:T(8,128)(2,1)S(1)}, u32[]{:S(2)}) copy-start(bf16[96,16,128]{2,1,0:T(8,128)(2,1)S(1)} %collective-permute-done.14) | copy-start | bytes 1179652
  84.3 8.3 %copy-start.4 = (bf16[96,16,128]{2,1,0:T(8,128)(2,1)}, bf16[96,16,128]{2,1,0:T(8,128)(2,1)S(1)}, u32[]{:S(2)}) copy-start(bf16[96,16,128]{2,1,0:T(8,128)(2,1)S(1)} %collective-permute-done.15) | copy-start | bytes 1179652
  84.3 3.6 %collective-permute-start.18 = (bf16[96,16,128]{2,1,0:T(8,128)(2,1)S(1)}, bf16[96,16,128]{2,1,0:T(8,128)(2,1)S(1)}, u32[]{:S(2)}, u32[]{:S(2)}) collective-permute-start(bf16[96,16,128]{2,1,0:T(8,128)(2,1)S(1)} %collective-permute-done.14), channel_id=1, source_target_pairs={{0,1},{1,0},{2,3},{3,2},{4,5},{5,4},{6,7},{7,6},{8,9},{9,8},{10,11... | collective-permute-start | bytes 1179656 | tf_op jit(solution)/shard_map/ppermute | solution.py:602
  84.3 3.5 %collective-permute-start.19 = (bf16[96,16,128]{2,1,0:T(8,128)(2,1)S(1)}, bf16[96,16,128]{2,1,0:T(8,128)(2,1)S(1)}, u32[]{:S(2)}, u32[]{:S(2)}) collective-permute-start(bf16[96,16,128]{2,1,0:T(8,128)(2,1)S(1)} %collective-permute-done.15), channel_id=1, source_target_pairs={{0,1},{1,0},{2,3},{3,2},{4,5},{5,4},{6,7},{7,6},{8,9},{9,8},{10,11... | collective-permute-start | bytes 1179656 | tf_op jit(solution)/shard_map/ppermute | solution.py:602
  84.8 3.0 %collective-permute-start.17 = (bf16[96,16,128]{2,1,0:T(8,128)(2,1)S(1)}, bf16[96,16,128]{2,1,0:T(8,128)(2,1)S(1)}, u32[]{:S(2)}, u32[]{:S(2)}) collective-permute-start(bf16[96,16,128]{2,1,0:T(8,128)(2,1)S(1)} %collective-permute-done.13), channel_id=1, source_target_pairs={{0,1},{1,0},{2,3},{3,2},{4,5},{5,4},{6,7},{7,6},{8,9},{9,8},{10,11... | collective-permute-start | bytes 1179656 | tf_op jit(solution)/shard_map/ppermute | solution.py:602
  87.9 4.7 %copy-start.5 = (bf16[96,16,128]{2,1,0:T(8,128)(2,1)}, bf16[96,16,128]{2,1,0:T(8,128)(2,1)S(1)}, u32[]{:S(2)}) copy-start(bf16[96,16,128]{2,1,0:T(8,128)(2,1)S(1)} %collective-permute-done.18) | copy-start | bytes 1179652
  87.9 4.7 %copy-start.6 = (bf16[96,16,128]{2,1,0:T(8,128)(2,1)}, bf16[96,16,128]{2,1,0:T(8,128)(2,1)S(1)}, u32[]{:S(2)}) copy-start(bf16[96,16,128]{2,1,0:T(8,128)(2,1)S(1)} %collective-permute-done.19) | copy-start | bytes 1179652
  87.9 4.7 %copy-start.7 = (bf16[96,16,128]{2,1,0:T(8,128)(2,1)}, bf16[96,16,128]{2,1,0:T(8,128)(2,1)S(1)}, u32[]{:S(2)}) copy-start(bf16[96,16,128]{2,1,0:T(8,128)(2,1)S(1)} %collective-permute-done.17) | copy-start | bytes 1179652

commit v2 on v1

--- a/solution.py
+++ b/solution.py
@@ -410,16 +410,15 @@
 def image_kernel(*refs, pieces, chunks, row_block):
     uv_refs, refs = refs[:pieces], refs[pieces:]
     corner_ref, phase_ref, columns_ref, unit_ref, count_ref, twist_ref = refs[:6]
-    out_ref, uv_wide, here, after, shifts, left_even, left_odd, total = refs[6:]
+    out_ref, uv_wide, uv_rows, here, after, shifts, left_even, left_odd, total, staged = refs[6:]
     step = pl.program_id(0)
-    size = uv_wide.shape[0] // HALF
+    size = uv_rows.shape[1]
     image_rows = phase_ref.shape[1]
 
     def products(pair, h, left):
-        rows = uv_wide[pl.ds(pair, size, stride=HALF), :].astype(bf16)
         at = pl.ds(2 * image_rows * h, 2 * image_rows)
         spread = lax.dot_general(
-            columns_ref[at, :], rows, (((1,), (1,)), ((), ())), preferred_element_type=f32
+            columns_ref[at, :], uv_rows[pair], (((1,), (1,)), ((), ())), preferred_element_type=f32
         ).astype(bf16)
         turned = cmul((spread[:image_rows], spread[image_rows:]), (phase_ref[0], phase_ref[1]))
         left[h, :image_rows] = turned[0]
@@ -448,8 +447,17 @@
     def chunk(first):
         held = 0
         for piece in uv_refs:
-            uv_wide[held : held + piece.shape[0]] = piece[...].astype(f32)
-            held += piece.shape[0]
+
+            def spread_out(s, carry, piece=piece, held=held):
+                block = piece[pl.ds(pl.multiple_of(s * HALF, HALF), HALF), :]
+                uv_wide[pl.ds((held + s) * (HALF + 1), HALF), :] = block.astype(f32)
+                return carry
+
+            count = piece.shape[0] // HALF
+            lax.fori_loop(0, count, spread_out, 0, unroll=math.gcd(count, 8))
+            held += count
+        for row in range(HALF):
+            uv_rows[row] = uv_wide[pl.ds(row, size, stride=HALF + 1), :].astype(bf16)
         corner = corner_ref[...]
         coarse, shift = corner // SUB, corner % SUB
 
@@ -498,7 +506,10 @@
                 for k, value in enumerate(short_transform(values)):
                     for part in range(2):
                         column = 2 * (k * (FINE // LANES) + tile) + part
-                        out_ref[pl.ds(group * 8 * wide + column, 8, stride=wide), :] = value[part]
+                        staged[pl.ds(column, 8, stride=wide + 1), :] = value[part]
+            for row in range(8):
+                at = pl.ds(pl.multiple_of((8 * group + row) * wide, wide), wide)
+                out_ref[at, :] = staged[row * (wide + 1) : row * (wide + 1) + wide, :]
             return carry
 
         lax.fori_loop(0, row_block // 8, eight_rows, 0)
@@ -550,13 +561,15 @@
         ),
         out_shape=jax.ShapeDtypeStruct((image_rows * wide, LANES), f32),
         scratch_shapes=[
-            pltpu.VMEM((size * HALF, PACK), f32),
+            pltpu.VMEM((size * (HALF + 1) + HALF, PACK), f32),
+            pltpu.VMEM((HALF, size, PACK), bf16),
             pltpu.VMEM((size, 2 * FINE), bf16),
             pltpu.VMEM((size, 2 * FINE), bf16),
             pltpu.VMEM((size, LANES), f32),
             pltpu.VMEM((2, 2 * image_rows, size), bf16),
             pltpu.VMEM((2, 2 * image_rows, size), bf16),
             pltpu.VMEM((SUB, 2, image_rows, FINE), f32),
+            pltpu.VMEM((8 * (wide + 1) + wide, LANES), f32),
         ],
         compiler_params=pltpu.CompilerParams(vmem_limit_bytes=VMEM_BYTES),
         name="image",

time: 139 us -> 133 us (0.957)
  Pallas kernels: 81.4 us -> 78.1 us
  waiting for transfers between devices: 4.29 us -> 1.69 us
    pallas_call x1, Pallas kernels: 44.4 us -> 37.3 us  [image_rows_of(): pl.pallas_call(functools.partial(image_kernel, pieces=len(uv), chunks=chu...]
    pallas_call x1, Pallas kernels: 11.1 us -> 14.9 us  [uv_tile_own(): pl.pallas_call(functools.partial(tile_kernel, pieces=len(uv), tile_rows=t...]
    ppermute x20, waiting for transfers between devices: 4.29 us -> 1.69 us  [from_partner(): return lax.ppermute(value, axis, [(i, i ^ mask) for i in range(count)])]
  transfers between devices with their start and end apart: 20 -> 20, of which waited for: 5 -> 4; matrix products, arithmetic and copies ran while one was open for 18% -> 19% of each run, Pallas kernels for 19% -> 23%
where the time goes in v2:
time: 133 us; the launch traced here: 132 us
  Pallas kernels  78.1 us (59%)
  other arithmetic  20.1 us (15%)
  starting transfers between devices  18.9 us (14%)
  local copies, waits for them, and re-layouts  11.8 us (9%)
  waiting for transfers between devices  1.69 us (1%)
    pallas_call x1, Pallas kernels, image_rows_of(): pl.pallas_call(functools.partial(image_kernel, pieces=len(uv), chunks=chu...  37.3 us
    ppermute x20, starting transfers between devices, from_partner(): return lax.ppermute(value, axis, [(i, i ^ mask) for i in range(count)])  18.9 us
    pallas_call x3, Pallas kernels, sky_sums(): pl.pallas_call(sky_kernel, grid=(1,), in_specs=[pl.BlockSpec((count, 2, v...  15.6 us
    pallas_call x1, Pallas kernels, uv_tile_own(): pl.pallas_call(functools.partial(tile_kernel, pieces=len(uv), tile_rows=t...  14.9 us
    pallas_call x1, Pallas kernels, corrected_subgrids(): pl.pallas_call(functools.partial(correct_kernel, pieces=len(tables), skie...  6.66 us
    unnamed x53, local copies, waits for them, and re-layouts  4.84 us
    another operation x3, other arithmetic  4.72 us
    pallas_call x1, Pallas kernels, uv_tile_spill(): pl.pallas_call(functools.partial(spill_kernel, pieces=len(uv), lanes=lane...  3.54 us
  transfers between devices with their start and end apart: 20, of which 4 were waited for; matrix products, arithmetic and copies ran while one was open for 19% of the time, Pallas kernels for 23%

profile of v2, /device:TPU:0, one launch (start us, length us, event | category | flops | bytes accessed | tf_op | source)
XLA Modules:
  0.0 131.8 jit_solution(16869978354709717728)
XLA Ops:
  0.6 1.0 reshape.711
  1.7 0.2 copy.44
  1.9 0.2 reshape.712
  2.1 0.8 and_select_fusion.15
  3.0 3.1 %collective-permute-start = (bf16[17,16,128]{2,1,0:T(8,128)(2,1)S(1)}, bf16[17,16,128]{2,1,0:T(8,128)(2,1)S(1)}, u32[]{:S(2)}, u32[]{:S(2)}) collective-permute-start(bf16[17,16,128]{2,1,0:T(8,128)(2,1)S(1)} %pad_maximum_fusion.3), channel_id=1, source_target_pairs={{0,2},{1,3},{2,0},{3,1},{4,6},{5,7},{6,4},{7,5},{8,10},{9,11},{10,... | collective-permute-start | bytes 208904 | tf_op jit(solution)/shard_map/ppermute | solution.py:615
  6.1 2.6 %collective-permute-start.1 = (bf16[17,16,128]{2,1,0:T(8,128)(2,1)S(1)}, bf16[17,16,128]{2,1,0:T(8,128)(2,1)S(1)}, u32[]{:S(2)}, u32[]{:S(2)}) collective-permute-start(bf16[17,16,128]{2,1,0:T(8,128)(2,1)S(1)} %pad_maximum_fusion.3), channel_id=1, source_target_pairs={{0,4},{1,5},{2,6},{3,7},{4,0},{5,1},{6,2},{7,3},{8,12},{9,13},{10,... | collective-permute-start | bytes 208904 | tf_op jit(solution)/shard_map/ppermute | solution.py:615
  8.7 0.7 and_select_fusion.2
  9.4 1.1 sine_convert_fusion.1
  10.5 0.1 fusion.21
  10.7 0.7 tile.2
  11.4 0.7 reshape_tile.3.scale_ref
  12.0 0.7 fusion.41
  12.8 0.7 broadcast_multiply_fusion
  13.4 0.2 fusion.35
  13.7 0.1 fusion.31
  13.9 0.2 multiply_convert_fusion
  14.3 0.6 pad_maximum_fusion.4.refs_13_
  14.9 0.7 pad_maximum_fusion.2.refs_11_
  15.7 0.6 maximum_multiply_fusion.refs_13_
  16.3 5.2 %sky_sums.3.refs_8_ = f32[8,16,128]{2,1,0:T(8,128)} custom-call(bf16[24,2,2048]{2,1,0:T(2,128)(2,1)} %vis_ref.5, f32[48,128]{1,0:T(8,128)} %bitcast.145, f32[1,2048]{1,0:T(1,128)} %reshape_tile.3.scale_ref), custom_call_target="tpu_custom_call" | custom-call | bytes 20000000 | tf_op jit(solution)/shard_map/sky_sums/pallas_call | solution.py:109
  21.6 1.8 %collective-permute-start.3 = (bf16[68,16,128]{2,1,0:T(8,128)(2,1)S(1)}, bf16[68,16,128]{2,1,0:T(8,128)(2,1)S(1)}, u32[]{:S(2)}, u32[]{:S(2)}) collective-permute-start(bf16[68,16,128]{2,1,0:T(8,128)(2,1)S(1)} %constant_dynamic-update-slice_fusion.refs_0_), channel_id=1, source_target_pairs={{0,8},{8,0},{16,24},{24,16},{1,9},{9,1},{17,25},{25,17},{2,10},{10... | collective-permute-start | bytes 835592 | tf_op jit(solution)/shard_map/ppermute | solution.py:615
  23.4 1.5 %collective-permute-start.4 = (bf16[68,16,128]{2,1,0:T(8,128)(2,1)S(1)}, bf16[68,16,128]{2,1,0:T(8,128)(2,1)S(1)}, u32[]{:S(2)}, u32[]{:S(2)}) collective-permute-start(bf16[68,16,128]{2,1,0:T(8,128)(2,1)S(1)} %constant_dynamic-update-slice_fusion.refs_0_), channel_id=1, source_target_pairs={{0,16},{8,24},{16,0},{24,8},{1,17},{9,25},{17,1},{25,9},{2,18},{10... | collective-permute-start | bytes 835592 | tf_op jit(solution)/shard_map/ppermute | solution.py:615
  24.9 0.3 collective-permute-start.5
  25.2 0.7 reshape.723.stations_ref
  25.9 0.7 convert_element_type.151.refs_12_
  26.6 0.9 copy.24.refs_10_
  27.5 1.5 %fusion.14.refs_11_ = f32[24,16,128]{2,1,0:T(8,128)} fusion(f32[16,128]{1,0:T(8,128)S(1)} %get-tuple-element.64, f32[128]{0:T(128)S(1)} %fusion.45, s32[16,128]{1,0:T(8,128)S(1)} %fusion.34, s32[24]{0:T(128)S(1)} %and_select_fusion.2, f32[16,128]{1,0:T(8,128)S(1)} %get-tuple-element.63, f32[24]{0:T(128)S(1)} %broadcast_multiply_fusion), kind=kLoop, calls=%fused_computation.38 | loop fusion | flops 884736 | bytes 221888 | tf_op jit(solution)/shard_map/mul | solution.py:610
  29.0 5.2 %sky_sums.4.refs_9_ = f32[8,16,128]{2,1,0:T(8,128)} custom-call(bf16[24,2,2048]{2,1,0:T(2,128)(2,1)} %vis_ref.5, f32[48,128]{1,0:T(8,128)} %bitcast.146, f32[1,2048]{1,0:T(1,128)} %reshape_tile.3.scale_ref), custom_call_target="tpu_custom_call" | custom-call | bytes 20000000 | tf_op jit(solution)/shard_map/sky_sums/pallas_call | solution.py:109
  34.2 5.2 %sky_sums.5.refs_10_ = f32[8,16,128]{2,1,0:T(8,128)} custom-call(bf16[24,2,2048]{2,1,0:T(2,128)(2,1)} %vis_ref.5, f32[48,128]{1,0:T(8,128)} %bitcast.147, f32[1,2048]{1,0:T(1,128)} %reshape_tile.3.scale_ref), custom_call_target="tpu_custom_call" | custom-call | bytes 20000000 | tf_op jit(solution)/shard_map/sky_sums/pallas_call | solution.py:109
  39.6 0.5 collective-permute-start.7
  40.1 0.4 collective-permute-start.9
  40.6 0.5 collective-permute-done.6.refs_1_
  41.1 0.4 collective-permute-done.7.refs_3_
  41.5 0.4 collective-permute-done.8.refs_5_
  41.9 0.4 collective-permute-done.9.refs_7_
  42.3 0.3 copy-done.14
  42.6 0.7 copy-done.15
  43.3 6.7 %correct.1 = bf16[24,16,128]{2,1,0:T(8,128)(2,1)} custom-call(s32[48]{0:T(128)} %reshape.723.stations_ref, bf16[68,16,128]{2,1,0:T(8,128)(2,1)} %copy-done.8, bf16[68,16,128]{2,1,0:T(8,128)(2,1)} %copy-done.12, bf16[68,16,128]{2,1,0:T(8,128)(2,1)} %copy-done.9, bf16[68,16,128]{2,1,0:T(8,128)(2,1)} %copy-done.13, bf16[68,16,128]{2,1,0:T(8,128)(2,1)} %copy-done.10, ...), custom_call_target="tpu_custom_call" | custom-call | bytes 16000000 | tf_op jit(solution)/shard_map/correct/pallas_call | solution.py:193
  50.0 3.8 %collective-permute-start.12 = (bf16[24,16,128]{2,1,0:T(8,128)(2,1)}, bf16[24,16,128]{2,1,0:T(8,128)(2,1)S(1)}, u32[]{:S(2)}, u32[]{:S(2)}) collective-permute-start(bf16[24,16,128]{2,1,0:T(8,128)(2,1)} %correct.1), channel_id=1, source_target_pairs={{0,6},{1,7},{2,4},{3,5},{4,2},{5,3},{6,0},{7,1},{8,14},{9,15},{10,... | collective-permute-start | bytes 294920 | tf_op jit(solution)/shard_map/ppermute | solution.py:615
  53.8 0.6 collective-permute-start.10
  54.4 0.7 slice_bitcast_fusion.6
  55.1 0.7 slice_bitcast_fusion.4
  55.9 0.7 slice_bitcast_fusion.2
  56.6 0.7 slice_bitcast_fusion
  57.3 0.1 concatenate.75
  57.8 3.5 %cosine_convert_fusion = (bf16[1,256,768]{2,1,0:T(8,128)(2,1)S(1)}, bf16[1,256,768]{2,1,0:T(8,128)(2,1)S(1)}) fusion(s32[768]{0:T(1024)S(1)} %add.360, s32[256]{0:T(256)S(1)} %iota_add_fusion.1), kind=kLoop, calls=%fused_computation.10 | loop fusion | flops 3145728 | bytes 790528 | tf_op jit(solution)/shard_map/convert.2
  61.2 1.4 %convert_reduce_fusion.3 = (s32[]{:T(128)}, pred[192]{0:T(512)(128)(4,1)S(1)}, s32[192]{0:T(256)}, s32[192]{0:T(256)}, s32[192]{0:T(256)}, /*index=5*/s32[]{:T(128)}, pred[192]{0:T(512)(128)(4,1)S(1)}, s32[192]{0:T(256)}) fusion(s32[]{:T(128)S(6)} %mul.426, s32[768]{0:T(1024)S(1)} %add.360, s32[]{:T(128)S(6)} %select_n.296, s32[]{:T(128)S(6)} %mul.428, ...), kind=kLoop, calls=%fused_computation.170 | loop fusion | flops 5374 | bytes 6552 | tf_op jit(solution)/shard_map/reduce_sum | solution.py:311
  62.9 0.1 convert_reduce_fusion.1
  63.0 0.9 pad_maximum_fusion.1
  64.0 1.8 %collective-permute-start.13 = (bf16[96,16,128]{2,1,0:T(8,128)(2,1)S(1)}, bf16[96,16,128]{2,1,0:T(8,128)(2,1)S(1)}, u32[]{:S(2)}, u32[]{:S(2)}) collective-permute-start(bf16[96,16,128]{2,1,0:T(8,128)(2,1)S(1)} %pad_maximum_fusion.1), channel_id=1, source_target_pairs={{0,8},{8,0},{16,24},{24,16},{1,9},{9,1},{17,25},{25,17},{2,10},{10... | collective-permute-start | bytes 1179656 | tf_op jit(solution)/shard_map/ppermute | solution.py:615
  65.7 1.5 %collective-permute-start.14 = (bf16[96,16,128]{2,1,0:T(8,128)(2,1)S(1)}, bf16[96,16,128]{2,1,0:T(8,128)(2,1)S(1)}, u32[]{:S(2)}, u32[]{:S(2)}) collective-permute-start(bf16[96,16,128]{2,1,0:T(8,128)(2,1)S(1)} %pad_maximum_fusion.1), channel_id=1, source_target_pairs={{0,16},{8,24},{16,0},{24,8},{1,17},{9,25},{17,1},{25,9},{2,18},{10... | collective-permute-start | bytes 1179656 | tf_op jit(solution)/shard_map/ppermute | solution.py:615
  67.2 0.3 collective-permute-start.15
  67.5 1.3 pad_add_fusion.1.list_ref
  68.8 1.0 pad_maximum_fusion.refs_9_
  69.8 0.7 copy-done.1
  70.5 14.9 %uv_tile.1.refs_2_ = f32[32768,128]{1,0:T(8,128)} custom-call(s32[1]{0:T(128)} %bitcast.15.block_ref, s32[193]{0:T(256)} %pad_add_fusion.1.list_ref, s32[192]{0:T(256)} %get-tuple-element.49.row_ref, s32[192]{0:T(256)} %get-tuple-element.52.col_ref, bf16[1536,128]{1,0:T(8,128)(2,1)} %bitcast.122, bf16[1536,128]{1,0:T(8,128)(2,1)} %bitcast.124), custom_call_target="tpu_custom_call" | custom-call | bytes 41943040 | tf_op jit(solution)/shard_map/uv_tile/pallas_call | solution.py:330
  85.6 0.5 collective-permute-start.19
  86.3 0.7 add.395.refs_8_
  87.0 1.3 %pad_add_fusion.list_ref = s32[193]{0:T(256)} fusion(s32[192]{0:T(256)S(1)} %select_reduce_fusion.1, s32[1]{0:T(128)} %bitcast.13), kind=kLoop, calls=%fused_computation.161 | loop fusion | flops 193 | bytes 1544 | tf_op jit(solution)/shard_map/concatenate | solution.py:311
  88.3 0.8 select_select_fusion.1
  89.2 1.0 select_select_fusion
  90.1 3.5 %uv_spill.1 = f32[32768,128]{1,0:T(8,128)} custom-call(s32[1]{0:T(128)} %constant.323.clone.1.block_ref, s32[193]{0:T(256)} %pad_add_fusion.list_ref, s32[192]{0:T(256)} %get-tuple-element.40.row_ref, s32[192]{0:T(256)} %get-tuple-element.39.col_ref, bf16[1536,128]{1,0:T(8,128)(2,1)} %bitcast.126, ...), custom_call_target="tpu_custom_call", output_to_operand_aliasing={{}: (6, {})} | custom-call | bytes 8000000 | tf_op jit(solution)/shard_map/uv_spill/pallas_call | solution.py:358
  93.8 0.7 broadcast_in_dim.35.refs_12_
  94.4 37.3 %image.1 = f32[32768,128]{1,0:T(8,128)} custom-call(bf16[1536,128]{1,0:T(8,128)(2,1)} %bitcast.123, bf16[1536,128]{1,0:T(8,128)(2,1)} %bitcast.125, bf16[1536,128]{1,0:T(8,128)(2,1)} %bitcast.128, bf16[1536,128]{1,0:T(8,128)(2,1)} %bitcast.133, bf16[1536,128]{1,0:T(8,128)(2,1)} %bitcast.129, bf16[1536,128]{1,0:T(8,128)(2,1)} %bitcast.131, ...), custom_call_target="tpu_custom_call" | custom-call | tf_op jit(solution)/shard_map/image/pallas_call | solution.py:547
  (98 shorter events, 1.8 us)
Async XLA Ops:
  3.0 18.5 %collective-permute-start = (bf16[17,16,128]{2,1,0:T(8,128)(2,1)S(1)}, bf16[17,16,128]{2,1,0:T(8,128)(2,1)S(1)}, u32[]{:S(2)}, u32[]{:S(2)}) collective-permute-start(bf16[17,16,128]{2,1,0:T(8,128)(2,1)S(1)} %pad_maximum_fusion.3), channel_id=1, source_target_pairs={{0,2},{1,3},{2,0},{3,1},{4,6},{5,7},{6,4},{7,5},{8,10},{9,11},{10,... | collective-permute-start | bytes 208904 | tf_op jit(solution)/shard_map/ppermute | solution.py:615
  6.1 15.4 %collective-permute-start.1 = (bf16[17,16,128]{2,1,0:T(8,128)(2,1)S(1)}, bf16[17,16,128]{2,1,0:T(8,128)(2,1)S(1)}, u32[]{:S(2)}, u32[]{:S(2)}) collective-permute-start(bf16[17,16,128]{2,1,0:T(8,128)(2,1)S(1)} %pad_maximum_fusion.3), channel_id=1, source_target_pairs={{0,4},{1,5},{2,6},{3,7},{4,0},{5,1},{6,2},{7,3},{8,12},{9,13},{10,... | collective-permute-start | bytes 208904 | tf_op jit(solution)/shard_map/ppermute | solution.py:615
  8.7 12.9 %collective-permute-start.2 = (bf16[17,16,128]{2,1,0:T(8,128)(2,1)S(1)}, bf16[17,16,128]{2,1,0:T(8,128)(2,1)S(1)}, u32[]{:S(2)}, u32[]{:S(2)}) collective-permute-start(bf16[17,16,128]{2,1,0:T(8,128)(2,1)S(1)} %pad_maximum_fusion.3), channel_id=1, source_target_pairs={{0,6},{1,7},{2,4},{3,5},{4,2},{5,3},{6,0},{7,1},{8,14},{9,15},{10,... | collective-permute-start | bytes 208904 | tf_op jit(solution)/shard_map/ppermute | solution.py:615
  21.6 20.7 %copy-start.8 = (bf16[68,16,128]{2,1,0:T(8,128)(2,1)}, bf16[68,16,128]{2,1,0:T(8,128)(2,1)S(1)}, u32[]{:S(2)}) copy-start(bf16[68,16,128]{2,1,0:T(8,128)(2,1)S(1)} %constant_dynamic-update-slice_fusion.refs_0_) | copy-start | bytes 835588
  21.6 17.9 %collective-permute-start.3 = (bf16[68,16,128]{2,1,0:T(8,128)(2,1)S(1)}, bf16[68,16,128]{2,1,0:T(8,128)(2,1)S(1)}, u32[]{:S(2)}, u32[]{:S(2)}) collective-permute-start(bf16[68,16,128]{2,1,0:T(8,128)(2,1)S(1)} %constant_dynamic-update-slice_fusion.refs_0_), channel_id=1, source_target_pairs={{0,8},{8,0},{16,24},{24,16},{1,9},{9,1},{17,25},{25,17},{2,10},{10... | collective-permute-start | bytes 835592 | tf_op jit(solution)/shard_map/ppermute | solution.py:615
  23.4 16.1 %collective-permute-start.4 = (bf16[68,16,128]{2,1,0:T(8,128)(2,1)S(1)}, bf16[68,16,128]{2,1,0:T(8,128)(2,1)S(1)}, u32[]{:S(2)}, u32[]{:S(2)}) collective-permute-start(bf16[68,16,128]{2,1,0:T(8,128)(2,1)S(1)} %constant_dynamic-update-slice_fusion.refs_0_), channel_id=1, source_target_pairs={{0,16},{8,24},{16,0},{24,8},{1,17},{9,25},{17,1},{25,9},{2,18},{10... | collective-permute-start | bytes 835592 | tf_op jit(solution)/shard_map/ppermute | solution.py:615
  24.9 14.6 %collective-permute-start.5 = (bf16[68,16,128]{2,1,0:T(8,128)(2,1)S(1)}, bf16[68,16,128]{2,1,0:T(8,128)(2,1)S(1)}, u32[]{:S(2)}, u32[]{:S(2)}) collective-permute-start(bf16[68,16,128]{2,1,0:T(8,128)(2,1)S(1)} %constant_dynamic-update-slice_fusion.refs_0_), channel_id=1, source_target_pairs={{0,24},{8,16},{16,8},{24,0},{1,25},{9,17},{17,9},{25,1},{2,26},{10... | collective-permute-start | bytes 835592 | tf_op jit(solution)/shard_map/ppermute | solution.py:615
  39.4 2.9 %copy-start.9 = (bf16[68,16,128]{2,1,0:T(8,128)(2,1)}, bf16[68,16,128]{2,1,0:T(8,128)(2,1)S(1)}, u32[]{:S(2)}) copy-start(bf16[68,16,128]{2,1,0:T(8,128)(2,1)S(1)} %collective-permute-done.3.refs_2_) | copy-start | bytes 835588
  39.4 2.9 %copy-start.10 = (bf16[68,16,128]{2,1,0:T(8,128)(2,1)}, bf16[68,16,128]{2,1,0:T(8,128)(2,1)S(1)}, u32[]{:S(2)}) copy-start(bf16[68,16,128]{2,1,0:T(8,128)(2,1)S(1)} %collective-permute-done.4.refs_4_) | copy-start | bytes 835588
  39.5 2.8 %copy-start.11 = (bf16[68,16,128]{2,1,0:T(8,128)(2,1)}, bf16[68,16,128]{2,1,0:T(8,128)(2,1)S(1)}, u32[]{:S(2)}) copy-start(bf16[68,16,128]{2,1,0:T(8,128)(2,1)S(1)} %collective-permute-done.5.refs_6_) | copy-start | bytes 835588
  39.5 1.6 %collective-permute-start.6 = (bf16[68,16,128]{2,1,0:T(8,128)(2,1)S(1)}, bf16[68,16,128]{2,1,0:T(8,128)(2,1)S(1)}, u32[]{:S(2)}, u32[]{:S(2)}) collective-permute-start(bf16[68,16,128]{2,1,0:T(8,128)(2,1)S(1)} %constant_dynamic-update-slice_fusion.refs_0_), channel_id=1, source_target_pairs={{0,1},{1,0},{2,3},{3,2},{4,5},{5,4},{6,7},{7,6},{8,9},{9,8},{10,11... | collective-permute-start | bytes 835592 | tf_op jit(solution)/shard_map/ppermute | solution.py:615
  39.6 1.9 %collective-permute-start.7 = (bf16[68,16,128]{2,1,0:T(8,128)(2,1)S(1)}, bf16[68,16,128]{2,1,0:T(8,128)(2,1)S(1)}, u32[]{:S(2)}, u32[]{:S(2)}) collective-permute-start(bf16[68,16,128]{2,1,0:T(8,128)(2,1)S(1)} %collective-permute-done.3.refs_2_), channel_id=1, source_target_pairs={{0,1},{1,0},{2,3},{3,2},{4,5},{5,4},{6,7},{7,6},{8,9},{9,8},{10,11... | collective-permute-start | bytes 835592 | tf_op jit(solution)/shard_map/ppermute | solution.py:615
  40.1 1.8 %collective-permute-start.8 = (bf16[68,16,128]{2,1,0:T(8,128)(2,1)S(1)}, bf16[68,16,128]{2,1,0:T(8,128)(2,1)S(1)}, u32[]{:S(2)}, u32[]{:S(2)}) collective-permute-start(bf16[68,16,128]{2,1,0:T(8,128)(2,1)S(1)} %collective-permute-done.4.refs_4_), channel_id=1, source_target_pairs={{0,1},{1,0},{2,3},{3,2},{4,5},{5,4},{6,7},{7,6},{8,9},{9,8},{10,11... | collective-permute-start | bytes 835592 | tf_op jit(solution)/shard_map/ppermute | solution.py:615
  40.1 2.2 %collective-permute-start.9 = (bf16[68,16,128]{2,1,0:T(8,128)(2,1)S(1)}, bf16[68,16,128]{2,1,0:T(8,128)(2,1)S(1)}, u32[]{:S(2)}, u32[]{:S(2)}) collective-permute-start(bf16[68,16,128]{2,1,0:T(8,128)(2,1)S(1)} %collective-permute-done.5.refs_6_), channel_id=1, source_target_pairs={{0,1},{1,0},{2,3},{3,2},{4,5},{5,4},{6,7},{7,6},{8,9},{9,8},{10,11... | collective-permute-start | bytes 835592 | tf_op jit(solution)/shard_map/ppermute | solution.py:615
  41.1 1.2 copy-start.12
  41.5 0.8 copy-start.13
  41.9 0.7 copy-start.14
  42.6 0.7 copy-start.15
  50.0 13.0 %collective-permute-start.12 = (bf16[24,16,128]{2,1,0:T(8,128)(2,1)}, bf16[24,16,128]{2,1,0:T(8,128)(2,1)S(1)}, u32[]{:S(2)}, u32[]{:S(2)}) collective-permute-start(bf16[24,16,128]{2,1,0:T(8,128)(2,1)} %correct.1), channel_id=1, source_target_pairs={{0,6},{1,7},{2,4},{3,5},{4,2},{5,3},{6,0},{7,1},{8,14},{9,15},{10,... | collective-permute-start | bytes 294920 | tf_op jit(solution)/shard_map/ppermute | solution.py:615
  53.8 9.2 %collective-permute-start.11 = (bf16[24,16,128]{2,1,0:T(8,128)(2,1)}, bf16[24,16,128]{2,1,0:T(8,128)(2,1)S(1)}, u32[]{:S(2)}, u32[]{:S(2)}) collective-permute-start(bf16[24,16,128]{2,1,0:T(8,128)(2,1)} %correct.1), channel_id=1, source_target_pairs={{0,4},{1,5},{2,6},{3,7},{4,0},{5,1},{6,2},{7,3},{8,12},{9,13},{10,... | collective-permute-start | bytes 294920 | tf_op jit(solution)/shard_map/ppermute | solution.py:615
  53.8 9.2 %collective-permute-start.10 = (bf16[24,16,128]{2,1,0:T(8,128)(2,1)}, bf16[24,16,128]{2,1,0:T(8,128)(2,1)S(1)}, u32[]{:S(2)}, u32[]{:S(2)}) collective-permute-start(bf16[24,16,128]{2,1,0:T(8,128)(2,1)} %correct.1), channel_id=1, source_target_pairs={{0,2},{1,3},{2,0},{3,1},{4,6},{5,7},{6,4},{7,5},{8,10},{9,11},{10,... | collective-permute-start | bytes 294920 | tf_op jit(solution)/shard_map/ppermute | solution.py:615
  64.0 5.8 %copy-start = (bf16[96,16,128]{2,1,0:T(8,128)(2,1)}, bf16[96,16,128]{2,1,0:T(8,128)(2,1)S(1)}, u32[]{:S(2)}) copy-start(bf16[96,16,128]{2,1,0:T(8,128)(2,1)S(1)} %pad_maximum_fusion.1) | copy-start | bytes 1179652
  64.0 21.5 %collective-permute-start.13 = (bf16[96,16,128]{2,1,0:T(8,128)(2,1)S(1)}, bf16[96,16,128]{2,1,0:T(8,128)(2,1)S(1)}, u32[]{:S(2)}, u32[]{:S(2)}) collective-permute-start(bf16[96,16,128]{2,1,0:T(8,128)(2,1)S(1)} %pad_maximum_fusion.1), channel_id=1, source_target_pairs={{0,8},{8,0},{16,24},{24,16},{1,9},{9,1},{17,25},{25,17},{2,10},{10... | collective-permute-start | bytes 1179656 | tf_op jit(solution)/shard_map/ppermute | solution.py:615
  65.7 19.8 %collective-permute-start.14 = (bf16[96,16,128]{2,1,0:T(8,128)(2,1)S(1)}, bf16[96,16,128]{2,1,0:T(8,128)(2,1)S(1)}, u32[]{:S(2)}, u32[]{:S(2)}) collective-permute-start(bf16[96,16,128]{2,1,0:T(8,128)(2,1)S(1)} %pad_maximum_fusion.1), channel_id=1, source_target_pairs={{0,16},{8,24},{16,0},{24,8},{1,17},{9,25},{17,1},{25,9},{2,18},{10... | collective-permute-start | bytes 1179656 | tf_op jit(solution)/shard_map/ppermute | solution.py:615
  67.2 18.3 %collective-permute-start.15 = (bf16[96,16,128]{2,1,0:T(8,128)(2,1)S(1)}, bf16[96,16,128]{2,1,0:T(8,128)(2,1)S(1)}, u32[]{:S(2)}, u32[]{:S(2)}) collective-permute-start(bf16[96,16,128]{2,1,0:T(8,128)(2,1)S(1)} %pad_maximum_fusion.1), channel_id=1, source_target_pairs={{0,24},{8,16},{16,8},{24,0},{1,25},{9,17},{17,9},{25,1},{2,26},{10... | collective-permute-start | bytes 1179656 | tf_op jit(solution)/shard_map/ppermute | solution.py:615
  67.5 2.3 %collective-permute-start.16 = (bf16[96,16,128]{2,1,0:T(8,128)(2,1)S(1)}, bf16[96,16,128]{2,1,0:T(8,128)(2,1)S(1)}, u32[]{:S(2)}, u32[]{:S(2)}) collective-permute-start(bf16[96,16,128]{2,1,0:T(8,128)(2,1)S(1)} %pad_maximum_fusion.1), channel_id=1, source_target_pairs={{0,1},{1,0},{2,3},{3,2},{4,5},{5,4},{6,7},{7,6},{8,9},{9,8},{10,11... | collective-permute-start | bytes 1179656 | tf_op jit(solution)/shard_map/ppermute | solution.py:615
  69.8 0.7 copy-start.1
  85.5 8.2 %copy-start.2 = (bf16[96,16,128]{2,1,0:T(8,128)(2,1)}, bf16[96,16,128]{2,1,0:T(8,128)(2,1)S(1)}, u32[]{:S(2)}) copy-start(bf16[96,16,128]{2,1,0:T(8,128)(2,1)S(1)} %collective-permute-done.13) | copy-start | bytes 1179652
  85.5 8.2 %copy-start.3 = (bf16[96,16,128]{2,1,0:T(8,128)(2,1)}, bf16[96,16,128]{2,1,0:T(8,128)(2,1)S(1)}, u32[]{:S(2)}) copy-start(bf16[96,16,128]{2,1,0:T(8,128)(2,1)S(1)} %collective-permute-done.14) | copy-start | bytes 1179652
  85.5 8.2 %copy-start.4 = (bf16[96,16,128]{2,1,0:T(8,128)(2,1)}, bf16[96,16,128]{2,1,0:T(8,128)(2,1)S(1)}, u32[]{:S(2)}) copy-start(bf16[96,16,128]{2,1,0:T(8,128)(2,1)S(1)} %collective-permute-done.15) | copy-start | bytes 1179652
  85.5 3.6 %collective-permute-start.18 = (bf16[96,16,128]{2,1,0:T(8,128)(2,1)S(1)}, bf16[96,16,128]{2,1,0:T(8,128)(2,1)S(1)}, u32[]{:S(2)}, u32[]{:S(2)}) collective-permute-start(bf16[96,16,128]{2,1,0:T(8,128)(2,1)S(1)} %collective-permute-done.14), channel_id=1, source_target_pairs={{0,1},{1,0},{2,3},{3,2},{4,5},{5,4},{6,7},{7,6},{8,9},{9,8},{10,11... | collective-permute-start | bytes 1179656 | tf_op jit(solution)/shard_map/ppermute | solution.py:615
  85.6 3.5 %collective-permute-start.19 = (bf16[96,16,128]{2,1,0:T(8,128)(2,1)S(1)}, bf16[96,16,128]{2,1,0:T(8,128)(2,1)S(1)}, u32[]{:S(2)}, u32[]{:S(2)}) collective-permute-start(bf16[96,16,128]{2,1,0:T(8,128)(2,1)S(1)} %collective-permute-done.15), channel_id=1, source_target_pairs={{0,1},{1,0},{2,3},{3,2},{4,5},{5,4},{6,7},{7,6},{8,9},{9,8},{10,11... | collective-permute-start | bytes 1179656 | tf_op jit(solution)/shard_map/ppermute | solution.py:615
  86.1 3.0 %collective-permute-start.17 = (bf16[96,16,128]{2,1,0:T(8,128)(2,1)S(1)}, bf16[96,16,128]{2,1,0:T(8,128)(2,1)S(1)}, u32[]{:S(2)}, u32[]{:S(2)}) collective-permute-start(bf16[96,16,128]{2,1,0:T(8,128)(2,1)S(1)} %collective-permute-done.13), channel_id=1, source_target_pairs={{0,1},{1,0},{2,3},{3,2},{4,5},{5,4},{6,7},{7,6},{8,9},{9,8},{10,11... | collective-permute-start | bytes 1179656 | tf_op jit(solution)/shard_map/ppermute | solution.py:615
  89.2 4.6 %copy-start.5 = (bf16[96,16,128]{2,1,0:T(8,128)(2,1)}, bf16[96,16,128]{2,1,0:T(8,128)(2,1)S(1)}, u32[]{:S(2)}) copy-start(bf16[96,16,128]{2,1,0:T(8,128)(2,1)S(1)} %collective-permute-done.18) | copy-start | bytes 1179652
  89.2 4.6 %copy-start.6 = (bf16[96,16,128]{2,1,0:T(8,128)(2,1)}, bf16[96,16,128]{2,1,0:T(8,128)(2,1)S(1)}, u32[]{:S(2)}) copy-start(bf16[96,16,128]{2,1,0:T(8,128)(2,1)S(1)} %collective-permute-done.19) | copy-start | bytes 1179652
  89.2 4.6 %copy-start.7 = (bf16[96,16,128]{2,1,0:T(8,128)(2,1)}, bf16[96,16,128]{2,1,0:T(8,128)(2,1)S(1)}, u32[]{:S(2)}) copy-start(bf16[96,16,128]{2,1,0:T(8,128)(2,1)S(1)} %collective-permute-done.17) | copy-start | bytes 1179652

commit v3 on v2

--- a/solution.py
+++ b/solution.py
@@ -3,6 +3,7 @@
 
 import jax
 import jax.numpy as jnp
+import numpy as np
 from jax import lax
 from jax.experimental import pallas as pl
 from jax.experimental.pallas import tpu as pltpu
@@ -30,7 +31,7 @@
     return (a[0], -a[1])
 
 
-def sky_kernel(vis_ref, offset_ref, scale_ref, out_ref, cos_ref, sin_ref):
+def sky_kernel(vis_ref, offset_ref, scale_ref, out_ref, power_ref):
     count, _, vis_count = vis_ref.shape
     times = offset_ref.shape[1]
     step = math.gcd(vis_count, 256)
@@ -42,36 +43,45 @@
     for _ in range(3):
         parts.append(offsets.astype(bf16))
         offsets = offsets - parts[-1].astype(f32)
-    for start in range(0, vis_count, 512):
-        width = min(512, vis_count - start)
+    channels = vis_count // times
+    repeats = max(1, LANES // channels)
+    scale = jnp.concatenate([scale_ref[...]] * repeats, axis=1)
+    width = math.gcd(vis_count, 512)
+    scale = jnp.concatenate([scale] * (width // (repeats * channels)), axis=1)
+    for start in range(0, vis_count, width):
         at = pl.ds(start, width)
         time = lax.broadcasted_iota(jnp.int32, (times, width), 0)
         place = lax.broadcasted_iota(jnp.int32, (times, width), 1) + start
-        one = (place // (vis_count // times) == time).astype(f32).astype(bf16)
+        one = (place // channels == time).astype(f32).astype(bf16)
         shifts = sum(jnp.dot(part, one, preferred_element_type=f32) for part in parts)
-        half = (math.pi / SUB) * (shifts * scale_ref[:, at])
+        half = (math.pi / SUB) * (shifts * scale)
         square = half * half
         sine, cosine = 1.0, 1.0
         for term in (12, 10, 8, 6, 4, 2):
             sine = 1.0 - square * (1.0 / (term * (term + 1))) * sine
             cosine = 1.0 - square * (1.0 / (term * (term - 1))) * cosine
         sine = sine * half
-        cos_ref[:, at] = 1.0 - 2.0 * sine * sine
-        sin_ref[:, at] = 2.0 * sine * cosine
-
-    def powers(c, s, extra):
-        z = (jnp.broadcast_to(c, (8, step)), jnp.broadcast_to(s, (8, step)))
-        low = (jnp.where(bits[0], z[0], 1.0), jnp.where(bits[0], z[1], 0.0))
-        power = z
+        power = (1.0 - 2.0 * sine * sine, 2.0 * sine * cosine)
+        for bit in range(5):
+            power_ref[bit, 0, :, at] = power[0]
+            power_ref[bit, 1, :, at] = power[1]
+            power = (power[0] * power[0] - power[1] * power[1], 2.0 * power[0] * power[1])
+
+    def powers(row, at, extra):
+        z = [
+            tuple(
+                jnp.broadcast_to(power_ref[bit, part, pl.ds(row, 1), at], (8, step))
+                for part in range(2)
+            )
+            for bit in range(5)
+        ]
+        low = (jnp.where(bits[0], z[0][0], 1.0), jnp.where(bits[0], z[0][1], 0.0))
         for bit in (1, 2):
-            power = (power[0] * power[0] - power[1] * power[1], 2.0 * power[0] * power[1])
-            more = cmul(low, power)
+            more = cmul(low, z[bit])
             low = (jnp.where(bits[bit], more[0], low[0]), jnp.where(bits[bit], more[1], low[1]))
-        eight = (power[0] * power[0] - power[1] * power[1], 2.0 * power[0] * power[1])
-        sixteen = (eight[0] * eight[0] - eight[1] * eight[1], 2.0 * eight[0] * eight[1])
         if extra is not None:
             low = cmul(low, extra)
-        blocks = [cmul(low, conj(sixteen)), cmul(low, conj(eight)), low, cmul(low, eight)]
+        blocks = [cmul(low, conj(z[4])), cmul(low, conj(z[3])), low, cmul(low, z[3])]
         return jnp.concatenate([block[part] for part in range(2) for block in blocks], axis=0).astype(bf16)
 
     def one_subgrid(s):
@@ -82,9 +92,8 @@
                 jnp.broadcast_to(vis_ref[s, part : part + 1, at].astype(f32), (8, step))
                 for part in range(2)
             )
-            u_row, v_row = pl.ds(2 * s, 1), pl.ds(2 * s + 1, 1)
-            left = powers(cos_ref[u_row, at], sin_ref[u_row, at], vis)
-            right = powers(cos_ref[v_row, at], sin_ref[v_row, at], None)
+            left = powers(2 * s, at, vis)
+            right = powers(2 * s + 1, at, None)
             both += lax.dot_general(
                 left, right, (((1,), (1,)), ((), ())), preferred_element_type=f32
             )
@@ -112,11 +121,11 @@
         in_specs=[
             pl.BlockSpec((count, 2, vis_count), lambda i: (at, 0, 0)),
             pl.BlockSpec((2 * count, times), lambda i: (at, 0)),
-            pl.BlockSpec((1, vis_count), lambda i: (0, 0)),
+            pl.BlockSpec(scale_row.shape, lambda i: (0, 0)),
         ],
         out_specs=pl.BlockSpec((count, HALF, PACK), lambda i: (0, 0, 0)),
         out_shape=jax.ShapeDtypeStruct((count, HALF, PACK), f32),
-        scratch_shapes=[pltpu.VMEM((2 * count, vis_count), f32)] * 2,
+        scratch_shapes=[pltpu.VMEM((5, 2, 2 * count, vis_count), f32)],
         compiler_params=pltpu.CompilerParams(vmem_limit_bytes=VMEM_BYTES),
         cost_estimate=pl.CostEstimate(
             flops=0, bytes_accessed=count * 2_500_000, transcendentals=0
@@ -170,20 +179,11 @@
 
 def corrected_subgrids(stations, tables, skies, factor, interpret=False):
     count = factor.shape[0]
-    centred = jnp.arange(SUB, dtype=jnp.int32) - HALF
-    index = jnp.arange(SUB, dtype=jnp.int32)
-    angle = 2.0 * math.pi / SUB * (centred[:, None] * centred[None, :] % SUB).astype(f32)
-    cols_re, cols_im = jnp.cos(angle) / SUB, -jnp.sin(angle) / SUB
-    block = jnp.concatenate(
-        [
-            jnp.concatenate([cols_re.T, cols_im.T], axis=1),
-            jnp.concatenate([-cols_im.T, cols_re.T], axis=1),
-        ],
-        axis=0,
-    )
-    right = jnp.kron(jnp.eye(2, dtype=f32), block).astype(bf16)
-    angle = 2.0 * math.pi / SUB * ((index - HALF)[:, None] * centred[None, :] % SUB).astype(f32)
-    left = jnp.concatenate([jnp.cos(angle) / SUB, -jnp.sin(angle) / SUB], axis=0).astype(bf16)
+    centred = np.arange(SUB) - HALF
+    angle = 2.0 * math.pi / SUB * (centred[:, None] * centred[None, :] % SUB)
+    re, im = np.cos(angle) / SUB, -np.sin(angle) / SUB
+    right = jnp.asarray(np.kron(np.eye(2), np.block([[re, im], [-im, re]])), bf16)
+    left = jnp.asarray(np.concatenate([re, im], axis=0), bf16)
     rows = sum(piece.shape[0] for piece in tables)
     operands = [*tables, *skies, factor, right, left]
 
@@ -424,8 +424,7 @@
         left[h, :image_rows] = turned[0]
         left[h, image_rows:] = turned[1]
 
-    def sums(pair, h, left, first):
-        index = pair + HALF * h
+    def sums_of(index, left):
         late = shifts[...] > index.astype(f32)
         table = jnp.concatenate(
             [
@@ -434,15 +433,23 @@
             ],
             axis=1,
         )
-        four = jnp.dot(left[h], table, preferred_element_type=f32)
+        four = jnp.dot(left, table, preferred_element_type=f32)
         got = (
             four[:image_rows, :FINE] - four[image_rows:, FINE:],
             four[:image_rows, FINE:] + four[image_rows:, :FINE],
         )
         twist = twist_ref[pl.ds(index, 1), :]
-        done = cmul(got, (twist[:, :FINE], twist[:, FINE:]))
-        for part in range(2):
-            total[index, part] = done[part] if first else total[index, part] + done[part]
+        return cmul(got, (twist[:, :FINE], twist[:, FINE:]))
+
+    def sums(pair, left, first):
+        low, high = sums_of(pair, left[0]), sums_of(pair + HALF, left[1])
+        turn = twist_ref[pl.ds(SUB + pair, 1), :]
+        even = (low[0] + high[0], low[1] + high[1])
+        odd = cmul((low[0] - high[0], low[1] - high[1]), (turn[:, :FINE], turn[:, FINE:]))
+        for half, done in enumerate((even, odd)):
+            for part in range(2):
+                at = (half * HALF + pair, part)
+                total[at] = done[part] if first else total[at] + done[part]
 
     def chunk(first):
         held = 0
@@ -475,10 +482,10 @@
         def two_pairs(i, carry):
             for h in range(2):
                 products(2 * i + 1, h, left_odd)
-                sums(2 * i, h, left_even, first)
+            sums(2 * i, left_even, first)
             for h in range(2):
                 products(jnp.minimum(2 * i + 2, HALF - 1), h, left_even)
-                sums(2 * i + 1, h, left_odd, first)
+            sums(2 * i + 1, left_odd, first)
             return carry
 
         lax.fori_loop(0, HALF // 2, two_pairs, 0)
@@ -502,11 +509,15 @@
             at = pl.ds(pl.multiple_of(first + 8 * group, 8), 8)
             for tile in range(FINE // LANES):
                 lanes = pl.ds(tile * LANES, LANES)
-                values = [(total[n, 0, at, lanes], total[n, 1, at, lanes]) for n in range(SUB)]
-                for k, value in enumerate(short_transform(values)):
-                    for part in range(2):
-                        column = 2 * (k * (FINE // LANES) + tile) + part
-                        staged[pl.ds(column, 8, stride=wide + 1), :] = value[part]
+                for half in range(2):
+                    values = [
+                        (total[half * HALF + n, 0, at, lanes], total[half * HALF + n, 1, at, lanes])
+                        for n in range(HALF)
+                    ]
+                    for k, value in enumerate(short_transform(values)):
+                        for part in range(2):
+                            column = 2 * ((2 * k + half) * (FINE // LANES) + tile) + part
+                            staged[pl.ds(column, 8, stride=wide + 1), :] = value[part]
             for row in range(8):
                 at = pl.ds(pl.multiple_of((8 * group + row) * wide, wide), wide)
                 out_ref[at, :] = staged[row * (wide + 1) : row * (wide + 1) + wide, :]
@@ -532,13 +543,16 @@
         [jnp.concatenate([re, -im], axis=1), jnp.concatenate([im, re], axis=1)], axis=0
     )
     columns = jnp.kron(jnp.eye(2, dtype=f32), block).astype(bf16)
-    fine = jnp.arange(FINE, dtype=jnp.int32)
-    angle = 2.0 * math.pi / FINE * (fine[:, None] * fine[None, :] % FINE).astype(f32)
-    unit = jnp.concatenate([jnp.cos(angle), jnp.sin(angle)], axis=1).astype(bf16)
-    angle = turn * (jnp.arange(SUB, dtype=jnp.int32)[:, None] * fine[None, :]).astype(f32)
+    fine = np.arange(FINE)
+    angle = 2.0 * math.pi / FINE * (fine[:, None] * fine[None, :] % FINE)
+    unit = jnp.asarray(np.concatenate([np.cos(angle), np.sin(angle)], axis=1), bf16)
     scale = 1.0 / (SUB * math.sqrt(total))
-    twist = jnp.concatenate([jnp.cos(angle), jnp.sin(angle)], axis=1) * scale
-    counts = jnp.broadcast_to(jnp.arange(SUB, dtype=f32)[:, None], (SUB, LANES)).astype(bf16)
+    angle = 2.0 * math.pi / G * (np.arange(SUB)[:, None] * fine[None, :])
+    twist = np.concatenate([np.cos(angle), np.sin(angle)], axis=1) * scale
+    angle = 2.0 * math.pi / SUB * np.arange(HALF)[:, None] + 0.0 * fine
+    turn_half = np.concatenate([np.cos(angle), np.sin(angle)], axis=1)
+    twist = jnp.asarray(np.concatenate([twist, turn_half], axis=0), f32)
+    counts = jnp.asarray(np.broadcast_to(np.arange(SUB)[:, None], (SUB, LANES)), bf16)
     last = chunks - 1
 
     def chunk_of(i):
@@ -670,7 +684,7 @@
 
     sent = jnp.concatenate([packed_beams(beam_terms), coded_corners(corners)], axis=0)
     offsets = baseline_offsets.reshape(2 * count, -1)
-    scale_row = jnp.tile(channel_scale, baseline_offsets.shape[2]).reshape(1, vis_count)
+    scale_row = channel_scale.reshape(1, -1)
     part = math.gcd(count, 8)
     skies = [sky_sums(visibilities, offsets, scale_row, 0, part)]
     if by_mask:

time: 133 us -> 126 us (0.947)
  Pallas kernels: 78.1 us -> 73.7 us
  other arithmetic: 20.1 us -> 16.4 us
  waiting for transfers between devices: 1.69 us -> 4.8 us
  local copies, waits for them, and re-layouts: 11.8 us -> 8.9 us
    pallas_call x1, Pallas kernels: 14.9 us -> 10.6 us  [uv_tile_own(): pl.pallas_call(functools.partial(tile_kernel, pieces=len(uv), tile_rows=t...]
    ppermute x20, waiting for transfers between devices: 1.69 us -> 4.8 us  [from_partner(): return lax.ppermute(value, axis, [(i, i ^ mask) for i in range(count)])]
    pallas_call x3, Pallas kernels: 15.6 us -> 13.8 us  [sky_sums(): pl.pallas_call(sky_kernel, grid=(1,), in_specs=[pl.BlockSpec((count, 2, v...]
    pallas_call x1, Pallas kernels: 37.3 us -> 38.9 us  [image_rows_of(): pl.pallas_call(functools.partial(image_kernel, pieces=len(uv), chunks=chu...]
    concatenate x3 -> x0, other arithmetic: 1.42 us -> none  [the longest x1 0.73 us: image_rows_of(): jnp.concatenate([jnp.cos(angle), jnp.sin(angle)], axis=1).astype(bf16)]
    another operation x2 -> x0, local copies, waits for them, and re-layouts: 1.35 us -> none  [on_device(): jnp.tile(channel_scale, baseline_offsets.shape[2]).reshape(1, vis_count)]
    another operation x3 -> x1, other arithmetic: 4.72 us -> 3.47 us
  transfers between devices with their start and end apart: 20 -> 20, of which waited for: 4 -> 5; matrix products, arithmetic and copies ran while one was open for 19% -> 16% of each run, Pallas kernels for 23% -> 20%
where the time goes in v3:
time: 126 us; the launch traced here: 124 us
  Pallas kernels  73.7 us (58%)
  starting transfers between devices  18.9 us (15%)
  other arithmetic  16.4 us (13%)
  local copies, waits for them, and re-layouts  8.9 us (7%)
  waiting for transfers between devices  4.8 us (4%)
    pallas_call x1, Pallas kernels, image_rows_of(): pl.pallas_call(functools.partial(image_kernel, pieces=len(uv), chunks=chu...  38.9 us
    ppermute x20, starting transfers between devices, from_partner(): return lax.ppermute(value, axis, [(i, i ^ mask) for i in range(count)])  18.9 us
    pallas_call x3, Pallas kernels, sky_sums(): pl.pallas_call(sky_kernel, grid=(1,), in_specs=[pl.BlockSpec((count, 2, v...  13.8 us
    pallas_call x1, Pallas kernels, uv_tile_own(): pl.pallas_call(functools.partial(tile_kernel, pieces=len(uv), tile_rows=t...  10.6 us
    pallas_call x1, Pallas kernels, corrected_subgrids(): pl.pallas_call(functools.partial(correct_kernel, pieces=len(tables), skie...  6.66 us
    unnamed x53, local copies, waits for them, and re-layouts  4.83 us
    ppermute x20, waiting for transfers between devices, from_partner(): return lax.ppermute(value, axis, [(i, i ^ mask) for i in range(count)])  4.8 us
    pallas_call x1, Pallas kernels, uv_tile_spill(): pl.pallas_call(functools.partial(spill_kernel, pieces=len(uv), lanes=lane...  3.72 us
  transfers between devices with their start and end apart: 20, of which 5 were waited for; matrix products, arithmetic and copies ran while one was open for 16% of the time, Pallas kernels for 20%

profile of v3, /device:TPU:0, one launch (start us, length us, event | category | flops | bytes accessed | tf_op | source)
XLA Modules:
  0.0 124.0 jit_solution(6166248072036227927)
XLA Ops:
  0.6 1.0 reshape.698
  1.7 0.2 copy.47
  1.9 0.2 reshape.699
  2.1 0.8 and_select_fusion.15
  2.9 0.1 convert_element_type.99
  3.0 3.1 %collective-permute-start = (bf16[17,16,128]{2,1,0:T(8,128)(2,1)S(1)}, bf16[17,16,128]{2,1,0:T(8,128)(2,1)S(1)}, u32[]{:S(2)}, u32[]{:S(2)}) collective-permute-start(bf16[17,16,128]{2,1,0:T(8,128)(2,1)S(1)} %pad_maximum_fusion.2), channel_id=1, source_target_pairs={{0,2},{1,3},{2,0},{3,1},{4,6},{5,7},{6,4},{7,5},{8,10},{9,11},{10,... | collective-permute-start | bytes 208904 | tf_op jit(solution)/shard_map/ppermute | solution.py:629
  6.1 2.6 %collective-permute-start.1 = (bf16[17,16,128]{2,1,0:T(8,128)(2,1)S(1)}, bf16[17,16,128]{2,1,0:T(8,128)(2,1)S(1)}, u32[]{:S(2)}, u32[]{:S(2)}) collective-permute-start(bf16[17,16,128]{2,1,0:T(8,128)(2,1)S(1)} %pad_maximum_fusion.2), channel_id=1, source_target_pairs={{0,4},{1,5},{2,6},{3,7},{4,0},{5,1},{6,2},{7,3},{8,12},{9,13},{10,... | collective-permute-start | bytes 208904 | tf_op jit(solution)/shard_map/ppermute | solution.py:629
  8.7 0.7 and_select_fusion.2
  9.4 0.7 fusion.27
  10.2 0.7 broadcast_multiply_fusion
  10.8 0.1 fusion.20
  11.0 0.2 multiply_convert_fusion
  11.2 4.6 %sky_sums.3.refs_8_ = f32[8,16,128]{2,1,0:T(8,128)} custom-call(bf16[24,2,2048]{2,1,0:T(2,128)(2,1)} %vis_ref.5, f32[48,128]{1,0:T(8,128)} %bitcast.146, f32[1,16]{1,0:T(1,128)} %bitcast.157), custom_call_target="tpu_custom_call" | custom-call | bytes 20000000 | tf_op jit(solution)/shard_map/sky_sums/pallas_call | solution.py:118
  16.0 1.8 %collective-permute-start.3 = (bf16[68,16,128]{2,1,0:T(8,128)(2,1)S(1)}, bf16[68,16,128]{2,1,0:T(8,128)(2,1)S(1)}, u32[]{:S(2)}, u32[]{:S(2)}) collective-permute-start(bf16[68,16,128]{2,1,0:T(8,128)(2,1)S(1)} %constant_dynamic-update-slice_fusion.refs_0_), channel_id=1, source_target_pairs={{0,8},{8,0},{16,24},{24,16},{1,9},{9,1},{17,25},{25,17},{2,10},{10... | collective-permute-start | bytes 835592 | tf_op jit(solution)/shard_map/ppermute | solution.py:629
  17.7 1.5 %collective-permute-start.4 = (bf16[68,16,128]{2,1,0:T(8,128)(2,1)S(1)}, bf16[68,16,128]{2,1,0:T(8,128)(2,1)S(1)}, u32[]{:S(2)}, u32[]{:S(2)}) collective-permute-start(bf16[68,16,128]{2,1,0:T(8,128)(2,1)S(1)} %constant_dynamic-update-slice_fusion.refs_0_), channel_id=1, source_target_pairs={{0,16},{8,24},{16,0},{24,8},{1,17},{9,25},{17,1},{25,9},{2,18},{10... | collective-permute-start | bytes 835592 | tf_op jit(solution)/shard_map/ppermute | solution.py:629
  19.3 0.3 collective-permute-start.5
  19.5 0.1 copy.25
  19.6 0.6 reshape.711.stations_ref
  20.3 0.8 copy.27.refs_10_
  21.1 1.5 %fusion.8.refs_11_ = f32[24,16,128]{2,1,0:T(8,128)} fusion(f32[16,128]{1,0:T(8,128)S(1)} %get-tuple-element.59, f32[128]{0:T(128)S(1)} %fusion.31, s32[16,128]{1,0:T(8,128)S(1)} %fusion.21, s32[24]{0:T(128)S(1)} %and_select_fusion.2, f32[16,128]{1,0:T(8,128)S(1)} %get-tuple-element.58, f32[24]{0:T(128)S(1)} %broadcast_multiply_fusion), kind=kLoop, calls=%fused_computation.26 | loop fusion | flops 884736 | bytes 221888 | tf_op jit(solution)/shard_map/mul | solution.py:624
  22.6 4.6 %sky_sums.4.refs_9_ = f32[8,16,128]{2,1,0:T(8,128)} custom-call(bf16[24,2,2048]{2,1,0:T(2,128)(2,1)} %vis_ref.5, f32[48,128]{1,0:T(8,128)} %bitcast.147, f32[1,16]{1,0:T(1,128)} %bitcast.158), custom_call_target="tpu_custom_call" | custom-call | bytes 20000000 | tf_op jit(solution)/shard_map/sky_sums/pallas_call | solution.py:118
  27.2 4.6 %sky_sums.5.refs_10_ = f32[8,16,128]{2,1,0:T(8,128)} custom-call(bf16[24,2,2048]{2,1,0:T(2,128)(2,1)} %vis_ref.5, f32[48,128]{1,0:T(8,128)} %bitcast.148, f32[1,16]{1,0:T(1,128)} %bitcast.159), custom_call_target="tpu_custom_call" | custom-call | bytes 20000000 | tf_op jit(solution)/shard_map/sky_sums/pallas_call | solution.py:118
  32.0 0.5 collective-permute-start.7
  32.5 0.1 collective-permute-start.8
  32.6 0.4 collective-permute-start.9
  33.1 0.5 collective-permute-done.6.refs_1_
  33.5 0.4 collective-permute-done.7.refs_3_
  33.9 0.4 collective-permute-done.8.refs_5_
  34.3 0.4 collective-permute-done.9.refs_7_
  34.8 0.3 copy-done.14
  35.0 0.7 copy-done.15
  35.7 6.7 %correct.1 = bf16[24,16,128]{2,1,0:T(8,128)(2,1)} custom-call(s32[48]{0:T(128)} %reshape.711.stations_ref, bf16[68,16,128]{2,1,0:T(8,128)(2,1)} %copy-done.8, bf16[68,16,128]{2,1,0:T(8,128)(2,1)} %copy-done.12, bf16[68,16,128]{2,1,0:T(8,128)(2,1)} %copy-done.9, bf16[68,16,128]{2,1,0:T(8,128)(2,1)} %copy-done.13, bf16[68,16,128]{2,1,0:T(8,128)(2,1)} %copy-done.10, ...), custom_call_target="tpu_custom_call" | custom-call | bytes 16000000 | tf_op jit(solution)/shard_map/correct/pallas_call | solution.py:193
  42.4 3.8 %collective-permute-start.12 = (bf16[24,16,128]{2,1,0:T(8,128)(2,1)}, bf16[24,16,128]{2,1,0:T(8,128)(2,1)S(1)}, u32[]{:S(2)}, u32[]{:S(2)}) collective-permute-start(bf16[24,16,128]{2,1,0:T(8,128)(2,1)} %correct.1), channel_id=1, source_target_pairs={{0,6},{1,7},{2,4},{3,5},{4,2},{5,3},{6,0},{7,1},{8,14},{9,15},{10,... | collective-permute-start | bytes 294920 | tf_op jit(solution)/shard_map/ppermute | solution.py:629
  46.2 0.6 collective-permute-start.10
  46.8 0.7 slice_bitcast_fusion.6
  47.5 0.7 slice_bitcast_fusion.4
  48.2 0.7 slice_bitcast_fusion.2
  49.0 0.7 slice_bitcast_fusion
  49.7 0.1 concatenate.55
  50.0 0.1 add.323
  50.1 0.1 add.331
  50.1 3.5 %cosine_convert_fusion = (bf16[1,256,768]{2,1,0:T(8,128)(2,1)S(1)}, bf16[1,256,768]{2,1,0:T(8,128)(2,1)S(1)}) fusion(s32[768]{0:T(1024)S(1)} %add.323, s32[256]{0:T(256)S(1)} %iota_add_fusion.1), kind=kLoop, calls=%fused_computation.10 | loop fusion | flops 3145728 | bytes 790528 | tf_op jit(solution)/shard_map/convert
  53.6 1.3 %convert_reduce_fusion.3 = (s32[]{:T(128)}, pred[192]{0:T(512)(128)(4,1)S(1)}, s32[192]{0:T(256)}, s32[192]{0:T(256)}, s32[192]{0:T(256)}, /*index=5*/s32[]{:T(128)}, pred[192]{0:T(512)(128)(4,1)S(1)}, s32[192]{0:T(256)}) fusion(s32[]{:T(128)S(6)} %mul.276, s32[768]{0:T(1024)S(1)} %add.323, s32[]{:T(128)S(6)} %select_n.268, s32[]{:T(128)S(6)} %mul.278, ...), kind=kLoop, calls=%fused_computation.138 | loop fusion | flops 5374 | bytes 6552 | tf_op jit(solution)/shard_map/reduce_sum | solution.py:311
  54.9 0.1 convert_reduce_fusion
  55.1 0.1 select_reduce_fusion
  55.2 0.1 convert_reduce_fusion.1
  55.3 0.9 pad_maximum_fusion.1
  56.3 1.8 %collective-permute-start.13 = (bf16[96,16,128]{2,1,0:T(8,128)(2,1)S(1)}, bf16[96,16,128]{2,1,0:T(8,128)(2,1)S(1)}, u32[]{:S(2)}, u32[]{:S(2)}) collective-permute-start(bf16[96,16,128]{2,1,0:T(8,128)(2,1)S(1)} %pad_maximum_fusion.1), channel_id=1, source_target_pairs={{0,8},{8,0},{16,24},{24,16},{1,9},{9,1},{17,25},{25,17},{2,10},{10... | collective-permute-start | bytes 1179656 | tf_op jit(solution)/shard_map/ppermute | solution.py:629
  58.1 1.5 %collective-permute-start.14 = (bf16[96,16,128]{2,1,0:T(8,128)(2,1)S(1)}, bf16[96,16,128]{2,1,0:T(8,128)(2,1)S(1)}, u32[]{:S(2)}, u32[]{:S(2)}) collective-permute-start(bf16[96,16,128]{2,1,0:T(8,128)(2,1)S(1)} %pad_maximum_fusion.1), channel_id=1, source_target_pairs={{0,16},{8,24},{16,0},{24,8},{1,17},{9,25},{17,1},{25,9},{2,18},{10... | collective-permute-start | bytes 1179656 | tf_op jit(solution)/shard_map/ppermute | solution.py:629
  59.6 0.3 collective-permute-start.15
  59.9 1.3 %pad_add_fusion.1.list_ref = s32[193]{0:T(256)} fusion(s32[192]{0:T(256)S(1)} %select_reduce_fusion, s32[1]{0:T(128)} %bitcast.17), kind=kLoop, calls=%fused_computation.130 | loop fusion | flops 193 | bytes 1544 | tf_op jit(solution)/shard_map/concatenate | solution.py:311
  61.2 1.0 pad_maximum_fusion.refs_9_
  62.1 0.7 copy-done.1
  62.9 10.6 %uv_tile.1.refs_2_ = f32[32768,128]{1,0:T(8,128)} custom-call(s32[1]{0:T(128)} %bitcast.16.block_ref, s32[193]{0:T(256)} %pad_add_fusion.1.list_ref, s32[192]{0:T(256)} %get-tuple-element.49.row_ref, s32[192]{0:T(256)} %get-tuple-element.52.col_ref, bf16[1536,128]{1,0:T(8,128)(2,1)} %bitcast.123, bf16[1536,128]{1,0:T(8,128)(2,1)} %bitcast.125), custom_call_target="tpu_custom_call" | custom-call | bytes 41943040 | tf_op jit(solution)/shard_map/uv_tile/pallas_call | solution.py:330
  73.5 3.1 %collective-permute-done.14 = bf16[96,16,128]{2,1,0:T(8,128)(2,1)S(1)} collective-permute-done((bf16[96,16,128]{2,1,0:T(8,128)(2,1)S(1)}, bf16[96,16,128]{2,1,0:T(8,128)(2,1)S(1)}, u32[]{:S(2)}, u32[]{:S(2)}) %collective-permute-start.14) | collective-permute-done | bytes 393248 | tf_op jit(solution)/shard_map/ppermute | solution.py:629
  76.7 0.5 collective-permute-start.19
  77.2 0.1 collective-permute-start.17
  77.2 0.1 select_reduce_fusion.1
  77.4 0.7 add.357.refs_8_
  78.0 1.2 pad_add_fusion.list_ref
  79.3 0.8 select_select_fusion.1
  80.1 1.0 select_select_fusion
  81.1 3.7 %uv_spill.1 = f32[32768,128]{1,0:T(8,128)} custom-call(s32[1]{0:T(128)} %constant.300.clone.1.block_ref, s32[193]{0:T(256)} %pad_add_fusion.list_ref, s32[192]{0:T(256)} %get-tuple-element.40.row_ref, s32[192]{0:T(256)} %get-tuple-element.39.col_ref, bf16[1536,128]{1,0:T(8,128)(2,1)} %bitcast.127, ...), custom_call_target="tpu_custom_call", output_to_operand_aliasing={{}: (6, {})} | custom-call | bytes 8000000 | tf_op jit(solution)/shard_map/uv_spill/pallas_call | solution.py:358
  84.9 38.9 %image.1 = f32[32768,128]{1,0:T(8,128)} custom-call(bf16[1536,128]{1,0:T(8,128)(2,1)} %bitcast.124, bf16[1536,128]{1,0:T(8,128)(2,1)} %bitcast.126, bf16[1536,128]{1,0:T(8,128)(2,1)} %bitcast.129, bf16[1536,128]{1,0:T(8,128)(2,1)} %bitcast.134, bf16[1536,128]{1,0:T(8,128)(2,1)} %bitcast.130, bf16[1536,128]{1,0:T(8,128)(2,1)} %bitcast.132, ...), custom_call_target="tpu_custom_call" | custom-call | tf_op jit(solution)/shard_map/image/pallas_call | solution.py:561
  (83 shorter events, 0.6 us)
Async XLA Ops:
  3.0 12.9 %collective-permute-start = (bf16[17,16,128]{2,1,0:T(8,128)(2,1)S(1)}, bf16[17,16,128]{2,1,0:T(8,128)(2,1)S(1)}, u32[]{:S(2)}, u32[]{:S(2)}) collective-permute-start(bf16[17,16,128]{2,1,0:T(8,128)(2,1)S(1)} %pad_maximum_fusion.2), channel_id=1, source_target_pairs={{0,2},{1,3},{2,0},{3,1},{4,6},{5,7},{6,4},{7,5},{8,10},{9,11},{10,... | collective-permute-start | bytes 208904 | tf_op jit(solution)/shard_map/ppermute | solution.py:629
  6.1 9.8 %collective-permute-start.1 = (bf16[17,16,128]{2,1,0:T(8,128)(2,1)S(1)}, bf16[17,16,128]{2,1,0:T(8,128)(2,1)S(1)}, u32[]{:S(2)}, u32[]{:S(2)}) collective-permute-start(bf16[17,16,128]{2,1,0:T(8,128)(2,1)S(1)} %pad_maximum_fusion.2), channel_id=1, source_target_pairs={{0,4},{1,5},{2,6},{3,7},{4,0},{5,1},{6,2},{7,3},{8,12},{9,13},{10,... | collective-permute-start | bytes 208904 | tf_op jit(solution)/shard_map/ppermute | solution.py:629
  8.7 7.2 %collective-permute-start.2 = (bf16[17,16,128]{2,1,0:T(8,128)(2,1)S(1)}, bf16[17,16,128]{2,1,0:T(8,128)(2,1)S(1)}, u32[]{:S(2)}, u32[]{:S(2)}) collective-permute-start(bf16[17,16,128]{2,1,0:T(8,128)(2,1)S(1)} %pad_maximum_fusion.2), channel_id=1, source_target_pairs={{0,6},{1,7},{2,4},{3,5},{4,2},{5,3},{6,0},{7,1},{8,14},{9,15},{10,... | collective-permute-start | bytes 208904 | tf_op jit(solution)/shard_map/ppermute | solution.py:629
  16.0 18.8 %copy-start.8 = (bf16[68,16,128]{2,1,0:T(8,128)(2,1)}, bf16[68,16,128]{2,1,0:T(8,128)(2,1)S(1)}, u32[]{:S(2)}) copy-start(bf16[68,16,128]{2,1,0:T(8,128)(2,1)S(1)} %constant_dynamic-update-slice_fusion.refs_0_) | copy-start | bytes 835588
  16.0 15.9 %collective-permute-start.3 = (bf16[68,16,128]{2,1,0:T(8,128)(2,1)S(1)}, bf16[68,16,128]{2,1,0:T(8,128)(2,1)S(1)}, u32[]{:S(2)}, u32[]{:S(2)}) collective-permute-start(bf16[68,16,128]{2,1,0:T(8,128)(2,1)S(1)} %constant_dynamic-update-slice_fusion.refs_0_), channel_id=1, source_target_pairs={{0,8},{8,0},{16,24},{24,16},{1,9},{9,1},{17,25},{25,17},{2,10},{10... | collective-permute-start | bytes 835592 | tf_op jit(solution)/shard_map/ppermute | solution.py:629
  17.7 14.1 %collective-permute-start.4 = (bf16[68,16,128]{2,1,0:T(8,128)(2,1)S(1)}, bf16[68,16,128]{2,1,0:T(8,128)(2,1)S(1)}, u32[]{:S(2)}, u32[]{:S(2)}) collective-permute-start(bf16[68,16,128]{2,1,0:T(8,128)(2,1)S(1)} %constant_dynamic-update-slice_fusion.refs_0_), channel_id=1, source_target_pairs={{0,16},{8,24},{16,0},{24,8},{1,17},{9,25},{17,1},{25,9},{2,18},{10... | collective-permute-start | bytes 835592 | tf_op jit(solution)/shard_map/ppermute | solution.py:629
  19.3 12.6 %collective-permute-start.5 = (bf16[68,16,128]{2,1,0:T(8,128)(2,1)S(1)}, bf16[68,16,128]{2,1,0:T(8,128)(2,1)S(1)}, u32[]{:S(2)}, u32[]{:S(2)}) collective-permute-start(bf16[68,16,128]{2,1,0:T(8,128)(2,1)S(1)} %constant_dynamic-update-slice_fusion.refs_0_), channel_id=1, source_target_pairs={{0,24},{8,16},{16,8},{24,0},{1,25},{9,17},{17,9},{25,1},{2,26},{10... | collective-permute-start | bytes 835592 | tf_op jit(solution)/shard_map/ppermute | solution.py:629
  31.9 2.9 %copy-start.9 = (bf16[68,16,128]{2,1,0:T(8,128)(2,1)}, bf16[68,16,128]{2,1,0:T(8,128)(2,1)S(1)}, u32[]{:S(2)}) copy-start(bf16[68,16,128]{2,1,0:T(8,128)(2,1)S(1)} %collective-permute-done.3.refs_2_) | copy-start | bytes 835588
  31.9 2.9 %copy-start.10 = (bf16[68,16,128]{2,1,0:T(8,128)(2,1)}, bf16[68,16,128]{2,1,0:T(8,128)(2,1)S(1)}, u32[]{:S(2)}) copy-start(bf16[68,16,128]{2,1,0:T(8,128)(2,1)S(1)} %collective-permute-done.4.refs_4_) | copy-start | bytes 835588
  31.9 2.8 %copy-start.11 = (bf16[68,16,128]{2,1,0:T(8,128)(2,1)}, bf16[68,16,128]{2,1,0:T(8,128)(2,1)S(1)}, u32[]{:S(2)}) copy-start(bf16[68,16,128]{2,1,0:T(8,128)(2,1)S(1)} %collective-permute-done.5.refs_6_) | copy-start | bytes 835588
  31.9 1.6 %collective-permute-start.6 = (bf16[68,16,128]{2,1,0:T(8,128)(2,1)S(1)}, bf16[68,16,128]{2,1,0:T(8,128)(2,1)S(1)}, u32[]{:S(2)}, u32[]{:S(2)}) collective-permute-start(bf16[68,16,128]{2,1,0:T(8,128)(2,1)S(1)} %constant_dynamic-update-slice_fusion.refs_0_), channel_id=1, source_target_pairs={{0,1},{1,0},{2,3},{3,2},{4,5},{5,4},{6,7},{7,6},{8,9},{9,8},{10,11... | collective-permute-start | bytes 835592 | tf_op jit(solution)/shard_map/ppermute | solution.py:629
  32.0 1.9 %collective-permute-start.7 = (bf16[68,16,128]{2,1,0:T(8,128)(2,1)S(1)}, bf16[68,16,128]{2,1,0:T(8,128)(2,1)S(1)}, u32[]{:S(2)}, u32[]{:S(2)}) collective-permute-start(bf16[68,16,128]{2,1,0:T(8,128)(2,1)S(1)} %collective-permute-done.3.refs_2_), channel_id=1, source_target_pairs={{0,1},{1,0},{2,3},{3,2},{4,5},{5,4},{6,7},{7,6},{8,9},{9,8},{10,11... | collective-permute-start | bytes 835592 | tf_op jit(solution)/shard_map/ppermute | solution.py:629
  32.5 1.8 %collective-permute-start.8 = (bf16[68,16,128]{2,1,0:T(8,128)(2,1)S(1)}, bf16[68,16,128]{2,1,0:T(8,128)(2,1)S(1)}, u32[]{:S(2)}, u32[]{:S(2)}) collective-permute-start(bf16[68,16,128]{2,1,0:T(8,128)(2,1)S(1)} %collective-permute-done.4.refs_4_), channel_id=1, source_target_pairs={{0,1},{1,0},{2,3},{3,2},{4,5},{5,4},{6,7},{7,6},{8,9},{9,8},{10,11... | collective-permute-start | bytes 835592 | tf_op jit(solution)/shard_map/ppermute | solution.py:629
  32.6 2.2 %collective-permute-start.9 = (bf16[68,16,128]{2,1,0:T(8,128)(2,1)S(1)}, bf16[68,16,128]{2,1,0:T(8,128)(2,1)S(1)}, u32[]{:S(2)}, u32[]{:S(2)}) collective-permute-start(bf16[68,16,128]{2,1,0:T(8,128)(2,1)S(1)} %collective-permute-done.5.refs_6_), channel_id=1, source_target_pairs={{0,1},{1,0},{2,3},{3,2},{4,5},{5,4},{6,7},{7,6},{8,9},{9,8},{10,11... | collective-permute-start | bytes 835592 | tf_op jit(solution)/shard_map/ppermute | solution.py:629
  33.5 1.2 copy-start.12
  33.9 0.8 copy-start.13
  34.3 0.7 copy-start.14
  35.0 0.7 copy-start.15
  42.4 12.9 %collective-permute-start.12 = (bf16[24,16,128]{2,1,0:T(8,128)(2,1)}, bf16[24,16,128]{2,1,0:T(8,128)(2,1)S(1)}, u32[]{:S(2)}, u32[]{:S(2)}) collective-permute-start(bf16[24,16,128]{2,1,0:T(8,128)(2,1)} %correct.1), channel_id=1, source_target_pairs={{0,6},{1,7},{2,4},{3,5},{4,2},{5,3},{6,0},{7,1},{8,14},{9,15},{10,... | collective-permute-start | bytes 294920 | tf_op jit(solution)/shard_map/ppermute | solution.py:629
  46.2 9.1 %collective-permute-start.11 = (bf16[24,16,128]{2,1,0:T(8,128)(2,1)}, bf16[24,16,128]{2,1,0:T(8,128)(2,1)S(1)}, u32[]{:S(2)}, u32[]{:S(2)}) collective-permute-start(bf16[24,16,128]{2,1,0:T(8,128)(2,1)} %correct.1), channel_id=1, source_target_pairs={{0,4},{1,5},{2,6},{3,7},{4,0},{5,1},{6,2},{7,3},{8,12},{9,13},{10,... | collective-permute-start | bytes 294920 | tf_op jit(solution)/shard_map/ppermute | solution.py:629
  46.2 9.1 %collective-permute-start.10 = (bf16[24,16,128]{2,1,0:T(8,128)(2,1)}, bf16[24,16,128]{2,1,0:T(8,128)(2,1)S(1)}, u32[]{:S(2)}, u32[]{:S(2)}) collective-permute-start(bf16[24,16,128]{2,1,0:T(8,128)(2,1)} %correct.1), channel_id=1, source_target_pairs={{0,2},{1,3},{2,0},{3,1},{4,6},{5,7},{6,4},{7,5},{8,10},{9,11},{10,... | collective-permute-start | bytes 294920 | tf_op jit(solution)/shard_map/ppermute | solution.py:629
  56.3 5.8 %copy-start = (bf16[96,16,128]{2,1,0:T(8,128)(2,1)}, bf16[96,16,128]{2,1,0:T(8,128)(2,1)S(1)}, u32[]{:S(2)}) copy-start(bf16[96,16,128]{2,1,0:T(8,128)(2,1)S(1)} %pad_maximum_fusion.1) | copy-start | bytes 1179652
  56.3 17.2 %collective-permute-start.13 = (bf16[96,16,128]{2,1,0:T(8,128)(2,1)S(1)}, bf16[96,16,128]{2,1,0:T(8,128)(2,1)S(1)}, u32[]{:S(2)}, u32[]{:S(2)}) collective-permute-start(bf16[96,16,128]{2,1,0:T(8,128)(2,1)S(1)} %pad_maximum_fusion.1), channel_id=1, source_target_pairs={{0,8},{8,0},{16,24},{24,16},{1,9},{9,1},{17,25},{25,17},{2,10},{10... | collective-permute-start | bytes 1179656 | tf_op jit(solution)/shard_map/ppermute | solution.py:629
  58.1 18.5 %collective-permute-start.14 = (bf16[96,16,128]{2,1,0:T(8,128)(2,1)S(1)}, bf16[96,16,128]{2,1,0:T(8,128)(2,1)S(1)}, u32[]{:S(2)}, u32[]{:S(2)}) collective-permute-start(bf16[96,16,128]{2,1,0:T(8,128)(2,1)S(1)} %pad_maximum_fusion.1), channel_id=1, source_target_pairs={{0,16},{8,24},{16,0},{24,8},{1,17},{9,25},{17,1},{25,9},{2,18},{10... | collective-permute-start | bytes 1179656 | tf_op jit(solution)/shard_map/ppermute | solution.py:629
  59.6 17.0 %collective-permute-start.15 = (bf16[96,16,128]{2,1,0:T(8,128)(2,1)S(1)}, bf16[96,16,128]{2,1,0:T(8,128)(2,1)S(1)}, u32[]{:S(2)}, u32[]{:S(2)}) collective-permute-start(bf16[96,16,128]{2,1,0:T(8,128)(2,1)S(1)} %pad_maximum_fusion.1), channel_id=1, source_target_pairs={{0,24},{8,16},{16,8},{24,0},{1,25},{9,17},{17,9},{25,1},{2,26},{10... | collective-permute-start | bytes 1179656 | tf_op jit(solution)/shard_map/ppermute | solution.py:629
  59.9 2.3 %collective-permute-start.16 = (bf16[96,16,128]{2,1,0:T(8,128)(2,1)S(1)}, bf16[96,16,128]{2,1,0:T(8,128)(2,1)S(1)}, u32[]{:S(2)}, u32[]{:S(2)}) collective-permute-start(bf16[96,16,128]{2,1,0:T(8,128)(2,1)S(1)} %pad_maximum_fusion.1), channel_id=1, source_target_pairs={{0,1},{1,0},{2,3},{3,2},{4,5},{5,4},{6,7},{7,6},{8,9},{9,8},{10,11... | collective-permute-start | bytes 1179656 | tf_op jit(solution)/shard_map/ppermute | solution.py:629
  62.1 0.8 copy-start.1
  73.5 11.3 %copy-start.2 = (bf16[96,16,128]{2,1,0:T(8,128)(2,1)}, bf16[96,16,128]{2,1,0:T(8,128)(2,1)S(1)}, u32[]{:S(2)}) copy-start(bf16[96,16,128]{2,1,0:T(8,128)(2,1)S(1)} %collective-permute-done.13) | copy-start | bytes 1179652
  76.6 8.2 %copy-start.3 = (bf16[96,16,128]{2,1,0:T(8,128)(2,1)}, bf16[96,16,128]{2,1,0:T(8,128)(2,1)S(1)}, u32[]{:S(2)}) copy-start(bf16[96,16,128]{2,1,0:T(8,128)(2,1)S(1)} %collective-permute-done.14) | copy-start | bytes 1179652
  76.6 8.2 %copy-start.4 = (bf16[96,16,128]{2,1,0:T(8,128)(2,1)}, bf16[96,16,128]{2,1,0:T(8,128)(2,1)S(1)}, u32[]{:S(2)}) copy-start(bf16[96,16,128]{2,1,0:T(8,128)(2,1)S(1)} %collective-permute-done.15) | copy-start | bytes 1179652
  76.6 3.5 %collective-permute-start.18 = (bf16[96,16,128]{2,1,0:T(8,128)(2,1)S(1)}, bf16[96,16,128]{2,1,0:T(8,128)(2,1)S(1)}, u32[]{:S(2)}, u32[]{:S(2)}) collective-permute-start(bf16[96,16,128]{2,1,0:T(8,128)(2,1)S(1)} %collective-permute-done.14), channel_id=1, source_target_pairs={{0,1},{1,0},{2,3},{3,2},{4,5},{5,4},{6,7},{7,6},{8,9},{9,8},{10,11... | collective-permute-start | bytes 1179656 | tf_op jit(solution)/shard_map/ppermute | solution.py:629
  76.7 3.4 %collective-permute-start.19 = (bf16[96,16,128]{2,1,0:T(8,128)(2,1)S(1)}, bf16[96,16,128]{2,1,0:T(8,128)(2,1)S(1)}, u32[]{:S(2)}, u32[]{:S(2)}) collective-permute-start(bf16[96,16,128]{2,1,0:T(8,128)(2,1)S(1)} %collective-permute-done.15), channel_id=1, source_target_pairs={{0,1},{1,0},{2,3},{3,2},{4,5},{5,4},{6,7},{7,6},{8,9},{9,8},{10,11... | collective-permute-start | bytes 1179656 | tf_op jit(solution)/shard_map/ppermute | solution.py:629
  77.2 2.9 %collective-permute-start.17 = (bf16[96,16,128]{2,1,0:T(8,128)(2,1)S(1)}, bf16[96,16,128]{2,1,0:T(8,128)(2,1)S(1)}, u32[]{:S(2)}, u32[]{:S(2)}) collective-permute-start(bf16[96,16,128]{2,1,0:T(8,128)(2,1)S(1)} %collective-permute-done.13), channel_id=1, source_target_pairs={{0,1},{1,0},{2,3},{3,2},{4,5},{5,4},{6,7},{7,6},{8,9},{9,8},{10,11... | collective-permute-start | bytes 1179656 | tf_op jit(solution)/shard_map/ppermute | solution.py:629
  80.1 4.8 %copy-start.5 = (bf16[96,16,128]{2,1,0:T(8,128)(2,1)}, bf16[96,16,128]{2,1,0:T(8,128)(2,1)S(1)}, u32[]{:S(2)}) copy-start(bf16[96,16,128]{2,1,0:T(8,128)(2,1)S(1)} %collective-permute-done.18) | copy-start | bytes 1179652
  80.1 4.8 %copy-start.6 = (bf16[96,16,128]{2,1,0:T(8,128)(2,1)}, bf16[96,16,128]{2,1,0:T(8,128)(2,1)S(1)}, u32[]{:S(2)}) copy-start(bf16[96,16,128]{2,1,0:T(8,128)(2,1)S(1)} %collective-permute-done.19) | copy-start | bytes 1179652
  80.1 4.8 %copy-start.7 = (bf16[96,16,128]{2,1,0:T(8,128)(2,1)}, bf16[96,16,128]{2,1,0:T(8,128)(2,1)S(1)}, u32[]{:S(2)}) copy-start(bf16[96,16,128]{2,1,0:T(8,128)(2,1)S(1)} %collective-permute-done.17) | copy-start | bytes 1179652

commit v4 on v3

--- a/solution.py
+++ b/solution.py
@@ -15,6 +15,7 @@
 PACK = 4 * SUB
 LANES = 128
 FINE = G // SUB
+LOW = FINE // 2
 CHUNK = 768
 MASK_VALUES = 1 << 22
 field_view = 0.1
@@ -424,31 +425,36 @@
         left[h, :image_rows] = turned[0]
         left[h, image_rows:] = turned[1]
 
-    def sums_of(index, left):
+    def sums(pair, h, left, first):
+        index = pair + HALF * h
         late = shifts[...] > index.astype(f32)
         table = jnp.concatenate(
             [
                 jnp.where(late, after[:, t : t + LANES], here[:, t : t + LANES])
-                for t in range(0, 2 * FINE, LANES)
+                for t in range(0, FINE, LANES)
             ],
             axis=1,
         )
-        four = jnp.dot(left, table, preferred_element_type=f32)
-        got = (
-            four[:image_rows, :FINE] - four[image_rows:, FINE:],
-            four[:image_rows, FINE:] + four[image_rows:, :FINE],
+        four = jnp.dot(left[h], table, preferred_element_type=f32)
+        even_re, odd_re = four[:image_rows, :LOW], four[:image_rows, LOW:]
+        even_im, odd_im = four[image_rows:, :LOW], four[image_rows:, LOW:]
+        edge = lax.broadcasted_iota(jnp.int32, (image_rows, LOW), 1) == 0
+        low = (
+            even_re - jnp.where(edge, 0.0, odd_im),
+            even_im + jnp.where(edge, 0.0, odd_re),
+        )
+        high = (
+            jnp.where(edge, odd_re, even_re + odd_im),
+            jnp.where(edge, odd_im, even_im - odd_re),
         )
         twist = twist_ref[pl.ds(index, 1), :]
-        return cmul(got, (twist[:, :FINE], twist[:, FINE:]))
-
-    def sums(pair, left, first):
-        low, high = sums_of(pair, left[0]), sums_of(pair + HALF, left[1])
-        turn = twist_ref[pl.ds(SUB + pair, 1), :]
-        even = (low[0] + high[0], low[1] + high[1])
-        odd = cmul((low[0] - high[0], low[1] - high[1]), (turn[:, :FINE], turn[:, FINE:]))
-        for half, done in enumerate((even, odd)):
+        for half, got in enumerate((low, high)):
+            start = 2 * LOW * half
+            done = cmul(
+                got, (twist[:, start : start + LOW], twist[:, start + LOW : start + 2 * LOW])
+            )
             for part in range(2):
-                at = (half * HALF + pair, part)
+                at = (index, part, slice(None), pl.ds(LOW * half, LOW))
                 total[at] = done[part] if first else total[at] + done[part]
 
     def chunk(first):
@@ -482,10 +488,10 @@
         def two_pairs(i, carry):
             for h in range(2):
                 products(2 * i + 1, h, left_odd)
-            sums(2 * i, left_even, first)
+                sums(2 * i, h, left_even, first)
             for h in range(2):
                 products(jnp.minimum(2 * i + 2, HALF - 1), h, left_even)
-            sums(2 * i + 1, left_odd, first)
+                sums(2 * i + 1, h, left_odd, first)
             return carry
 
         lax.fori_loop(0, HALF // 2, two_pairs, 0)
@@ -504,20 +510,22 @@
     def _():
         first = (step - chunks) * row_block
         wide = 2 * G // LANES
+        backward = lax.rem(LOW - lax.broadcasted_iota(jnp.int32, (8, LOW), 1), LOW)
 
         def eight_rows(group, carry):
             at = pl.ds(pl.multiple_of(first + 8 * group, 8), 8)
             for tile in range(FINE // LANES):
                 lanes = pl.ds(tile * LANES, LANES)
-                for half in range(2):
-                    values = [
-                        (total[half * HALF + n, 0, at, lanes], total[half * HALF + n, 1, at, lanes])
-                        for n in range(HALF)
-                    ]
-                    for k, value in enumerate(short_transform(values)):
-                        for part in range(2):
-                            column = 2 * ((2 * k + half) * (FINE // LANES) + tile) + part
-                            staged[pl.ds(column, 8, stride=wide + 1), :] = value[part]
+                values = [(total[n, 0, at, lanes], total[n, 1, at, lanes]) for n in range(SUB)]
+                for k, value in enumerate(short_transform(values)):
+                    for part in range(2):
+                        ordered = value[part]
+                        if tile > 0:
+                            ordered = jnp.take_along_axis(
+                                ordered, backward, axis=1, mode="promise_in_bounds"
+                            )
+                        column = 2 * (k * (FINE // LANES) + tile) + part
+                        staged[pl.ds(column, 8, stride=wide + 1), :] = ordered
             for row in range(8):
                 at = pl.ds(pl.multiple_of((8 * group + row) * wide, wide), wide)
                 out_ref[at, :] = staged[row * (wide + 1) : row * (wide + 1) + wide, :]
@@ -543,15 +551,15 @@
         [jnp.concatenate([re, -im], axis=1), jnp.concatenate([im, re], axis=1)], axis=0
     )
     columns = jnp.kron(jnp.eye(2, dtype=f32), block).astype(bf16)
-    fine = np.arange(FINE)
-    angle = 2.0 * math.pi / FINE * (fine[:, None] * fine[None, :] % FINE)
-    unit = jnp.asarray(np.concatenate([np.cos(angle), np.sin(angle)], axis=1), bf16)
+    fine, low = np.arange(FINE), np.arange(LOW)
+    angle = 2.0 * math.pi / FINE * (fine[:, None] * low[None, :] % FINE)
+    odd = np.where(low == 0, 1.0 - 2.0 * (fine[:, None] % 2), np.sin(angle))
+    unit = jnp.asarray(np.concatenate([np.cos(angle), odd], axis=1), bf16)
     scale = 1.0 / (SUB * math.sqrt(total))
-    angle = 2.0 * math.pi / G * (np.arange(SUB)[:, None] * fine[None, :])
-    twist = np.concatenate([np.cos(angle), np.sin(angle)], axis=1) * scale
-    angle = 2.0 * math.pi / SUB * np.arange(HALF)[:, None] + 0.0 * fine
-    turn_half = np.concatenate([np.cos(angle), np.sin(angle)], axis=1)
-    twist = jnp.asarray(np.concatenate([twist, turn_half], axis=0), f32)
+    high = np.where(low == 0, LOW, FINE - low)
+    angles = [2.0 * math.pi / G * (np.arange(SUB)[:, None] * k[None, :]) for k in (low, high)]
+    twist = [f(angle) * scale for angle in angles for f in (np.cos, np.sin)]
+    twist = jnp.asarray(np.concatenate(twist, axis=1), f32)
     counts = jnp.asarray(np.broadcast_to(np.arange(SUB)[:, None], (SUB, LANES)), bf16)
     last = chunks - 1
 
@@ -577,8 +585,8 @@
         scratch_shapes=[
             pltpu.VMEM((size * (HALF + 1) + HALF, PACK), f32),
             pltpu.VMEM((HALF, size, PACK), bf16),
-            pltpu.VMEM((size, 2 * FINE), bf16),
-            pltpu.VMEM((size, 2 * FINE), bf16),
+            pltpu.VMEM((size, FINE), bf16),
+            pltpu.VMEM((size, FINE), bf16),
             pltpu.VMEM((size, LANES), f32),
             pltpu.VMEM((2, 2 * image_rows, size), bf16),
             pltpu.VMEM((2, 2 * image_rows, size), bf16),

time: 126 us -> 119 us (0.944)
  Pallas kernels: 73.7 us -> 67.3 us
    pallas_call x1, Pallas kernels: 38.9 us -> 32.1 us  [image_rows_of(): pl.pallas_call(functools.partial(image_kernel, pieces=len(uv), chunks=chu...]
  transfers between devices with their start and end apart: 20 -> 20, of which waited for: 5 -> 5; matrix products, arithmetic and copies ran while one was open for 16% -> 16% of each run, Pallas kernels for 20% -> 21%
where the time goes in v4:
time: 119 us; the launch traced here: 117 us
  Pallas kernels  67.3 us (57%)
  starting transfers between devices  18.9 us (16%)
  other arithmetic  16.4 us (14%)
  local copies, waits for them, and re-layouts  8.9 us (7%)
  waiting for transfers between devices  4.39 us (4%)
  between operations  1.25 us (1%)
    pallas_call x1, Pallas kernels, image_rows_of(): pl.pallas_call(functools.partial(image_kernel, pieces=len(uv), chunks=chu...  32.1 us
    ppermute x20, starting transfers between devices, from_partner(): return lax.ppermute(value, axis, [(i, i ^ mask) for i in range(count)])  18.9 us
    pallas_call x3, Pallas kernels, sky_sums(): pl.pallas_call(sky_kernel, grid=(1,), in_specs=[pl.BlockSpec((count, 2, v...  13.8 us
    pallas_call x1, Pallas kernels, uv_tile_own(): pl.pallas_call(functools.partial(tile_kernel, pieces=len(uv), tile_rows=t...  11 us
    pallas_call x1, Pallas kernels, corrected_subgrids(): pl.pallas_call(functools.partial(correct_kernel, pieces=len(tables), skie...  6.66 us
    unnamed x53, local copies, waits for them, and re-layouts  4.83 us
    ppermute x20, waiting for transfers between devices, from_partner(): return lax.ppermute(value, axis, [(i, i ^ mask) for i in range(count)])  4.39 us
    pallas_call x1, Pallas kernels, uv_tile_spill(): pl.pallas_call(functools.partial(spill_kernel, pieces=len(uv), lanes=lane...  3.72 us
  transfers between devices with their start and end apart: 20, of which 5 were waited for; matrix products, arithmetic and copies ran while one was open for 16% of the time, Pallas kernels for 21%

profile of v4, /device:TPU:0, one launch (start us, length us, event | category | flops | bytes accessed | tf_op | source)
XLA Modules:
  0.0 117.1 jit_solution(16695979497374661144)
XLA Ops:
  0.6 1.0 reshape.698
  1.7 0.2 copy.47
  1.9 0.2 reshape.699
  2.1 0.8 and_select_fusion.15
  2.9 0.1 convert_element_type.99
  3.0 3.1 %collective-permute-start = (bf16[17,16,128]{2,1,0:T(8,128)(2,1)S(1)}, bf16[17,16,128]{2,1,0:T(8,128)(2,1)S(1)}, u32[]{:S(2)}, u32[]{:S(2)}) collective-permute-start(bf16[17,16,128]{2,1,0:T(8,128)(2,1)S(1)} %pad_maximum_fusion.2), channel_id=1, source_target_pairs={{0,2},{1,3},{2,0},{3,1},{4,6},{5,7},{6,4},{7,5},{8,10},{9,11},{10,... | collective-permute-start | bytes 208904 | tf_op jit(solution)/shard_map/ppermute | solution.py:637
  6.1 2.6 %collective-permute-start.1 = (bf16[17,16,128]{2,1,0:T(8,128)(2,1)S(1)}, bf16[17,16,128]{2,1,0:T(8,128)(2,1)S(1)}, u32[]{:S(2)}, u32[]{:S(2)}) collective-permute-start(bf16[17,16,128]{2,1,0:T(8,128)(2,1)S(1)} %pad_maximum_fusion.2), channel_id=1, source_target_pairs={{0,4},{1,5},{2,6},{3,7},{4,0},{5,1},{6,2},{7,3},{8,12},{9,13},{10,... | collective-permute-start | bytes 208904 | tf_op jit(solution)/shard_map/ppermute | solution.py:637
  8.7 0.7 and_select_fusion.2
  9.4 0.7 fusion.27
  10.2 0.7 broadcast_multiply_fusion
  10.8 0.1 fusion.20
  11.0 0.2 multiply_convert_fusion
  11.2 4.6 %sky_sums.3.refs_8_ = f32[8,16,128]{2,1,0:T(8,128)} custom-call(bf16[24,2,2048]{2,1,0:T(2,128)(2,1)} %vis_ref.5, f32[48,128]{1,0:T(8,128)} %bitcast.146, f32[1,16]{1,0:T(1,128)} %bitcast.157), custom_call_target="tpu_custom_call" | custom-call | bytes 20000000 | tf_op jit(solution)/shard_map/sky_sums/pallas_call | solution.py:119
  16.0 1.8 %collective-permute-start.3 = (bf16[68,16,128]{2,1,0:T(8,128)(2,1)S(1)}, bf16[68,16,128]{2,1,0:T(8,128)(2,1)S(1)}, u32[]{:S(2)}, u32[]{:S(2)}) collective-permute-start(bf16[68,16,128]{2,1,0:T(8,128)(2,1)S(1)} %constant_dynamic-update-slice_fusion.refs_0_), channel_id=1, source_target_pairs={{0,8},{8,0},{16,24},{24,16},{1,9},{9,1},{17,25},{25,17},{2,10},{10... | collective-permute-start | bytes 835592 | tf_op jit(solution)/shard_map/ppermute | solution.py:637
  17.7 1.5 %collective-permute-start.4 = (bf16[68,16,128]{2,1,0:T(8,128)(2,1)S(1)}, bf16[68,16,128]{2,1,0:T(8,128)(2,1)S(1)}, u32[]{:S(2)}, u32[]{:S(2)}) collective-permute-start(bf16[68,16,128]{2,1,0:T(8,128)(2,1)S(1)} %constant_dynamic-update-slice_fusion.refs_0_), channel_id=1, source_target_pairs={{0,16},{8,24},{16,0},{24,8},{1,17},{9,25},{17,1},{25,9},{2,18},{10... | collective-permute-start | bytes 835592 | tf_op jit(solution)/shard_map/ppermute | solution.py:637
  19.3 0.3 collective-permute-start.5
  19.5 0.1 copy.25
  19.6 0.6 reshape.711.stations_ref
  20.3 0.8 copy.27.refs_10_
  21.1 1.5 %fusion.8.refs_11_ = f32[24,16,128]{2,1,0:T(8,128)} fusion(f32[16,128]{1,0:T(8,128)S(1)} %get-tuple-element.59, f32[128]{0:T(128)S(1)} %fusion.31, s32[16,128]{1,0:T(8,128)S(1)} %fusion.21, s32[24]{0:T(128)S(1)} %and_select_fusion.2, f32[16,128]{1,0:T(8,128)S(1)} %get-tuple-element.58, f32[24]{0:T(128)S(1)} %broadcast_multiply_fusion), kind=kLoop, calls=%fused_computation.26 | loop fusion | flops 884736 | bytes 221888 | tf_op jit(solution)/shard_map/mul | solution.py:632
  22.6 4.6 %sky_sums.4.refs_9_ = f32[8,16,128]{2,1,0:T(8,128)} custom-call(bf16[24,2,2048]{2,1,0:T(2,128)(2,1)} %vis_ref.5, f32[48,128]{1,0:T(8,128)} %bitcast.147, f32[1,16]{1,0:T(1,128)} %bitcast.158), custom_call_target="tpu_custom_call" | custom-call | bytes 20000000 | tf_op jit(solution)/shard_map/sky_sums/pallas_call | solution.py:119
  27.2 4.6 %sky_sums.5.refs_10_ = f32[8,16,128]{2,1,0:T(8,128)} custom-call(bf16[24,2,2048]{2,1,0:T(2,128)(2,1)} %vis_ref.5, f32[48,128]{1,0:T(8,128)} %bitcast.148, f32[1,16]{1,0:T(1,128)} %bitcast.159), custom_call_target="tpu_custom_call" | custom-call | bytes 20000000 | tf_op jit(solution)/shard_map/sky_sums/pallas_call | solution.py:119
  32.0 0.5 collective-permute-start.7
  32.5 0.1 collective-permute-start.8
  32.6 0.4 collective-permute-start.9
  33.1 0.5 collective-permute-done.6.refs_1_
  33.5 0.4 collective-permute-done.7.refs_3_
  33.9 0.4 collective-permute-done.8.refs_5_
  34.3 0.4 collective-permute-done.9.refs_7_
  34.8 0.3 copy-done.14
  35.0 0.7 copy-done.15
  35.7 6.7 %correct.1 = bf16[24,16,128]{2,1,0:T(8,128)(2,1)} custom-call(s32[48]{0:T(128)} %reshape.711.stations_ref, bf16[68,16,128]{2,1,0:T(8,128)(2,1)} %copy-done.8, bf16[68,16,128]{2,1,0:T(8,128)(2,1)} %copy-done.12, bf16[68,16,128]{2,1,0:T(8,128)(2,1)} %copy-done.9, bf16[68,16,128]{2,1,0:T(8,128)(2,1)} %copy-done.13, bf16[68,16,128]{2,1,0:T(8,128)(2,1)} %copy-done.10, ...), custom_call_target="tpu_custom_call" | custom-call | bytes 16000000 | tf_op jit(solution)/shard_map/correct/pallas_call | solution.py:194
  42.4 3.8 %collective-permute-start.12 = (bf16[24,16,128]{2,1,0:T(8,128)(2,1)}, bf16[24,16,128]{2,1,0:T(8,128)(2,1)S(1)}, u32[]{:S(2)}, u32[]{:S(2)}) collective-permute-start(bf16[24,16,128]{2,1,0:T(8,128)(2,1)} %correct.1), channel_id=1, source_target_pairs={{0,6},{1,7},{2,4},{3,5},{4,2},{5,3},{6,0},{7,1},{8,14},{9,15},{10,... | collective-permute-start | bytes 294920 | tf_op jit(solution)/shard_map/ppermute | solution.py:637
  46.2 0.6 collective-permute-start.10
  46.8 0.7 slice_bitcast_fusion.6
  47.5 0.7 slice_bitcast_fusion.4
  48.2 0.7 slice_bitcast_fusion.2
  49.0 0.7 slice_bitcast_fusion
  49.7 0.1 concatenate.55
  50.0 0.1 add.323
  50.1 0.1 add.331
  50.1 3.5 %cosine_convert_fusion = (bf16[1,256,768]{2,1,0:T(8,128)(2,1)S(1)}, bf16[1,256,768]{2,1,0:T(8,128)(2,1)S(1)}) fusion(s32[768]{0:T(1024)S(1)} %add.323, s32[256]{0:T(256)S(1)} %iota_add_fusion.1), kind=kLoop, calls=%fused_computation.10 | loop fusion | flops 3145728 | bytes 790528 | tf_op jit(solution)/shard_map/convert
  53.6 1.3 %convert_reduce_fusion.3 = (s32[]{:T(128)}, pred[192]{0:T(512)(128)(4,1)S(1)}, s32[192]{0:T(256)}, s32[192]{0:T(256)}, s32[192]{0:T(256)}, /*index=5*/s32[]{:T(128)}, pred[192]{0:T(512)(128)(4,1)S(1)}, s32[192]{0:T(256)}) fusion(s32[]{:T(128)S(6)} %mul.276, s32[768]{0:T(1024)S(1)} %add.323, s32[]{:T(128)S(6)} %select_n.268, s32[]{:T(128)S(6)} %mul.278, ...), kind=kLoop, calls=%fused_computation.138 | loop fusion | flops 5374 | bytes 6552 | tf_op jit(solution)/shard_map/reduce_sum | solution.py:312
  54.9 0.1 convert_reduce_fusion
  55.1 0.1 select_reduce_fusion
  55.2 0.1 convert_reduce_fusion.1
  55.3 0.9 pad_maximum_fusion.1
  56.3 1.8 %collective-permute-start.13 = (bf16[96,16,128]{2,1,0:T(8,128)(2,1)S(1)}, bf16[96,16,128]{2,1,0:T(8,128)(2,1)S(1)}, u32[]{:S(2)}, u32[]{:S(2)}) collective-permute-start(bf16[96,16,128]{2,1,0:T(8,128)(2,1)S(1)} %pad_maximum_fusion.1), channel_id=1, source_target_pairs={{0,8},{8,0},{16,24},{24,16},{1,9},{9,1},{17,25},{25,17},{2,10},{10... | collective-permute-start | bytes 1179656 | tf_op jit(solution)/shard_map/ppermute | solution.py:637
  58.1 1.5 %collective-permute-start.14 = (bf16[96,16,128]{2,1,0:T(8,128)(2,1)S(1)}, bf16[96,16,128]{2,1,0:T(8,128)(2,1)S(1)}, u32[]{:S(2)}, u32[]{:S(2)}) collective-permute-start(bf16[96,16,128]{2,1,0:T(8,128)(2,1)S(1)} %pad_maximum_fusion.1), channel_id=1, source_target_pairs={{0,16},{8,24},{16,0},{24,8},{1,17},{9,25},{17,1},{25,9},{2,18},{10... | collective-permute-start | bytes 1179656 | tf_op jit(solution)/shard_map/ppermute | solution.py:637
  59.6 0.3 collective-permute-start.15
  59.9 1.3 %pad_add_fusion.1.list_ref = s32[193]{0:T(256)} fusion(s32[192]{0:T(256)S(1)} %select_reduce_fusion, s32[1]{0:T(128)} %bitcast.17), kind=kLoop, calls=%fused_computation.130 | loop fusion | flops 193 | bytes 1544 | tf_op jit(solution)/shard_map/concatenate | solution.py:312
  61.2 1.0 pad_maximum_fusion.refs_9_
  62.1 0.7 copy-done.1
  62.9 11.0 %uv_tile.1.refs_2_ = f32[32768,128]{1,0:T(8,128)} custom-call(s32[1]{0:T(128)} %bitcast.16.block_ref, s32[193]{0:T(256)} %pad_add_fusion.1.list_ref, s32[192]{0:T(256)} %get-tuple-element.49.row_ref, s32[192]{0:T(256)} %get-tuple-element.52.col_ref, bf16[1536,128]{1,0:T(8,128)(2,1)} %bitcast.123, bf16[1536,128]{1,0:T(8,128)(2,1)} %bitcast.125), custom_call_target="tpu_custom_call" | custom-call | bytes 41943040 | tf_op jit(solution)/shard_map/uv_tile/pallas_call | solution.py:331
  73.9 2.7 %collective-permute-done.14 = bf16[96,16,128]{2,1,0:T(8,128)(2,1)S(1)} collective-permute-done((bf16[96,16,128]{2,1,0:T(8,128)(2,1)S(1)}, bf16[96,16,128]{2,1,0:T(8,128)(2,1)S(1)}, u32[]{:S(2)}, u32[]{:S(2)}) %collective-permute-start.14) | collective-permute-done | bytes 393248 | tf_op jit(solution)/shard_map/ppermute | solution.py:637
  76.7 0.5 collective-permute-start.19
  77.2 0.1 collective-permute-start.17
  77.2 0.1 select_reduce_fusion.1
  77.4 0.7 add.357.refs_8_
  78.0 1.2 %pad_add_fusion.list_ref = s32[193]{0:T(256)} fusion(s32[192]{0:T(256)S(1)} %select_reduce_fusion.1, s32[1]{0:T(128)} %bitcast.14), kind=kLoop, calls=%fused_computation.129 | loop fusion | flops 193 | bytes 1544 | tf_op jit(solution)/shard_map/concatenate | solution.py:312
  79.3 0.8 select_select_fusion.1
  80.1 1.0 select_select_fusion
  81.1 3.7 %uv_spill.1 = f32[32768,128]{1,0:T(8,128)} custom-call(s32[1]{0:T(128)} %constant.300.clone.1.block_ref, s32[193]{0:T(256)} %pad_add_fusion.list_ref, s32[192]{0:T(256)} %get-tuple-element.40.row_ref, s32[192]{0:T(256)} %get-tuple-element.39.col_ref, bf16[1536,128]{1,0:T(8,128)(2,1)} %bitcast.127, ...), custom_call_target="tpu_custom_call", output_to_operand_aliasing={{}: (6, {})} | custom-call | bytes 8000000 | tf_op jit(solution)/shard_map/uv_spill/pallas_call | solution.py:359
  84.9 32.1 %image.1 = f32[32768,128]{1,0:T(8,128)} custom-call(bf16[1536,128]{1,0:T(8,128)(2,1)} %bitcast.124, bf16[1536,128]{1,0:T(8,128)(2,1)} %bitcast.126, bf16[1536,128]{1,0:T(8,128)(2,1)} %bitcast.129, bf16[1536,128]{1,0:T(8,128)(2,1)} %bitcast.134, bf16[1536,128]{1,0:T(8,128)(2,1)} %bitcast.130, bf16[1536,128]{1,0:T(8,128)(2,1)} %bitcast.132, ...), custom_call_target="tpu_custom_call" | custom-call | tf_op jit(solution)/shard_map/image/pallas_call | solution.py:569
  (83 shorter events, 0.6 us)
Async XLA Ops:
  3.0 12.9 %collective-permute-start = (bf16[17,16,128]{2,1,0:T(8,128)(2,1)S(1)}, bf16[17,16,128]{2,1,0:T(8,128)(2,1)S(1)}, u32[]{:S(2)}, u32[]{:S(2)}) collective-permute-start(bf16[17,16,128]{2,1,0:T(8,128)(2,1)S(1)} %pad_maximum_fusion.2), channel_id=1, source_target_pairs={{0,2},{1,3},{2,0},{3,1},{4,6},{5,7},{6,4},{7,5},{8,10},{9,11},{10,... | collective-permute-start | bytes 208904 | tf_op jit(solution)/shard_map/ppermute | solution.py:637
  6.1 9.8 %collective-permute-start.1 = (bf16[17,16,128]{2,1,0:T(8,128)(2,1)S(1)}, bf16[17,16,128]{2,1,0:T(8,128)(2,1)S(1)}, u32[]{:S(2)}, u32[]{:S(2)}) collective-permute-start(bf16[17,16,128]{2,1,0:T(8,128)(2,1)S(1)} %pad_maximum_fusion.2), channel_id=1, source_target_pairs={{0,4},{1,5},{2,6},{3,7},{4,0},{5,1},{6,2},{7,3},{8,12},{9,13},{10,... | collective-permute-start | bytes 208904 | tf_op jit(solution)/shard_map/ppermute | solution.py:637
  8.7 7.2 %collective-permute-start.2 = (bf16[17,16,128]{2,1,0:T(8,128)(2,1)S(1)}, bf16[17,16,128]{2,1,0:T(8,128)(2,1)S(1)}, u32[]{:S(2)}, u32[]{:S(2)}) collective-permute-start(bf16[17,16,128]{2,1,0:T(8,128)(2,1)S(1)} %pad_maximum_fusion.2), channel_id=1, source_target_pairs={{0,6},{1,7},{2,4},{3,5},{4,2},{5,3},{6,0},{7,1},{8,14},{9,15},{10,... | collective-permute-start | bytes 208904 | tf_op jit(solution)/shard_map/ppermute | solution.py:637
  16.0 18.8 %copy-start.8 = (bf16[68,16,128]{2,1,0:T(8,128)(2,1)}, bf16[68,16,128]{2,1,0:T(8,128)(2,1)S(1)}, u32[]{:S(2)}) copy-start(bf16[68,16,128]{2,1,0:T(8,128)(2,1)S(1)} %constant_dynamic-update-slice_fusion.refs_0_) | copy-start | bytes 835588
  16.0 15.9 %collective-permute-start.3 = (bf16[68,16,128]{2,1,0:T(8,128)(2,1)S(1)}, bf16[68,16,128]{2,1,0:T(8,128)(2,1)S(1)}, u32[]{:S(2)}, u32[]{:S(2)}) collective-permute-start(bf16[68,16,128]{2,1,0:T(8,128)(2,1)S(1)} %constant_dynamic-update-slice_fusion.refs_0_), channel_id=1, source_target_pairs={{0,8},{8,0},{16,24},{24,16},{1,9},{9,1},{17,25},{25,17},{2,10},{10... | collective-permute-start | bytes 835592 | tf_op jit(solution)/shard_map/ppermute | solution.py:637
  17.7 14.1 %collective-permute-start.4 = (bf16[68,16,128]{2,1,0:T(8,128)(2,1)S(1)}, bf16[68,16,128]{2,1,0:T(8,128)(2,1)S(1)}, u32[]{:S(2)}, u32[]{:S(2)}) collective-permute-start(bf16[68,16,128]{2,1,0:T(8,128)(2,1)S(1)} %constant_dynamic-update-slice_fusion.refs_0_), channel_id=1, source_target_pairs={{0,16},{8,24},{16,0},{24,8},{1,17},{9,25},{17,1},{25,9},{2,18},{10... | collective-permute-start | bytes 835592 | tf_op jit(solution)/shard_map/ppermute | solution.py:637
  19.3 12.6 %collective-permute-start.5 = (bf16[68,16,128]{2,1,0:T(8,128)(2,1)S(1)}, bf16[68,16,128]{2,1,0:T(8,128)(2,1)S(1)}, u32[]{:S(2)}, u32[]{:S(2)}) collective-permute-start(bf16[68,16,128]{2,1,0:T(8,128)(2,1)S(1)} %constant_dynamic-update-slice_fusion.refs_0_), channel_id=1, source_target_pairs={{0,24},{8,16},{16,8},{24,0},{1,25},{9,17},{17,9},{25,1},{2,26},{10... | collective-permute-start | bytes 835592 | tf_op jit(solution)/shard_map/ppermute | solution.py:637
  31.9 2.9 %copy-start.9 = (bf16[68,16,128]{2,1,0:T(8,128)(2,1)}, bf16[68,16,128]{2,1,0:T(8,128)(2,1)S(1)}, u32[]{:S(2)}) copy-start(bf16[68,16,128]{2,1,0:T(8,128)(2,1)S(1)} %collective-permute-done.3.refs_2_) | copy-start | bytes 835588
  31.9 2.9 %copy-start.10 = (bf16[68,16,128]{2,1,0:T(8,128)(2,1)}, bf16[68,16,128]{2,1,0:T(8,128)(2,1)S(1)}, u32[]{:S(2)}) copy-start(bf16[68,16,128]{2,1,0:T(8,128)(2,1)S(1)} %collective-permute-done.4.refs_4_) | copy-start | bytes 835588
  31.9 2.8 %copy-start.11 = (bf16[68,16,128]{2,1,0:T(8,128)(2,1)}, bf16[68,16,128]{2,1,0:T(8,128)(2,1)S(1)}, u32[]{:S(2)}) copy-start(bf16[68,16,128]{2,1,0:T(8,128)(2,1)S(1)} %collective-permute-done.5.refs_6_) | copy-start | bytes 835588
  31.9 1.6 %collective-permute-start.6 = (bf16[68,16,128]{2,1,0:T(8,128)(2,1)S(1)}, bf16[68,16,128]{2,1,0:T(8,128)(2,1)S(1)}, u32[]{:S(2)}, u32[]{:S(2)}) collective-permute-start(bf16[68,16,128]{2,1,0:T(8,128)(2,1)S(1)} %constant_dynamic-update-slice_fusion.refs_0_), channel_id=1, source_target_pairs={{0,1},{1,0},{2,3},{3,2},{4,5},{5,4},{6,7},{7,6},{8,9},{9,8},{10,11... | collective-permute-start | bytes 835592 | tf_op jit(solution)/shard_map/ppermute | solution.py:637
  32.0 1.9 %collective-permute-start.7 = (bf16[68,16,128]{2,1,0:T(8,128)(2,1)S(1)}, bf16[68,16,128]{2,1,0:T(8,128)(2,1)S(1)}, u32[]{:S(2)}, u32[]{:S(2)}) collective-permute-start(bf16[68,16,128]{2,1,0:T(8,128)(2,1)S(1)} %collective-permute-done.3.refs_2_), channel_id=1, source_target_pairs={{0,1},{1,0},{2,3},{3,2},{4,5},{5,4},{6,7},{7,6},{8,9},{9,8},{10,11... | collective-permute-start | bytes 835592 | tf_op jit(solution)/shard_map/ppermute | solution.py:637
  32.5 1.8 %collective-permute-start.8 = (bf16[68,16,128]{2,1,0:T(8,128)(2,1)S(1)}, bf16[68,16,128]{2,1,0:T(8,128)(2,1)S(1)}, u32[]{:S(2)}, u32[]{:S(2)}) collective-permute-start(bf16[68,16,128]{2,1,0:T(8,128)(2,1)S(1)} %collective-permute-done.4.refs_4_), channel_id=1, source_target_pairs={{0,1},{1,0},{2,3},{3,2},{4,5},{5,4},{6,7},{7,6},{8,9},{9,8},{10,11... | collective-permute-start | bytes 835592 | tf_op jit(solution)/shard_map/ppermute | solution.py:637
  32.6 2.2 %collective-permute-start.9 = (bf16[68,16,128]{2,1,0:T(8,128)(2,1)S(1)}, bf16[68,16,128]{2,1,0:T(8,128)(2,1)S(1)}, u32[]{:S(2)}, u32[]{:S(2)}) collective-permute-start(bf16[68,16,128]{2,1,0:T(8,128)(2,1)S(1)} %collective-permute-done.5.refs_6_), channel_id=1, source_target_pairs={{0,1},{1,0},{2,3},{3,2},{4,5},{5,4},{6,7},{7,6},{8,9},{9,8},{10,11... | collective-permute-start | bytes 835592 | tf_op jit(solution)/shard_map/ppermute | solution.py:637
  33.5 1.2 %copy-start.12 = (bf16[68,16,128]{2,1,0:T(8,128)(2,1)}, bf16[68,16,128]{2,1,0:T(8,128)(2,1)S(1)}, u32[]{:S(2)}) copy-start(bf16[68,16,128]{2,1,0:T(8,128)(2,1)S(1)} %collective-permute-done.6.refs_1_) | copy-start | bytes 835588
  33.9 0.8 copy-start.13
  34.3 0.7 copy-start.14
  35.0 0.7 copy-start.15
  42.4 12.9 %collective-permute-start.12 = (bf16[24,16,128]{2,1,0:T(8,128)(2,1)}, bf16[24,16,128]{2,1,0:T(8,128)(2,1)S(1)}, u32[]{:S(2)}, u32[]{:S(2)}) collective-permute-start(bf16[24,16,128]{2,1,0:T(8,128)(2,1)} %correct.1), channel_id=1, source_target_pairs={{0,6},{1,7},{2,4},{3,5},{4,2},{5,3},{6,0},{7,1},{8,14},{9,15},{10,... | collective-permute-start | bytes 294920 | tf_op jit(solution)/shard_map/ppermute | solution.py:637
  46.2 9.1 %collective-permute-start.11 = (bf16[24,16,128]{2,1,0:T(8,128)(2,1)}, bf16[24,16,128]{2,1,0:T(8,128)(2,1)S(1)}, u32[]{:S(2)}, u32[]{:S(2)}) collective-permute-start(bf16[24,16,128]{2,1,0:T(8,128)(2,1)} %correct.1), channel_id=1, source_target_pairs={{0,4},{1,5},{2,6},{3,7},{4,0},{5,1},{6,2},{7,3},{8,12},{9,13},{10,... | collective-permute-start | bytes 294920 | tf_op jit(solution)/shard_map/ppermute | solution.py:637
  46.2 9.1 %collective-permute-start.10 = (bf16[24,16,128]{2,1,0:T(8,128)(2,1)}, bf16[24,16,128]{2,1,0:T(8,128)(2,1)S(1)}, u32[]{:S(2)}, u32[]{:S(2)}) collective-permute-start(bf16[24,16,128]{2,1,0:T(8,128)(2,1)} %correct.1), channel_id=1, source_target_pairs={{0,2},{1,3},{2,0},{3,1},{4,6},{5,7},{6,4},{7,5},{8,10},{9,11},{10,... | collective-permute-start | bytes 294920 | tf_op jit(solution)/shard_map/ppermute | solution.py:637
  56.3 5.8 %copy-start = (bf16[96,16,128]{2,1,0:T(8,128)(2,1)}, bf16[96,16,128]{2,1,0:T(8,128)(2,1)S(1)}, u32[]{:S(2)}) copy-start(bf16[96,16,128]{2,1,0:T(8,128)(2,1)S(1)} %pad_maximum_fusion.1) | copy-start | bytes 1179652
  56.3 17.6 %collective-permute-start.13 = (bf16[96,16,128]{2,1,0:T(8,128)(2,1)S(1)}, bf16[96,16,128]{2,1,0:T(8,128)(2,1)S(1)}, u32[]{:S(2)}, u32[]{:S(2)}) collective-permute-start(bf16[96,16,128]{2,1,0:T(8,128)(2,1)S(1)} %pad_maximum_fusion.1), channel_id=1, source_target_pairs={{0,8},{8,0},{16,24},{24,16},{1,9},{9,1},{17,25},{25,17},{2,10},{10... | collective-permute-start | bytes 1179656 | tf_op jit(solution)/shard_map/ppermute | solution.py:637
  58.1 18.5 %collective-permute-start.14 = (bf16[96,16,128]{2,1,0:T(8,128)(2,1)S(1)}, bf16[96,16,128]{2,1,0:T(8,128)(2,1)S(1)}, u32[]{:S(2)}, u32[]{:S(2)}) collective-permute-start(bf16[96,16,128]{2,1,0:T(8,128)(2,1)S(1)} %pad_maximum_fusion.1), channel_id=1, source_target_pairs={{0,16},{8,24},{16,0},{24,8},{1,17},{9,25},{17,1},{25,9},{2,18},{10... | collective-permute-start | bytes 1179656 | tf_op jit(solution)/shard_map/ppermute | solution.py:637
  59.6 17.0 %collective-permute-start.15 = (bf16[96,16,128]{2,1,0:T(8,128)(2,1)S(1)}, bf16[96,16,128]{2,1,0:T(8,128)(2,1)S(1)}, u32[]{:S(2)}, u32[]{:S(2)}) collective-permute-start(bf16[96,16,128]{2,1,0:T(8,128)(2,1)S(1)} %pad_maximum_fusion.1), channel_id=1, source_target_pairs={{0,24},{8,16},{16,8},{24,0},{1,25},{9,17},{17,9},{25,1},{2,26},{10... | collective-permute-start | bytes 1179656 | tf_op jit(solution)/shard_map/ppermute | solution.py:637
  59.9 2.3 %collective-permute-start.16 = (bf16[96,16,128]{2,1,0:T(8,128)(2,1)S(1)}, bf16[96,16,128]{2,1,0:T(8,128)(2,1)S(1)}, u32[]{:S(2)}, u32[]{:S(2)}) collective-permute-start(bf16[96,16,128]{2,1,0:T(8,128)(2,1)S(1)} %pad_maximum_fusion.1), channel_id=1, source_target_pairs={{0,1},{1,0},{2,3},{3,2},{4,5},{5,4},{6,7},{7,6},{8,9},{9,8},{10,11... | collective-permute-start | bytes 1179656 | tf_op jit(solution)/shard_map/ppermute | solution.py:637
  62.1 0.8 copy-start.1
  73.9 10.9 %copy-start.2 = (bf16[96,16,128]{2,1,0:T(8,128)(2,1)}, bf16[96,16,128]{2,1,0:T(8,128)(2,1)S(1)}, u32[]{:S(2)}) copy-start(bf16[96,16,128]{2,1,0:T(8,128)(2,1)S(1)} %collective-permute-done.13) | copy-start | bytes 1179652
  76.6 8.2 %copy-start.3 = (bf16[96,16,128]{2,1,0:T(8,128)(2,1)}, bf16[96,16,128]{2,1,0:T(8,128)(2,1)S(1)}, u32[]{:S(2)}) copy-start(bf16[96,16,128]{2,1,0:T(8,128)(2,1)S(1)} %collective-permute-done.14) | copy-start | bytes 1179652
  76.6 8.2 %copy-start.4 = (bf16[96,16,128]{2,1,0:T(8,128)(2,1)}, bf16[96,16,128]{2,1,0:T(8,128)(2,1)S(1)}, u32[]{:S(2)}) copy-start(bf16[96,16,128]{2,1,0:T(8,128)(2,1)S(1)} %collective-permute-done.15) | copy-start | bytes 1179652
  76.6 3.5 %collective-permute-start.18 = (bf16[96,16,128]{2,1,0:T(8,128)(2,1)S(1)}, bf16[96,16,128]{2,1,0:T(8,128)(2,1)S(1)}, u32[]{:S(2)}, u32[]{:S(2)}) collective-permute-start(bf16[96,16,128]{2,1,0:T(8,128)(2,1)S(1)} %collective-permute-done.14), channel_id=1, source_target_pairs={{0,1},{1,0},{2,3},{3,2},{4,5},{5,4},{6,7},{7,6},{8,9},{9,8},{10,11... | collective-permute-start | bytes 1179656 | tf_op jit(solution)/shard_map/ppermute | solution.py:637
  76.7 3.4 %collective-permute-start.19 = (bf16[96,16,128]{2,1,0:T(8,128)(2,1)S(1)}, bf16[96,16,128]{2,1,0:T(8,128)(2,1)S(1)}, u32[]{:S(2)}, u32[]{:S(2)}) collective-permute-start(bf16[96,16,128]{2,1,0:T(8,128)(2,1)S(1)} %collective-permute-done.15), channel_id=1, source_target_pairs={{0,1},{1,0},{2,3},{3,2},{4,5},{5,4},{6,7},{7,6},{8,9},{9,8},{10,11... | collective-permute-start | bytes 1179656 | tf_op jit(solution)/shard_map/ppermute | solution.py:637
  77.2 2.9 %collective-permute-start.17 = (bf16[96,16,128]{2,1,0:T(8,128)(2,1)S(1)}, bf16[96,16,128]{2,1,0:T(8,128)(2,1)S(1)}, u32[]{:S(2)}, u32[]{:S(2)}) collective-permute-start(bf16[96,16,128]{2,1,0:T(8,128)(2,1)S(1)} %collective-permute-done.13), channel_id=1, source_target_pairs={{0,1},{1,0},{2,3},{3,2},{4,5},{5,4},{6,7},{7,6},{8,9},{9,8},{10,11... | collective-permute-start | bytes 1179656 | tf_op jit(solution)/shard_map/ppermute | solution.py:637
  80.1 4.8 %copy-start.5 = (bf16[96,16,128]{2,1,0:T(8,128)(2,1)}, bf16[96,16,128]{2,1,0:T(8,128)(2,1)S(1)}, u32[]{:S(2)}) copy-start(bf16[96,16,128]{2,1,0:T(8,128)(2,1)S(1)} %collective-permute-done.18) | copy-start | bytes 1179652
  80.1 4.8 %copy-start.6 = (bf16[96,16,128]{2,1,0:T(8,128)(2,1)}, bf16[96,16,128]{2,1,0:T(8,128)(2,1)S(1)}, u32[]{:S(2)}) copy-start(bf16[96,16,128]{2,1,0:T(8,128)(2,1)S(1)} %collective-permute-done.19) | copy-start | bytes 1179652
  80.1 4.8 %copy-start.7 = (bf16[96,16,128]{2,1,0:T(8,128)(2,1)}, bf16[96,16,128]{2,1,0:T(8,128)(2,1)S(1)}, u32[]{:S(2)}) copy-start(bf16[96,16,128]{2,1,0:T(8,128)(2,1)S(1)} %collective-permute-done.17) | copy-start | bytes 1179652

commit v5 on v4

--- a/solution.py
+++ b/solution.py
@@ -167,10 +167,11 @@
         sky = product(sky_refs[s // per][s % per], factor_ref[s])
         mid_ref[HALF * s : HALF * (s + 1), :] = product(sky, pair).astype(bf16)
     mid = jnp.dot(mid_ref[...], right_ref[...], preferred_element_type=f32).astype(bf16)
+    wide = jnp.concatenate([mid[HALF * s : HALF * (s + 1)] for s in range(count)], axis=1)
+    every = jnp.dot(left_ref[...], wide, preferred_element_type=f32)
     for s in range(count):
-        rows = mid[HALF * s : HALF * (s + 1)]
-        tall = jnp.concatenate([rows[:, : 2 * SUB], rows[:, 2 * SUB :]], axis=0)
-        four = jnp.dot(left_ref[...], tall, preferred_element_type=f32)
+        block = every[:, PACK * s : PACK * (s + 1)]
+        four = block[: 2 * SUB, : 2 * SUB] + block[2 * SUB :, 2 * SUB :]
         real = four[:SUB, :SUB] - four[SUB:, SUB:]
         image = four[:SUB, SUB:] + four[SUB:, :SUB]
         out_ref[s] = jnp.concatenate(
@@ -184,7 +185,8 @@
     angle = 2.0 * math.pi / SUB * (centred[:, None] * centred[None, :] % SUB)
     re, im = np.cos(angle) / SUB, -np.sin(angle) / SUB
     right = jnp.asarray(np.kron(np.eye(2), np.block([[re, im], [-im, re]])), bf16)
-    left = jnp.asarray(np.concatenate([re, im], axis=0), bf16)
+    left = np.concatenate([re, im], axis=0)
+    left = jnp.asarray(np.concatenate([left[:, :HALF], left[:, HALF:]], axis=0), bf16)
     rows = sum(piece.shape[0] for piece in tables)
     operands = [*tables, *skies, factor, right, left]
 
@@ -211,57 +213,54 @@
     )(stations.reshape(-1), *operands)
 
 
-def add_subgrids(uv_refs, list_ref, row_ref, col_ref, held_ref, total_ref, lanes):
-    first = 0
-    for piece in uv_refs:
-        held_ref[first : first + piece.shape[0]] = piece[...]
-        first += piece.shape[0]
+def listed(list_ref, first, count, wanted):
+    def scan(i, found):
+        list_ref[found] = first + i
+        return found + wanted(first + i).astype(jnp.int32)
+
+    return lax.fori_loop(0, count, scan, jnp.int32(0), unroll=math.gcd(count, 8))
+
+
+def add_subgrid(packed, row_at, col_at, total_ref, lanes):
     lane = lax.broadcasted_iota(jnp.int32, (8, LANES), 1)
     row = lax.broadcasted_iota(jnp.int32, (8, LANES), 0)
-
-    def one(entry, carry):
-        s = list_ref[entry + 1]
-        row_at, col_at = row_ref[s], col_ref[s]
-        packed = held_ref[pl.ds(pl.multiple_of(s * HALF, HALF), HALF), :].astype(f32)
-        tile = col_at // LANES
-        offset = col_at % LANES
-        shift = row_at % SUB
-        base = row_at - shift
-
-        def place(over):
-            inside = lane < offset + SUB - LANES
-            if not over:
-                inside = (lane >= offset) & (lane < offset + SUB)
-            for h in range(2):
-                for part in range(2):
-                    from_lane = (2 * h + part) * SUB
-                    moved = pltpu.roll(packed, lax.rem(offset - from_lane + LANES, LANES), 1)
-                    for group in range(2):
-                        values = moved[8 * group : 8 * (group + 1)]
-                        first_row = HALF * h + 8 * group
-                        late = row + first_row >= shift
-                        for wrapped in range(2):
-                            keep = jnp.logical_and(inside, late if wrapped == 0 else ~late)
-                            start = (base + SUB * wrapped + first_row) * lanes
-                            start = start + 2 * (tile + over) + part
-                            at = pl.ds(start, 8, stride=lanes)
-                            total_ref[at, :] = total_ref[at, :] + jnp.where(keep, values, 0.0)
-
-        place(0)
-
-        @pl.when(offset + SUB > LANES)
-        def _():
-            place(1)
-
-        return carry
-
-    lax.fori_loop(0, list_ref[0], one, 0)
-
-
-def tile_kernel(block_ref, list_ref, row_ref, col_ref, *refs, pieces, tile_rows, lanes):
-    del block_ref
+    tile = col_at // LANES
+    offset = col_at % LANES
+    shift = row_at % SUB
+    base = row_at - shift
+
+    def place(over):
+        inside = lane < offset + SUB - LANES
+        if not over:
+            inside = (lane >= offset) & (lane < offset + SUB)
+        for h in range(2):
+            for part in range(2):
+                from_lane = (2 * h + part) * SUB
+                moved = pltpu.roll(packed, lax.rem(offset - from_lane + LANES, LANES), 1)
+                for group in range(2):
+                    values = moved[8 * group : 8 * (group + 1)]
+                    first_row = HALF * h + 8 * group
+                    late = row + first_row >= shift
+                    for wrapped in range(2):
+                        keep = jnp.logical_and(inside, late if wrapped == 0 else ~late)
+                        start = (base + SUB * wrapped + first_row) * lanes
+                        start = start + 2 * (tile + over) + part
+                        at = pl.ds(start, 8, stride=lanes)
+                        total_ref[at, :] = total_ref[at, :] + jnp.where(keep, values, 0.0)
+
+    place(0)
+
+    @pl.when(offset + SUB > LANES)
+    def _():
+        place(1)
+
+
+def tile_kernel(info_ref, row_ref, col_ref, *refs, pieces, tile_rows, tile_cols):
     uv_refs = refs[:pieces]
-    out_ref, held_ref, total_ref, sems = refs[pieces:]
+    out_ref, held_ref, total_ref, list_ref, sems = refs[pieces:]
+    lanes = 2 * tile_cols // LANES
+    count = held_ref.shape[0] // HALF
+    first, row_first, col_first = info_ref[0] * count, info_ref[1], info_ref[2]
     rows_all = total_ref.shape[0]
     zero_rows = math.gcd(rows_all, 1024)
 
@@ -271,14 +270,30 @@
         return carry
 
     lax.fori_loop(0, rows_all // zero_rows, clear, 0)
-    add_subgrids(uv_refs, list_ref, row_ref, col_ref, held_ref, total_ref, lanes)
-    pieces = sems.shape[0]
-    size = tile_rows * lanes // pieces
+    held = 0
+    for piece in uv_refs:
+        held_ref[held : held + piece.shape[0]] = piece[...]
+        held += piece.shape[0]
+
+    def wanted(s):
+        col_at = col_ref[s] - col_first
+        return (col_at >= 0) & (col_at < tile_cols)
+
+    def one(entry, carry):
+        s = list_ref[entry]
+        at = pl.ds(pl.multiple_of((s - first) * HALF, HALF), HALF)
+        packed = held_ref[at, :].astype(f32)
+        add_subgrid(packed, row_ref[s] - row_first, col_ref[s] - col_first, total_ref, lanes)
+        return carry
+
+    lax.fori_loop(0, listed(list_ref, first, count, wanted), one, 0)
+    parts = sems.shape[0]
+    size = tile_rows * lanes // parts
     copies = [
         pltpu.make_async_copy(
             total_ref.at[pl.ds(i * size, size), :], out_ref.at[pl.ds(i * size, size), :], sems.at[i]
         )
-        for i in range(pieces)
+        for i in range(parts)
     ]
     for copy in copies:
         copy.start()
@@ -286,58 +301,22 @@
         copy.wait()
 
 
-def spill_kernel(block_ref, list_ref, row_ref, col_ref, *refs, pieces, lanes):
-    del block_ref
-    uv_refs = refs[:pieces]
-    _, out_ref, held_ref, total_ref, sem = refs[pieces:]
-    size = SUB * lanes
-    kept = total_ref.at[pl.ds(size, size), :]
-    copy = pltpu.make_async_copy(out_ref.at[pl.ds(0, size), :], kept, sem)
-    copy.start()
-    copy.wait()
-    add_subgrids(uv_refs, list_ref, row_ref, col_ref, held_ref, total_ref, lanes)
-    copy = pltpu.make_async_copy(kept, out_ref.at[pl.ds(0, size), :], sem)
-    copy.start()
-    copy.wait()
-
-
-def listed(valid):
-    count = valid.shape[0]
-    index = jnp.arange(count, dtype=jnp.int32)
-    before = jnp.sum((index[None, :] < index[:, None]) & valid[None, :], axis=1, dtype=jnp.int32)
-    rank = jnp.where(valid, before, -1)
-    entries = jnp.sum(
-        jnp.where(rank[None, :] == index[:, None], index[None, :], 0), axis=1, dtype=jnp.int32
-    )
-    return jnp.concatenate([jnp.sum(valid, dtype=jnp.int32)[None], entries])
-
-
-def tile_places(corners, au_index, vert_index, au_count, vert_count, spilled):
-    tile_rows, tile_cols = G // au_count, G // vert_count
-    col_at = corners[1] - vert_index * tile_cols
-    valid = (col_at >= 0) & (col_at < tile_cols)
-    row_at = corners[0] - au_index * tile_rows
-    if spilled:
-        row_at = (row_at + SUB + G) % G
-        valid = valid & (row_at < SUB)
-    return listed(valid), row_at, col_at
-
-
-def uv_tile_own(uv, block, places, au_count, vert_count, interpret=False):
-    count = places[1].shape[0]
-    tile_rows, tile_cols = G // au_count, G // vert_count
+def uv_tile_own(uv, info, corners, count, tile_rows, tile_cols, interpret=False):
     lanes = 2 * tile_cols // LANES
     rows = count * HALF // len(uv)
     return pl.pallas_call(
-        functools.partial(tile_kernel, pieces=len(uv), tile_rows=tile_rows, lanes=lanes),
+        functools.partial(
+            tile_kernel, pieces=len(uv), tile_rows=tile_rows, tile_cols=tile_cols
+        ),
         grid_spec=pltpu.PrefetchScalarGridSpec(
-            num_scalar_prefetch=4,
+            num_scalar_prefetch=3,
             grid=(1,),
-            in_specs=[pl.BlockSpec((rows, PACK), lambda i, block, *_: (block[0], 0))] * len(uv),
+            in_specs=[pl.BlockSpec((rows, PACK), lambda i, info, *_: (info[0], 0))] * len(uv),
             out_specs=pl.BlockSpec(memory_space=pl.ANY),
             scratch_shapes=[
                 pltpu.VMEM((count * HALF, PACK), bf16),
                 pltpu.VMEM(((tile_rows + 2 * SUB) * lanes, LANES), f32),
+                pltpu.SMEM((count + 1,), jnp.int32),
                 pltpu.SemaphoreType.DMA((4,)),
             ],
         ),
@@ -348,37 +327,7 @@
         ),
         name="uv_tile",
         interpret=interpret,
-    )(block.reshape(1), *places, *[piece.reshape(-1, PACK) for piece in uv])
-
-
-def uv_tile_spill(tile, uv, block, places, au_count, vert_count, interpret=False):
-    count = places[1].shape[0]
-    tile_rows, tile_cols = G // au_count, G // vert_count
-    lanes = 2 * tile_cols // LANES
-    rows = count * HALF // len(uv)
-    result = pl.pallas_call(
-        functools.partial(spill_kernel, pieces=len(uv), lanes=lanes),
-        grid_spec=pltpu.PrefetchScalarGridSpec(
-            num_scalar_prefetch=4,
-            grid=(1,),
-            in_specs=[pl.BlockSpec((rows, PACK), lambda i, block, *_: (block[0], 0))] * len(uv)
-            + [pl.BlockSpec(memory_space=pl.ANY)],
-            out_specs=pl.BlockSpec(memory_space=pl.ANY),
-            scratch_shapes=[
-                pltpu.VMEM((count * HALF, PACK), bf16),
-                pltpu.VMEM((3 * SUB * lanes, LANES), f32),
-                pltpu.SemaphoreType.DMA(()),
-            ],
-        ),
-        out_shape=jax.ShapeDtypeStruct(tile.shape, f32),
-        input_output_aliases={4 + len(uv): 0},
-        compiler_params=pltpu.CompilerParams(vmem_limit_bytes=VMEM_BYTES),
-        cost_estimate=pl.CostEstimate(flops=0, bytes_accessed=8_000_000, transcendentals=0),
-        name="uv_spill",
-        interpret=interpret,
-    )(block.reshape(1), *places, *[piece.reshape(-1, PACK) for piece in uv], tile)
-    result = result.reshape(tile_rows, tile_cols // LANES, 2, LANES)
-    return jnp.transpose(result, (0, 2, 1, 3)).reshape(tile_rows, 2, tile_cols)
+    )(info, *corners, *[piece.reshape(-1, PACK) for piece in uv])
 
 
 def short_transform(values):
@@ -408,11 +357,40 @@
     return low + high
 
 
-def image_kernel(*refs, pieces, chunks, row_block):
+def image_kernel(
+    info_ref, row_ref, col_ref, *refs, pieces, chunks, row_block, per_row, tile_cols
+):
     uv_refs, refs = refs[:pieces], refs[pieces:]
     corner_ref, phase_ref, columns_ref, unit_ref, count_ref, twist_ref = refs[:6]
-    out_ref, uv_wide, uv_rows, here, after, shifts, left_even, left_odd, total, staged = refs[6:]
+    out_ref, tile_ref, uv_wide, uv_rows, here, after, shifts, left_even, left_odd, total = refs[7:17]
+    staged, spill, list_ref, sem = refs[17:]
     step = pl.program_id(0)
+    lanes = 2 * tile_cols // LANES
+    head = pltpu.make_async_copy(
+        tile_ref.at[pl.ds(0, SUB * lanes), :], spill.at[pl.ds(SUB * lanes, SUB * lanes), :], sem
+    )
+    back = pltpu.make_async_copy(
+        spill.at[pl.ds(SUB * lanes, SUB * lanes), :], tile_ref.at[pl.ds(0, SUB * lanes), :], sem
+    )
+
+    def add_spilled():
+        def row_of(s):
+            return lax.rem(row_ref[s] - info_ref[1] + SUB + G, G)
+
+        def wanted(s):
+            col_at = col_ref[s] - info_ref[2]
+            mine = (col_at >= 0) & (col_at < tile_cols) & (row_of(s) < SUB)
+            return mine & (s >= step * size) & (s < (step + 1) * size)
+
+        def one(entry, carry):
+            s = list_ref[entry]
+            packed = uv_wide[pl.ds((s - step * size) * (HALF + 1), HALF), :]
+            add_subgrid(packed, row_of(s), col_ref[s] - info_ref[2], spill, lanes)
+            return carry
+
+        found = listed(list_ref, info_ref[0] * per_row, per_row, wanted)
+        lax.fori_loop(0, found, one, 0)
+
     size = uv_rows.shape[1]
     image_rows = phase_ref.shape[1]
 
@@ -458,6 +436,8 @@
                 total[at] = done[part] if first else total[at] + done[part]
 
     def chunk(first):
+        if first:
+            head.start()
         held = 0
         for piece in uv_refs:
 
@@ -471,6 +451,10 @@
             held += count
         for row in range(HALF):
             uv_rows[row] = uv_wide[pl.ds(row, size, stride=HALF + 1), :].astype(bf16)
+        if first:
+            head.wait()
+        add_spilled()
+        pl.when(step == chunks - 1)(back.start)
         corner = corner_ref[...]
         coarse, shift = corner // SUB, corner % SUB
 
@@ -495,6 +479,7 @@
             return carry
 
         lax.fori_loop(0, HALF // 2, two_pairs, 0)
+        pl.when(step == chunks - 1)(back.wait)
 
     @pl.when(step == 0)
     def _():
@@ -534,7 +519,8 @@
         lax.fori_loop(0, row_block // 8, eight_rows, 0)
 
 
-def image_rows_of(uv, corners_all, first_row, image_rows, interpret=False):
+def image_rows_of(uv, corners_all, first_row, image_rows, tile, info, per_row, tile_rows, tile_cols, interpret=False):
+    lanes = 2 * tile_cols // LANES
     total = corners_all[0].shape[0]
     size = math.gcd(total, CHUNK) if len(uv) == 1 else total
     chunks = total // size
@@ -566,42 +552,67 @@
     def chunk_of(i):
         return jnp.minimum(i, last)
 
-    result = pl.pallas_call(
-        functools.partial(image_kernel, pieces=len(uv), chunks=chunks, row_block=row_block),
-        grid=(chunks + outs,),
-        in_specs=[
-            *[pl.BlockSpec((size * HALF // len(uv), PACK), lambda i: (chunk_of(i), 0))] * len(uv),
-            pl.BlockSpec((1, size), lambda i: (0, chunk_of(i))),
-            pl.BlockSpec((2, image_rows, size), lambda i: (0, 0, chunk_of(i))),
-            pl.BlockSpec(columns.shape, lambda i: (0, 0)),
-            pl.BlockSpec(unit.shape, lambda i: (0, 0)),
-            pl.BlockSpec(counts.shape, lambda i: (0, 0)),
-            pl.BlockSpec(twist.shape, lambda i: (0, 0)),
+    def fixed(operand):
+        return pl.BlockSpec(operand.shape, lambda i, *_: (0, 0))
+
+    image, tile = pl.pallas_call(
+        functools.partial(
+            image_kernel, pieces=len(uv), chunks=chunks, row_block=row_block, per_row=per_row,
+            tile_cols=tile_cols,
+        ),
+        grid_spec=pltpu.PrefetchScalarGridSpec(
+            num_scalar_prefetch=3,
+            grid=(chunks + outs,),
+            in_specs=[
+                *[pl.BlockSpec((size * HALF // len(uv), PACK), lambda i, *_: (chunk_of(i), 0))]
+                * len(uv),
+                pl.BlockSpec((1, size), lambda i, *_: (0, chunk_of(i))),
+                pl.BlockSpec((2, image_rows, size), lambda i, *_: (0, 0, chunk_of(i))),
+                fixed(columns),
+                fixed(unit),
+                fixed(counts),
+                fixed(twist),
+                pl.BlockSpec(memory_space=pl.ANY),
+            ],
+            out_specs=[
+                pl.BlockSpec(
+                    (row_block * wide, LANES), lambda i, *_: (jnp.maximum(i - chunks, 0), 0)
+                ),
+                pl.BlockSpec(memory_space=pl.ANY),
+            ],
+            scratch_shapes=[
+                pltpu.VMEM((size * (HALF + 1) + HALF, PACK), f32),
+                pltpu.VMEM((HALF, size, PACK), bf16),
+                pltpu.VMEM((size, FINE), bf16),
+                pltpu.VMEM((size, FINE), bf16),
+                pltpu.VMEM((size, LANES), f32),
+                pltpu.VMEM((2, 2 * image_rows, size), bf16),
+                pltpu.VMEM((2, 2 * image_rows, size), bf16),
+                pltpu.VMEM((SUB, 2, image_rows, FINE), f32),
+                pltpu.VMEM((8 * (wide + 1) + wide, LANES), f32),
+                pltpu.VMEM((3 * SUB * lanes, LANES), f32),
+                pltpu.SMEM((per_row + 1,), jnp.int32),
+                pltpu.SemaphoreType.DMA(()),
+            ],
+        ),
+        out_shape=[
+            jax.ShapeDtypeStruct((image_rows * wide, LANES), f32),
+            jax.ShapeDtypeStruct(tile.shape, f32),
         ],
-        out_specs=pl.BlockSpec(
-            (row_block * wide, LANES), lambda i: (jnp.maximum(i - chunks, 0), 0)
-        ),
-        out_shape=jax.ShapeDtypeStruct((image_rows * wide, LANES), f32),
-        scratch_shapes=[
-            pltpu.VMEM((size * (HALF + 1) + HALF, PACK), f32),
-            pltpu.VMEM((HALF, size, PACK), bf16),
-            pltpu.VMEM((size, FINE), bf16),
-            pltpu.VMEM((size, FINE), bf16),
-            pltpu.VMEM((size, LANES), f32),
-            pltpu.VMEM((2, 2 * image_rows, size), bf16),
-            pltpu.VMEM((2, 2 * image_rows, size), bf16),
-            pltpu.VMEM((SUB, 2, image_rows, FINE), f32),
-            pltpu.VMEM((8 * (wide + 1) + wide, LANES), f32),
-        ],
+        input_output_aliases={9 + len(uv): 1},
         compiler_params=pltpu.CompilerParams(vmem_limit_bytes=VMEM_BYTES),
         name="image",
         interpret=interpret,
     )(
-        *[piece.reshape(-1, PACK) for piece in uv], corners_all[0].reshape(1, total),
-        phase, columns, unit, counts, twist,
+        info, *corners_all, *[piece.reshape(-1, PACK) for piece in uv],
+        corners_all[0].reshape(1, total), phase, columns, unit, counts, twist, tile,
     )
-    result = result.reshape(image_rows, G // LANES, 2, LANES)
-    return jnp.transpose(result, (0, 2, 1, 3)).reshape(image_rows, 2, G)
+    image = image.reshape(image_rows, G // LANES, 2, LANES)
+    tile = tile.reshape(tile_rows, tile_cols // LANES, 2, LANES)
+    return (
+        jnp.transpose(tile, (0, 2, 1, 3)).reshape(tile_rows, 2, tile_cols),
+        jnp.transpose(image, (0, 2, 1, 3)).reshape(image_rows, 2, G),
+    )
 
 
 def packed_beams(beam_terms):
@@ -697,7 +708,9 @@
     skies = [sky_sums(visibilities, offsets, scale_row, 0, part)]
     if by_mask:
         line = z_line(sent)
-        line, offsets, skies[0] = lax.optimization_barrier((line, offsets, skies[0]))
+        line, offsets, skies[0], corners, stations, screen_depth = lax.optimization_barrier(
+            (line, offsets, skies[0], corners, stations, screen_depth)
+        )
     for s in range(part, count, part):
         skies.append(sky_sums(visibilities, offsets, scale_row, s, part))
     factor = pixel_factor(screen_depth, corners[:, 0] % SUB, vis_count)
@@ -716,36 +729,27 @@
     uv_own = corrected_subgrids(station_rows, tables, skies, factor)
 
     per_row = vert_count * count
-
-    def row_place(index):
-        return gathered_place(index * vert_count + vert_index, by_mask) // vert_count
-
-    def places_of(place, spilled):
-        chosen = [lax.dynamic_slice_in_dim(x, place * per_row, per_row) for x in corners_all]
-        return tile_places(chosen, au_index, vert_index, au_count, vert_count, spilled)
-
-    own_place = row_place(au_index)
-    before_place = row_place(lax.rem(au_index + au_count - 1, au_count))
-    own_list, spill_list = places_of(own_place, False), places_of(before_place, True)
+    tile_rows, tile_cols = G // au_count, G // vert_count
+
+    def tile_info(row):
+        place = gathered_place(row * vert_count + vert_index, by_mask) // vert_count
+        return jnp.stack([place, au_index * tile_rows, vert_index * tile_cols])
+
+    own_info = tile_info(au_index)
+    before_info = tile_info(lax.rem(au_index + au_count - 1, au_count))
     if by_mask:
         lines = au_lines(z_line(uv_own))
         own_row = with_core(lines[:1])
-        tile = uv_tile_own(own_row, own_place, own_list, au_count, vert_count)
+        tile = uv_tile_own(own_row, own_info, corners_all, per_row, tile_rows, tile_cols)
         lines, own_row, tile = lax.optimization_barrier((lines, own_row, tile))
         uv = own_row + with_core(lines[1:])
-        before = [
-            lax.select_n(before_place, *uv[core::2]) if au_count > 2 else uv[core + 2]
-            for core in range(2)
-        ]
-        before_block = jnp.zeros((), jnp.int32)
     else:
-        uv = before = whole_gather(uv_own)
-        tile = uv_tile_own(uv, own_place, own_list, au_count, vert_count)
-        before_block = before_place
-    gridded = uv_tile_spill(tile, before, before_block, spill_list, au_count, vert_count)
+        uv = whole_gather(uv_own)
+        tile = uv_tile_own(uv, own_info, corners_all, per_row, tile_rows, tile_cols)
     first_row = (au_index * vert_count + vert_index) * image_rows
-    dirty_image = image_rows_of(uv, corners_all, first_row, image_rows)
-    return (gridded, dirty_image)
+    return image_rows_of(
+        uv, corners_all, first_row, image_rows, tile, before_info, per_row, tile_rows, tile_cols
+    )
 
 
 def solution(mesh):

time: 119 us -> 123 us (1.034)
  waiting for transfers between devices: 4.39 us -> 9.5 us
  other arithmetic: 16.4 us -> 11.4 us
  local copies, waits for them, and re-layouts: 8.9 us -> 11.6 us
  Pallas kernels: 67.3 us -> 68.9 us
    ppermute x20, waiting for transfers between devices: 4.39 us -> 9.5 us  [from_partner(): return lax.ppermute(value, axis, [(i, i ^ mask) for i in range(count)])]
    pallas_call x1 -> x0, Pallas kernels: 3.72 us -> none  [uv_tile_spill(): pl.pallas_call(functools.partial(spill_kernel, pieces=len(uv), lanes=lane...]
    pallas_call x1, Pallas kernels: 32.1 us -> 34.7 us  [image_rows_of(): pl.pallas_call(functools.partial(image_kernel, pieces=len(uv), chunks=chu...]
    concatenate x2 -> x0, other arithmetic: 2.5 us -> none  [listed(): return jnp.concatenate([jnp.sum(valid, dtype=jnp.int32)[None], entries])]
    select_n x4 -> x0, other arithmetic: 1.8 us -> none  [the longest x2 1.79 us: on_device(): lax.select_n(before_place, *uv[core::2])]
    reduce_sum x5 -> x0, other arithmetic: 1.79 us -> none  [the longest x1 1.32 us: listed(): return jnp.concatenate([jnp.sum(valid, dtype=jnp.int32)[None], entries])]
    pallas_call x1, Pallas kernels: 6.66 us -> 8.28 us  [corrected_subgrids(): pl.pallas_call(functools.partial(correct_kernel, pieces=len(tables), skie...]
    unnamed x53 -> x55, local copies, waits for them, and re-layouts: 4.83 us -> 6.27 us
  transfers between devices with their start and end apart: 20 -> 20, of which waited for: 5 -> 6; matrix products, arithmetic and copies ran while one was open for 16% -> 14% of each run, Pallas kernels for 21% -> 21%
where the time goes in v5:
time: 123 us; the launch traced here: 122 us
  Pallas kernels  68.9 us (56%)
  starting transfers between devices  18.9 us (15%)
  local copies, waits for them, and re-layouts  11.6 us (9%)
  other arithmetic  11.4 us (9%)
  waiting for transfers between devices  9.5 us (8%)
  between operations  1.27 us (1%)
    pallas_call x1, Pallas kernels, image_rows_of(): pl.pallas_call(functools.partial(image_kernel, pieces=len(uv), chunks=chu...  34.7 us
    ppermute x20, starting transfers between devices, from_partner(): return lax.ppermute(value, axis, [(i, i ^ mask) for i in range(count)])  18.9 us
    pallas_call x3, Pallas kernels, sky_sums(): pl.pallas_call(sky_kernel, grid=(1,), in_specs=[pl.BlockSpec((count, 2, v...  13.8 us
    pallas_call x1, Pallas kernels, uv_tile_own(): pl.pallas_call(functools.partial(tile_kernel, pieces=len(uv), tile_rows=t...  12.1 us
    ppermute x20, waiting for transfers between devices, from_partner(): return lax.ppermute(value, axis, [(i, i ^ mask) for i in range(count)])  9.5 us
    pallas_call x1, Pallas kernels, corrected_subgrids(): pl.pallas_call(functools.partial(correct_kernel, pieces=len(tables), skie...  8.28 us
    unnamed x55, local copies, waits for them, and re-layouts  6.27 us
    another operation x1, other arithmetic  3.45 us
  transfers between devices with their start and end apart: 20, of which 6 were waited for; matrix products, arithmetic and copies ran while one was open for 14% of the time, Pallas kernels for 21%

profile of v5, /device:TPU:0, one launch (start us, length us, event | category | flops | bytes accessed | tf_op | source)
XLA Modules:
  0.0 121.6 jit_solution(5785778334665906676)
XLA Ops:
  0.6 0.8 and_select_fusion.14
  1.4 0.1 convert_element_type.87
  1.5 1.0 reshape.685
  2.6 0.2 copy.42
  2.8 0.2 reshape.686
  3.0 5.1 %collective-permute-start.2 = (bf16[17,16,128]{2,1,0:T(8,128)(2,1)S(1)}, bf16[17,16,128]{2,1,0:T(8,128)(2,1)S(1)}, u32[]{:S(2)}, u32[]{:S(2)}) collective-permute-start(bf16[17,16,128]{2,1,0:T(8,128)(2,1)S(1)} %pad_maximum_fusion.2), channel_id=1, source_target_pairs={{0,6},{1,7},{2,4},{3,5},{4,2},{5,3},{6,0},{7,1},{8,14},{9,15},{10,... | collective-permute-start | bytes 208904 | tf_op jit(solution)/shard_map/ppermute | solution.py:648
  8.1 0.6 collective-permute-start
  8.9 0.1 fusion.18
  9.1 0.2 multiply_convert_fusion
  9.3 4.6 %sky_sums.3.refs_8_ = f32[8,16,128]{2,1,0:T(8,128)} custom-call(bf16[24,2,2048]{2,1,0:T(2,128)(2,1)} %vis_ref.5, f32[48,128]{1,0:T(8,128)} %bitcast.142, f32[1,16]{1,0:T(1,128)} %bitcast.153), custom_call_target="tpu_custom_call" | custom-call | bytes 20000000 | tf_op jit(solution)/shard_map/sky_sums/pallas_call | solution.py:119
  14.0 0.6 add_add_fusion.1.info_ref
  14.6 2.7 %collective-permute-start.5 = (bf16[68,16,128]{2,1,0:T(8,128)(2,1)S(1)}, bf16[68,16,128]{2,1,0:T(8,128)(2,1)S(1)}, u32[]{:S(2)}, u32[]{:S(2)}) collective-permute-start(bf16[68,16,128]{2,1,0:T(8,128)(2,1)S(1)} %constant_dynamic-update-slice_fusion.refs_0_), channel_id=1, source_target_pairs={{0,24},{8,16},{16,8},{24,0},{1,25},{9,17},{17,9},{25,1},{2,26},{10... | collective-permute-start | bytes 835592 | tf_op jit(solution)/shard_map/ppermute | solution.py:648
  17.3 0.5 collective-permute-start.4
  17.8 0.4 collective-permute-start.3
  18.2 0.7 fusion.25
  18.9 0.7 and_select_fusion.2
  19.6 0.7 broadcast_multiply_fusion
  20.2 4.6 %sky_sums.5.refs_10_ = f32[8,16,128]{2,1,0:T(8,128)} custom-call(bf16[24,2,2048]{2,1,0:T(2,128)(2,1)} %vis_ref.5, f32[48,128]{1,0:T(8,128)} %bitcast.143, f32[1,16]{1,0:T(1,128)} %bitcast.154), custom_call_target="tpu_custom_call" | custom-call | bytes 20000000 | tf_op jit(solution)/shard_map/sky_sums/pallas_call | solution.py:119
  24.9 4.6 %sky_sums.4.refs_9_ = f32[8,16,128]{2,1,0:T(8,128)} custom-call(bf16[24,2,2048]{2,1,0:T(2,128)(2,1)} %vis_ref.5, f32[48,128]{1,0:T(8,128)} %bitcast.144, f32[1,16]{1,0:T(1,128)} %bitcast.155), custom_call_target="tpu_custom_call" | custom-call | bytes 20000000 | tf_op jit(solution)/shard_map/sky_sums/pallas_call | solution.py:119
  29.5 0.1 copy.20
  29.6 0.7 reshape.698.stations_ref
  30.2 1.5 %fusion.8.refs_11_ = f32[24,16,128]{2,1,0:T(8,128)} fusion(f32[16,128]{1,0:T(8,128)S(1)} %get-tuple-element.58, f32[128]{0:T(128)S(1)} %fusion.28, s32[16,128]{1,0:T(8,128)S(1)} %fusion.19, s32[24]{0:T(128)S(1)} %and_select_fusion.2, f32[16,128]{1,0:T(8,128)S(1)} %get-tuple-element.57, f32[24]{0:T(128)S(1)} %broadcast_multiply_fusion), kind=kLoop, calls=%fused_computation.24 | loop fusion | flops 884736 | bytes 221888 | tf_op jit(solution)/shard_map/mul | solution.py:643
  31.8 0.1 collective-permute-start.9
  31.8 0.5 collective-permute-start.8
  32.3 0.1 collective-permute-start.6
  32.4 0.4 collective-permute-start.7
  32.9 1.3 %collective-permute-done.6.refs_1_ = bf16[68,16,128]{2,1,0:T(8,128)(2,1)S(1)} collective-permute-done((bf16[68,16,128]{2,1,0:T(8,128)(2,1)S(1)}, bf16[68,16,128]{2,1,0:T(8,128)(2,1)S(1)}, u32[]{:S(2)}, u32[]{:S(2)}) %collective-permute-start.6) | collective-permute-done | bytes 278560 | tf_op jit(solution)/shard_map/ppermute | solution.py:648
  34.2 0.4 collective-permute-done.7.refs_3_
  34.6 0.3 copy-done.14
  34.9 0.4 copy-done.15
  35.3 0.1 copy-done.13
  35.4 0.7 copy-done.9
  36.1 8.3 %correct.1 = bf16[24,16,128]{2,1,0:T(8,128)(2,1)} custom-call(s32[48]{0:T(128)} %reshape.698.stations_ref, bf16[68,16,128]{2,1,0:T(8,128)(2,1)} %copy-done.2, bf16[68,16,128]{2,1,0:T(8,128)(2,1)} %copy-done.14, bf16[68,16,128]{2,1,0:T(8,128)(2,1)} %copy-done.12, bf16[68,16,128]{2,1,0:T(8,128)(2,1)} %copy-done.15, bf16[68,16,128]{2,1,0:T(8,128)(2,1)} %copy-done.11, ...), custom_call_target="tpu_custom_call" | custom-call | bytes 16000000 | tf_op jit(solution)/shard_map/correct/pallas_call | solution.py:196
  44.4 3.7 %collective-permute-start.12 = (bf16[24,16,128]{2,1,0:T(8,128)(2,1)}, bf16[24,16,128]{2,1,0:T(8,128)(2,1)S(1)}, u32[]{:S(2)}, u32[]{:S(2)}) collective-permute-start(bf16[24,16,128]{2,1,0:T(8,128)(2,1)} %correct.1), channel_id=1, source_target_pairs={{0,6},{1,7},{2,4},{3,5},{4,2},{5,3},{6,0},{7,1},{8,14},{9,15},{10,... | collective-permute-start | bytes 294920 | tf_op jit(solution)/shard_map/ppermute | solution.py:648
  48.1 0.6 collective-permute-start.10
  48.8 0.7 slice_bitcast_fusion.6
  49.5 0.7 slice_bitcast_fusion.4
  50.2 0.7 slice_bitcast_fusion.2
  51.0 1.1 collective-permute-done.12
  52.1 4.5 %collective-permute-done.11 = bf16[24,16,128]{2,1,0:T(8,128)(2,1)S(1)} collective-permute-done((bf16[24,16,128]{2,1,0:T(8,128)(2,1)}, bf16[24,16,128]{2,1,0:T(8,128)(2,1)S(1)}, u32[]{:S(2)}, u32[]{:S(2)}) %collective-permute-start.11) | collective-permute-done | bytes 98336 | tf_op jit(solution)/shard_map/ppermute | solution.py:648
  56.6 0.9 pad_maximum_fusion.1
  57.5 0.1 collective-permute-start.16
  57.6 2.5 %collective-permute-start.15 = (bf16[96,16,128]{2,1,0:T(8,128)(2,1)S(1)}, bf16[96,16,128]{2,1,0:T(8,128)(2,1)S(1)}, u32[]{:S(2)}, u32[]{:S(2)}) collective-permute-start(bf16[96,16,128]{2,1,0:T(8,128)(2,1)S(1)} %pad_maximum_fusion.1), channel_id=1, source_target_pairs={{0,24},{8,16},{16,8},{24,0},{1,25},{9,17},{17,9},{25,1},{2,26},{10... | collective-permute-start | bytes 1179656 | tf_op jit(solution)/shard_map/ppermute | solution.py:648
  60.1 0.5 collective-permute-start.14
  60.6 0.5 collective-permute-start.13
  61.2 0.7 slice_bitcast_fusion
  61.9 0.1 concatenate.49
  62.1 0.1 slice_add_fusion
  62.2 0.7 add.293.col_ref
  62.8 0.7 add.291.row_ref
  63.5 0.8 copy-done.1
  64.3 12.1 %uv_tile.1.refs_14_ = f32[32768,128]{1,0:T(8,128)} custom-call(s32[3]{0:T(128)} %add_add_fusion.1.info_ref, s32[768]{0:T(1024)} %add.291.row_ref, s32[768]{0:T(1024)} %add.293.col_ref, bf16[1536,128]{1,0:T(8,128)(2,1)} %bitcast.121, bf16[1536,128]{1,0:T(8,128)(2,1)} %bitcast.123), custom_call_target="tpu_custom_call" | custom-call | bytes 41943040 | tf_op jit(solution)/shard_map/uv_tile/pallas_call | solution.py:307
  76.4 2.1 %collective-permute-done.14 = bf16[96,16,128]{2,1,0:T(8,128)(2,1)S(1)} collective-permute-done((bf16[96,16,128]{2,1,0:T(8,128)(2,1)S(1)}, bf16[96,16,128]{2,1,0:T(8,128)(2,1)S(1)}, u32[]{:S(2)}, u32[]{:S(2)}) %collective-permute-start.14) | collective-permute-done | bytes 393248 | tf_op jit(solution)/shard_map/ppermute | solution.py:648
  78.5 0.1 collective-permute-done.13
  78.6 0.5 collective-permute-start.18
  79.1 0.6 add_add_fusion.info_ref
  79.8 0.8 copy.21.refs_10_
  80.6 0.7 add.315.refs_8_
  81.3 3.4 %cosine_convert_fusion = (bf16[1,256,768]{2,1,0:T(8,128)(2,1)S(1)}, bf16[1,256,768]{2,1,0:T(8,128)(2,1)S(1)}) fusion(s32[768]{0:T(1024)S(1)} %copy-done.16, s32[256]{0:T(256)S(1)} %iota_add_fusion.1), kind=kLoop, calls=%fused_computation.10 | loop fusion | flops 3145728 | bytes 790528 | tf_op jit(solution)/shard_map/convert
  84.8 1.0 pad_maximum_fusion.refs_9_
  85.8 0.7 copy-done.6
  86.5 0.1 copy-done.7
  86.6 0.1 copy-done.8
  86.8 34.7 %image.1 = (f32[32768,128]{1,0:T(8,128)}, f32[32768,128]{1,0:T(8,128)}) custom-call(s32[3]{0:T(128)} %add_add_fusion.info_ref, s32[768]{0:T(1024)} %add.291.row_ref, s32[768]{0:T(1024)} %add.293.col_ref, bf16[1536,128]{1,0:T(8,128)(2,1)} %bitcast.122, bf16[1536,128]{1,0:T(8,128)(2,1)} %bitcast.124, ...), custom_call_target="tpu_custom_call", output_to_operand_aliasing={{1}: (17, {})} | custom-call | tf_op jit(solution)/shard_map/image/pallas_call | solution.py:558
  (75 shorter events, 0.4 us)
Async XLA Ops:
  3.0 11.6 %collective-permute-start.2 = (bf16[17,16,128]{2,1,0:T(8,128)(2,1)S(1)}, bf16[17,16,128]{2,1,0:T(8,128)(2,1)S(1)}, u32[]{:S(2)}, u32[]{:S(2)}) collective-permute-start(bf16[17,16,128]{2,1,0:T(8,128)(2,1)S(1)} %pad_maximum_fusion.2), channel_id=1, source_target_pairs={{0,6},{1,7},{2,4},{3,5},{4,2},{5,3},{6,0},{7,1},{8,14},{9,15},{10,... | collective-permute-start | bytes 208904 | tf_op jit(solution)/shard_map/ppermute | solution.py:648
  8.1 6.4 %collective-permute-start.1 = (bf16[17,16,128]{2,1,0:T(8,128)(2,1)S(1)}, bf16[17,16,128]{2,1,0:T(8,128)(2,1)S(1)}, u32[]{:S(2)}, u32[]{:S(2)}) collective-permute-start(bf16[17,16,128]{2,1,0:T(8,128)(2,1)S(1)} %pad_maximum_fusion.2), channel_id=1, source_target_pairs={{0,4},{1,5},{2,6},{3,7},{4,0},{5,1},{6,2},{7,3},{8,12},{9,13},{10,... | collective-permute-start | bytes 208904 | tf_op jit(solution)/shard_map/ppermute | solution.py:648
  8.1 6.4 %collective-permute-start = (bf16[17,16,128]{2,1,0:T(8,128)(2,1)S(1)}, bf16[17,16,128]{2,1,0:T(8,128)(2,1)S(1)}, u32[]{:S(2)}, u32[]{:S(2)}) collective-permute-start(bf16[17,16,128]{2,1,0:T(8,128)(2,1)S(1)} %pad_maximum_fusion.2), channel_id=1, source_target_pairs={{0,2},{1,3},{2,0},{3,1},{4,6},{5,7},{6,4},{7,5},{8,10},{9,11},{10,... | collective-permute-start | bytes 208904 | tf_op jit(solution)/shard_map/ppermute | solution.py:648
  14.6 20.0 %copy-start.2 = (bf16[68,16,128]{2,1,0:T(8,128)(2,1)}, bf16[68,16,128]{2,1,0:T(8,128)(2,1)S(1)}, u32[]{:S(2)}) copy-start(bf16[68,16,128]{2,1,0:T(8,128)(2,1)S(1)} %constant_dynamic-update-slice_fusion.refs_0_) | copy-start | bytes 835588
  14.6 17.1 %collective-permute-start.5 = (bf16[68,16,128]{2,1,0:T(8,128)(2,1)S(1)}, bf16[68,16,128]{2,1,0:T(8,128)(2,1)S(1)}, u32[]{:S(2)}, u32[]{:S(2)}) collective-permute-start(bf16[68,16,128]{2,1,0:T(8,128)(2,1)S(1)} %constant_dynamic-update-slice_fusion.refs_0_), channel_id=1, source_target_pairs={{0,24},{8,16},{16,8},{24,0},{1,25},{9,17},{17,9},{25,1},{2,26},{10... | collective-permute-start | bytes 835592 | tf_op jit(solution)/shard_map/ppermute | solution.py:648
  17.3 14.4 %collective-permute-start.4 = (bf16[68,16,128]{2,1,0:T(8,128)(2,1)S(1)}, bf16[68,16,128]{2,1,0:T(8,128)(2,1)S(1)}, u32[]{:S(2)}, u32[]{:S(2)}) collective-permute-start(bf16[68,16,128]{2,1,0:T(8,128)(2,1)S(1)} %constant_dynamic-update-slice_fusion.refs_0_), channel_id=1, source_target_pairs={{0,16},{8,24},{16,0},{24,8},{1,17},{9,25},{17,1},{25,9},{2,18},{10... | collective-permute-start | bytes 835592 | tf_op jit(solution)/shard_map/ppermute | solution.py:648
  17.8 13.9 %collective-permute-start.3 = (bf16[68,16,128]{2,1,0:T(8,128)(2,1)S(1)}, bf16[68,16,128]{2,1,0:T(8,128)(2,1)S(1)}, u32[]{:S(2)}, u32[]{:S(2)}) collective-permute-start(bf16[68,16,128]{2,1,0:T(8,128)(2,1)S(1)} %constant_dynamic-update-slice_fusion.refs_0_), channel_id=1, source_target_pairs={{0,8},{8,0},{16,24},{24,16},{1,9},{9,1},{17,25},{25,17},{2,10},{10... | collective-permute-start | bytes 835592 | tf_op jit(solution)/shard_map/ppermute | solution.py:648
  31.7 2.9 %copy-start.10 = (bf16[68,16,128]{2,1,0:T(8,128)(2,1)}, bf16[68,16,128]{2,1,0:T(8,128)(2,1)S(1)}, u32[]{:S(2)}) copy-start(bf16[68,16,128]{2,1,0:T(8,128)(2,1)S(1)} %collective-permute-done.5.refs_6_) | copy-start | bytes 835588
  31.7 2.9 %copy-start.11 = (bf16[68,16,128]{2,1,0:T(8,128)(2,1)}, bf16[68,16,128]{2,1,0:T(8,128)(2,1)S(1)}, u32[]{:S(2)}) copy-start(bf16[68,16,128]{2,1,0:T(8,128)(2,1)S(1)} %collective-permute-done.4.refs_4_) | copy-start | bytes 835588
  31.7 2.9 %copy-start.12 = (bf16[68,16,128]{2,1,0:T(8,128)(2,1)}, bf16[68,16,128]{2,1,0:T(8,128)(2,1)S(1)}, u32[]{:S(2)}) copy-start(bf16[68,16,128]{2,1,0:T(8,128)(2,1)S(1)} %collective-permute-done.3.refs_2_) | copy-start | bytes 835588
  31.8 2.8 %collective-permute-start.9 = (bf16[68,16,128]{2,1,0:T(8,128)(2,1)S(1)}, bf16[68,16,128]{2,1,0:T(8,128)(2,1)S(1)}, u32[]{:S(2)}, u32[]{:S(2)}) collective-permute-start(bf16[68,16,128]{2,1,0:T(8,128)(2,1)S(1)} %collective-permute-done.5.refs_6_), channel_id=1, source_target_pairs={{0,1},{1,0},{2,3},{3,2},{4,5},{5,4},{6,7},{7,6},{8,9},{9,8},{10,11... | collective-permute-start | bytes 835592 | tf_op jit(solution)/shard_map/ppermute | solution.py:648
  31.8 2.7 %collective-permute-start.8 = (bf16[68,16,128]{2,1,0:T(8,128)(2,1)S(1)}, bf16[68,16,128]{2,1,0:T(8,128)(2,1)S(1)}, u32[]{:S(2)}, u32[]{:S(2)}) collective-permute-start(bf16[68,16,128]{2,1,0:T(8,128)(2,1)S(1)} %collective-permute-done.4.refs_4_), channel_id=1, source_target_pairs={{0,1},{1,0},{2,3},{3,2},{4,5},{5,4},{6,7},{7,6},{8,9},{9,8},{10,11... | collective-permute-start | bytes 835592 | tf_op jit(solution)/shard_map/ppermute | solution.py:648
  32.3 1.8 %collective-permute-start.6 = (bf16[68,16,128]{2,1,0:T(8,128)(2,1)S(1)}, bf16[68,16,128]{2,1,0:T(8,128)(2,1)S(1)}, u32[]{:S(2)}, u32[]{:S(2)}) collective-permute-start(bf16[68,16,128]{2,1,0:T(8,128)(2,1)S(1)} %constant_dynamic-update-slice_fusion.refs_0_), channel_id=1, source_target_pairs={{0,1},{1,0},{2,3},{3,2},{4,5},{5,4},{6,7},{7,6},{8,9},{9,8},{10,11... | collective-permute-start | bytes 835592 | tf_op jit(solution)/shard_map/ppermute | solution.py:648
  32.4 2.2 %collective-permute-start.7 = (bf16[68,16,128]{2,1,0:T(8,128)(2,1)S(1)}, bf16[68,16,128]{2,1,0:T(8,128)(2,1)S(1)}, u32[]{:S(2)}, u32[]{:S(2)}) collective-permute-start(bf16[68,16,128]{2,1,0:T(8,128)(2,1)S(1)} %collective-permute-done.3.refs_2_), channel_id=1, source_target_pairs={{0,1},{1,0},{2,3},{3,2},{4,5},{5,4},{6,7},{7,6},{8,9},{9,8},{10,11... | collective-permute-start | bytes 835592 | tf_op jit(solution)/shard_map/ppermute | solution.py:648
  34.2 0.7 copy-start.14
  34.6 0.7 copy-start.15
  34.6 0.8 copy-start.13
  35.4 0.7 copy-start.9
  44.4 7.7 %collective-permute-start.12 = (bf16[24,16,128]{2,1,0:T(8,128)(2,1)}, bf16[24,16,128]{2,1,0:T(8,128)(2,1)S(1)}, u32[]{:S(2)}, u32[]{:S(2)}) collective-permute-start(bf16[24,16,128]{2,1,0:T(8,128)(2,1)} %correct.1), channel_id=1, source_target_pairs={{0,6},{1,7},{2,4},{3,5},{4,2},{5,3},{6,0},{7,1},{8,14},{9,15},{10,... | collective-permute-start | bytes 294920 | tf_op jit(solution)/shard_map/ppermute | solution.py:648
  48.1 8.4 %collective-permute-start.11 = (bf16[24,16,128]{2,1,0:T(8,128)(2,1)}, bf16[24,16,128]{2,1,0:T(8,128)(2,1)S(1)}, u32[]{:S(2)}, u32[]{:S(2)}) collective-permute-start(bf16[24,16,128]{2,1,0:T(8,128)(2,1)} %correct.1), channel_id=1, source_target_pairs={{0,4},{1,5},{2,6},{3,7},{4,0},{5,1},{6,2},{7,3},{8,12},{9,13},{10,... | collective-permute-start | bytes 294920 | tf_op jit(solution)/shard_map/ppermute | solution.py:648
  48.1 8.4 %collective-permute-start.10 = (bf16[24,16,128]{2,1,0:T(8,128)(2,1)}, bf16[24,16,128]{2,1,0:T(8,128)(2,1)S(1)}, u32[]{:S(2)}, u32[]{:S(2)}) collective-permute-start(bf16[24,16,128]{2,1,0:T(8,128)(2,1)} %correct.1), channel_id=1, source_target_pairs={{0,2},{1,3},{2,0},{3,1},{4,6},{5,7},{6,4},{7,5},{8,10},{9,11},{10,... | collective-permute-start | bytes 294920 | tf_op jit(solution)/shard_map/ppermute | solution.py:648
  57.5 6.0 %copy-start = (bf16[96,16,128]{2,1,0:T(8,128)(2,1)}, bf16[96,16,128]{2,1,0:T(8,128)(2,1)S(1)}, u32[]{:S(2)}) copy-start(bf16[96,16,128]{2,1,0:T(8,128)(2,1)S(1)} %pad_maximum_fusion.1) | copy-start | bytes 1179652
  57.5 6.0 %collective-permute-start.16 = (bf16[96,16,128]{2,1,0:T(8,128)(2,1)S(1)}, bf16[96,16,128]{2,1,0:T(8,128)(2,1)S(1)}, u32[]{:S(2)}, u32[]{:S(2)}) collective-permute-start(bf16[96,16,128]{2,1,0:T(8,128)(2,1)S(1)} %pad_maximum_fusion.1), channel_id=1, source_target_pairs={{0,1},{1,0},{2,3},{3,2},{4,5},{5,4},{6,7},{7,6},{8,9},{9,8},{10,11... | collective-permute-start | bytes 1179656 | tf_op jit(solution)/shard_map/ppermute | solution.py:648
  57.6 18.7 %collective-permute-start.15 = (bf16[96,16,128]{2,1,0:T(8,128)(2,1)S(1)}, bf16[96,16,128]{2,1,0:T(8,128)(2,1)S(1)}, u32[]{:S(2)}, u32[]{:S(2)}) collective-permute-start(bf16[96,16,128]{2,1,0:T(8,128)(2,1)S(1)} %pad_maximum_fusion.1), channel_id=1, source_target_pairs={{0,24},{8,16},{16,8},{24,0},{1,25},{9,17},{17,9},{25,1},{2,26},{10... | collective-permute-start | bytes 1179656 | tf_op jit(solution)/shard_map/ppermute | solution.py:648
  60.1 18.3 %collective-permute-start.14 = (bf16[96,16,128]{2,1,0:T(8,128)(2,1)S(1)}, bf16[96,16,128]{2,1,0:T(8,128)(2,1)S(1)}, u32[]{:S(2)}, u32[]{:S(2)}) collective-permute-start(bf16[96,16,128]{2,1,0:T(8,128)(2,1)S(1)} %pad_maximum_fusion.1), channel_id=1, source_target_pairs={{0,16},{8,24},{16,0},{24,8},{1,17},{9,25},{17,1},{25,9},{2,18},{10... | collective-permute-start | bytes 1179656 | tf_op jit(solution)/shard_map/ppermute | solution.py:648
  60.6 17.9 %collective-permute-start.13 = (bf16[96,16,128]{2,1,0:T(8,128)(2,1)S(1)}, bf16[96,16,128]{2,1,0:T(8,128)(2,1)S(1)}, u32[]{:S(2)}, u32[]{:S(2)}) collective-permute-start(bf16[96,16,128]{2,1,0:T(8,128)(2,1)S(1)} %pad_maximum_fusion.1), channel_id=1, source_target_pairs={{0,8},{8,0},{16,24},{24,16},{1,9},{9,1},{17,25},{25,17},{2,10},{10... | collective-permute-start | bytes 1179656 | tf_op jit(solution)/shard_map/ppermute | solution.py:648
  62.8 18.5 %copy-start.16 = (s32[768]{0:T(1024)S(1)}, s32[768]{0:T(1024)}, u32[]{:S(2)}) copy-start(s32[768]{0:T(1024)} %add.293.col_ref) | copy-start | bytes 9220
  63.5 0.8 copy-start.1
  76.4 9.4 %copy-start.3 = (bf16[96,16,128]{2,1,0:T(8,128)(2,1)}, bf16[96,16,128]{2,1,0:T(8,128)(2,1)S(1)}, u32[]{:S(2)}) copy-start(bf16[96,16,128]{2,1,0:T(8,128)(2,1)S(1)} %collective-permute-done.15) | copy-start | bytes 1179652
  78.5 7.3 %copy-start.4 = (bf16[96,16,128]{2,1,0:T(8,128)(2,1)}, bf16[96,16,128]{2,1,0:T(8,128)(2,1)S(1)}, u32[]{:S(2)}) copy-start(bf16[96,16,128]{2,1,0:T(8,128)(2,1)S(1)} %collective-permute-done.14) | copy-start | bytes 1179652
  78.6 7.2 %copy-start.5 = (bf16[96,16,128]{2,1,0:T(8,128)(2,1)}, bf16[96,16,128]{2,1,0:T(8,128)(2,1)S(1)}, u32[]{:S(2)}) copy-start(bf16[96,16,128]{2,1,0:T(8,128)(2,1)S(1)} %collective-permute-done.13) | copy-start | bytes 1179652
  78.6 7.1 %collective-permute-start.17 = (bf16[96,16,128]{2,1,0:T(8,128)(2,1)S(1)}, bf16[96,16,128]{2,1,0:T(8,128)(2,1)S(1)}, u32[]{:S(2)}, u32[]{:S(2)}) collective-permute-start(bf16[96,16,128]{2,1,0:T(8,128)(2,1)S(1)} %collective-permute-done.13), channel_id=1, source_target_pairs={{0,1},{1,0},{2,3},{3,2},{4,5},{5,4},{6,7},{7,6},{8,9},{9,8},{10,11... | collective-permute-start | bytes 1179656 | tf_op jit(solution)/shard_map/ppermute | solution.py:648
  78.6 7.1 %collective-permute-start.18 = (bf16[96,16,128]{2,1,0:T(8,128)(2,1)S(1)}, bf16[96,16,128]{2,1,0:T(8,128)(2,1)S(1)}, u32[]{:S(2)}, u32[]{:S(2)}) collective-permute-start(bf16[96,16,128]{2,1,0:T(8,128)(2,1)S(1)} %collective-permute-done.14), channel_id=1, source_target_pairs={{0,1},{1,0},{2,3},{3,2},{4,5},{5,4},{6,7},{7,6},{8,9},{9,8},{10,11... | collective-permute-start | bytes 1179656 | tf_op jit(solution)/shard_map/ppermute | solution.py:648
  79.1 6.6 %collective-permute-start.19 = (bf16[96,16,128]{2,1,0:T(8,128)(2,1)S(1)}, bf16[96,16,128]{2,1,0:T(8,128)(2,1)S(1)}, u32[]{:S(2)}, u32[]{:S(2)}) collective-permute-start(bf16[96,16,128]{2,1,0:T(8,128)(2,1)S(1)} %collective-permute-done.15), channel_id=1, source_target_pairs={{0,1},{1,0},{2,3},{3,2},{4,5},{5,4},{6,7},{7,6},{8,9},{9,8},{10,11... | collective-permute-start | bytes 1179656 | tf_op jit(solution)/shard_map/ppermute | solution.py:648
  85.7 0.8 copy-start.6
  85.7 0.9 copy-start.7
  85.8 1.0 copy-start.8

commit v6 on v5

--- a/solution.py
+++ b/solution.py
@@ -167,11 +167,10 @@
         sky = product(sky_refs[s // per][s % per], factor_ref[s])
         mid_ref[HALF * s : HALF * (s + 1), :] = product(sky, pair).astype(bf16)
     mid = jnp.dot(mid_ref[...], right_ref[...], preferred_element_type=f32).astype(bf16)
-    wide = jnp.concatenate([mid[HALF * s : HALF * (s + 1)] for s in range(count)], axis=1)
-    every = jnp.dot(left_ref[...], wide, preferred_element_type=f32)
     for s in range(count):
-        block = every[:, PACK * s : PACK * (s + 1)]
-        four = block[: 2 * SUB, : 2 * SUB] + block[2 * SUB :, 2 * SUB :]
+        rows = mid[HALF * s : HALF * (s + 1)]
+        tall = jnp.concatenate([rows[:, : 2 * SUB], rows[:, 2 * SUB :]], axis=0)
+        four = jnp.dot(left_ref[...], tall, preferred_element_type=f32)
         real = four[:SUB, :SUB] - four[SUB:, SUB:]
         image = four[:SUB, SUB:] + four[SUB:, :SUB]
         out_ref[s] = jnp.concatenate(
@@ -185,8 +184,7 @@
     angle = 2.0 * math.pi / SUB * (centred[:, None] * centred[None, :] % SUB)
     re, im = np.cos(angle) / SUB, -np.sin(angle) / SUB
     right = jnp.asarray(np.kron(np.eye(2), np.block([[re, im], [-im, re]])), bf16)
-    left = np.concatenate([re, im], axis=0)
-    left = jnp.asarray(np.concatenate([left[:, :HALF], left[:, HALF:]], axis=0), bf16)
+    left = jnp.asarray(np.concatenate([re, im], axis=0), bf16)
     rows = sum(piece.shape[0] for piece in tables)
     operands = [*tables, *skies, factor, right, left]
 
@@ -303,7 +301,11 @@
 
 def uv_tile_own(uv, info, corners, count, tile_rows, tile_cols, interpret=False):
     lanes = 2 * tile_cols // LANES
-    rows = count * HALF // len(uv)
+    uv = [piece.reshape(-1, PACK) for piece in uv]
+    if len(uv) == 1:
+        uv_specs = [pl.BlockSpec((count * HALF, PACK), lambda i, info, *_: (info[0], 0))]
+    else:
+        uv_specs = [pl.BlockSpec(piece.shape, lambda i, *_: (0, 0)) for piece in uv]
     return pl.pallas_call(
         functools.partial(
             tile_kernel, pieces=len(uv), tile_rows=tile_rows, tile_cols=tile_cols
@@ -311,7 +313,7 @@
         grid_spec=pltpu.PrefetchScalarGridSpec(
             num_scalar_prefetch=3,
             grid=(1,),
-            in_specs=[pl.BlockSpec((rows, PACK), lambda i, info, *_: (info[0], 0))] * len(uv),
+            in_specs=uv_specs,
             out_specs=pl.BlockSpec(memory_space=pl.ANY),
             scratch_shapes=[
                 pltpu.VMEM((count * HALF, PACK), bf16),
@@ -327,7 +329,7 @@
         ),
         name="uv_tile",
         interpret=interpret,
-    )(info, *corners, *[piece.reshape(-1, PACK) for piece in uv])
+    )(info, *corners, *uv)
 
 
 def short_transform(values):
@@ -519,17 +521,10 @@
         lax.fori_loop(0, row_block // 8, eight_rows, 0)
 
 
-def image_rows_of(uv, corners_all, first_row, image_rows, tile, info, per_row, tile_rows, tile_cols, interpret=False):
-    lanes = 2 * tile_cols // LANES
-    total = corners_all[0].shape[0]
-    size = math.gcd(total, CHUNK) if len(uv) == 1 else total
-    chunks = total // size
-    row_block = math.gcd(image_rows, 32)
-    outs = image_rows // row_block
-    wide = 2 * G // LANES
+def image_tables(corner_cols, first_row, image_rows):
     rows = first_row + jnp.arange(image_rows, dtype=jnp.int32)
     turn = 2.0 * math.pi / G
-    angle = turn * (rows[:, None] * corners_all[1][None, :] % G).astype(f32)
+    angle = turn * (rows[:, None] * corner_cols[None, :] % G).astype(f32)
     phase = jnp.stack([jnp.cos(angle), jnp.sin(angle)]).astype(bf16)
     angle = turn * (rows[:, None] * jnp.arange(SUB, dtype=jnp.int32)[None, :] % G).astype(f32)
     re, im = jnp.cos(angle), jnp.sin(angle)
@@ -537,6 +532,22 @@
         [jnp.concatenate([re, -im], axis=1), jnp.concatenate([im, re], axis=1)], axis=0
     )
     columns = jnp.kron(jnp.eye(2, dtype=f32), block).astype(bf16)
+    return phase, columns
+
+
+def image_rows_of(
+    uv, corners_all, tables, tile, info, per_row, tile_rows, tile_cols, interpret=False
+):
+    phase, columns = tables
+    image_rows = phase.shape[1]
+    lanes = 2 * tile_cols // LANES
+    uv = [piece.reshape(-1, PACK) for piece in uv]
+    total = corners_all[0].shape[0]
+    size = math.gcd(total, CHUNK) if len(uv) == 1 else total
+    chunks = total // size
+    row_block = math.gcd(image_rows, 32)
+    outs = image_rows // row_block
+    wide = 2 * G // LANES
     fine, low = np.arange(FINE), np.arange(LOW)
     angle = 2.0 * math.pi / FINE * (fine[:, None] * low[None, :] % FINE)
     odd = np.where(low == 0, 1.0 - 2.0 * (fine[:, None] % 2), np.sin(angle))
@@ -552,6 +563,11 @@
     def chunk_of(i):
         return jnp.minimum(i, last)
 
+    if len(uv) == 1:
+        uv_specs = [pl.BlockSpec((size * HALF, PACK), lambda i, *_: (chunk_of(i), 0))]
+    else:
+        uv_specs = [pl.BlockSpec(piece.shape, lambda i, *_: (0, 0)) for piece in uv]
+
     def fixed(operand):
         return pl.BlockSpec(operand.shape, lambda i, *_: (0, 0))
 
@@ -564,8 +580,7 @@
             num_scalar_prefetch=3,
             grid=(chunks + outs,),
             in_specs=[
-                *[pl.BlockSpec((size * HALF // len(uv), PACK), lambda i, *_: (chunk_of(i), 0))]
-                * len(uv),
+                *uv_specs,
                 pl.BlockSpec((1, size), lambda i, *_: (0, chunk_of(i))),
                 pl.BlockSpec((2, image_rows, size), lambda i, *_: (0, 0, chunk_of(i))),
                 fixed(columns),
@@ -604,7 +619,7 @@
         name="image",
         interpret=interpret,
     )(
-        info, *corners_all, *[piece.reshape(-1, PACK) for piece in uv],
+        info, *corners_all, *uv,
         corners_all[0].reshape(1, total), phase, columns, unit, counts, twist, tile,
     )
     image = image.reshape(image_rows, G // LANES, 2, LANES)
@@ -648,10 +663,10 @@
     return lax.ppermute(value, axis, [(i, i ^ mask) for i in range(count)])
 
 
-def z_line(own):
+def z_line(own, with_own):
     vert_count = lax.axis_size("vert")
-    line = [own] + [from_partner(own, "vert", 2 * mask) for mask in range(1, vert_count // 2)]
-    return jnp.concatenate(line, axis=0)
+    line = [from_partner(own, "vert", 2 * mask) for mask in range(1, vert_count // 2)]
+    return jnp.concatenate([own] * with_own + line, axis=0)
 
 
 def au_lines(line):
@@ -707,7 +722,7 @@
     part = math.gcd(count, 8)
     skies = [sky_sums(visibilities, offsets, scale_row, 0, part)]
     if by_mask:
-        line = z_line(sent)
+        line = z_line(sent, True)
         line, offsets, skies[0], corners, stations, screen_depth = lax.optimization_barrier(
             (line, offsets, skies[0], corners, stations, screen_depth)
         )
@@ -737,18 +752,25 @@
 
     own_info = tile_info(au_index)
     before_info = tile_info(lax.rem(au_index + au_count - 1, au_count))
+    first_row = (au_index * vert_count + vert_index) * image_rows
+    tables = image_tables(corners_all[1], first_row, image_rows)
     if by_mask:
-        lines = au_lines(z_line(uv_own))
-        own_row = with_core(lines[:1])
+        blocks, line = au_lines(uv_own), z_line(uv_own, False)
+        blocks, line, tables, corners_all, own_info, before_info = lax.optimization_barrier(
+            (blocks, line, tables, corners_all, own_info, before_info)
+        )
+        lines = au_lines(line)
+        own_row = [uv_own, line] + [from_partner(piece, "vert", 1) for piece in (uv_own, line)]
         tile = uv_tile_own(own_row, own_info, corners_all, per_row, tile_rows, tile_cols)
         lines, own_row, tile = lax.optimization_barrier((lines, own_row, tile))
-        uv = own_row + with_core(lines[1:])
+        uv = own_row
+        for pair in zip(blocks[1:], lines[1:]):
+            uv = uv + [*pair, *[from_partner(piece, "vert", 1) for piece in pair]]
     else:
         uv = whole_gather(uv_own)
         tile = uv_tile_own(uv, own_info, corners_all, per_row, tile_rows, tile_cols)
-    first_row = (au_index * vert_count + vert_index) * image_rows
     return image_rows_of(
-        uv, corners_all, first_row, image_rows, tile, before_info, per_row, tile_rows, tile_cols
+        uv, corners_all, tables, tile, before_info, per_row, tile_rows, tile_cols
     )
 
 

time: 123 us -> 125 us (1.016)
  the two profiles are of different devices: /device:TPU:0 before, /device:TPU:25 now
where the time goes in v6:
time: 125 us; the launch traced here: 124 us
  Pallas kernels  66.6 us (53%)
  starting transfers between devices  28 us (22%)
  local copies, waits for them, and re-layouts  10.8 us (9%)
  other arithmetic  10 us (8%)
  waiting for transfers between devices  7.41 us (6%)
  between operations  1.4 us (1%)
    pallas_call x1, Pallas kernels, image_rows_of(): pl.pallas_call(functools.partial(image_kernel, pieces=len(uv), chunks=chu...  34.6 us
    ppermute x27, starting transfers between devices, from_partner(): return lax.ppermute(value, axis, [(i, i ^ mask) for i in range(count)])  28 us
    pallas_call x3, Pallas kernels, sky_sums(): pl.pallas_call(sky_kernel, grid=(1,), in_specs=[pl.BlockSpec((count, 2, v...  13.8 us
    pallas_call x1, Pallas kernels, uv_tile_own(): pl.pallas_call(functools.partial(tile_kernel, pieces=len(uv), tile_rows=t...  11.5 us
    ppermute x27, waiting for transfers between devices, from_partner(): return lax.ppermute(value, axis, [(i, i ^ mask) for i in range(count)])  7.41 us
    pallas_call x1, Pallas kernels, corrected_subgrids(): pl.pallas_call(functools.partial(correct_kernel, pieces=len(tables), skie...  6.65 us
    unnamed x71, local copies, waits for them, and re-layouts  6.22 us
    another operation x1, other arithmetic  3.47 us
  transfers between devices with their start and end apart: 27, of which 5 were waited for; matrix products, arithmetic and copies ran while one was open for 12% of the time, Pallas kernels for 20%

profile of v6, /device:TPU:25, one launch (start us, length us, event | category | flops | bytes accessed | tf_op | source)
XLA Modules:
  0.0 124.2 jit_solution(16621359118096153189)
XLA Ops:
  0.6 0.8 and_select_fusion.14
  1.5 1.0 reshape.694
  2.6 0.2 copy.42
  2.8 0.2 reshape.695
  3.1 1.3 %collective-permute-start.1 = (bf16[17,16,128]{2,1,0:T(8,128)(2,1)S(1)}, bf16[17,16,128]{2,1,0:T(8,128)(2,1)S(1)}, u32[]{:S(2)}, u32[]{:S(2)}) collective-permute-start(bf16[17,16,128]{2,1,0:T(8,128)(2,1)S(1)} %pad_maximum_fusion.2), channel_id=1, source_target_pairs={{0,4},{1,5},{2,6},{3,7},{4,0},{5,1},{6,2},{7,3},{8,12},{9,13},{10,... | collective-permute-start | bytes 208904 | tf_op jit(solution)/shard_map/ppermute | solution.py:663
  4.4 2.2 %collective-permute-start = (bf16[17,16,128]{2,1,0:T(8,128)(2,1)S(1)}, bf16[17,16,128]{2,1,0:T(8,128)(2,1)S(1)}, u32[]{:S(2)}, u32[]{:S(2)}) collective-permute-start(bf16[17,16,128]{2,1,0:T(8,128)(2,1)S(1)} %pad_maximum_fusion.2), channel_id=1, source_target_pairs={{0,2},{1,3},{2,0},{3,1},{4,6},{5,7},{6,4},{7,5},{8,10},{9,11},{10,... | collective-permute-start | bytes 208904 | tf_op jit(solution)/shard_map/ppermute | solution.py:663
  6.7 0.1 fusion.18
  6.9 0.2 multiply_convert_fusion
  7.2 4.6 %sky_sums.3.refs_8_ = f32[8,16,128]{2,1,0:T(8,128)} custom-call(bf16[24,2,2048]{2,1,0:T(2,128)(2,1)} %vis_ref.5, f32[48,128]{1,0:T(8,128)} %bitcast.156, f32[1,16]{1,0:T(1,128)} %bitcast.173), custom_call_target="tpu_custom_call" | custom-call | bytes 20000000 | tf_op jit(solution)/shard_map/sky_sums/pallas_call | solution.py:119
  11.8 0.6 add_add_fusion
  12.6 2.2 %collective-permute-start.5 = (bf16[68,16,128]{2,1,0:T(8,128)(2,1)S(1)}, bf16[68,16,128]{2,1,0:T(8,128)(2,1)S(1)}, u32[]{:S(2)}, u32[]{:S(2)}) collective-permute-start(bf16[68,16,128]{2,1,0:T(8,128)(2,1)S(1)} %constant_dynamic-update-slice_fusion.refs_0_), channel_id=1, source_target_pairs={{0,24},{8,16},{16,8},{24,0},{1,25},{9,17},{17,9},{25,1},{2,26},{10... | collective-permute-start | bytes 835592 | tf_op jit(solution)/shard_map/ppermute | solution.py:663
  14.8 0.2 collective-permute-start.4
  15.0 0.3 collective-permute-start.3
  15.3 0.7 fusion.25
  16.0 0.7 and_select_fusion.2
  16.7 0.7 broadcast_multiply_fusion
  17.3 4.6 %sky_sums.5.refs_10_ = f32[8,16,128]{2,1,0:T(8,128)} custom-call(bf16[24,2,2048]{2,1,0:T(2,128)(2,1)} %vis_ref.5, f32[48,128]{1,0:T(8,128)} %bitcast.157, f32[1,16]{1,0:T(1,128)} %bitcast.174), custom_call_target="tpu_custom_call" | custom-call | bytes 20000000 | tf_op jit(solution)/shard_map/sky_sums/pallas_call | solution.py:119
  21.9 4.6 %sky_sums.4.refs_9_ = f32[8,16,128]{2,1,0:T(8,128)} custom-call(bf16[24,2,2048]{2,1,0:T(2,128)(2,1)} %vis_ref.5, f32[48,128]{1,0:T(8,128)} %bitcast.158, f32[1,16]{1,0:T(1,128)} %bitcast.175), custom_call_target="tpu_custom_call" | custom-call | bytes 20000000 | tf_op jit(solution)/shard_map/sky_sums/pallas_call | solution.py:119
  26.6 0.6 reshape.699.stations_ref
  27.3 1.5 %fusion.8.refs_11_ = f32[24,16,128]{2,1,0:T(8,128)} fusion(f32[16,128]{1,0:T(8,128)S(1)} %get-tuple-element.82, f32[128]{0:T(128)S(1)} %fusion.28, s32[16,128]{1,0:T(8,128)S(1)} %fusion.19, s32[24]{0:T(128)S(1)} %and_select_fusion.2, f32[16,128]{1,0:T(8,128)S(1)} %get-tuple-element.81, f32[24]{0:T(128)S(1)} %broadcast_multiply_fusion), kind=kLoop, calls=%fused_computation.24 | loop fusion | flops 884736 | bytes 221888 | tf_op jit(solution)/shard_map/mul | solution.py:658
  28.8 2.4 %collective-permute-start.9 = (bf16[68,16,128]{2,1,0:T(8,128)(2,1)S(1)}, bf16[68,16,128]{2,1,0:T(8,128)(2,1)S(1)}, u32[]{:S(2)}, u32[]{:S(2)}) collective-permute-start(bf16[68,16,128]{2,1,0:T(8,128)(2,1)S(1)} %collective-permute-done.5.refs_6_), channel_id=1, source_target_pairs={{0,1},{1,0},{2,3},{3,2},{4,5},{5,4},{6,7},{7,6},{8,9},{9,8},{10,11... | collective-permute-start | bytes 835592 | tf_op jit(solution)/shard_map/ppermute | solution.py:663
  31.2 0.1 collective-permute-start.8
  31.3 0.4 collective-permute-start.6
  31.9 1.3 %collective-permute-done.6.refs_1_ = bf16[68,16,128]{2,1,0:T(8,128)(2,1)S(1)} collective-permute-done((bf16[68,16,128]{2,1,0:T(8,128)(2,1)S(1)}, bf16[68,16,128]{2,1,0:T(8,128)(2,1)S(1)}, u32[]{:S(2)}, u32[]{:S(2)}) %collective-permute-start.6) | collective-permute-done | bytes 278560 | tf_op jit(solution)/shard_map/ppermute | solution.py:663
  33.2 0.4 collective-permute-done.7.refs_3_
  33.7 0.3 copy-done.9
  33.9 0.4 copy-done.10
  34.3 0.1 copy-done.8
  34.4 0.7 copy-done.5
  35.1 6.7 %correct.1 = bf16[24,16,128]{2,1,0:T(8,128)(2,1)} custom-call(s32[48]{0:T(128)} %reshape.699.stations_ref, bf16[68,16,128]{2,1,0:T(8,128)(2,1)} %copy-done.2, bf16[68,16,128]{2,1,0:T(8,128)(2,1)} %copy-done.9, bf16[68,16,128]{2,1,0:T(8,128)(2,1)} %copy-done.7, bf16[68,16,128]{2,1,0:T(8,128)(2,1)} %copy-done.10, bf16[68,16,128]{2,1,0:T(8,128)(2,1)} %copy-done.6, ...), custom_call_target="tpu_custom_call" | custom-call | bytes 16000000 | tf_op jit(solution)/shard_map/correct/pallas_call | solution.py:194
  41.8 0.9 collective-permute-start.14
  42.7 2.6 %collective-permute-start.13 = (bf16[24,16,128]{2,1,0:T(8,128)(2,1)}, bf16[24,16,128]{2,1,0:T(8,128)(2,1)S(1)}, u32[]{:S(2)}, u32[]{:S(2)}) collective-permute-start(bf16[24,16,128]{2,1,0:T(8,128)(2,1)} %correct.1), channel_id=1, source_target_pairs={{0,2},{1,3},{2,0},{3,1},{4,6},{5,7},{6,4},{7,5},{8,10},{9,11},{10,... | collective-permute-start | bytes 294920 | tf_op jit(solution)/shard_map/ppermute | solution.py:663
  45.3 2.2 %collective-permute-start.12 = (bf16[24,16,128]{2,1,0:T(8,128)(2,1)}, bf16[24,16,128]{2,1,0:T(8,128)(2,1)S(1)}, u32[]{:S(2)}, u32[]{:S(2)}) collective-permute-start(bf16[24,16,128]{2,1,0:T(8,128)(2,1)} %correct.1), channel_id=1, source_target_pairs={{0,24},{8,16},{16,8},{24,0},{1,25},{9,17},{17,9},{25,1},{2,26},{10... | collective-permute-start | bytes 294920 | tf_op jit(solution)/shard_map/ppermute | solution.py:663
  47.5 0.2 collective-permute-start.11
  47.7 0.7 slice_bitcast_fusion.6
  48.5 0.7 slice_bitcast_fusion.4
  49.2 0.7 slice_bitcast_fusion.2
  49.9 0.7 slice_bitcast_fusion
  50.7 0.1 concatenate.50
  50.9 0.7 add.313.row_ref
  51.7 3.5 %cosine_convert_fusion = (bf16[1,256,768]{2,1,0:T(8,128)(2,1)S(1)}, bf16[1,256,768]{2,1,0:T(8,128)(2,1)S(1)}) fusion(s32[768]{0:T(1024)S(1)} %add.309.col_ref, s32[256]{0:T(256)S(1)} %iota_add_fusion.1), kind=kLoop, calls=%fused_computation.10 | loop fusion | flops 3145728 | bytes 790528 | tf_op jit(solution)/shard_map/convert
  55.2 1.0 pad_maximum_fusion.refs_17_
  56.2 0.3 collective-permute-start.10
  56.5 3.3 %collective-permute-done.10 = bf16[24,16,128]{2,1,0:T(8,128)(2,1)S(1)} collective-permute-done((bf16[24,16,128]{2,1,0:T(8,128)(2,1)}, bf16[24,16,128]{2,1,0:T(8,128)(2,1)S(1)}, u32[]{:S(2)}, u32[]{:S(2)}) %collective-permute-start.10) | collective-permute-done | bytes 98336 | tf_op jit(solution)/shard_map/ppermute | solution.py:663
  59.9 2.9 %collective-permute-start.20 = (bf16[72,16,128]{2,1,0:T(8,128)(2,1)S(1)}, bf16[72,16,128]{2,1,0:T(8,128)(2,1)S(1)}, u32[]{:S(2)}, u32[]{:S(2)}) collective-permute-start(bf16[72,16,128]{2,1,0:T(8,128)(2,1)S(1)} %pad_maximum_fusion.1), channel_id=1, source_target_pairs={{0,1},{1,0},{2,3},{3,2},{4,5},{5,4},{6,7},{7,6},{8,9},{9,8},{10,11... | collective-permute-start | bytes 884744 | tf_op jit(solution)/shard_map/ppermute | solution.py:663
  62.8 1.2 collective-permute-start.18
  64.0 0.2 collective-permute-start.17
  64.2 1.2 collective-permute-start.16
  65.4 0.8 collective-permute-start.19
  66.3 1.2 collective-permute-done.19
  67.4 0.6 copy-done.3
  68.1 0.2 copy-done.1
  68.2 11.5 %uv_tile.1.refs_22_ = f32[32768,128]{1,0:T(8,128)} custom-call(s32[3]{0:T(128)} %get-tuple-element.52.info_ref, s32[768]{0:T(1024)} %add.313.row_ref, s32[768]{0:T(1024)} %copy-done.23, bf16[384,128]{1,0:T(8,128)(2,1)} %bitcast.138, bf16[1152,128]{1,0:T(8,128)(2,1)} %bitcast.131, bf16[384,128]{1,0:T(8,128)(2,1)} %bitcast.141, bf16[1152,128]{1,0:T(8,128)(2,1)} %bitcast.133), custom_call_target="tpu_custom_call" | custom-call | bytes 41943040 | tf_op jit(solution)/shard_map/uv_tile/pallas_call | solution.py:309
  79.8 4.7 %collective-permute-start.22 = (bf16[72,16,128]{2,1,0:T(8,128)(2,1)S(1)}, bf16[72,16,128]{2,1,0:T(8,128)(2,1)S(1)}, u32[]{:S(2)}, u32[]{:S(2)}) collective-permute-start(bf16[72,16,128]{2,1,0:T(8,128)(2,1)S(1)} %collective-permute-done.16), channel_id=1, source_target_pairs={{0,1},{1,0},{2,3},{3,2},{4,5},{5,4},{6,7},{7,6},{8,9},{9,8},{10,11... | collective-permute-start | bytes 884744 | tf_op jit(solution)/shard_map/ppermute | solution.py:663
  84.5 0.4 collective-permute-start.26
  85.0 0.4 collective-permute-start.23
  85.5 1.2 collective-permute-done.21
  86.6 0.4 collective-permute-start.25
  87.0 0.6 reshape.728.refs_16_
  87.6 0.8 copy.21.refs_18_
  88.6 0.5 copy-done.21
  89.1 0.1 copy-done.14
  89.2 0.1 copy-done.15
  89.4 34.6 %image.1 = (f32[32768,128]{1,0:T(8,128)}, f32[32768,128]{1,0:T(8,128)}) custom-call(s32[3]{0:T(128)} %get-tuple-element.48.info_ref, s32[768]{0:T(1024)} %add.313.row_ref, s32[768]{0:T(1024)} %copy-done.23, bf16[384,128]{1,0:T(8,128)(2,1)} %bitcast.139, bf16[1152,128]{1,0:T(8,128)(2,1)} %bitcast.132, ...), custom_call_target="tpu_custom_call", output_to_operand_aliasing={{1}: (25, {})} | custom-call | tf_op jit(solution)/shard_map/image/pallas_call | solution.py:574
  (104 shorter events, 1.2 us)
Async XLA Ops:
  3.0 9.5 %collective-permute-start.2 = (bf16[17,16,128]{2,1,0:T(8,128)(2,1)S(1)}, bf16[17,16,128]{2,1,0:T(8,128)(2,1)S(1)}, u32[]{:S(2)}, u32[]{:S(2)}) collective-permute-start(bf16[17,16,128]{2,1,0:T(8,128)(2,1)S(1)} %pad_maximum_fusion.2), channel_id=1, source_target_pairs={{0,6},{1,7},{2,4},{3,5},{4,2},{5,3},{6,0},{7,1},{8,14},{9,15},{10,... | collective-permute-start | bytes 208904 | tf_op jit(solution)/shard_map/ppermute | solution.py:663
  3.1 9.4 %collective-permute-start.1 = (bf16[17,16,128]{2,1,0:T(8,128)(2,1)S(1)}, bf16[17,16,128]{2,1,0:T(8,128)(2,1)S(1)}, u32[]{:S(2)}, u32[]{:S(2)}) collective-permute-start(bf16[17,16,128]{2,1,0:T(8,128)(2,1)S(1)} %pad_maximum_fusion.2), channel_id=1, source_target_pairs={{0,4},{1,5},{2,6},{3,7},{4,0},{5,1},{6,2},{7,3},{8,12},{9,13},{10,... | collective-permute-start | bytes 208904 | tf_op jit(solution)/shard_map/ppermute | solution.py:663
  4.4 8.0 %collective-permute-start = (bf16[17,16,128]{2,1,0:T(8,128)(2,1)S(1)}, bf16[17,16,128]{2,1,0:T(8,128)(2,1)S(1)}, u32[]{:S(2)}, u32[]{:S(2)}) collective-permute-start(bf16[17,16,128]{2,1,0:T(8,128)(2,1)S(1)} %pad_maximum_fusion.2), channel_id=1, source_target_pairs={{0,2},{1,3},{2,0},{3,1},{4,6},{5,7},{6,4},{7,5},{8,10},{9,11},{10,... | collective-permute-start | bytes 208904 | tf_op jit(solution)/shard_map/ppermute | solution.py:663
  12.5 21.1 %copy-start.2 = (bf16[68,16,128]{2,1,0:T(8,128)(2,1)}, bf16[68,16,128]{2,1,0:T(8,128)(2,1)S(1)}, u32[]{:S(2)}) copy-start(bf16[68,16,128]{2,1,0:T(8,128)(2,1)S(1)} %constant_dynamic-update-slice_fusion.refs_0_) | copy-start | bytes 835588
  12.6 16.2 %collective-permute-start.5 = (bf16[68,16,128]{2,1,0:T(8,128)(2,1)S(1)}, bf16[68,16,128]{2,1,0:T(8,128)(2,1)S(1)}, u32[]{:S(2)}, u32[]{:S(2)}) collective-permute-start(bf16[68,16,128]{2,1,0:T(8,128)(2,1)S(1)} %constant_dynamic-update-slice_fusion.refs_0_), channel_id=1, source_target_pairs={{0,24},{8,16},{16,8},{24,0},{1,25},{9,17},{17,9},{25,1},{2,26},{10... | collective-permute-start | bytes 835592 | tf_op jit(solution)/shard_map/ppermute | solution.py:663
  14.8 14.0 %collective-permute-start.4 = (bf16[68,16,128]{2,1,0:T(8,128)(2,1)S(1)}, bf16[68,16,128]{2,1,0:T(8,128)(2,1)S(1)}, u32[]{:S(2)}, u32[]{:S(2)}) collective-permute-start(bf16[68,16,128]{2,1,0:T(8,128)(2,1)S(1)} %constant_dynamic-update-slice_fusion.refs_0_), channel_id=1, source_target_pairs={{0,16},{8,24},{16,0},{24,8},{1,17},{9,25},{17,1},{25,9},{2,18},{10... | collective-permute-start | bytes 835592 | tf_op jit(solution)/shard_map/ppermute | solution.py:663
  15.0 13.8 %collective-permute-start.3 = (bf16[68,16,128]{2,1,0:T(8,128)(2,1)S(1)}, bf16[68,16,128]{2,1,0:T(8,128)(2,1)S(1)}, u32[]{:S(2)}, u32[]{:S(2)}) collective-permute-start(bf16[68,16,128]{2,1,0:T(8,128)(2,1)S(1)} %constant_dynamic-update-slice_fusion.refs_0_), channel_id=1, source_target_pairs={{0,8},{8,0},{16,24},{24,16},{1,9},{9,1},{17,25},{25,17},{2,10},{10... | collective-permute-start | bytes 835592 | tf_op jit(solution)/shard_map/ppermute | solution.py:663
  28.8 4.9 %copy-start.4 = (bf16[68,16,128]{2,1,0:T(8,128)(2,1)}, bf16[68,16,128]{2,1,0:T(8,128)(2,1)S(1)}, u32[]{:S(2)}) copy-start(bf16[68,16,128]{2,1,0:T(8,128)(2,1)S(1)} %collective-permute-done.5.refs_6_) | copy-start | bytes 835588
  28.8 4.9 %copy-start.6 = (bf16[68,16,128]{2,1,0:T(8,128)(2,1)}, bf16[68,16,128]{2,1,0:T(8,128)(2,1)S(1)}, u32[]{:S(2)}) copy-start(bf16[68,16,128]{2,1,0:T(8,128)(2,1)S(1)} %collective-permute-done.4.refs_4_) | copy-start | bytes 835588
  28.8 4.9 %copy-start.7 = (bf16[68,16,128]{2,1,0:T(8,128)(2,1)}, bf16[68,16,128]{2,1,0:T(8,128)(2,1)S(1)}, u32[]{:S(2)}) copy-start(bf16[68,16,128]{2,1,0:T(8,128)(2,1)S(1)} %collective-permute-done.3.refs_2_) | copy-start | bytes 835588
  28.8 4.8 %collective-permute-start.9 = (bf16[68,16,128]{2,1,0:T(8,128)(2,1)S(1)}, bf16[68,16,128]{2,1,0:T(8,128)(2,1)S(1)}, u32[]{:S(2)}, u32[]{:S(2)}) collective-permute-start(bf16[68,16,128]{2,1,0:T(8,128)(2,1)S(1)} %collective-permute-done.5.refs_6_), channel_id=1, source_target_pairs={{0,1},{1,0},{2,3},{3,2},{4,5},{5,4},{6,7},{7,6},{8,9},{9,8},{10,11... | collective-permute-start | bytes 835592 | tf_op jit(solution)/shard_map/ppermute | solution.py:663
  31.2 2.4 %collective-permute-start.8 = (bf16[68,16,128]{2,1,0:T(8,128)(2,1)S(1)}, bf16[68,16,128]{2,1,0:T(8,128)(2,1)S(1)}, u32[]{:S(2)}, u32[]{:S(2)}) collective-permute-start(bf16[68,16,128]{2,1,0:T(8,128)(2,1)S(1)} %collective-permute-done.4.refs_4_), channel_id=1, source_target_pairs={{0,1},{1,0},{2,3},{3,2},{4,5},{5,4},{6,7},{7,6},{8,9},{9,8},{10,11... | collective-permute-start | bytes 835592 | tf_op jit(solution)/shard_map/ppermute | solution.py:663
  31.3 1.9 %collective-permute-start.6 = (bf16[68,16,128]{2,1,0:T(8,128)(2,1)S(1)}, bf16[68,16,128]{2,1,0:T(8,128)(2,1)S(1)}, u32[]{:S(2)}, u32[]{:S(2)}) collective-permute-start(bf16[68,16,128]{2,1,0:T(8,128)(2,1)S(1)} %constant_dynamic-update-slice_fusion.refs_0_), channel_id=1, source_target_pairs={{0,1},{1,0},{2,3},{3,2},{4,5},{5,4},{6,7},{7,6},{8,9},{9,8},{10,11... | collective-permute-start | bytes 835592 | tf_op jit(solution)/shard_map/ppermute | solution.py:663
  31.7 1.9 %collective-permute-start.7 = (bf16[68,16,128]{2,1,0:T(8,128)(2,1)S(1)}, bf16[68,16,128]{2,1,0:T(8,128)(2,1)S(1)}, u32[]{:S(2)}, u32[]{:S(2)}) collective-permute-start(bf16[68,16,128]{2,1,0:T(8,128)(2,1)S(1)} %collective-permute-done.3.refs_2_), channel_id=1, source_target_pairs={{0,1},{1,0},{2,3},{3,2},{4,5},{5,4},{6,7},{7,6},{8,9},{9,8},{10,11... | collective-permute-start | bytes 835592 | tf_op jit(solution)/shard_map/ppermute | solution.py:663
  33.2 0.7 copy-start.9
  33.6 0.7 copy-start.10
  33.6 0.8 copy-start.8
  34.4 0.7 copy-start.5
  41.8 14.4 %collective-permute-start.15 = (bf16[24,16,128]{2,1,0:T(8,128)(2,1)}, bf16[24,16,128]{2,1,0:T(8,128)(2,1)S(1)}, u32[]{:S(2)}, u32[]{:S(2)}) collective-permute-start(bf16[24,16,128]{2,1,0:T(8,128)(2,1)} %correct.1), channel_id=1, source_target_pairs={{0,6},{1,7},{2,4},{3,5},{4,2},{5,3},{6,0},{7,1},{8,14},{9,15},{10,... | collective-permute-start | bytes 294920 | tf_op jit(solution)/shard_map/ppermute | solution.py:663
  41.8 14.6 %collective-permute-start.14 = (bf16[24,16,128]{2,1,0:T(8,128)(2,1)}, bf16[24,16,128]{2,1,0:T(8,128)(2,1)S(1)}, u32[]{:S(2)}, u32[]{:S(2)}) collective-permute-start(bf16[24,16,128]{2,1,0:T(8,128)(2,1)} %correct.1), channel_id=1, source_target_pairs={{0,4},{1,5},{2,6},{3,7},{4,0},{5,1},{6,2},{7,3},{8,12},{9,13},{10,... | collective-permute-start | bytes 294920 | tf_op jit(solution)/shard_map/ppermute | solution.py:663
  42.7 13.7 %collective-permute-start.13 = (bf16[24,16,128]{2,1,0:T(8,128)(2,1)}, bf16[24,16,128]{2,1,0:T(8,128)(2,1)S(1)}, u32[]{:S(2)}, u32[]{:S(2)}) collective-permute-start(bf16[24,16,128]{2,1,0:T(8,128)(2,1)} %correct.1), channel_id=1, source_target_pairs={{0,2},{1,3},{2,0},{3,1},{4,6},{5,7},{6,4},{7,5},{8,10},{9,11},{10,... | collective-permute-start | bytes 294920 | tf_op jit(solution)/shard_map/ppermute | solution.py:663
  45.3 11.1 %collective-permute-start.12 = (bf16[24,16,128]{2,1,0:T(8,128)(2,1)}, bf16[24,16,128]{2,1,0:T(8,128)(2,1)S(1)}, u32[]{:S(2)}, u32[]{:S(2)}) collective-permute-start(bf16[24,16,128]{2,1,0:T(8,128)(2,1)} %correct.1), channel_id=1, source_target_pairs={{0,24},{8,16},{16,8},{24,0},{1,25},{9,17},{17,9},{25,1},{2,26},{10... | collective-permute-start | bytes 294920 | tf_op jit(solution)/shard_map/ppermute | solution.py:663
  47.5 9.0 %collective-permute-start.11 = (bf16[24,16,128]{2,1,0:T(8,128)(2,1)}, bf16[24,16,128]{2,1,0:T(8,128)(2,1)S(1)}, u32[]{:S(2)}, u32[]{:S(2)}) collective-permute-start(bf16[24,16,128]{2,1,0:T(8,128)(2,1)} %correct.1), channel_id=1, source_target_pairs={{0,16},{8,24},{16,0},{24,8},{1,17},{9,25},{17,1},{25,9},{2,18},{10... | collective-permute-start | bytes 294920 | tf_op jit(solution)/shard_map/ppermute | solution.py:663
  51.6 35.4 %copy-start.24 = (s32[768]{0:T(1024)S(1)}, s32[768]{0:T(1024)}, u32[]{:S(2)}) copy-start(s32[768]{0:T(1024)} %add.313.row_ref) | copy-start | bytes 9220
  51.7 15.7 %copy-start.23 = (s32[768]{0:T(1024)}, s32[768]{0:T(1024)S(1)}, u32[]{:S(2)}) copy-start(s32[768]{0:T(1024)S(1)} %add.309.col_ref) | copy-start | bytes 9220
  56.2 3.7 %collective-permute-start.10 = (bf16[24,16,128]{2,1,0:T(8,128)(2,1)}, bf16[24,16,128]{2,1,0:T(8,128)(2,1)S(1)}, u32[]{:S(2)}, u32[]{:S(2)}) collective-permute-start(bf16[24,16,128]{2,1,0:T(8,128)(2,1)} %correct.1), channel_id=1, source_target_pairs={{0,8},{8,0},{16,24},{24,16},{1,9},{9,1},{17,25},{25,17},{2,10},{10... | collective-permute-start | bytes 294920 | tf_op jit(solution)/shard_map/ppermute | solution.py:663
  56.5 11.0 %copy-start = (bf16[72,16,128]{2,1,0:T(8,128)(2,1)}, bf16[72,16,128]{2,1,0:T(8,128)(2,1)S(1)}, u32[]{:S(2)}) copy-start(bf16[72,16,128]{2,1,0:T(8,128)(2,1)S(1)} %pad_maximum_fusion.1) | copy-start | bytes 884740
  56.5 32.0 %copy-start.17 = (bf16[24,16,128]{2,1,0:T(8,128)(2,1)}, bf16[24,16,128]{2,1,0:T(8,128)(2,1)S(1)}, u32[]{:S(2)}) copy-start(bf16[24,16,128]{2,1,0:T(8,128)(2,1)S(1)} %collective-permute-done.12) | copy-start | bytes 294916
  56.5 32.0 %copy-start.18 = (bf16[24,16,128]{2,1,0:T(8,128)(2,1)}, bf16[24,16,128]{2,1,0:T(8,128)(2,1)S(1)}, u32[]{:S(2)}) copy-start(bf16[24,16,128]{2,1,0:T(8,128)(2,1)S(1)} %collective-permute-done.11) | copy-start | bytes 294916
  59.9 28.7 %copy-start.19 = (bf16[24,16,128]{2,1,0:T(8,128)(2,1)}, bf16[24,16,128]{2,1,0:T(8,128)(2,1)S(1)}, u32[]{:S(2)}) copy-start(bf16[24,16,128]{2,1,0:T(8,128)(2,1)S(1)} %collective-permute-done.10) | copy-start | bytes 294916
  59.9 7.6 %collective-permute-start.20 = (bf16[72,16,128]{2,1,0:T(8,128)(2,1)S(1)}, bf16[72,16,128]{2,1,0:T(8,128)(2,1)S(1)}, u32[]{:S(2)}, u32[]{:S(2)}) collective-permute-start(bf16[72,16,128]{2,1,0:T(8,128)(2,1)S(1)} %pad_maximum_fusion.1), channel_id=1, source_target_pairs={{0,1},{1,0},{2,3},{3,2},{4,5},{5,4},{6,7},{7,6},{8,9},{9,8},{10,11... | collective-permute-start | bytes 884744 | tf_op jit(solution)/shard_map/ppermute | solution.py:663
  62.8 16.9 %collective-permute-start.18 = (bf16[72,16,128]{2,1,0:T(8,128)(2,1)S(1)}, bf16[72,16,128]{2,1,0:T(8,128)(2,1)S(1)}, u32[]{:S(2)}, u32[]{:S(2)}) collective-permute-start(bf16[72,16,128]{2,1,0:T(8,128)(2,1)S(1)} %pad_maximum_fusion.1), channel_id=1, source_target_pairs={{0,24},{8,16},{16,8},{24,0},{1,25},{9,17},{17,9},{25,1},{2,26},{10... | collective-permute-start | bytes 884744 | tf_op jit(solution)/shard_map/ppermute | solution.py:663
  64.0 15.8 %collective-permute-start.17 = (bf16[72,16,128]{2,1,0:T(8,128)(2,1)S(1)}, bf16[72,16,128]{2,1,0:T(8,128)(2,1)S(1)}, u32[]{:S(2)}, u32[]{:S(2)}) collective-permute-start(bf16[72,16,128]{2,1,0:T(8,128)(2,1)S(1)} %pad_maximum_fusion.1), channel_id=1, source_target_pairs={{0,16},{8,24},{16,0},{24,8},{1,17},{9,25},{17,1},{25,9},{2,18},{10... | collective-permute-start | bytes 884744 | tf_op jit(solution)/shard_map/ppermute | solution.py:663
  64.2 15.5 %collective-permute-start.16 = (bf16[72,16,128]{2,1,0:T(8,128)(2,1)S(1)}, bf16[72,16,128]{2,1,0:T(8,128)(2,1)S(1)}, u32[]{:S(2)}, u32[]{:S(2)}) collective-permute-start(bf16[72,16,128]{2,1,0:T(8,128)(2,1)S(1)} %pad_maximum_fusion.1), channel_id=1, source_target_pairs={{0,8},{8,0},{16,24},{24,16},{1,9},{9,1},{17,25},{25,17},{2,10},{10... | collective-permute-start | bytes 884744 | tf_op jit(solution)/shard_map/ppermute | solution.py:663
  65.4 2.0 %collective-permute-start.19 = (bf16[24,16,128]{2,1,0:T(8,128)(2,1)}, bf16[24,16,128]{2,1,0:T(8,128)(2,1)S(1)}, u32[]{:S(2)}, u32[]{:S(2)}) collective-permute-start(bf16[24,16,128]{2,1,0:T(8,128)(2,1)} %correct.1), channel_id=1, source_target_pairs={{0,1},{1,0},{2,3},{3,2},{4,5},{5,4},{6,7},{7,6},{8,9},{9,8},{10,11... | collective-permute-start | bytes 294920 | tf_op jit(solution)/shard_map/ppermute | solution.py:663
  67.4 0.6 copy-start.3
  67.4 0.8 copy-start.1
  79.7 8.8 %copy-start.11 = (bf16[72,16,128]{2,1,0:T(8,128)(2,1)}, bf16[72,16,128]{2,1,0:T(8,128)(2,1)S(1)}, u32[]{:S(2)}) copy-start(bf16[72,16,128]{2,1,0:T(8,128)(2,1)S(1)} %collective-permute-done.18) | copy-start | bytes 884740
  79.7 8.8 %copy-start.12 = (bf16[72,16,128]{2,1,0:T(8,128)(2,1)}, bf16[72,16,128]{2,1,0:T(8,128)(2,1)S(1)}, u32[]{:S(2)}) copy-start(bf16[72,16,128]{2,1,0:T(8,128)(2,1)S(1)} %collective-permute-done.17) | copy-start | bytes 884740
  79.8 8.8 %copy-start.13 = (bf16[72,16,128]{2,1,0:T(8,128)(2,1)}, bf16[72,16,128]{2,1,0:T(8,128)(2,1)S(1)}, u32[]{:S(2)}) copy-start(bf16[72,16,128]{2,1,0:T(8,128)(2,1)S(1)} %collective-permute-done.16) | copy-start | bytes 884740
  79.8 8.7 %collective-permute-start.22 = (bf16[72,16,128]{2,1,0:T(8,128)(2,1)S(1)}, bf16[72,16,128]{2,1,0:T(8,128)(2,1)S(1)}, u32[]{:S(2)}, u32[]{:S(2)}) collective-permute-start(bf16[72,16,128]{2,1,0:T(8,128)(2,1)S(1)} %collective-permute-done.16), channel_id=1, source_target_pairs={{0,1},{1,0},{2,3},{3,2},{4,5},{5,4},{6,7},{7,6},{8,9},{9,8},{10,11... | collective-permute-start | bytes 884744 | tf_op jit(solution)/shard_map/ppermute | solution.py:663
  84.5 4.0 %collective-permute-start.24 = (bf16[72,16,128]{2,1,0:T(8,128)(2,1)S(1)}, bf16[72,16,128]{2,1,0:T(8,128)(2,1)S(1)}, u32[]{:S(2)}, u32[]{:S(2)}) collective-permute-start(bf16[72,16,128]{2,1,0:T(8,128)(2,1)S(1)} %collective-permute-done.17), channel_id=1, source_target_pairs={{0,1},{1,0},{2,3},{3,2},{4,5},{5,4},{6,7},{7,6},{8,9},{9,8},{10,11... | collective-permute-start | bytes 884744 | tf_op jit(solution)/shard_map/ppermute | solution.py:663
  84.5 4.0 %collective-permute-start.26 = (bf16[72,16,128]{2,1,0:T(8,128)(2,1)S(1)}, bf16[72,16,128]{2,1,0:T(8,128)(2,1)S(1)}, u32[]{:S(2)}, u32[]{:S(2)}) collective-permute-start(bf16[72,16,128]{2,1,0:T(8,128)(2,1)S(1)} %collective-permute-done.18), channel_id=1, source_target_pairs={{0,1},{1,0},{2,3},{3,2},{4,5},{5,4},{6,7},{7,6},{8,9},{9,8},{10,11... | collective-permute-start | bytes 884744 | tf_op jit(solution)/shard_map/ppermute | solution.py:663
  85.0 1.7 %collective-permute-start.21 = (bf16[24,16,128]{2,1,0:T(8,128)(2,1)S(1)}, bf16[24,16,128]{2,1,0:T(8,128)(2,1)S(1)}, u32[]{:S(2)}, u32[]{:S(2)}) collective-permute-start(bf16[24,16,128]{2,1,0:T(8,128)(2,1)S(1)} %collective-permute-done.10), channel_id=1, source_target_pairs={{0,1},{1,0},{2,3},{3,2},{4,5},{5,4},{6,7},{7,6},{8,9},{9,8},{10,11... | collective-permute-start | bytes 294920 | tf_op jit(solution)/shard_map/ppermute | solution.py:663
  85.0 3.4 %collective-permute-start.23 = (bf16[24,16,128]{2,1,0:T(8,128)(2,1)S(1)}, bf16[24,16,128]{2,1,0:T(8,128)(2,1)S(1)}, u32[]{:S(2)}, u32[]{:S(2)}) collective-permute-start(bf16[24,16,128]{2,1,0:T(8,128)(2,1)S(1)} %collective-permute-done.11), channel_id=1, source_target_pairs={{0,1},{1,0},{2,3},{3,2},{4,5},{5,4},{6,7},{7,6},{8,9},{9,8},{10,11... | collective-permute-start | bytes 294920 | tf_op jit(solution)/shard_map/ppermute | solution.py:663
  86.6 1.9 %copy-start.20 = (bf16[24,16,128]{2,1,0:T(8,128)(2,1)}, bf16[24,16,128]{2,1,0:T(8,128)(2,1)S(1)}, u32[]{:S(2)}) copy-start(bf16[24,16,128]{2,1,0:T(8,128)(2,1)S(1)} %collective-permute-done.21) | copy-start | bytes 294916
  86.6 1.8 %collective-permute-start.25 = (bf16[24,16,128]{2,1,0:T(8,128)(2,1)S(1)}, bf16[24,16,128]{2,1,0:T(8,128)(2,1)S(1)}, u32[]{:S(2)}, u32[]{:S(2)}) collective-permute-start(bf16[24,16,128]{2,1,0:T(8,128)(2,1)S(1)} %collective-permute-done.12), channel_id=1, source_target_pairs={{0,1},{1,0},{2,3},{3,2},{4,5},{5,4},{6,7},{7,6},{8,9},{9,8},{10,11... | collective-permute-start | bytes 294920 | tf_op jit(solution)/shard_map/ppermute | solution.py:663
  88.4 0.6 copy-start.21
  88.4 0.7 copy-start.22
  88.5 0.8 copy-start.14
  88.5 0.9 copy-start.15
  88.5 0.9 copy-start.16

commit v7 on v6

--- a/solution.py
+++ b/solution.py
@@ -396,28 +396,32 @@
     size = uv_rows.shape[1]
     image_rows = phase_ref.shape[1]
 
-    def products(pair, h, left):
+    def products(pair, h, left, start, width):
         at = pl.ds(2 * image_rows * h, 2 * image_rows)
+        items = pl.ds(start, width)
         spread = lax.dot_general(
-            columns_ref[at, :], uv_rows[pair], (((1,), (1,)), ((), ())), preferred_element_type=f32
+            columns_ref[at, :], uv_rows[pair, items, :], (((1,), (1,)), ((), ())),
+            preferred_element_type=f32,
         ).astype(bf16)
-        turned = cmul((spread[:image_rows], spread[image_rows:]), (phase_ref[0], phase_ref[1]))
-        left[h, :image_rows] = turned[0]
-        left[h, image_rows:] = turned[1]
-
-    def sums(pair, h, left, first):
-        index = pair + HALF * h
+        turned = cmul(
+            (spread[:image_rows], spread[image_rows:]), (phase_ref[0, :, items], phase_ref[1, :, items])
+        )
+        left[h, :image_rows, items] = turned[0]
+        left[h, image_rows:, items] = turned[1]
+
+    def table_of(index):
         late = shifts[...] > index.astype(f32)
-        table = jnp.concatenate(
+        return jnp.concatenate(
             [
                 jnp.where(late, after[:, t : t + LANES], here[:, t : t + LANES])
                 for t in range(0, FINE, LANES)
             ],
             axis=1,
         )
-        four = jnp.dot(left[h], table, preferred_element_type=f32)
-        even_re, odd_re = four[:image_rows, :LOW], four[:image_rows, LOW:]
-        even_im, odd_im = four[image_rows:, :LOW], four[image_rows:, LOW:]
+
+    def keep_sums(index, real, image, first):
+        even_re, odd_re = real[:, :LOW], real[:, LOW:]
+        even_im, odd_im = image[:, :LOW], image[:, LOW:]
         edge = lax.broadcasted_iota(jnp.int32, (image_rows, LOW), 1) == 0
         low = (
             even_re - jnp.where(edge, 0.0, odd_im),
@@ -437,6 +441,22 @@
                 at = (index, part, slice(None), pl.ds(LOW * half, LOW))
                 total[at] = done[part] if first else total[at] + done[part]
 
+    third = size // 3 if size % (3 * LANES) == 0 else size
+
+    def products_and_sums(later, left_later, pair, left, first):
+        for h in range(2):
+            starts = list(range(0, size, third))
+            index = pair + HALF * h
+            products(later, h, left_later, starts[0], third)
+            table = table_of(index)
+            real = jnp.dot(left[h, :image_rows], table, preferred_element_type=f32)
+            for start in starts[1:2]:
+                products(later, h, left_later, start, third)
+            image = jnp.dot(left[h, image_rows:], table, preferred_element_type=f32)
+            for start in starts[2:]:
+                products(later, h, left_later, start, third)
+            keep_sums(index, real, image, first)
+
     def chunk(first):
         if first:
             head.start()
@@ -469,15 +489,13 @@
         after[...] = looked_up(lax.rem(coarse + 1, FINE), FINE, unit_ref[...]).astype(bf16)
         shifts[...] = looked_up(shift, SUB, count_ref[...])
         for h in range(2):
-            products(0, h, left_even)
+            products(0, h, left_even, 0, size)
 
         def two_pairs(i, carry):
-            for h in range(2):
-                products(2 * i + 1, h, left_odd)
-                sums(2 * i, h, left_even, first)
-            for h in range(2):
-                products(jnp.minimum(2 * i + 2, HALF - 1), h, left_even)
-                sums(2 * i + 1, h, left_odd, first)
+            products_and_sums(2 * i + 1, left_odd, 2 * i, left_even, first)
+            products_and_sums(
+                jnp.minimum(2 * i + 2, HALF - 1), left_even, 2 * i + 1, left_odd, first
+            )
             return carry
 
         lax.fori_loop(0, HALF // 2, two_pairs, 0)
@@ -663,10 +681,10 @@
     return lax.ppermute(value, axis, [(i, i ^ mask) for i in range(count)])
 
 
-def z_line(own, with_own):
+def z_line(own):
     vert_count = lax.axis_size("vert")
-    line = [from_partner(own, "vert", 2 * mask) for mask in range(1, vert_count // 2)]
-    return jnp.concatenate([own] * with_own + line, axis=0)
+    line = [own] + [from_partner(own, "vert", 2 * mask) for mask in range(1, vert_count // 2)]
+    return jnp.concatenate(line, axis=0)
 
 
 def au_lines(line):
@@ -722,7 +740,7 @@
     part = math.gcd(count, 8)
     skies = [sky_sums(visibilities, offsets, scale_row, 0, part)]
     if by_mask:
-        line = z_line(sent, True)
+        line = z_line(sent)
         line, offsets, skies[0], corners, stations, screen_depth = lax.optimization_barrier(
             (line, offsets, skies[0], corners, stations, screen_depth)
         )
@@ -755,17 +773,15 @@
     first_row = (au_index * vert_count + vert_index) * image_rows
     tables = image_tables(corners_all[1], first_row, image_rows)
     if by_mask:
-        blocks, line = au_lines(uv_own), z_line(uv_own, False)
-        blocks, line, tables, corners_all, own_info, before_info = lax.optimization_barrier(
-            (blocks, line, tables, corners_all, own_info, before_info)
+        line = z_line(uv_own)
+        line, tables, corners_all, own_info, before_info = lax.optimization_barrier(
+            (line, tables, corners_all, own_info, before_info)
         )
         lines = au_lines(line)
-        own_row = [uv_own, line] + [from_partner(piece, "vert", 1) for piece in (uv_own, line)]
+        own_row = with_core(lines[:1])
         tile = uv_tile_own(own_row, own_info, corners_all, per_row, tile_rows, tile_cols)
         lines, own_row, tile = lax.optimization_barrier((lines, own_row, tile))
-        uv = own_row
-        for pair in zip(blocks[1:], lines[1:]):
-            uv = uv + [*pair, *[from_partner(piece, "vert", 1) for piece in pair]]
+        uv = own_row + with_core(lines[1:])
     else:
         uv = whole_gather(uv_own)
         tile = uv_tile_own(uv, own_info, corners_all, per_row, tile_rows, tile_cols)

time: 125 us -> 118 us (0.944)
  the two profiles are of different devices: /device:TPU:25 before, /device:TPU:0 now
where the time goes in v7:
time: 118 us; the launch traced here: 117 us
  Pallas kernels  68.2 us (58%)
  starting transfers between devices  18.9 us (16%)
  other arithmetic  10.9 us (9%)
  local copies, waits for them, and re-layouts  10.7 us (9%)
  waiting for transfers between devices  7.33 us (6%)
  between operations  1.24 us (1%)
    pallas_call x1, Pallas kernels, image_rows_of(): pl.pallas_call(functools.partial(image_kernel, pieces=len(uv), chunks=chu...  35.7 us
    ppermute x20, starting transfers between devices, from_partner(): return lax.ppermute(value, axis, [(i, i ^ mask) for i in range(count)])  18.9 us
    pallas_call x3, Pallas kernels, sky_sums(): pl.pallas_call(sky_kernel, grid=(1,), in_specs=[pl.BlockSpec((count, 2, v...  13.8 us
    pallas_call x1, Pallas kernels, uv_tile_own(): pl.pallas_call(functools.partial(tile_kernel, pieces=len(uv), tile_rows=t...  12 us
    ppermute x20, waiting for transfers between devices, from_partner(): return lax.ppermute(value, axis, [(i, i ^ mask) for i in range(count)])  7.33 us
    pallas_call x1, Pallas kernels, corrected_subgrids(): pl.pallas_call(functools.partial(correct_kernel, pieces=len(tables), skie...  6.66 us
    unnamed x57, local copies, waits for them, and re-layouts  6.06 us
    another operation x1, other arithmetic  3.47 us
  transfers between devices with their start and end apart: 20, of which 6 were waited for; matrix products, arithmetic and copies ran while one was open for 13% of the time, Pallas kernels for 22%

profile of v7, /device:TPU:0, one launch (start us, length us, event | category | flops | bytes accessed | tf_op | source)
XLA Modules:
  0.0 117.2 jit_solution(2037185794644560441)
XLA Ops:
  0.6 0.8 and_select_fusion.14
  1.4 0.1 convert_element_type.88
  1.5 1.0 reshape.664
  2.6 0.2 copy.42
  2.8 0.2 reshape.665
  3.0 5.1 %collective-permute-start.2 = (bf16[17,16,128]{2,1,0:T(8,128)(2,1)S(1)}, bf16[17,16,128]{2,1,0:T(8,128)(2,1)S(1)}, u32[]{:S(2)}, u32[]{:S(2)}) collective-permute-start(bf16[17,16,128]{2,1,0:T(8,128)(2,1)S(1)} %pad_maximum_fusion.2), channel_id=1, source_target_pairs={{0,6},{1,7},{2,4},{3,5},{4,2},{5,3},{6,0},{7,1},{8,14},{9,15},{10,... | collective-permute-start | bytes 208904 | tf_op jit(solution)/shard_map/ppermute | solution.py:681
  8.1 0.0 collective-permute-start.1
  8.1 0.6 collective-permute-start
  8.9 0.1 fusion.18
  9.0 0.2 multiply_convert_fusion
  9.4 4.6 %sky_sums.3.refs_8_ = f32[8,16,128]{2,1,0:T(8,128)} custom-call(bf16[24,2,2048]{2,1,0:T(2,128)(2,1)} %vis_ref.5, f32[48,128]{1,0:T(8,128)} %bitcast.142, f32[1,16]{1,0:T(1,128)} %bitcast.153), custom_call_target="tpu_custom_call" | custom-call | bytes 20000000 | tf_op jit(solution)/shard_map/sky_sums/pallas_call | solution.py:119
  14.0 0.6 add_add_fusion
  14.7 2.7 %collective-permute-start.5 = (bf16[68,16,128]{2,1,0:T(8,128)(2,1)S(1)}, bf16[68,16,128]{2,1,0:T(8,128)(2,1)S(1)}, u32[]{:S(2)}, u32[]{:S(2)}) collective-permute-start(bf16[68,16,128]{2,1,0:T(8,128)(2,1)S(1)} %constant_dynamic-update-slice_fusion.refs_0_), channel_id=1, source_target_pairs={{0,24},{8,16},{16,8},{24,0},{1,25},{9,17},{17,9},{25,1},{2,26},{10... | collective-permute-start | bytes 835592 | tf_op jit(solution)/shard_map/ppermute | solution.py:681
  17.4 0.5 collective-permute-start.4
  17.9 0.4 collective-permute-start.3
  18.3 0.7 fusion.25
  19.0 0.7 and_select_fusion.2
  19.7 0.7 broadcast_multiply_fusion
  20.3 4.6 %sky_sums.5.refs_10_ = f32[8,16,128]{2,1,0:T(8,128)} custom-call(bf16[24,2,2048]{2,1,0:T(2,128)(2,1)} %vis_ref.5, f32[48,128]{1,0:T(8,128)} %bitcast.143, f32[1,16]{1,0:T(1,128)} %bitcast.154), custom_call_target="tpu_custom_call" | custom-call | bytes 20000000 | tf_op jit(solution)/shard_map/sky_sums/pallas_call | solution.py:119
  24.9 4.6 %sky_sums.4.refs_9_ = f32[8,16,128]{2,1,0:T(8,128)} custom-call(bf16[24,2,2048]{2,1,0:T(2,128)(2,1)} %vis_ref.5, f32[48,128]{1,0:T(8,128)} %bitcast.144, f32[1,16]{1,0:T(1,128)} %bitcast.155), custom_call_target="tpu_custom_call" | custom-call | bytes 20000000 | tf_op jit(solution)/shard_map/sky_sums/pallas_call | solution.py:119
  29.6 0.1 copy.20
  29.7 0.6 reshape.669.stations_ref
  30.3 1.5 %fusion.8.refs_11_ = f32[24,16,128]{2,1,0:T(8,128)} fusion(f32[16,128]{1,0:T(8,128)S(1)} %get-tuple-element.72, f32[128]{0:T(128)S(1)} %fusion.28, s32[16,128]{1,0:T(8,128)S(1)} %fusion.19, s32[24]{0:T(128)S(1)} %and_select_fusion.2, f32[16,128]{1,0:T(8,128)S(1)} %get-tuple-element.71, f32[24]{0:T(128)S(1)} %broadcast_multiply_fusion), kind=kLoop, calls=%fused_computation.24 | loop fusion | flops 884736 | bytes 221888 | tf_op jit(solution)/shard_map/mul | solution.py:676
  31.8 0.1 collective-permute-start.9
  31.9 0.5 collective-permute-start.8
  32.4 0.1 collective-permute-start.6
  32.5 0.4 collective-permute-start.7
  33.0 1.3 %collective-permute-done.6.refs_1_ = bf16[68,16,128]{2,1,0:T(8,128)(2,1)S(1)} collective-permute-done((bf16[68,16,128]{2,1,0:T(8,128)(2,1)S(1)}, bf16[68,16,128]{2,1,0:T(8,128)(2,1)S(1)}, u32[]{:S(2)}, u32[]{:S(2)}) %collective-permute-start.6) | collective-permute-done | bytes 278560 | tf_op jit(solution)/shard_map/ppermute | solution.py:681
  34.3 0.4 collective-permute-done.7.refs_3_
  34.7 0.3 copy-done.14
  35.0 0.4 copy-done.15
  35.4 0.1 copy-done.13
  35.5 0.7 copy-done.12
  36.2 6.7 %correct.1 = bf16[24,16,128]{2,1,0:T(8,128)(2,1)} custom-call(s32[48]{0:T(128)} %reshape.669.stations_ref, bf16[68,16,128]{2,1,0:T(8,128)(2,1)} %copy-done.2, bf16[68,16,128]{2,1,0:T(8,128)(2,1)} %copy-done.14, bf16[68,16,128]{2,1,0:T(8,128)(2,1)} %copy-done.11, bf16[68,16,128]{2,1,0:T(8,128)(2,1)} %copy-done.15, bf16[68,16,128]{2,1,0:T(8,128)(2,1)} %copy-done.10, ...), custom_call_target="tpu_custom_call" | custom-call | bytes 16000000 | tf_op jit(solution)/shard_map/correct/pallas_call | solution.py:194
  42.8 3.7 %collective-permute-start.12 = (bf16[24,16,128]{2,1,0:T(8,128)(2,1)}, bf16[24,16,128]{2,1,0:T(8,128)(2,1)S(1)}, u32[]{:S(2)}, u32[]{:S(2)}) collective-permute-start(bf16[24,16,128]{2,1,0:T(8,128)(2,1)} %correct.1), channel_id=1, source_target_pairs={{0,6},{1,7},{2,4},{3,5},{4,2},{5,3},{6,0},{7,1},{8,14},{9,15},{10,... | collective-permute-start | bytes 294920 | tf_op jit(solution)/shard_map/ppermute | solution.py:681
  46.6 0.6 collective-permute-start.10
  47.2 0.7 slice_bitcast_fusion.6
  48.0 0.7 slice_bitcast_fusion.4
  48.7 0.7 slice_bitcast_fusion.2
  49.4 0.7 slice_bitcast_fusion
  50.2 0.1 concatenate.50
  50.3 0.1 slice_add_fusion
  50.4 0.7 add.313.row_ref
  51.1 0.1 add.309.col_ref
  51.2 3.5 %cosine_convert_fusion = (bf16[1,256,768]{2,1,0:T(8,128)(2,1)S(1)}, bf16[1,256,768]{2,1,0:T(8,128)(2,1)S(1)}) fusion(s32[768]{0:T(1024)S(1)} %add.309.col_ref, s32[256]{0:T(256)S(1)} %iota_add_fusion.1), kind=kLoop, calls=%fused_computation.10 | loop fusion | flops 3145728 | bytes 790528 | tf_op jit(solution)/shard_map/convert
  54.7 1.0 pad_maximum_fusion.refs_9_
  55.7 0.9 pad_maximum_fusion.1
  56.6 0.1 collective-permute-start.16
  56.7 2.7 %collective-permute-start.15 = (bf16[96,16,128]{2,1,0:T(8,128)(2,1)S(1)}, bf16[96,16,128]{2,1,0:T(8,128)(2,1)S(1)}, u32[]{:S(2)}, u32[]{:S(2)}) collective-permute-start(bf16[96,16,128]{2,1,0:T(8,128)(2,1)S(1)} %pad_maximum_fusion.1), channel_id=1, source_target_pairs={{0,24},{8,16},{16,8},{24,0},{1,25},{9,17},{17,9},{25,1},{2,26},{10... | collective-permute-start | bytes 1179656 | tf_op jit(solution)/shard_map/ppermute | solution.py:681
  59.4 0.5 collective-permute-start.14
  59.9 0.4 collective-permute-start.13
  60.3 0.7 copy-done.1
  61.0 12.0 %uv_tile.1.refs_14_ = f32[32768,128]{1,0:T(8,128)} custom-call(s32[3]{0:T(128)} %get-tuple-element.47.info_ref, s32[768]{0:T(1024)} %add.313.row_ref, s32[768]{0:T(1024)} %copy-done.16, bf16[1536,128]{1,0:T(8,128)(2,1)} %bitcast.121, bf16[1536,128]{1,0:T(8,128)(2,1)} %bitcast.123), custom_call_target="tpu_custom_call" | custom-call | bytes 41943040 | tf_op jit(solution)/shard_map/uv_tile/pallas_call | solution.py:309
  73.0 4.5 %collective-permute-done.14 = bf16[96,16,128]{2,1,0:T(8,128)(2,1)S(1)} collective-permute-done((bf16[96,16,128]{2,1,0:T(8,128)(2,1)S(1)}, bf16[96,16,128]{2,1,0:T(8,128)(2,1)S(1)}, u32[]{:S(2)}, u32[]{:S(2)}) %collective-permute-start.14) | collective-permute-done | bytes 393248 | tf_op jit(solution)/shard_map/ppermute | solution.py:681
  77.6 0.2 collective-permute-done.13
  77.8 0.5 collective-permute-start.18
  78.3 0.0 collective-permute-start.19
  78.3 0.6 reshape.688.refs_8_
  78.9 0.9 copy.21.refs_10_
  79.8 0.3 collective-permute-done.18
  80.1 0.6 collective-permute-done.19
  80.7 0.2 copy-done.7
  80.8 0.6 copy-done.8
  81.4 35.7 %image.1 = (f32[32768,128]{1,0:T(8,128)}, f32[32768,128]{1,0:T(8,128)}) custom-call(s32[3]{0:T(128)} %get-tuple-element.43.info_ref, s32[768]{0:T(1024)} %add.313.row_ref, s32[768]{0:T(1024)} %copy-done.16, bf16[1536,128]{1,0:T(8,128)(2,1)} %bitcast.122, bf16[1536,128]{1,0:T(8,128)(2,1)} %bitcast.124, ...), custom_call_target="tpu_custom_call", output_to_operand_aliasing={{1}: (17, {})} | custom-call | tf_op jit(solution)/shard_map/image/pallas_call | solution.py:592
  (76 shorter events, 0.4 us)
Async XLA Ops:
  3.0 11.7 %collective-permute-start.2 = (bf16[17,16,128]{2,1,0:T(8,128)(2,1)S(1)}, bf16[17,16,128]{2,1,0:T(8,128)(2,1)S(1)}, u32[]{:S(2)}, u32[]{:S(2)}) collective-permute-start(bf16[17,16,128]{2,1,0:T(8,128)(2,1)S(1)} %pad_maximum_fusion.2), channel_id=1, source_target_pairs={{0,6},{1,7},{2,4},{3,5},{4,2},{5,3},{6,0},{7,1},{8,14},{9,15},{10,... | collective-permute-start | bytes 208904 | tf_op jit(solution)/shard_map/ppermute | solution.py:681
  8.1 6.5 %collective-permute-start.1 = (bf16[17,16,128]{2,1,0:T(8,128)(2,1)S(1)}, bf16[17,16,128]{2,1,0:T(8,128)(2,1)S(1)}, u32[]{:S(2)}, u32[]{:S(2)}) collective-permute-start(bf16[17,16,128]{2,1,0:T(8,128)(2,1)S(1)} %pad_maximum_fusion.2), channel_id=1, source_target_pairs={{0,4},{1,5},{2,6},{3,7},{4,0},{5,1},{6,2},{7,3},{8,12},{9,13},{10,... | collective-permute-start | bytes 208904 | tf_op jit(solution)/shard_map/ppermute | solution.py:681
  8.1 6.5 %collective-permute-start = (bf16[17,16,128]{2,1,0:T(8,128)(2,1)S(1)}, bf16[17,16,128]{2,1,0:T(8,128)(2,1)S(1)}, u32[]{:S(2)}, u32[]{:S(2)}) collective-permute-start(bf16[17,16,128]{2,1,0:T(8,128)(2,1)S(1)} %pad_maximum_fusion.2), channel_id=1, source_target_pairs={{0,2},{1,3},{2,0},{3,1},{4,6},{5,7},{6,4},{7,5},{8,10},{9,11},{10,... | collective-permute-start | bytes 208904 | tf_op jit(solution)/shard_map/ppermute | solution.py:681
  14.7 19.9 %copy-start.2 = (bf16[68,16,128]{2,1,0:T(8,128)(2,1)}, bf16[68,16,128]{2,1,0:T(8,128)(2,1)S(1)}, u32[]{:S(2)}) copy-start(bf16[68,16,128]{2,1,0:T(8,128)(2,1)S(1)} %constant_dynamic-update-slice_fusion.refs_0_) | copy-start | bytes 835588
  14.7 17.1 %collective-permute-start.5 = (bf16[68,16,128]{2,1,0:T(8,128)(2,1)S(1)}, bf16[68,16,128]{2,1,0:T(8,128)(2,1)S(1)}, u32[]{:S(2)}, u32[]{:S(2)}) collective-permute-start(bf16[68,16,128]{2,1,0:T(8,128)(2,1)S(1)} %constant_dynamic-update-slice_fusion.refs_0_), channel_id=1, source_target_pairs={{0,24},{8,16},{16,8},{24,0},{1,25},{9,17},{17,9},{25,1},{2,26},{10... | collective-permute-start | bytes 835592 | tf_op jit(solution)/shard_map/ppermute | solution.py:681
  17.4 14.4 %collective-permute-start.4 = (bf16[68,16,128]{2,1,0:T(8,128)(2,1)S(1)}, bf16[68,16,128]{2,1,0:T(8,128)(2,1)S(1)}, u32[]{:S(2)}, u32[]{:S(2)}) collective-permute-start(bf16[68,16,128]{2,1,0:T(8,128)(2,1)S(1)} %constant_dynamic-update-slice_fusion.refs_0_), channel_id=1, source_target_pairs={{0,16},{8,24},{16,0},{24,8},{1,17},{9,25},{17,1},{25,9},{2,18},{10... | collective-permute-start | bytes 835592 | tf_op jit(solution)/shard_map/ppermute | solution.py:681
  17.9 13.9 %collective-permute-start.3 = (bf16[68,16,128]{2,1,0:T(8,128)(2,1)S(1)}, bf16[68,16,128]{2,1,0:T(8,128)(2,1)S(1)}, u32[]{:S(2)}, u32[]{:S(2)}) collective-permute-start(bf16[68,16,128]{2,1,0:T(8,128)(2,1)S(1)} %constant_dynamic-update-slice_fusion.refs_0_), channel_id=1, source_target_pairs={{0,8},{8,0},{16,24},{24,16},{1,9},{9,1},{17,25},{25,17},{2,10},{10... | collective-permute-start | bytes 835592 | tf_op jit(solution)/shard_map/ppermute | solution.py:681
  31.8 2.9 %copy-start.9 = (bf16[68,16,128]{2,1,0:T(8,128)(2,1)}, bf16[68,16,128]{2,1,0:T(8,128)(2,1)S(1)}, u32[]{:S(2)}) copy-start(bf16[68,16,128]{2,1,0:T(8,128)(2,1)S(1)} %collective-permute-done.5.refs_6_) | copy-start | bytes 835588
  31.8 2.9 %copy-start.10 = (bf16[68,16,128]{2,1,0:T(8,128)(2,1)}, bf16[68,16,128]{2,1,0:T(8,128)(2,1)S(1)}, u32[]{:S(2)}) copy-start(bf16[68,16,128]{2,1,0:T(8,128)(2,1)S(1)} %collective-permute-done.4.refs_4_) | copy-start | bytes 835588
  31.8 2.9 %copy-start.11 = (bf16[68,16,128]{2,1,0:T(8,128)(2,1)}, bf16[68,16,128]{2,1,0:T(8,128)(2,1)S(1)}, u32[]{:S(2)}) copy-start(bf16[68,16,128]{2,1,0:T(8,128)(2,1)S(1)} %collective-permute-done.3.refs_2_) | copy-start | bytes 835588
  31.8 2.8 %collective-permute-start.9 = (bf16[68,16,128]{2,1,0:T(8,128)(2,1)S(1)}, bf16[68,16,128]{2,1,0:T(8,128)(2,1)S(1)}, u32[]{:S(2)}, u32[]{:S(2)}) collective-permute-start(bf16[68,16,128]{2,1,0:T(8,128)(2,1)S(1)} %collective-permute-done.5.refs_6_), channel_id=1, source_target_pairs={{0,1},{1,0},{2,3},{3,2},{4,5},{5,4},{6,7},{7,6},{8,9},{9,8},{10,11... | collective-permute-start | bytes 835592 | tf_op jit(solution)/shard_map/ppermute | solution.py:681
  31.9 2.7 %collective-permute-start.8 = (bf16[68,16,128]{2,1,0:T(8,128)(2,1)S(1)}, bf16[68,16,128]{2,1,0:T(8,128)(2,1)S(1)}, u32[]{:S(2)}, u32[]{:S(2)}) collective-permute-start(bf16[68,16,128]{2,1,0:T(8,128)(2,1)S(1)} %collective-permute-done.4.refs_4_), channel_id=1, source_target_pairs={{0,1},{1,0},{2,3},{3,2},{4,5},{5,4},{6,7},{7,6},{8,9},{9,8},{10,11... | collective-permute-start | bytes 835592 | tf_op jit(solution)/shard_map/ppermute | solution.py:681
  32.4 1.8 %collective-permute-start.6 = (bf16[68,16,128]{2,1,0:T(8,128)(2,1)S(1)}, bf16[68,16,128]{2,1,0:T(8,128)(2,1)S(1)}, u32[]{:S(2)}, u32[]{:S(2)}) collective-permute-start(bf16[68,16,128]{2,1,0:T(8,128)(2,1)S(1)} %constant_dynamic-update-slice_fusion.refs_0_), channel_id=1, source_target_pairs={{0,1},{1,0},{2,3},{3,2},{4,5},{5,4},{6,7},{7,6},{8,9},{9,8},{10,11... | collective-permute-start | bytes 835592 | tf_op jit(solution)/shard_map/ppermute | solution.py:681
  32.5 2.2 %collective-permute-start.7 = (bf16[68,16,128]{2,1,0:T(8,128)(2,1)S(1)}, bf16[68,16,128]{2,1,0:T(8,128)(2,1)S(1)}, u32[]{:S(2)}, u32[]{:S(2)}) collective-permute-start(bf16[68,16,128]{2,1,0:T(8,128)(2,1)S(1)} %collective-permute-done.3.refs_2_), channel_id=1, source_target_pairs={{0,1},{1,0},{2,3},{3,2},{4,5},{5,4},{6,7},{7,6},{8,9},{9,8},{10,11... | collective-permute-start | bytes 835592 | tf_op jit(solution)/shard_map/ppermute | solution.py:681
  34.3 0.7 copy-start.14
  34.7 0.7 copy-start.15
  34.7 0.8 copy-start.13
  35.5 0.7 copy-start.12
  42.8 12.8 %collective-permute-start.12 = (bf16[24,16,128]{2,1,0:T(8,128)(2,1)}, bf16[24,16,128]{2,1,0:T(8,128)(2,1)S(1)}, u32[]{:S(2)}, u32[]{:S(2)}) collective-permute-start(bf16[24,16,128]{2,1,0:T(8,128)(2,1)} %correct.1), channel_id=1, source_target_pairs={{0,6},{1,7},{2,4},{3,5},{4,2},{5,3},{6,0},{7,1},{8,14},{9,15},{10,... | collective-permute-start | bytes 294920 | tf_op jit(solution)/shard_map/ppermute | solution.py:681
  46.6 9.1 %collective-permute-start.11 = (bf16[24,16,128]{2,1,0:T(8,128)(2,1)}, bf16[24,16,128]{2,1,0:T(8,128)(2,1)S(1)}, u32[]{:S(2)}, u32[]{:S(2)}) collective-permute-start(bf16[24,16,128]{2,1,0:T(8,128)(2,1)} %correct.1), channel_id=1, source_target_pairs={{0,4},{1,5},{2,6},{3,7},{4,0},{5,1},{6,2},{7,3},{8,12},{9,13},{10,... | collective-permute-start | bytes 294920 | tf_op jit(solution)/shard_map/ppermute | solution.py:681
  46.6 9.1 %collective-permute-start.10 = (bf16[24,16,128]{2,1,0:T(8,128)(2,1)}, bf16[24,16,128]{2,1,0:T(8,128)(2,1)S(1)}, u32[]{:S(2)}, u32[]{:S(2)}) collective-permute-start(bf16[24,16,128]{2,1,0:T(8,128)(2,1)} %correct.1), channel_id=1, source_target_pairs={{0,2},{1,3},{2,0},{3,1},{4,6},{5,7},{6,4},{7,5},{8,10},{9,11},{10,... | collective-permute-start | bytes 294920 | tf_op jit(solution)/shard_map/ppermute | solution.py:681
  51.1 27.2 %copy-start.17 = (s32[768]{0:T(1024)S(1)}, s32[768]{0:T(1024)}, u32[]{:S(2)}) copy-start(s32[768]{0:T(1024)} %add.313.row_ref) | copy-start | bytes 9220
  51.2 9.1 %copy-start.16 = (s32[768]{0:T(1024)}, s32[768]{0:T(1024)S(1)}, u32[]{:S(2)}) copy-start(s32[768]{0:T(1024)S(1)} %add.309.col_ref) | copy-start | bytes 9220
  56.6 3.7 %copy-start = (bf16[96,16,128]{2,1,0:T(8,128)(2,1)}, bf16[96,16,128]{2,1,0:T(8,128)(2,1)S(1)}, u32[]{:S(2)}) copy-start(bf16[96,16,128]{2,1,0:T(8,128)(2,1)S(1)} %pad_maximum_fusion.1) | copy-start | bytes 1179652
  56.6 3.6 %collective-permute-start.16 = (bf16[96,16,128]{2,1,0:T(8,128)(2,1)S(1)}, bf16[96,16,128]{2,1,0:T(8,128)(2,1)S(1)}, u32[]{:S(2)}, u32[]{:S(2)}) collective-permute-start(bf16[96,16,128]{2,1,0:T(8,128)(2,1)S(1)} %pad_maximum_fusion.1), channel_id=1, source_target_pairs={{0,1},{1,0},{2,3},{3,2},{4,5},{5,4},{6,7},{7,6},{8,9},{9,8},{10,11... | collective-permute-start | bytes 1179656 | tf_op jit(solution)/shard_map/ppermute | solution.py:681
  56.7 16.3 %collective-permute-start.15 = (bf16[96,16,128]{2,1,0:T(8,128)(2,1)S(1)}, bf16[96,16,128]{2,1,0:T(8,128)(2,1)S(1)}, u32[]{:S(2)}, u32[]{:S(2)}) collective-permute-start(bf16[96,16,128]{2,1,0:T(8,128)(2,1)S(1)} %pad_maximum_fusion.1), channel_id=1, source_target_pairs={{0,24},{8,16},{16,8},{24,0},{1,25},{9,17},{17,9},{25,1},{2,26},{10... | collective-permute-start | bytes 1179656 | tf_op jit(solution)/shard_map/ppermute | solution.py:681
  59.4 18.2 %collective-permute-start.14 = (bf16[96,16,128]{2,1,0:T(8,128)(2,1)S(1)}, bf16[96,16,128]{2,1,0:T(8,128)(2,1)S(1)}, u32[]{:S(2)}, u32[]{:S(2)}) collective-permute-start(bf16[96,16,128]{2,1,0:T(8,128)(2,1)S(1)} %pad_maximum_fusion.1), channel_id=1, source_target_pairs={{0,16},{8,24},{16,0},{24,8},{1,17},{9,25},{17,1},{25,9},{2,18},{10... | collective-permute-start | bytes 1179656 | tf_op jit(solution)/shard_map/ppermute | solution.py:681
  59.9 17.9 %collective-permute-start.13 = (bf16[96,16,128]{2,1,0:T(8,128)(2,1)S(1)}, bf16[96,16,128]{2,1,0:T(8,128)(2,1)S(1)}, u32[]{:S(2)}, u32[]{:S(2)}) collective-permute-start(bf16[96,16,128]{2,1,0:T(8,128)(2,1)S(1)} %pad_maximum_fusion.1), channel_id=1, source_target_pairs={{0,8},{8,0},{16,24},{24,16},{1,9},{9,1},{17,25},{25,17},{2,10},{10... | collective-permute-start | bytes 1179656 | tf_op jit(solution)/shard_map/ppermute | solution.py:681
  60.3 0.8 copy-start.1
  73.0 7.6 %copy-start.3 = (bf16[96,16,128]{2,1,0:T(8,128)(2,1)}, bf16[96,16,128]{2,1,0:T(8,128)(2,1)S(1)}, u32[]{:S(2)}) copy-start(bf16[96,16,128]{2,1,0:T(8,128)(2,1)S(1)} %collective-permute-done.15) | copy-start | bytes 1179652
  77.6 3.1 %copy-start.4 = (bf16[96,16,128]{2,1,0:T(8,128)(2,1)}, bf16[96,16,128]{2,1,0:T(8,128)(2,1)S(1)}, u32[]{:S(2)}) copy-start(bf16[96,16,128]{2,1,0:T(8,128)(2,1)S(1)} %collective-permute-done.14) | copy-start | bytes 1179652
  77.8 2.9 %copy-start.5 = (bf16[96,16,128]{2,1,0:T(8,128)(2,1)}, bf16[96,16,128]{2,1,0:T(8,128)(2,1)S(1)}, u32[]{:S(2)}) copy-start(bf16[96,16,128]{2,1,0:T(8,128)(2,1)S(1)} %collective-permute-done.13) | copy-start | bytes 1179652
  77.8 2.0 %collective-permute-start.17 = (bf16[96,16,128]{2,1,0:T(8,128)(2,1)S(1)}, bf16[96,16,128]{2,1,0:T(8,128)(2,1)S(1)}, u32[]{:S(2)}, u32[]{:S(2)}) collective-permute-start(bf16[96,16,128]{2,1,0:T(8,128)(2,1)S(1)} %collective-permute-done.13), channel_id=1, source_target_pairs={{0,1},{1,0},{2,3},{3,2},{4,5},{5,4},{6,7},{7,6},{8,9},{9,8},{10,11... | collective-permute-start | bytes 1179656 | tf_op jit(solution)/shard_map/ppermute | solution.py:681
  77.8 2.3 %collective-permute-start.18 = (bf16[96,16,128]{2,1,0:T(8,128)(2,1)S(1)}, bf16[96,16,128]{2,1,0:T(8,128)(2,1)S(1)}, u32[]{:S(2)}, u32[]{:S(2)}) collective-permute-start(bf16[96,16,128]{2,1,0:T(8,128)(2,1)S(1)} %collective-permute-done.14), channel_id=1, source_target_pairs={{0,1},{1,0},{2,3},{3,2},{4,5},{5,4},{6,7},{7,6},{8,9},{9,8},{10,11... | collective-permute-start | bytes 1179656 | tf_op jit(solution)/shard_map/ppermute | solution.py:681
  78.3 2.3 %collective-permute-start.19 = (bf16[96,16,128]{2,1,0:T(8,128)(2,1)S(1)}, bf16[96,16,128]{2,1,0:T(8,128)(2,1)S(1)}, u32[]{:S(2)}, u32[]{:S(2)}) collective-permute-start(bf16[96,16,128]{2,1,0:T(8,128)(2,1)S(1)} %collective-permute-done.15), channel_id=1, source_target_pairs={{0,1},{1,0},{2,3},{3,2},{4,5},{5,4},{6,7},{7,6},{8,9},{9,8},{10,11... | collective-permute-start | bytes 1179656 | tf_op jit(solution)/shard_map/ppermute | solution.py:681
  79.8 0.9 copy-start.6
  80.1 0.8 copy-start.7
  80.6 0.8 copy-start.8

commit v8 on v7

--- a/solution.py
+++ b/solution.py
@@ -359,13 +359,57 @@
     return low + high
 
 
+def fill_lookups(corner, unit, counts, here, after, shifts):
+    size = corner.shape[1]
+    coarse, shift = corner // SUB, corner % SUB
+
+    def looked_up(index, length, table):
+        place = lax.broadcasted_iota(jnp.int32, (length, size), 0)
+        one = (place == index).astype(f32).astype(bf16)
+        return lax.dot_general(one, table, (((0,), (0,)), ((), ())), preferred_element_type=f32)
+
+    here[...] = looked_up(coarse, FINE, unit).astype(bf16)
+    after[...] = looked_up(lax.rem(coarse + 1, FINE), FINE, unit).astype(bf16)
+    shifts[...] = looked_up(shift, SUB, counts)
+
+
+def lookup_kernel(corner_ref, unit_ref, count_ref, here, after, shifts):
+    fill_lookups(corner_ref[...], unit_ref[...], count_ref[...], here, after, shifts)
+
+
+def lookup_tables():
+    fine, low = np.arange(FINE), np.arange(LOW)
+    angle = 2.0 * math.pi / FINE * (fine[:, None] * low[None, :] % FINE)
+    odd = np.where(low == 0, 1.0 - 2.0 * (fine[:, None] % 2), np.sin(angle))
+    unit = jnp.asarray(np.concatenate([np.cos(angle), odd], axis=1), bf16)
+    counts = jnp.asarray(np.broadcast_to(np.arange(SUB)[:, None], (SUB, LANES)), bf16)
+    return unit, counts
+
+
+def lookups(corner_rows, interpret=False):
+    total = corner_rows.shape[0]
+    return pl.pallas_call(
+        lookup_kernel,
+        out_shape=[
+            jax.ShapeDtypeStruct((total, FINE), bf16),
+            jax.ShapeDtypeStruct((total, FINE), bf16),
+            jax.ShapeDtypeStruct((total, LANES), f32),
+        ],
+        compiler_params=pltpu.CompilerParams(vmem_limit_bytes=VMEM_BYTES),
+        cost_estimate=pl.CostEstimate(flops=0, bytes_accessed=8_000_000, transcendentals=0),
+        name="lookups",
+        interpret=interpret,
+    )(corner_rows.reshape(1, total), *lookup_tables())
+
+
 def image_kernel(
     info_ref, row_ref, col_ref, *refs, pieces, chunks, row_block, per_row, tile_cols
 ):
     uv_refs, refs = refs[:pieces], refs[pieces:]
-    corner_ref, phase_ref, columns_ref, unit_ref, count_ref, twist_ref = refs[:6]
-    out_ref, tile_ref, uv_wide, uv_rows, here, after, shifts, left_even, left_odd, total = refs[7:17]
-    staged, spill, list_ref, sem = refs[17:]
+    given, (phase_ref, columns_ref, twist_ref), refs = refs[:3], refs[3:6], refs[7:]
+    out_ref, tile_ref, uv_wide, uv_rows, left_even, left_odd, total, staged, ready = refs[:9]
+    spill, list_ref, sem, out_sems = refs[9:13]
+    here, after, shifts = refs[13:] or given
     step = pl.program_id(0)
     lanes = 2 * tile_cols // LANES
     head = pltpu.make_async_copy(
@@ -477,17 +521,8 @@
             head.wait()
         add_spilled()
         pl.when(step == chunks - 1)(back.start)
-        corner = corner_ref[...]
-        coarse, shift = corner // SUB, corner % SUB
-
-        def looked_up(index, length, table):
-            place = lax.broadcasted_iota(jnp.int32, (length, size), 0)
-            one = (place == index).astype(f32).astype(bf16)
-            return lax.dot_general(one, table, (((0,), (0,)), ((), ())), preferred_element_type=f32)
-
-        here[...] = looked_up(coarse, FINE, unit_ref[...]).astype(bf16)
-        after[...] = looked_up(lax.rem(coarse + 1, FINE), FINE, unit_ref[...]).astype(bf16)
-        shifts[...] = looked_up(shift, SUB, count_ref[...])
+        if refs[13:]:
+            fill_lookups(given[0][...], given[1][...], given[2][...], here, after, shifts)
         for h in range(2):
             products(0, h, left_even, 0, size)
 
@@ -511,32 +546,55 @@
         def _():
             chunk(False)
 
-    @pl.when(step >= chunks)
+    wide = 2 * G // LANES
+
+    def eight_rows(first, slot, group):
+        backward = lax.rem(LOW - lax.broadcasted_iota(jnp.int32, (8, LOW), 1), LOW)
+        at = pl.ds(pl.multiple_of(first, 8), 8)
+        for tile in range(FINE // LANES):
+            at_lanes = pl.ds(tile * LANES, LANES)
+            values = [(total[n, 0, at, at_lanes], total[n, 1, at, at_lanes]) for n in range(SUB)]
+            for k, value in enumerate(short_transform(values)):
+                for part in range(2):
+                    ordered = value[part]
+                    if tile > 0:
+                        ordered = jnp.take_along_axis(
+                            ordered, backward, axis=1, mode="promise_in_bounds"
+                        )
+                    column = 2 * (k * (FINE // LANES) + tile) + part
+                    staged[pl.ds(column, 8, stride=wide + 1), :] = ordered
+        for row in range(8):
+            ready[slot, pl.ds((8 * group + row) * wide, wide), :] = staged[
+                row * (wide + 1) : row * (wide + 1) + wide, :
+            ]
+
+    @pl.when(step == chunks - 1)
     def _():
-        first = (step - chunks) * row_block
-        wide = 2 * G // LANES
-        backward = lax.rem(LOW - lax.broadcasted_iota(jnp.int32, (8, LOW), 1), LOW)
-
-        def eight_rows(group, carry):
-            at = pl.ds(pl.multiple_of(first + 8 * group, 8), 8)
-            for tile in range(FINE // LANES):
-                lanes = pl.ds(tile * LANES, LANES)
-                values = [(total[n, 0, at, lanes], total[n, 1, at, lanes]) for n in range(SUB)]
-                for k, value in enumerate(short_transform(values)):
-                    for part in range(2):
-                        ordered = value[part]
-                        if tile > 0:
-                            ordered = jnp.take_along_axis(
-                                ordered, backward, axis=1, mode="promise_in_bounds"
-                            )
-                        column = 2 * (k * (FINE // LANES) + tile) + part
-                        staged[pl.ds(column, 8, stride=wide + 1), :] = ordered
-            for row in range(8):
-                at = pl.ds(pl.multiple_of((8 * group + row) * wide, wide), wide)
-                out_ref[at, :] = staged[row * (wide + 1) : row * (wide + 1) + wide, :]
+        block = row_block * wide
+        blocks = image_rows // row_block
+
+        def sent(number, slot):
+            return pltpu.make_async_copy(
+                ready.at[slot], out_ref.at[pl.ds(pl.multiple_of(number * block, block), block), :],
+                out_sems.at[slot],
+            )
+
+        def two_blocks(i, carry):
+            for slot in range(2):
+                number = 2 * i + slot
+
+                @pl.when(i > 0)
+                def _():
+                    sent(number - 2, slot).wait()
+
+                for group in range(row_block // 8):
+                    eight_rows(number * row_block + 8 * group, slot, group)
+                sent(number, slot).start()
             return carry
 
-        lax.fori_loop(0, row_block // 8, eight_rows, 0)
+        lax.fori_loop(0, blocks // 2, two_blocks, 0)
+        for slot in range(2):
+            sent(blocks - 2 + slot, slot).wait()
 
 
 def image_tables(corner_cols, first_row, image_rows):
@@ -544,17 +602,17 @@
     turn = 2.0 * math.pi / G
     angle = turn * (rows[:, None] * corner_cols[None, :] % G).astype(f32)
     phase = jnp.stack([jnp.cos(angle), jnp.sin(angle)]).astype(bf16)
-    angle = turn * (rows[:, None] * jnp.arange(SUB, dtype=jnp.int32)[None, :] % G).astype(f32)
-    re, im = jnp.cos(angle), jnp.sin(angle)
-    block = jnp.concatenate(
-        [jnp.concatenate([re, -im], axis=1), jnp.concatenate([im, re], axis=1)], axis=0
-    )
-    columns = jnp.kron(jnp.eye(2, dtype=f32), block).astype(bf16)
+    lane = jnp.arange(PACK, dtype=jnp.int32)[None, None, :]
+    line = jnp.arange(4, dtype=jnp.int32)[:, None, None]
+    angle = turn * (rows[None, :, None] * (lane % SUB) % G).astype(f32)
+    angle = angle + (0.5 * math.pi) * (lane // SUB % 2 - line % 2).astype(f32)
+    columns = jnp.where(lane // (2 * SUB) == line // 2, jnp.cos(angle), 0.0).astype(bf16)
+    columns = columns.reshape(4 * image_rows, PACK)
     return phase, columns
 
 
 def image_rows_of(
-    uv, corners_all, tables, tile, info, per_row, tile_rows, tile_cols, interpret=False
+    uv, corners_all, tables, given, tile, info, per_row, tile_rows, tile_cols, interpret=False
 ):
     phase, columns = tables
     image_rows = phase.shape[1]
@@ -563,31 +621,32 @@
     total = corners_all[0].shape[0]
     size = math.gcd(total, CHUNK) if len(uv) == 1 else total
     chunks = total // size
-    row_block = math.gcd(image_rows, 32)
-    outs = image_rows // row_block
+    row_block = math.gcd(image_rows // 2, 16)
     wide = 2 * G // LANES
     fine, low = np.arange(FINE), np.arange(LOW)
-    angle = 2.0 * math.pi / FINE * (fine[:, None] * low[None, :] % FINE)
-    odd = np.where(low == 0, 1.0 - 2.0 * (fine[:, None] % 2), np.sin(angle))
-    unit = jnp.asarray(np.concatenate([np.cos(angle), odd], axis=1), bf16)
     scale = 1.0 / (SUB * math.sqrt(total))
     high = np.where(low == 0, LOW, FINE - low)
     angles = [2.0 * math.pi / G * (np.arange(SUB)[:, None] * k[None, :]) for k in (low, high)]
     twist = [f(angle) * scale for angle in angles for f in (np.cos, np.sin)]
     twist = jnp.asarray(np.concatenate(twist, axis=1), f32)
-    counts = jnp.asarray(np.broadcast_to(np.arange(SUB)[:, None], (SUB, LANES)), bf16)
-    last = chunks - 1
-
-    def chunk_of(i):
-        return jnp.minimum(i, last)
-
     if len(uv) == 1:
-        uv_specs = [pl.BlockSpec((size * HALF, PACK), lambda i, *_: (chunk_of(i), 0))]
+        uv_specs = [pl.BlockSpec((size * HALF, PACK), lambda i, *_: (i, 0))]
     else:
         uv_specs = [pl.BlockSpec(piece.shape, lambda i, *_: (0, 0)) for piece in uv]
 
     def fixed(operand):
         return pl.BlockSpec(operand.shape, lambda i, *_: (0, 0))
+
+    given_specs = [fixed(operand) for operand in given or ()]
+    scratch = []
+    if not given:
+        given = [corners_all[0].reshape(1, total), *lookup_tables()]
+        given_specs = [pl.BlockSpec((1, size), lambda i, *_: (0, i)), *map(fixed, given[1:])]
+        scratch = [
+            pltpu.VMEM((size, FINE), bf16),
+            pltpu.VMEM((size, FINE), bf16),
+            pltpu.VMEM((size, LANES), f32),
+        ]
 
     image, tile = pl.pallas_call(
         functools.partial(
@@ -596,36 +655,29 @@
         ),
         grid_spec=pltpu.PrefetchScalarGridSpec(
             num_scalar_prefetch=3,
-            grid=(chunks + outs,),
+            grid=(chunks,),
             in_specs=[
                 *uv_specs,
-                pl.BlockSpec((1, size), lambda i, *_: (0, chunk_of(i))),
-                pl.BlockSpec((2, image_rows, size), lambda i, *_: (0, 0, chunk_of(i))),
+                *given_specs,
+                pl.BlockSpec((2, image_rows, size), lambda i, *_: (0, 0, i)),
                 fixed(columns),
-                fixed(unit),
-                fixed(counts),
                 fixed(twist),
                 pl.BlockSpec(memory_space=pl.ANY),
             ],
-            out_specs=[
-                pl.BlockSpec(
-                    (row_block * wide, LANES), lambda i, *_: (jnp.maximum(i - chunks, 0), 0)
-                ),
-                pl.BlockSpec(memory_space=pl.ANY),
-            ],
+            out_specs=[pl.BlockSpec(memory_space=pl.ANY)] * 2,
             scratch_shapes=[
                 pltpu.VMEM((size * (HALF + 1) + HALF, PACK), f32),
                 pltpu.VMEM((HALF, size, PACK), bf16),
-                pltpu.VMEM((size, FINE), bf16),
-                pltpu.VMEM((size, FINE), bf16),
-                pltpu.VMEM((size, LANES), f32),
                 pltpu.VMEM((2, 2 * image_rows, size), bf16),
                 pltpu.VMEM((2, 2 * image_rows, size), bf16),
                 pltpu.VMEM((SUB, 2, image_rows, FINE), f32),
                 pltpu.VMEM((8 * (wide + 1) + wide, LANES), f32),
+                pltpu.VMEM((2, row_block * wide, LANES), f32),
                 pltpu.VMEM((3 * SUB * lanes, LANES), f32),
                 pltpu.SMEM((per_row + 1,), jnp.int32),
                 pltpu.SemaphoreType.DMA(()),
+                pltpu.SemaphoreType.DMA((2,)),
+                *scratch,
             ],
         ),
         out_shape=[
@@ -638,7 +690,7 @@
         interpret=interpret,
     )(
         info, *corners_all, *uv,
-        corners_all[0].reshape(1, total), phase, columns, unit, counts, twist, tile,
+        *given, phase, columns, twist, tile,
     )
     image = image.reshape(image_rows, G // LANES, 2, LANES)
     tile = tile.reshape(tile_rows, tile_cols // LANES, 2, LANES)
@@ -780,13 +832,14 @@
         lines = au_lines(line)
         own_row = with_core(lines[:1])
         tile = uv_tile_own(own_row, own_info, corners_all, per_row, tile_rows, tile_cols)
-        lines, own_row, tile = lax.optimization_barrier((lines, own_row, tile))
+        given = lookups(corners_all[0])
+        lines, own_row, tile, given = lax.optimization_barrier((lines, own_row, tile, given))
         uv = own_row + with_core(lines[1:])
     else:
-        uv = whole_gather(uv_own)
+        uv, given = whole_gather(uv_own), None
         tile = uv_tile_own(uv, own_info, corners_all, per_row, tile_rows, tile_cols)
     return image_rows_of(
-        uv, corners_all, tables, tile, before_info, per_row, tile_rows, tile_cols
+        uv, corners_all, tables, given, tile, before_info, per_row, tile_rows, tile_cols
     )
 
 

time: 118 us -> 122 us (1.034)
  Pallas kernels: 68.2 us -> 72.7 us
  other arithmetic: 10.9 us -> 13.2 us
  waiting for transfers between devices: 7.33 us -> 5.56 us
  local copies, waits for them, and re-layouts: 10.7 us -> 9.16 us
    pallas_call x0 -> x1, Pallas kernels: none -> 2.33 us  [lookups(): pl.pallas_call(lookup_kernel, out_shape=[jax.ShapeDtypeStruct((total, FIN...]
    convert_element_type x2 -> x1, other arithmetic: 0.24 us -> 2.41 us  [image_tables(): jnp.where(lane // (2 * SUB) == line // 2, jnp.cos(angle), 0.0).astype(bf16)]
    pallas_call x1, Pallas kernels: 35.7 us -> 37.6 us  [image_rows_of(): pl.pallas_call(functools.partial(image_kernel, pieces=len(uv), chunks=chu...]
    ppermute x20, waiting for transfers between devices: 7.33 us -> 5.56 us  [from_partner(): return lax.ppermute(value, axis, [(i, i ^ mask) for i in range(count)])]
    unnamed x57 -> x56, local copies, waits for them, and re-layouts: 6.06 us -> 6.02 us
  transfers between devices with their start and end apart: 20 -> 20, of which waited for: 6 -> 7; matrix products, arithmetic and copies ran while one was open for 13% -> 13% of each run, Pallas kernels for 22% -> 24%
where the time goes in v8:
time: 122 us; the launch traced here: 121 us
  Pallas kernels  72.7 us (60%)
  starting transfers between devices  18.9 us (15%)
  other arithmetic  13.2 us (11%)
  local copies, waits for them, and re-layouts  9.16 us (8%)
  waiting for transfers between devices  5.56 us (5%)
  between operations  1.28 us (1%)
    pallas_call x1, Pallas kernels, image_rows_of(): pl.pallas_call(functools.partial(image_kernel, pieces=len(uv), chunks=chu...  37.6 us
    ppermute x20, starting transfers between devices, from_partner(): return lax.ppermute(value, axis, [(i, i ^ mask) for i in range(count)])  18.9 us
    pallas_call x3, Pallas kernels, sky_sums(): pl.pallas_call(sky_kernel, grid=(1,), in_specs=[pl.BlockSpec((count, 2, v...  13.8 us
    pallas_call x1, Pallas kernels, uv_tile_own(): pl.pallas_call(functools.partial(tile_kernel, pieces=len(uv), tile_rows=t...  12.3 us
    pallas_call x1, Pallas kernels, corrected_subgrids(): pl.pallas_call(functools.partial(correct_kernel, pieces=len(tables), skie...  6.66 us
    unnamed x56, local copies, waits for them, and re-layouts  6.02 us
    ppermute x20, waiting for transfers between devices, from_partner(): return lax.ppermute(value, axis, [(i, i ^ mask) for i in range(count)])  5.56 us
    another operation x1, other arithmetic  3.47 us
  transfers between devices with their start and end apart: 20, of which 7 were waited for; matrix products, arithmetic and copies ran while one was open for 13% of the time, Pallas kernels for 24%

profile of v8, /device:TPU:0, one launch (start us, length us, event | category | flops | bytes accessed | tf_op | source)
XLA Modules:
  0.0 120.8 jit_solution(286677328994535892)
XLA Ops:
  0.6 0.8 and_select_fusion.16
  1.4 0.1 convert_element_type.95
  1.5 1.0 reshape.911
  2.6 0.2 copy.40
  2.8 0.2 reshape.912
  3.0 5.1 %collective-permute-start.2 = (bf16[17,16,128]{2,1,0:T(8,128)(2,1)S(1)}, bf16[17,16,128]{2,1,0:T(8,128)(2,1)S(1)}, u32[]{:S(2)}, u32[]{:S(2)}) collective-permute-start(bf16[17,16,128]{2,1,0:T(8,128)(2,1)S(1)} %pad_maximum_fusion.2), channel_id=1, source_target_pairs={{0,6},{1,7},{2,4},{3,5},{4,2},{5,3},{6,0},{7,1},{8,14},{9,15},{10,... | collective-permute-start | bytes 208904 | tf_op jit(solution)/shard_map/ppermute | solution.py:733
  8.1 0.6 collective-permute-start
  8.9 0.1 broadcast_compare_fusion
  9.0 0.1 convert_multiply_fusion
  9.1 0.1 fusion.11
  9.2 4.6 %sky_sums.3.refs_8_ = f32[8,16,128]{2,1,0:T(8,128)} custom-call(bf16[24,2,2048]{2,1,0:T(2,128)(2,1)} %vis_ref.5, f32[48,128]{1,0:T(8,128)} %bitcast.137, f32[1,16]{1,0:T(1,128)} %bitcast.148), custom_call_target="tpu_custom_call" | custom-call | bytes 20000000 | tf_op jit(solution)/shard_map/sky_sums/pallas_call | solution.py:119
  13.9 2.4 %select_convert_fusion = bf16[4,256,128]{2,1,0:T(8,128)(2,1)} fusion(f32[4,128]{1,0:T(4,128)S(1)} %convert_multiply_fusion, f32[256,128]{1,0:T(8,128)S(1)} %fusion.11, pred[4,128]{1,0:T(4,128)(4,1)S(1)} %broadcast_compare_fusion), kind=kLoop, calls=%fused_computation.11 | loop fusion | flops 393216 | bytes 395776 | tf_op jit(solution)/shard_map/convert_element_type | solution.py:609
  16.3 0.6 add_add_fusion
  17.0 2.7 %collective-permute-start.5 = (bf16[68,16,128]{2,1,0:T(8,128)(2,1)S(1)}, bf16[68,16,128]{2,1,0:T(8,128)(2,1)S(1)}, u32[]{:S(2)}, u32[]{:S(2)}) collective-permute-start(bf16[68,16,128]{2,1,0:T(8,128)(2,1)S(1)} %constant_dynamic-update-slice_fusion.refs_0_), channel_id=1, source_target_pairs={{0,24},{8,16},{16,8},{24,0},{1,25},{9,17},{17,9},{25,1},{2,26},{10... | collective-permute-start | bytes 835592 | tf_op jit(solution)/shard_map/ppermute | solution.py:733
  19.6 0.5 collective-permute-start.4
  20.1 0.4 collective-permute-start.3
  20.5 0.7 fusion.19
  21.2 0.7 and_select_fusion.4
  21.9 0.7 broadcast_multiply_fusion.1
  22.6 4.6 %sky_sums.5.refs_10_ = f32[8,16,128]{2,1,0:T(8,128)} custom-call(bf16[24,2,2048]{2,1,0:T(2,128)(2,1)} %vis_ref.5, f32[48,128]{1,0:T(8,128)} %bitcast.138, f32[1,16]{1,0:T(1,128)} %bitcast.149), custom_call_target="tpu_custom_call" | custom-call | bytes 20000000 | tf_op jit(solution)/shard_map/sky_sums/pallas_call | solution.py:119
  27.2 4.6 %sky_sums.4.refs_9_ = f32[8,16,128]{2,1,0:T(8,128)} custom-call(bf16[24,2,2048]{2,1,0:T(2,128)(2,1)} %vis_ref.5, f32[48,128]{1,0:T(8,128)} %bitcast.139, f32[1,16]{1,0:T(1,128)} %bitcast.150), custom_call_target="tpu_custom_call" | custom-call | bytes 20000000 | tf_op jit(solution)/shard_map/sky_sums/pallas_call | solution.py:119
  31.8 0.1 copy.20
  31.9 0.6 reshape.916.stations_ref
  32.5 1.5 %fusion.8.refs_11_ = f32[24,16,128]{2,1,0:T(8,128)} fusion(f32[16,128]{1,0:T(8,128)S(1)} %get-tuple-element.81, f32[128]{0:T(128)S(1)} %convert_multiply_fusion.1, s32[16,128]{1,0:T(8,128)S(1)} %fusion.13, s32[24]{0:T(128)S(1)} %and_select_fusion.4, f32[16,128]{1,0:T(8,128)S(1)} %get-tuple-element.80, f32[24]{0:T(128)S(1)} %broadcast_multiply_fusion.1), kind=kLoop, calls=%fused_computation.27 | loop fusion | flops 884736 | bytes 221888 | tf_op jit(solution)/shard_map/mul | solution.py:728
  34.1 0.1 collective-permute-start.9
  34.1 0.5 collective-permute-start.8
  34.6 0.1 collective-permute-start.6
  34.7 0.4 collective-permute-start.7
  35.2 1.3 %collective-permute-done.6.refs_1_ = bf16[68,16,128]{2,1,0:T(8,128)(2,1)S(1)} collective-permute-done((bf16[68,16,128]{2,1,0:T(8,128)(2,1)S(1)}, bf16[68,16,128]{2,1,0:T(8,128)(2,1)S(1)}, u32[]{:S(2)}, u32[]{:S(2)}) %collective-permute-start.6) | collective-permute-done | bytes 278560 | tf_op jit(solution)/shard_map/ppermute | solution.py:733
  36.5 0.4 collective-permute-done.7.refs_3_
  36.9 0.3 copy-done.14
  37.2 0.4 copy-done.15
  37.6 0.1 copy-done.13
  37.7 0.7 copy-done.12
  38.4 6.7 %correct.1 = bf16[24,16,128]{2,1,0:T(8,128)(2,1)} custom-call(s32[48]{0:T(128)} %reshape.916.stations_ref, bf16[68,16,128]{2,1,0:T(8,128)(2,1)} %copy-done.2, bf16[68,16,128]{2,1,0:T(8,128)(2,1)} %copy-done.14, bf16[68,16,128]{2,1,0:T(8,128)(2,1)} %copy-done.11, bf16[68,16,128]{2,1,0:T(8,128)(2,1)} %copy-done.15, bf16[68,16,128]{2,1,0:T(8,128)(2,1)} %copy-done.10, ...), custom_call_target="tpu_custom_call" | custom-call | bytes 16000000 | tf_op jit(solution)/shard_map/correct/pallas_call | solution.py:194
  45.1 3.7 %collective-permute-start.12 = (bf16[24,16,128]{2,1,0:T(8,128)(2,1)}, bf16[24,16,128]{2,1,0:T(8,128)(2,1)S(1)}, u32[]{:S(2)}, u32[]{:S(2)}) collective-permute-start(bf16[24,16,128]{2,1,0:T(8,128)(2,1)} %correct.1), channel_id=1, source_target_pairs={{0,6},{1,7},{2,4},{3,5},{4,2},{5,3},{6,0},{7,1},{8,14},{9,15},{10,... | collective-permute-start | bytes 294920 | tf_op jit(solution)/shard_map/ppermute | solution.py:733
  48.8 0.6 collective-permute-start.10
  49.5 0.7 slice_bitcast_fusion.6
  50.2 0.7 slice_bitcast_fusion.4
  50.9 0.7 slice_bitcast_fusion.2
  51.7 0.7 slice_bitcast_fusion
  52.4 0.1 concatenate.41
  52.6 0.1 slice_add_fusion
  52.6 0.1 add.388.row_ref
  52.7 0.1 add.380.col_ref
  52.8 3.5 %cosine_convert_fusion = (bf16[1,256,768]{2,1,0:T(8,128)(2,1)S(1)}, bf16[1,256,768]{2,1,0:T(8,128)(2,1)S(1)}) fusion(s32[768]{0:T(1024)S(1)} %add.380.col_ref, s32[256]{0:T(256)S(1)} %iota_add_fusion.1), kind=kLoop, calls=%fused_computation.10 | loop fusion | flops 3145728 | bytes 790528 | tf_op jit(solution)/shard_map/convert
  56.3 1.0 pad_maximum_fusion.refs_11_
  57.3 0.9 pad_maximum_fusion.1
  58.3 2.7 %collective-permute-start.15 = (bf16[96,16,128]{2,1,0:T(8,128)(2,1)S(1)}, bf16[96,16,128]{2,1,0:T(8,128)(2,1)S(1)}, u32[]{:S(2)}, u32[]{:S(2)}) collective-permute-start(bf16[96,16,128]{2,1,0:T(8,128)(2,1)S(1)} %pad_maximum_fusion.1), channel_id=1, source_target_pairs={{0,24},{8,16},{16,8},{24,0},{1,25},{9,17},{17,9},{25,1},{2,26},{10... | collective-permute-start | bytes 1179656 | tf_op jit(solution)/shard_map/ppermute | solution.py:733
  61.0 0.5 collective-permute-start.14
  61.5 0.4 collective-permute-start.13
  61.9 0.6 reshape.927.corner_ref
  62.5 2.3 %lookups.1 = (bf16[768,256]{1,0:T(8,128)(2,1)}, bf16[768,256]{1,0:T(8,128)(2,1)}, f32[768,128]{1,0:T(8,128)}) custom-call(s32[1,768]{1,0:T(1,128)} %reshape.927.corner_ref, bf16[256,256]{1,0:T(8,128)(2,1)} %constant.376.clone.unit_ref, bf16[32,128]{1,0:T(8,128)(2,1)} %constant.377.clone.count_ref), custom_call_target="tpu_custom_call" | custom-call | bytes 8000000 | tf_op jit(solution)/shard_map/lookups/pallas_call | solution.py:391
  64.8 0.7 copy-done.1
  65.6 12.3 %uv_tile.1.refs_14_ = f32[32768,128]{1,0:T(8,128)} custom-call(s32[3]{0:T(128)} %get-tuple-element.53.info_ref, s32[768]{0:T(1024)} %copy-done.17, s32[768]{0:T(1024)} %copy-done.16, bf16[1536,128]{1,0:T(8,128)(2,1)} %bitcast.117, bf16[1536,128]{1,0:T(8,128)(2,1)} %bitcast.119), custom_call_target="tpu_custom_call" | custom-call | bytes 41943040 | tf_op jit(solution)/shard_map/uv_tile/pallas_call | solution.py:309
  77.9 1.3 %collective-permute-done.14 = bf16[96,16,128]{2,1,0:T(8,128)(2,1)S(1)} collective-permute-done((bf16[96,16,128]{2,1,0:T(8,128)(2,1)S(1)}, bf16[96,16,128]{2,1,0:T(8,128)(2,1)S(1)}, u32[]{:S(2)}, u32[]{:S(2)}) %collective-permute-start.14) | collective-permute-done | bytes 393248 | tf_op jit(solution)/shard_map/ppermute | solution.py:733
  79.2 0.2 collective-permute-done.13
  79.4 0.5 collective-permute-start.18
  80.0 1.2 collective-permute-done.17
  81.2 0.6 collective-permute-done.18
  81.7 0.6 collective-permute-done.19
  82.3 0.2 copy-done.7
  82.5 0.6 copy-done.8
  83.0 37.6 %image.1 = (f32[32768,128]{1,0:T(8,128)}, f32[32768,128]{1,0:T(8,128)}) custom-call(s32[3]{0:T(128)} %get-tuple-element.49.info_ref, s32[768]{0:T(1024)} %copy-done.17, s32[768]{0:T(1024)} %copy-done.16, bf16[1536,128]{1,0:T(8,128)(2,1)} %bitcast.118, bf16[1536,128]{1,0:T(8,128)(2,1)} %bitcast.120, ...), custom_call_target="tpu_custom_call", output_to_operand_aliasing={{1}: (17, {})} | custom-call | tf_op jit(solution)/shard_map/image/pallas_call | solution.py:651
  (80 shorter events, 0.4 us)
Async XLA Ops:
  3.0 13.9 %collective-permute-start.2 = (bf16[17,16,128]{2,1,0:T(8,128)(2,1)S(1)}, bf16[17,16,128]{2,1,0:T(8,128)(2,1)S(1)}, u32[]{:S(2)}, u32[]{:S(2)}) collective-permute-start(bf16[17,16,128]{2,1,0:T(8,128)(2,1)S(1)} %pad_maximum_fusion.2), channel_id=1, source_target_pairs={{0,6},{1,7},{2,4},{3,5},{4,2},{5,3},{6,0},{7,1},{8,14},{9,15},{10,... | collective-permute-start | bytes 208904 | tf_op jit(solution)/shard_map/ppermute | solution.py:733
  8.1 8.8 %collective-permute-start.1 = (bf16[17,16,128]{2,1,0:T(8,128)(2,1)S(1)}, bf16[17,16,128]{2,1,0:T(8,128)(2,1)S(1)}, u32[]{:S(2)}, u32[]{:S(2)}) collective-permute-start(bf16[17,16,128]{2,1,0:T(8,128)(2,1)S(1)} %pad_maximum_fusion.2), channel_id=1, source_target_pairs={{0,4},{1,5},{2,6},{3,7},{4,0},{5,1},{6,2},{7,3},{8,12},{9,13},{10,... | collective-permute-start | bytes 208904 | tf_op jit(solution)/shard_map/ppermute | solution.py:733
  8.1 8.7 %collective-permute-start = (bf16[17,16,128]{2,1,0:T(8,128)(2,1)S(1)}, bf16[17,16,128]{2,1,0:T(8,128)(2,1)S(1)}, u32[]{:S(2)}, u32[]{:S(2)}) collective-permute-start(bf16[17,16,128]{2,1,0:T(8,128)(2,1)S(1)} %pad_maximum_fusion.2), channel_id=1, source_target_pairs={{0,2},{1,3},{2,0},{3,1},{4,6},{5,7},{6,4},{7,5},{8,10},{9,11},{10,... | collective-permute-start | bytes 208904 | tf_op jit(solution)/shard_map/ppermute | solution.py:733
  17.0 19.9 %copy-start.2 = (bf16[68,16,128]{2,1,0:T(8,128)(2,1)}, bf16[68,16,128]{2,1,0:T(8,128)(2,1)S(1)}, u32[]{:S(2)}) copy-start(bf16[68,16,128]{2,1,0:T(8,128)(2,1)S(1)} %constant_dynamic-update-slice_fusion.refs_0_) | copy-start | bytes 835588
  17.0 17.0 %collective-permute-start.5 = (bf16[68,16,128]{2,1,0:T(8,128)(2,1)S(1)}, bf16[68,16,128]{2,1,0:T(8,128)(2,1)S(1)}, u32[]{:S(2)}, u32[]{:S(2)}) collective-permute-start(bf16[68,16,128]{2,1,0:T(8,128)(2,1)S(1)} %constant_dynamic-update-slice_fusion.refs_0_), channel_id=1, source_target_pairs={{0,24},{8,16},{16,8},{24,0},{1,25},{9,17},{17,9},{25,1},{2,26},{10... | collective-permute-start | bytes 835592 | tf_op jit(solution)/shard_map/ppermute | solution.py:733
  19.6 14.4 %collective-permute-start.4 = (bf16[68,16,128]{2,1,0:T(8,128)(2,1)S(1)}, bf16[68,16,128]{2,1,0:T(8,128)(2,1)S(1)}, u32[]{:S(2)}, u32[]{:S(2)}) collective-permute-start(bf16[68,16,128]{2,1,0:T(8,128)(2,1)S(1)} %constant_dynamic-update-slice_fusion.refs_0_), channel_id=1, source_target_pairs={{0,16},{8,24},{16,0},{24,8},{1,17},{9,25},{17,1},{25,9},{2,18},{10... | collective-permute-start | bytes 835592 | tf_op jit(solution)/shard_map/ppermute | solution.py:733
  20.1 13.9 %collective-permute-start.3 = (bf16[68,16,128]{2,1,0:T(8,128)(2,1)S(1)}, bf16[68,16,128]{2,1,0:T(8,128)(2,1)S(1)}, u32[]{:S(2)}, u32[]{:S(2)}) collective-permute-start(bf16[68,16,128]{2,1,0:T(8,128)(2,1)S(1)} %constant_dynamic-update-slice_fusion.refs_0_), channel_id=1, source_target_pairs={{0,8},{8,0},{16,24},{24,16},{1,9},{9,1},{17,25},{25,17},{2,10},{10... | collective-permute-start | bytes 835592 | tf_op jit(solution)/shard_map/ppermute | solution.py:733
  34.0 2.9 %copy-start.9 = (bf16[68,16,128]{2,1,0:T(8,128)(2,1)}, bf16[68,16,128]{2,1,0:T(8,128)(2,1)S(1)}, u32[]{:S(2)}) copy-start(bf16[68,16,128]{2,1,0:T(8,128)(2,1)S(1)} %collective-permute-done.5.refs_6_) | copy-start | bytes 835588
  34.0 2.9 %copy-start.10 = (bf16[68,16,128]{2,1,0:T(8,128)(2,1)}, bf16[68,16,128]{2,1,0:T(8,128)(2,1)S(1)}, u32[]{:S(2)}) copy-start(bf16[68,16,128]{2,1,0:T(8,128)(2,1)S(1)} %collective-permute-done.4.refs_4_) | copy-start | bytes 835588
  34.0 2.9 %copy-start.11 = (bf16[68,16,128]{2,1,0:T(8,128)(2,1)}, bf16[68,16,128]{2,1,0:T(8,128)(2,1)S(1)}, u32[]{:S(2)}) copy-start(bf16[68,16,128]{2,1,0:T(8,128)(2,1)S(1)} %collective-permute-done.3.refs_2_) | copy-start | bytes 835588
  34.1 2.8 %collective-permute-start.9 = (bf16[68,16,128]{2,1,0:T(8,128)(2,1)S(1)}, bf16[68,16,128]{2,1,0:T(8,128)(2,1)S(1)}, u32[]{:S(2)}, u32[]{:S(2)}) collective-permute-start(bf16[68,16,128]{2,1,0:T(8,128)(2,1)S(1)} %collective-permute-done.5.refs_6_), channel_id=1, source_target_pairs={{0,1},{1,0},{2,3},{3,2},{4,5},{5,4},{6,7},{7,6},{8,9},{9,8},{10,11... | collective-permute-start | bytes 835592 | tf_op jit(solution)/shard_map/ppermute | solution.py:733
  34.1 2.7 %collective-permute-start.8 = (bf16[68,16,128]{2,1,0:T(8,128)(2,1)S(1)}, bf16[68,16,128]{2,1,0:T(8,128)(2,1)S(1)}, u32[]{:S(2)}, u32[]{:S(2)}) collective-permute-start(bf16[68,16,128]{2,1,0:T(8,128)(2,1)S(1)} %collective-permute-done.4.refs_4_), channel_id=1, source_target_pairs={{0,1},{1,0},{2,3},{3,2},{4,5},{5,4},{6,7},{7,6},{8,9},{9,8},{10,11... | collective-permute-start | bytes 835592 | tf_op jit(solution)/shard_map/ppermute | solution.py:733
  34.6 1.8 %collective-permute-start.6 = (bf16[68,16,128]{2,1,0:T(8,128)(2,1)S(1)}, bf16[68,16,128]{2,1,0:T(8,128)(2,1)S(1)}, u32[]{:S(2)}, u32[]{:S(2)}) collective-permute-start(bf16[68,16,128]{2,1,0:T(8,128)(2,1)S(1)} %constant_dynamic-update-slice_fusion.refs_0_), channel_id=1, source_target_pairs={{0,1},{1,0},{2,3},{3,2},{4,5},{5,4},{6,7},{7,6},{8,9},{9,8},{10,11... | collective-permute-start | bytes 835592 | tf_op jit(solution)/shard_map/ppermute | solution.py:733
  34.7 2.2 %collective-permute-start.7 = (bf16[68,16,128]{2,1,0:T(8,128)(2,1)S(1)}, bf16[68,16,128]{2,1,0:T(8,128)(2,1)S(1)}, u32[]{:S(2)}, u32[]{:S(2)}) collective-permute-start(bf16[68,16,128]{2,1,0:T(8,128)(2,1)S(1)} %collective-permute-done.3.refs_2_), channel_id=1, source_target_pairs={{0,1},{1,0},{2,3},{3,2},{4,5},{5,4},{6,7},{7,6},{8,9},{9,8},{10,11... | collective-permute-start | bytes 835592 | tf_op jit(solution)/shard_map/ppermute | solution.py:733
  36.5 0.7 copy-start.14
  36.9 0.7 copy-start.15
  36.9 0.8 copy-start.13
  37.7 0.7 copy-start.12
  45.1 12.2 %collective-permute-start.12 = (bf16[24,16,128]{2,1,0:T(8,128)(2,1)}, bf16[24,16,128]{2,1,0:T(8,128)(2,1)S(1)}, u32[]{:S(2)}, u32[]{:S(2)}) collective-permute-start(bf16[24,16,128]{2,1,0:T(8,128)(2,1)} %correct.1), channel_id=1, source_target_pairs={{0,6},{1,7},{2,4},{3,5},{4,2},{5,3},{6,0},{7,1},{8,14},{9,15},{10,... | collective-permute-start | bytes 294920 | tf_op jit(solution)/shard_map/ppermute | solution.py:733
  48.8 8.5 %collective-permute-start.11 = (bf16[24,16,128]{2,1,0:T(8,128)(2,1)}, bf16[24,16,128]{2,1,0:T(8,128)(2,1)S(1)}, u32[]{:S(2)}, u32[]{:S(2)}) collective-permute-start(bf16[24,16,128]{2,1,0:T(8,128)(2,1)} %correct.1), channel_id=1, source_target_pairs={{0,4},{1,5},{2,6},{3,7},{4,0},{5,1},{6,2},{7,3},{8,12},{9,13},{10,... | collective-permute-start | bytes 294920 | tf_op jit(solution)/shard_map/ppermute | solution.py:733
  48.8 8.5 %collective-permute-start.10 = (bf16[24,16,128]{2,1,0:T(8,128)(2,1)}, bf16[24,16,128]{2,1,0:T(8,128)(2,1)S(1)}, u32[]{:S(2)}, u32[]{:S(2)}) collective-permute-start(bf16[24,16,128]{2,1,0:T(8,128)(2,1)} %correct.1), channel_id=1, source_target_pairs={{0,2},{1,3},{2,0},{3,1},{4,6},{5,7},{6,4},{7,5},{8,10},{9,11},{10,... | collective-permute-start | bytes 294920 | tf_op jit(solution)/shard_map/ppermute | solution.py:733
  52.7 12.1 %copy-start.17 = (s32[768]{0:T(1024)}, s32[768]{0:T(1024)S(1)}, u32[]{:S(2)}) copy-start(s32[768]{0:T(1024)S(1)} %add.388.row_ref) | copy-start | bytes 9220
  52.8 12.0 %copy-start.16 = (s32[768]{0:T(1024)}, s32[768]{0:T(1024)S(1)}, u32[]{:S(2)}) copy-start(s32[768]{0:T(1024)S(1)} %add.380.col_ref) | copy-start | bytes 9220
  58.2 6.6 %copy-start = (bf16[96,16,128]{2,1,0:T(8,128)(2,1)}, bf16[96,16,128]{2,1,0:T(8,128)(2,1)S(1)}, u32[]{:S(2)}) copy-start(bf16[96,16,128]{2,1,0:T(8,128)(2,1)S(1)} %pad_maximum_fusion.1) | copy-start | bytes 1179652
  58.3 6.5 %collective-permute-start.16 = (bf16[96,16,128]{2,1,0:T(8,128)(2,1)S(1)}, bf16[96,16,128]{2,1,0:T(8,128)(2,1)S(1)}, u32[]{:S(2)}, u32[]{:S(2)}) collective-permute-start(bf16[96,16,128]{2,1,0:T(8,128)(2,1)S(1)} %pad_maximum_fusion.1), channel_id=1, source_target_pairs={{0,1},{1,0},{2,3},{3,2},{4,5},{5,4},{6,7},{7,6},{8,9},{9,8},{10,11... | collective-permute-start | bytes 1179656 | tf_op jit(solution)/shard_map/ppermute | solution.py:733
  58.3 19.5 %collective-permute-start.15 = (bf16[96,16,128]{2,1,0:T(8,128)(2,1)S(1)}, bf16[96,16,128]{2,1,0:T(8,128)(2,1)S(1)}, u32[]{:S(2)}, u32[]{:S(2)}) collective-permute-start(bf16[96,16,128]{2,1,0:T(8,128)(2,1)S(1)} %pad_maximum_fusion.1), channel_id=1, source_target_pairs={{0,24},{8,16},{16,8},{24,0},{1,25},{9,17},{17,9},{25,1},{2,26},{10... | collective-permute-start | bytes 1179656 | tf_op jit(solution)/shard_map/ppermute | solution.py:733
  61.0 18.2 %collective-permute-start.14 = (bf16[96,16,128]{2,1,0:T(8,128)(2,1)S(1)}, bf16[96,16,128]{2,1,0:T(8,128)(2,1)S(1)}, u32[]{:S(2)}, u32[]{:S(2)}) collective-permute-start(bf16[96,16,128]{2,1,0:T(8,128)(2,1)S(1)} %pad_maximum_fusion.1), channel_id=1, source_target_pairs={{0,16},{8,24},{16,0},{24,8},{1,17},{9,25},{17,1},{25,9},{2,18},{10... | collective-permute-start | bytes 1179656 | tf_op jit(solution)/shard_map/ppermute | solution.py:733
  61.5 17.9 %collective-permute-start.13 = (bf16[96,16,128]{2,1,0:T(8,128)(2,1)S(1)}, bf16[96,16,128]{2,1,0:T(8,128)(2,1)S(1)}, u32[]{:S(2)}, u32[]{:S(2)}) collective-permute-start(bf16[96,16,128]{2,1,0:T(8,128)(2,1)S(1)} %pad_maximum_fusion.1), channel_id=1, source_target_pairs={{0,8},{8,0},{16,24},{24,16},{1,9},{9,1},{17,25},{25,17},{2,10},{10... | collective-permute-start | bytes 1179656 | tf_op jit(solution)/shard_map/ppermute | solution.py:733
  64.8 0.8 copy-start.1
  77.9 4.4 %copy-start.3 = (bf16[96,16,128]{2,1,0:T(8,128)(2,1)}, bf16[96,16,128]{2,1,0:T(8,128)(2,1)S(1)}, u32[]{:S(2)}) copy-start(bf16[96,16,128]{2,1,0:T(8,128)(2,1)S(1)} %collective-permute-done.15) | copy-start | bytes 1179652
  79.2 3.1 %copy-start.4 = (bf16[96,16,128]{2,1,0:T(8,128)(2,1)}, bf16[96,16,128]{2,1,0:T(8,128)(2,1)S(1)}, u32[]{:S(2)}) copy-start(bf16[96,16,128]{2,1,0:T(8,128)(2,1)S(1)} %collective-permute-done.14) | copy-start | bytes 1179652
  79.4 2.9 %copy-start.5 = (bf16[96,16,128]{2,1,0:T(8,128)(2,1)}, bf16[96,16,128]{2,1,0:T(8,128)(2,1)S(1)}, u32[]{:S(2)}) copy-start(bf16[96,16,128]{2,1,0:T(8,128)(2,1)S(1)} %collective-permute-done.13) | copy-start | bytes 1179652
  79.4 1.7 %collective-permute-start.17 = (bf16[96,16,128]{2,1,0:T(8,128)(2,1)S(1)}, bf16[96,16,128]{2,1,0:T(8,128)(2,1)S(1)}, u32[]{:S(2)}, u32[]{:S(2)}) collective-permute-start(bf16[96,16,128]{2,1,0:T(8,128)(2,1)S(1)} %collective-permute-done.13), channel_id=1, source_target_pairs={{0,1},{1,0},{2,3},{3,2},{4,5},{5,4},{6,7},{7,6},{8,9},{9,8},{10,11... | collective-permute-start | bytes 1179656 | tf_op jit(solution)/shard_map/ppermute | solution.py:733
  79.4 2.3 %collective-permute-start.18 = (bf16[96,16,128]{2,1,0:T(8,128)(2,1)S(1)}, bf16[96,16,128]{2,1,0:T(8,128)(2,1)S(1)}, u32[]{:S(2)}, u32[]{:S(2)}) collective-permute-start(bf16[96,16,128]{2,1,0:T(8,128)(2,1)S(1)} %collective-permute-done.14), channel_id=1, source_target_pairs={{0,1},{1,0},{2,3},{3,2},{4,5},{5,4},{6,7},{7,6},{8,9},{9,8},{10,11... | collective-permute-start | bytes 1179656 | tf_op jit(solution)/shard_map/ppermute | solution.py:733
  79.9 2.3 %collective-permute-start.19 = (bf16[96,16,128]{2,1,0:T(8,128)(2,1)S(1)}, bf16[96,16,128]{2,1,0:T(8,128)(2,1)S(1)}, u32[]{:S(2)}, u32[]{:S(2)}) collective-permute-start(bf16[96,16,128]{2,1,0:T(8,128)(2,1)S(1)} %collective-permute-done.15), channel_id=1, source_target_pairs={{0,1},{1,0},{2,3},{3,2},{4,5},{5,4},{6,7},{7,6},{8,9},{9,8},{10,11... | collective-permute-start | bytes 1179656 | tf_op jit(solution)/shard_map/ppermute | solution.py:733
  81.2 1.1 copy-start.6
  81.7 0.8 copy-start.7
  82.3 0.8 copy-start.8

commit v9 on v6

--- a/solution.py
+++ b/solution.py
@@ -359,13 +359,57 @@
     return low + high
 
 
+def fill_lookups(corner, unit, counts, here, after, shifts):
+    size = corner.shape[1]
+    coarse, shift = corner // SUB, corner % SUB
+
+    def looked_up(index, length, table):
+        place = lax.broadcasted_iota(jnp.int32, (length, size), 0)
+        one = (place == index).astype(f32).astype(bf16)
+        return lax.dot_general(one, table, (((0,), (0,)), ((), ())), preferred_element_type=f32)
+
+    here[...] = looked_up(coarse, FINE, unit).astype(bf16)
+    after[...] = looked_up(lax.rem(coarse + 1, FINE), FINE, unit).astype(bf16)
+    shifts[...] = looked_up(shift, SUB, counts)
+
+
+def lookup_kernel(corner_ref, unit_ref, count_ref, here, after, shifts):
+    fill_lookups(corner_ref[...], unit_ref[...], count_ref[...], here, after, shifts)
+
+
+def lookup_tables():
+    fine, low = np.arange(FINE), np.arange(LOW)
+    angle = 2.0 * math.pi / FINE * (fine[:, None] * low[None, :] % FINE)
+    odd = np.where(low == 0, 1.0 - 2.0 * (fine[:, None] % 2), np.sin(angle))
+    unit = jnp.asarray(np.concatenate([np.cos(angle), odd], axis=1), bf16)
+    counts = jnp.asarray(np.broadcast_to(np.arange(SUB)[:, None], (SUB, LANES)), bf16)
+    return unit, counts
+
+
+def lookups(corner_rows, interpret=False):
+    total = corner_rows.shape[0]
+    return pl.pallas_call(
+        lookup_kernel,
+        out_shape=[
+            jax.ShapeDtypeStruct((total, FINE), bf16),
+            jax.ShapeDtypeStruct((total, FINE), bf16),
+            jax.ShapeDtypeStruct((total, LANES), f32),
+        ],
+        compiler_params=pltpu.CompilerParams(vmem_limit_bytes=VMEM_BYTES),
+        cost_estimate=pl.CostEstimate(flops=0, bytes_accessed=8_000_000, transcendentals=0),
+        name="lookups",
+        interpret=interpret,
+    )(corner_rows.reshape(1, total), *lookup_tables())
+
+
 def image_kernel(
     info_ref, row_ref, col_ref, *refs, pieces, chunks, row_block, per_row, tile_cols
 ):
     uv_refs, refs = refs[:pieces], refs[pieces:]
-    corner_ref, phase_ref, columns_ref, unit_ref, count_ref, twist_ref = refs[:6]
-    out_ref, tile_ref, uv_wide, uv_rows, here, after, shifts, left_even, left_odd, total = refs[7:17]
-    staged, spill, list_ref, sem = refs[17:]
+    given, (phase_ref, columns_ref, twist_ref), refs = refs[:3], refs[3:6], refs[7:]
+    out_ref, tile_ref, uv_wide, uv_rows, left, total, staged, spill = refs[:8]
+    list_ref, sem = refs[8:10]
+    here, after, shifts = refs[10:] or given
     step = pl.program_id(0)
     lanes = 2 * tile_cols // LANES
     head = pltpu.make_async_copy(
@@ -396,7 +440,7 @@
     size = uv_rows.shape[1]
     image_rows = phase_ref.shape[1]
 
-    def products(pair, h, left):
+    def products(pair, h):
         at = pl.ds(2 * image_rows * h, 2 * image_rows)
         spread = lax.dot_general(
             columns_ref[at, :], uv_rows[pair], (((1,), (1,)), ((), ())), preferred_element_type=f32
@@ -405,19 +449,19 @@
         left[h, :image_rows] = turned[0]
         left[h, image_rows:] = turned[1]
 
-    def sums(pair, h, left, first):
-        index = pair + HALF * h
+    def table_of(index):
         late = shifts[...] > index.astype(f32)
-        table = jnp.concatenate(
+        return jnp.concatenate(
             [
                 jnp.where(late, after[:, t : t + LANES], here[:, t : t + LANES])
                 for t in range(0, FINE, LANES)
             ],
             axis=1,
         )
-        four = jnp.dot(left[h], table, preferred_element_type=f32)
-        even_re, odd_re = four[:image_rows, :LOW], four[:image_rows, LOW:]
-        even_im, odd_im = four[image_rows:, :LOW], four[image_rows:, LOW:]
+
+    def keep_sums(index, real, image, first):
+        even_re, odd_re = real[:, :LOW], real[:, LOW:]
+        even_im, odd_im = image[:, :LOW], image[:, LOW:]
         edge = lax.broadcasted_iota(jnp.int32, (image_rows, LOW), 1) == 0
         low = (
             even_re - jnp.where(edge, 0.0, odd_im),
@@ -437,6 +481,11 @@
                 at = (index, part, slice(None), pl.ds(LOW * half, LOW))
                 total[at] = done[part] if first else total[at] + done[part]
 
+    def sums(pair, h, first):
+        index = pair + HALF * h
+        four = jnp.dot(left[h], table_of(index), preferred_element_type=f32)
+        keep_sums(index, four[:image_rows], four[image_rows:], first)
+
     def chunk(first):
         if first:
             head.start()
@@ -457,30 +506,17 @@
             head.wait()
         add_spilled()
         pl.when(step == chunks - 1)(back.start)
-        corner = corner_ref[...]
-        coarse, shift = corner // SUB, corner % SUB
-
-        def looked_up(index, length, table):
-            place = lax.broadcasted_iota(jnp.int32, (length, size), 0)
-            one = (place == index).astype(f32).astype(bf16)
-            return lax.dot_general(one, table, (((0,), (0,)), ((), ())), preferred_element_type=f32)
-
-        here[...] = looked_up(coarse, FINE, unit_ref[...]).astype(bf16)
-        after[...] = looked_up(lax.rem(coarse + 1, FINE), FINE, unit_ref[...]).astype(bf16)
-        shifts[...] = looked_up(shift, SUB, count_ref[...])
-        for h in range(2):
-            products(0, h, left_even)
-
-        def two_pairs(i, carry):
+        if refs[10:]:
+            fill_lookups(given[0][...], given[1][...], given[2][...], here, after, shifts)
+
+        def one_pair(pair, carry):
             for h in range(2):
-                products(2 * i + 1, h, left_odd)
-                sums(2 * i, h, left_even, first)
+                products(pair, h)
             for h in range(2):
-                products(jnp.minimum(2 * i + 2, HALF - 1), h, left_even)
-                sums(2 * i + 1, h, left_odd, first)
+                sums(pair, h, first)
             return carry
 
-        lax.fori_loop(0, HALF // 2, two_pairs, 0)
+        lax.fori_loop(0, HALF, one_pair, 0)
         pl.when(step == chunks - 1)(back.wait)
 
     @pl.when(step == 0)
@@ -521,22 +557,27 @@
         lax.fori_loop(0, row_block // 8, eight_rows, 0)
 
 
-def image_tables(corner_cols, first_row, image_rows):
+def phase_table(corner_cols, first_row, image_rows):
     rows = first_row + jnp.arange(image_rows, dtype=jnp.int32)
-    turn = 2.0 * math.pi / G
-    angle = turn * (rows[:, None] * corner_cols[None, :] % G).astype(f32)
-    phase = jnp.stack([jnp.cos(angle), jnp.sin(angle)]).astype(bf16)
-    angle = turn * (rows[:, None] * jnp.arange(SUB, dtype=jnp.int32)[None, :] % G).astype(f32)
-    re, im = jnp.cos(angle), jnp.sin(angle)
-    block = jnp.concatenate(
-        [jnp.concatenate([re, -im], axis=1), jnp.concatenate([im, re], axis=1)], axis=0
-    )
-    columns = jnp.kron(jnp.eye(2, dtype=f32), block).astype(bf16)
-    return phase, columns
+    angle = 2.0 * math.pi / G * (rows[:, None] * corner_cols[None, :] % G).astype(f32)
+    return jnp.stack([jnp.cos(angle), jnp.sin(angle)]).astype(bf16)
+
+
+def column_table(first_row, image_rows):
+    lane, line = np.arange(PACK)[None, None, :], np.arange(4)[:, None, None]
+    angle = 2.0 * math.pi / G * (np.arange(image_rows)[None, :, None] * (lane % SUB))
+    angle = angle + 0.5 * math.pi * (lane // SUB % 2 - line % 2)
+    same = lane // (2 * SUB) == line // 2
+    re, im = [
+        jnp.asarray(np.where(same, f(angle), 0.0).reshape(-1, PACK), f32) for f in (np.cos, np.sin)
+    ]
+    turn = first_row * (jnp.arange(PACK, dtype=jnp.int32) % SUB) % G
+    turn = 2.0 * math.pi / G * turn.astype(f32)
+    return (re * jnp.cos(turn) - im * jnp.sin(turn)).astype(bf16)
 
 
 def image_rows_of(
-    uv, corners_all, tables, tile, info, per_row, tile_rows, tile_cols, interpret=False
+    uv, corners_all, tables, given, tile, info, per_row, tile_rows, tile_cols, interpret=False
 ):
     phase, columns = tables
     image_rows = phase.shape[1]
@@ -549,15 +590,11 @@
     outs = image_rows // row_block
     wide = 2 * G // LANES
     fine, low = np.arange(FINE), np.arange(LOW)
-    angle = 2.0 * math.pi / FINE * (fine[:, None] * low[None, :] % FINE)
-    odd = np.where(low == 0, 1.0 - 2.0 * (fine[:, None] % 2), np.sin(angle))
-    unit = jnp.asarray(np.concatenate([np.cos(angle), odd], axis=1), bf16)
     scale = 1.0 / (SUB * math.sqrt(total))
     high = np.where(low == 0, LOW, FINE - low)
     angles = [2.0 * math.pi / G * (np.arange(SUB)[:, None] * k[None, :]) for k in (low, high)]
     twist = [f(angle) * scale for angle in angles for f in (np.cos, np.sin)]
     twist = jnp.asarray(np.concatenate(twist, axis=1), f32)
-    counts = jnp.asarray(np.broadcast_to(np.arange(SUB)[:, None], (SUB, LANES)), bf16)
     last = chunks - 1
 
     def chunk_of(i):
@@ -570,6 +607,17 @@
 
     def fixed(operand):
         return pl.BlockSpec(operand.shape, lambda i, *_: (0, 0))
+
+    given_specs = [fixed(operand) for operand in given or ()]
+    scratch = []
+    if not given:
+        given = [corners_all[0].reshape(1, total), *lookup_tables()]
+        given_specs = [pl.BlockSpec((1, size), lambda i, *_: (0, chunk_of(i))), *map(fixed, given[1:])]
+        scratch = [
+            pltpu.VMEM((size, FINE), bf16),
+            pltpu.VMEM((size, FINE), bf16),
+            pltpu.VMEM((size, LANES), f32),
+        ]
 
     image, tile = pl.pallas_call(
         functools.partial(
@@ -581,11 +629,9 @@
             grid=(chunks + outs,),
             in_specs=[
                 *uv_specs,
-                pl.BlockSpec((1, size), lambda i, *_: (0, chunk_of(i))),
+                *given_specs,
                 pl.BlockSpec((2, image_rows, size), lambda i, *_: (0, 0, chunk_of(i))),
                 fixed(columns),
-                fixed(unit),
-                fixed(counts),
                 fixed(twist),
                 pl.BlockSpec(memory_space=pl.ANY),
             ],
@@ -598,16 +644,13 @@
             scratch_shapes=[
                 pltpu.VMEM((size * (HALF + 1) + HALF, PACK), f32),
                 pltpu.VMEM((HALF, size, PACK), bf16),
-                pltpu.VMEM((size, FINE), bf16),
-                pltpu.VMEM((size, FINE), bf16),
-                pltpu.VMEM((size, LANES), f32),
-                pltpu.VMEM((2, 2 * image_rows, size), bf16),
                 pltpu.VMEM((2, 2 * image_rows, size), bf16),
                 pltpu.VMEM((SUB, 2, image_rows, FINE), f32),
                 pltpu.VMEM((8 * (wide + 1) + wide, LANES), f32),
                 pltpu.VMEM((3 * SUB * lanes, LANES), f32),
                 pltpu.SMEM((per_row + 1,), jnp.int32),
                 pltpu.SemaphoreType.DMA(()),
+                *scratch,
             ],
         ),
         out_shape=[
@@ -620,7 +663,7 @@
         interpret=interpret,
     )(
         info, *corners_all, *uv,
-        corners_all[0].reshape(1, total), phase, columns, unit, counts, twist, tile,
+        *given, phase, columns, twist, tile,
     )
     image = image.reshape(image_rows, G // LANES, 2, LANES)
     tile = tile.reshape(tile_rows, tile_cols // LANES, 2, LANES)
@@ -663,10 +706,10 @@
     return lax.ppermute(value, axis, [(i, i ^ mask) for i in range(count)])
 
 
-def z_line(own, with_own):
+def z_line(own):
     vert_count = lax.axis_size("vert")
-    line = [from_partner(own, "vert", 2 * mask) for mask in range(1, vert_count // 2)]
-    return jnp.concatenate([own] * with_own + line, axis=0)
+    line = [own] + [from_partner(own, "vert", 2 * mask) for mask in range(1, vert_count // 2)]
+    return jnp.concatenate(line, axis=0)
 
 
 def au_lines(line):
@@ -722,7 +765,7 @@
     part = math.gcd(count, 8)
     skies = [sky_sums(visibilities, offsets, scale_row, 0, part)]
     if by_mask:
-        line = z_line(sent, True)
+        line = z_line(sent)
         line, offsets, skies[0], corners, stations, screen_depth = lax.optimization_barrier(
             (line, offsets, skies[0], corners, stations, screen_depth)
         )
@@ -753,24 +796,27 @@
     own_info = tile_info(au_index)
     before_info = tile_info(lax.rem(au_index + au_count - 1, au_count))
     first_row = (au_index * vert_count + vert_index) * image_rows
-    tables = image_tables(corners_all[1], first_row, image_rows)
+    phase = phase_table(corners_all[1], first_row, image_rows)
     if by_mask:
-        blocks, line = au_lines(uv_own), z_line(uv_own, False)
-        blocks, line, tables, corners_all, own_info, before_info = lax.optimization_barrier(
-            (blocks, line, tables, corners_all, own_info, before_info)
+        line = z_line(uv_own)
+        line, phase, corners_all, own_info, before_info, first_row = lax.optimization_barrier(
+            (line, phase, corners_all, own_info, before_info, first_row)
         )
         lines = au_lines(line)
-        own_row = [uv_own, line] + [from_partner(piece, "vert", 1) for piece in (uv_own, line)]
+        own_row = with_core(lines[:1])
         tile = uv_tile_own(own_row, own_info, corners_all, per_row, tile_rows, tile_cols)
-        lines, own_row, tile = lax.optimization_barrier((lines, own_row, tile))
-        uv = own_row
-        for pair in zip(blocks[1:], lines[1:]):
-            uv = uv + [*pair, *[from_partner(piece, "vert", 1) for piece in pair]]
+        given = lookups(corners_all[0])
+        columns = column_table(first_row, image_rows)
+        lines, own_row, tile, given, columns = lax.optimization_barrier(
+            (lines, own_row, tile, given, columns)
+        )
+        uv = own_row + with_core(lines[1:])
     else:
-        uv = whole_gather(uv_own)
+        uv, given = whole_gather(uv_own), None
+        columns = column_table(first_row, image_rows)
         tile = uv_tile_own(uv, own_info, corners_all, per_row, tile_rows, tile_cols)
     return image_rows_of(
-        uv, corners_all, tables, tile, before_info, per_row, tile_rows, tile_cols
+        uv, corners_all, (phase, columns), given, tile, before_info, per_row, tile_rows, tile_cols
     )
 
 

time: 125 us -> 119 us (0.952)
  the two profiles are of different devices: /device:TPU:25 before, /device:TPU:17 now
where the time goes in v9:
time: 119 us; the launch traced here: 118 us
  Pallas kernels  70.2 us (59%)
  starting transfers between devices  21.2 us (18%)
  other arithmetic  12.6 us (11%)
  local copies, waits for them, and re-layouts  9.18 us (8%)
  waiting for transfers between devices  3.7 us (3%)
    pallas_call x1, Pallas kernels, image_rows_of(): pl.pallas_call(functools.partial(image_kernel, pieces=len(uv), chunks=chu...  35.2 us
    ppermute x20, starting transfers between devices, from_partner(): return lax.ppermute(value, axis, [(i, i ^ mask) for i in range(count)])  21.2 us
    pallas_call x3, Pallas kernels, sky_sums(): pl.pallas_call(sky_kernel, grid=(1,), in_specs=[pl.BlockSpec((count, 2, v...  13.8 us
    pallas_call x1, Pallas kernels, uv_tile_own(): pl.pallas_call(functools.partial(tile_kernel, pieces=len(uv), tile_rows=t...  12.2 us
    pallas_call x1, Pallas kernels, corrected_subgrids(): pl.pallas_call(functools.partial(correct_kernel, pieces=len(tables), skie...  6.66 us
    unnamed x56, local copies, waits for them, and re-layouts  6.02 us
    ppermute x20, waiting for transfers between devices, from_partner(): return lax.ppermute(value, axis, [(i, i ^ mask) for i in range(count)])  3.7 us
    another operation x1, other arithmetic  3.47 us
  transfers between devices with their start and end apart: 20, of which 5 were waited for; matrix products, arithmetic and copies ran while one was open for 13% of the time, Pallas kernels for 24%

profile of v9, /device:TPU:17, one launch (start us, length us, event | category | flops | bytes accessed | tf_op | source)
XLA Modules:
  0.0 117.9 jit_solution(6987748707358641896)
XLA Ops:
  0.6 0.8 and_select_fusion.15
  1.4 0.1 convert_element_type.85
  1.5 1.0 reshape.669
  2.6 0.2 copy.42
  2.8 0.2 reshape.670
  3.0 0.2 collective-permute-start.2
  3.3 3.2 %collective-permute-start.1 = (bf16[17,16,128]{2,1,0:T(8,128)(2,1)S(1)}, bf16[17,16,128]{2,1,0:T(8,128)(2,1)S(1)}, u32[]{:S(2)}, u32[]{:S(2)}) collective-permute-start(bf16[17,16,128]{2,1,0:T(8,128)(2,1)S(1)} %pad_maximum_fusion.2), channel_id=1, source_target_pairs={{0,4},{1,5},{2,6},{3,7},{4,0},{5,1},{6,2},{7,3},{8,12},{9,13},{10,... | collective-permute-start | bytes 208904 | tf_op jit(solution)/shard_map/ppermute | solution.py:706
  6.6 4.6 %sky_sums.3.refs_8_ = f32[8,16,128]{2,1,0:T(8,128)} custom-call(bf16[24,2,2048]{2,1,0:T(2,128)(2,1)} %vis_ref.5, f32[48,128]{1,0:T(8,128)} %bitcast.135, f32[1,16]{1,0:T(1,128)} %bitcast.146), custom_call_target="tpu_custom_call" | custom-call | bytes 20000000 | tf_op jit(solution)/shard_map/sky_sums/pallas_call | solution.py:119
  11.2 0.6 add_add_fusion
  11.9 2.2 %collective-permute-start.5 = (bf16[68,16,128]{2,1,0:T(8,128)(2,1)S(1)}, bf16[68,16,128]{2,1,0:T(8,128)(2,1)S(1)}, u32[]{:S(2)}, u32[]{:S(2)}) collective-permute-start(bf16[68,16,128]{2,1,0:T(8,128)(2,1)S(1)} %constant_dynamic-update-slice_fusion.refs_0_), channel_id=1, source_target_pairs={{0,24},{8,16},{16,8},{24,0},{1,25},{9,17},{17,9},{25,1},{2,26},{10... | collective-permute-start | bytes 835592 | tf_op jit(solution)/shard_map/ppermute | solution.py:706
  14.2 0.2 collective-permute-start.4
  14.4 0.3 collective-permute-start.3
  14.6 0.7 fusion.16
  15.4 0.7 and_select_fusion.3
  16.0 0.7 broadcast_multiply_fusion
  16.7 4.6 %sky_sums.5.refs_10_ = f32[8,16,128]{2,1,0:T(8,128)} custom-call(bf16[24,2,2048]{2,1,0:T(2,128)(2,1)} %vis_ref.5, f32[48,128]{1,0:T(8,128)} %bitcast.136, f32[1,16]{1,0:T(1,128)} %bitcast.147), custom_call_target="tpu_custom_call" | custom-call | bytes 20000000 | tf_op jit(solution)/shard_map/sky_sums/pallas_call | solution.py:119
  21.3 4.6 %sky_sums.4.refs_9_ = f32[8,16,128]{2,1,0:T(8,128)} custom-call(bf16[24,2,2048]{2,1,0:T(2,128)(2,1)} %vis_ref.5, f32[48,128]{1,0:T(8,128)} %bitcast.137, f32[1,16]{1,0:T(1,128)} %bitcast.148), custom_call_target="tpu_custom_call" | custom-call | bytes 20000000 | tf_op jit(solution)/shard_map/sky_sums/pallas_call | solution.py:119
  25.9 0.1 copy.22
  26.0 0.6 reshape.674.stations_ref
  26.6 1.5 %fusion.8.refs_11_ = f32[24,16,128]{2,1,0:T(8,128)} fusion(f32[16,128]{1,0:T(8,128)S(1)} %get-tuple-element.83, f32[128]{0:T(128)S(1)} %fusion.19, s32[16,128]{1,0:T(8,128)S(1)} %fusion.10, s32[24]{0:T(128)S(1)} %and_select_fusion.3, f32[16,128]{1,0:T(8,128)S(1)} %get-tuple-element.82, f32[24]{0:T(128)S(1)} %broadcast_multiply_fusion), kind=kLoop, calls=%fused_computation.24 | loop fusion | flops 884736 | bytes 221888 | tf_op jit(solution)/shard_map/mul | solution.py:701
  28.2 2.1 %collective-permute-start.9 = (bf16[68,16,128]{2,1,0:T(8,128)(2,1)S(1)}, bf16[68,16,128]{2,1,0:T(8,128)(2,1)S(1)}, u32[]{:S(2)}, u32[]{:S(2)}) collective-permute-start(bf16[68,16,128]{2,1,0:T(8,128)(2,1)S(1)} %collective-permute-done.5.refs_6_), channel_id=1, source_target_pairs={{0,1},{1,0},{2,3},{3,2},{4,5},{5,4},{6,7},{7,6},{8,9},{9,8},{10,11... | collective-permute-start | bytes 835592 | tf_op jit(solution)/shard_map/ppermute | solution.py:706
  30.3 0.1 collective-permute-start.8
  30.4 0.4 collective-permute-start.6
  30.8 0.1 collective-permute-start.7
  31.0 1.3 %collective-permute-done.6.refs_1_ = bf16[68,16,128]{2,1,0:T(8,128)(2,1)S(1)} collective-permute-done((bf16[68,16,128]{2,1,0:T(8,128)(2,1)S(1)}, bf16[68,16,128]{2,1,0:T(8,128)(2,1)S(1)}, u32[]{:S(2)}, u32[]{:S(2)}) %collective-permute-start.6) | collective-permute-done | bytes 278560 | tf_op jit(solution)/shard_map/ppermute | solution.py:706
  32.3 0.4 collective-permute-done.7.refs_3_
  32.8 0.3 copy-done.14
  33.0 0.4 copy-done.15
  33.4 0.1 copy-done.13
  33.5 0.7 copy-done.12
  34.2 6.7 %correct.1 = bf16[24,16,128]{2,1,0:T(8,128)(2,1)} custom-call(s32[48]{0:T(128)} %reshape.674.stations_ref, bf16[68,16,128]{2,1,0:T(8,128)(2,1)} %copy-done.2, bf16[68,16,128]{2,1,0:T(8,128)(2,1)} %copy-done.14, bf16[68,16,128]{2,1,0:T(8,128)(2,1)} %copy-done.11, bf16[68,16,128]{2,1,0:T(8,128)(2,1)} %copy-done.15, bf16[68,16,128]{2,1,0:T(8,128)(2,1)} %copy-done.10, ...), custom_call_target="tpu_custom_call" | custom-call | bytes 16000000 | tf_op jit(solution)/shard_map/correct/pallas_call | solution.py:194
  40.9 0.3 collective-permute-start.12
  41.2 3.5 %collective-permute-start.11 = (bf16[24,16,128]{2,1,0:T(8,128)(2,1)}, bf16[24,16,128]{2,1,0:T(8,128)(2,1)S(1)}, u32[]{:S(2)}, u32[]{:S(2)}) collective-permute-start(bf16[24,16,128]{2,1,0:T(8,128)(2,1)} %correct.1), channel_id=1, source_target_pairs={{0,4},{1,5},{2,6},{3,7},{4,0},{5,1},{6,2},{7,3},{8,12},{9,13},{10,... | collective-permute-start | bytes 294920 | tf_op jit(solution)/shard_map/ppermute | solution.py:706
  44.7 0.7 slice_bitcast_fusion.6
  45.5 0.7 slice_bitcast_fusion.4
  46.2 0.7 slice_bitcast_fusion.2
  46.9 0.7 slice_bitcast_fusion
  47.7 0.1 concatenate.41
  47.8 0.1 slice_add_fusion
  47.9 0.1 add.327.row_ref
  48.0 0.1 add.324.col_ref
  48.1 3.5 %cosine_convert_fusion = (bf16[1,256,768]{2,1,0:T(8,128)(2,1)S(1)}, bf16[1,256,768]{2,1,0:T(8,128)(2,1)S(1)}) fusion(s32[768]{0:T(1024)S(1)} %add.324.col_ref, s32[256]{0:T(256)S(1)} %iota_add_fusion.1), kind=kLoop, calls=%fused_computation.10 | loop fusion | flops 3145728 | bytes 790528 | tf_op jit(solution)/shard_map/convert
  51.6 1.0 pad_maximum_fusion.refs_11_
  52.6 0.9 pad_maximum_fusion.1
  53.5 1.0 collective-permute-start.16
  54.5 2.2 %collective-permute-start.15 = (bf16[96,16,128]{2,1,0:T(8,128)(2,1)S(1)}, bf16[96,16,128]{2,1,0:T(8,128)(2,1)S(1)}, u32[]{:S(2)}, u32[]{:S(2)}) collective-permute-start(bf16[96,16,128]{2,1,0:T(8,128)(2,1)S(1)} %pad_maximum_fusion.1), channel_id=1, source_target_pairs={{0,24},{8,16},{16,8},{24,0},{1,25},{9,17},{17,9},{25,1},{2,26},{10... | collective-permute-start | bytes 1179656 | tf_op jit(solution)/shard_map/ppermute | solution.py:706
  56.7 0.2 collective-permute-start.14
  56.9 0.3 collective-permute-start.13
  57.2 0.1 fusion.25
  57.2 0.6 reshape.685.corner_ref
  57.8 2.3 %lookups.1 = (bf16[768,256]{1,0:T(8,128)(2,1)}, bf16[768,256]{1,0:T(8,128)(2,1)}, f32[768,128]{1,0:T(8,128)}) custom-call(s32[1,768]{1,0:T(1,128)} %reshape.685.corner_ref, bf16[256,256]{1,0:T(8,128)(2,1)} %constant.325.clone.unit_ref, bf16[32,128]{1,0:T(8,128)(2,1)} %constant.326.clone.count_ref), custom_call_target="tpu_custom_call" | custom-call | bytes 8000000 | tf_op jit(solution)/shard_map/lookups/pallas_call | solution.py:391
  60.2 0.1 fusion.26
  60.2 2.0 %subtract_convert_fusion.refs_12_ = bf16[1024,128]{1,0:T(8,128)(2,1)} fusion(f32[1024,128]{1,0:T(8,128)} %constant.328.clone, f32[1024,128]{1,0:T(8,128)} %constant.327.clone, f32[128]{0:T(128)S(1)} %fusion.25, f32[128]{0:T(128)S(1)} %fusion.26), kind=kLoop, calls=%fused_computation.11 | loop fusion | flops 524288 | bytes 1311744 | tf_op jit(solution)/shard_map/convert_element_type | solution.py:576
  62.2 0.7 copy-done.1
  62.9 12.2 %uv_tile.1.refs_14_ = f32[32768,128]{1,0:T(8,128)} custom-call(s32[3]{0:T(128)} %get-tuple-element.54.info_ref, s32[768]{0:T(1024)} %copy-done.17, s32[768]{0:T(1024)} %copy-done.16, bf16[1536,128]{1,0:T(8,128)(2,1)} %bitcast.116, bf16[1536,128]{1,0:T(8,128)(2,1)} %bitcast.118), custom_call_target="tpu_custom_call" | custom-call | bytes 41943040 | tf_op jit(solution)/shard_map/uv_tile/pallas_call | solution.py:309
  75.2 4.3 %collective-permute-start.17 = (bf16[96,16,128]{2,1,0:T(8,128)(2,1)S(1)}, bf16[96,16,128]{2,1,0:T(8,128)(2,1)S(1)}, u32[]{:S(2)}, u32[]{:S(2)}) collective-permute-start(bf16[96,16,128]{2,1,0:T(8,128)(2,1)S(1)} %collective-permute-done.13), channel_id=1, source_target_pairs={{0,1},{1,0},{2,3},{3,2},{4,5},{5,4},{6,7},{7,6},{8,9},{9,8},{10,11... | collective-permute-start | bytes 1179656 | tf_op jit(solution)/shard_map/ppermute | solution.py:706
  79.5 0.1 collective-permute-start.18
  79.6 0.4 collective-permute-start.19
  80.0 0.8 collective-permute-done.17
  80.9 0.6 collective-permute-done.18
  81.4 0.6 collective-permute-done.19
  82.0 0.2 copy-done.7
  82.2 0.6 copy-done.8
  82.7 35.2 %image.1 = (f32[32768,128]{1,0:T(8,128)}, f32[32768,128]{1,0:T(8,128)}) custom-call(s32[3]{0:T(128)} %get-tuple-element.50.info_ref, s32[768]{0:T(1024)} %copy-done.17, s32[768]{0:T(1024)} %copy-done.16, bf16[1536,128]{1,0:T(8,128)(2,1)} %bitcast.117, bf16[1536,128]{1,0:T(8,128)(2,1)} %bitcast.119, ...), custom_call_target="tpu_custom_call", output_to_operand_aliasing={{1}: (17, {})} | custom-call | tf_op jit(solution)/shard_map/image/pallas_call | solution.py:622
  (74 shorter events, 0.4 us)
Async XLA Ops:
  3.0 8.9 %collective-permute-start.2 = (bf16[17,16,128]{2,1,0:T(8,128)(2,1)S(1)}, bf16[17,16,128]{2,1,0:T(8,128)(2,1)S(1)}, u32[]{:S(2)}, u32[]{:S(2)}) collective-permute-start(bf16[17,16,128]{2,1,0:T(8,128)(2,1)S(1)} %pad_maximum_fusion.2), channel_id=1, source_target_pairs={{0,6},{1,7},{2,4},{3,5},{4,2},{5,3},{6,0},{7,1},{8,14},{9,15},{10,... | collective-permute-start | bytes 208904 | tf_op jit(solution)/shard_map/ppermute | solution.py:706
  3.3 8.6 %collective-permute-start.1 = (bf16[17,16,128]{2,1,0:T(8,128)(2,1)S(1)}, bf16[17,16,128]{2,1,0:T(8,128)(2,1)S(1)}, u32[]{:S(2)}, u32[]{:S(2)}) collective-permute-start(bf16[17,16,128]{2,1,0:T(8,128)(2,1)S(1)} %pad_maximum_fusion.2), channel_id=1, source_target_pairs={{0,4},{1,5},{2,6},{3,7},{4,0},{5,1},{6,2},{7,3},{8,12},{9,13},{10,... | collective-permute-start | bytes 208904 | tf_op jit(solution)/shard_map/ppermute | solution.py:706
  6.5 5.4 %collective-permute-start = (bf16[17,16,128]{2,1,0:T(8,128)(2,1)S(1)}, bf16[17,16,128]{2,1,0:T(8,128)(2,1)S(1)}, u32[]{:S(2)}, u32[]{:S(2)}) collective-permute-start(bf16[17,16,128]{2,1,0:T(8,128)(2,1)S(1)} %pad_maximum_fusion.2), channel_id=1, source_target_pairs={{0,2},{1,3},{2,0},{3,1},{4,6},{5,7},{6,4},{7,5},{8,10},{9,11},{10,... | collective-permute-start | bytes 208904 | tf_op jit(solution)/shard_map/ppermute | solution.py:706
  11.9 20.8 %copy-start.2 = (bf16[68,16,128]{2,1,0:T(8,128)(2,1)}, bf16[68,16,128]{2,1,0:T(8,128)(2,1)S(1)}, u32[]{:S(2)}) copy-start(bf16[68,16,128]{2,1,0:T(8,128)(2,1)S(1)} %constant_dynamic-update-slice_fusion.refs_0_) | copy-start | bytes 835588
  11.9 16.2 %collective-permute-start.5 = (bf16[68,16,128]{2,1,0:T(8,128)(2,1)S(1)}, bf16[68,16,128]{2,1,0:T(8,128)(2,1)S(1)}, u32[]{:S(2)}, u32[]{:S(2)}) collective-permute-start(bf16[68,16,128]{2,1,0:T(8,128)(2,1)S(1)} %constant_dynamic-update-slice_fusion.refs_0_), channel_id=1, source_target_pairs={{0,24},{8,16},{16,8},{24,0},{1,25},{9,17},{17,9},{25,1},{2,26},{10... | collective-permute-start | bytes 835592 | tf_op jit(solution)/shard_map/ppermute | solution.py:706
  14.2 14.0 %collective-permute-start.4 = (bf16[68,16,128]{2,1,0:T(8,128)(2,1)S(1)}, bf16[68,16,128]{2,1,0:T(8,128)(2,1)S(1)}, u32[]{:S(2)}, u32[]{:S(2)}) collective-permute-start(bf16[68,16,128]{2,1,0:T(8,128)(2,1)S(1)} %constant_dynamic-update-slice_fusion.refs_0_), channel_id=1, source_target_pairs={{0,16},{8,24},{16,0},{24,8},{1,17},{9,25},{17,1},{25,9},{2,18},{10... | collective-permute-start | bytes 835592 | tf_op jit(solution)/shard_map/ppermute | solution.py:706
  14.4 13.8 %collective-permute-start.3 = (bf16[68,16,128]{2,1,0:T(8,128)(2,1)S(1)}, bf16[68,16,128]{2,1,0:T(8,128)(2,1)S(1)}, u32[]{:S(2)}, u32[]{:S(2)}) collective-permute-start(bf16[68,16,128]{2,1,0:T(8,128)(2,1)S(1)} %constant_dynamic-update-slice_fusion.refs_0_), channel_id=1, source_target_pairs={{0,8},{8,0},{16,24},{24,16},{1,9},{9,1},{17,25},{25,17},{2,10},{10... | collective-permute-start | bytes 835592 | tf_op jit(solution)/shard_map/ppermute | solution.py:706
  28.1 4.6 %copy-start.9 = (bf16[68,16,128]{2,1,0:T(8,128)(2,1)}, bf16[68,16,128]{2,1,0:T(8,128)(2,1)S(1)}, u32[]{:S(2)}) copy-start(bf16[68,16,128]{2,1,0:T(8,128)(2,1)S(1)} %collective-permute-done.5.refs_6_) | copy-start | bytes 835588
  28.2 4.6 %copy-start.10 = (bf16[68,16,128]{2,1,0:T(8,128)(2,1)}, bf16[68,16,128]{2,1,0:T(8,128)(2,1)S(1)}, u32[]{:S(2)}) copy-start(bf16[68,16,128]{2,1,0:T(8,128)(2,1)S(1)} %collective-permute-done.4.refs_4_) | copy-start | bytes 835588
  28.2 4.6 %copy-start.11 = (bf16[68,16,128]{2,1,0:T(8,128)(2,1)}, bf16[68,16,128]{2,1,0:T(8,128)(2,1)S(1)}, u32[]{:S(2)}) copy-start(bf16[68,16,128]{2,1,0:T(8,128)(2,1)S(1)} %collective-permute-done.3.refs_2_) | copy-start | bytes 835588
  28.2 4.5 %collective-permute-start.9 = (bf16[68,16,128]{2,1,0:T(8,128)(2,1)S(1)}, bf16[68,16,128]{2,1,0:T(8,128)(2,1)S(1)}, u32[]{:S(2)}, u32[]{:S(2)}) collective-permute-start(bf16[68,16,128]{2,1,0:T(8,128)(2,1)S(1)} %collective-permute-done.5.refs_6_), channel_id=1, source_target_pairs={{0,1},{1,0},{2,3},{3,2},{4,5},{5,4},{6,7},{7,6},{8,9},{9,8},{10,11... | collective-permute-start | bytes 835592 | tf_op jit(solution)/shard_map/ppermute | solution.py:706
  30.3 2.4 %collective-permute-start.8 = (bf16[68,16,128]{2,1,0:T(8,128)(2,1)S(1)}, bf16[68,16,128]{2,1,0:T(8,128)(2,1)S(1)}, u32[]{:S(2)}, u32[]{:S(2)}) collective-permute-start(bf16[68,16,128]{2,1,0:T(8,128)(2,1)S(1)} %collective-permute-done.4.refs_4_), channel_id=1, source_target_pairs={{0,1},{1,0},{2,3},{3,2},{4,5},{5,4},{6,7},{7,6},{8,9},{9,8},{10,11... | collective-permute-start | bytes 835592 | tf_op jit(solution)/shard_map/ppermute | solution.py:706
  30.4 1.9 %collective-permute-start.6 = (bf16[68,16,128]{2,1,0:T(8,128)(2,1)S(1)}, bf16[68,16,128]{2,1,0:T(8,128)(2,1)S(1)}, u32[]{:S(2)}, u32[]{:S(2)}) collective-permute-start(bf16[68,16,128]{2,1,0:T(8,128)(2,1)S(1)} %constant_dynamic-update-slice_fusion.refs_0_), channel_id=1, source_target_pairs={{0,1},{1,0},{2,3},{3,2},{4,5},{5,4},{6,7},{7,6},{8,9},{9,8},{10,11... | collective-permute-start | bytes 835592 | tf_op jit(solution)/shard_map/ppermute | solution.py:706
  30.8 1.9 %collective-permute-start.7 = (bf16[68,16,128]{2,1,0:T(8,128)(2,1)S(1)}, bf16[68,16,128]{2,1,0:T(8,128)(2,1)S(1)}, u32[]{:S(2)}, u32[]{:S(2)}) collective-permute-start(bf16[68,16,128]{2,1,0:T(8,128)(2,1)S(1)} %collective-permute-done.3.refs_2_), channel_id=1, source_target_pairs={{0,1},{1,0},{2,3},{3,2},{4,5},{5,4},{6,7},{7,6},{8,9},{9,8},{10,11... | collective-permute-start | bytes 835592 | tf_op jit(solution)/shard_map/ppermute | solution.py:706
  32.3 0.7 copy-start.14
  32.7 0.7 copy-start.15
  32.7 0.8 copy-start.13
  33.5 0.7 copy-start.12
  40.9 11.7 %collective-permute-start.12 = (bf16[24,16,128]{2,1,0:T(8,128)(2,1)}, bf16[24,16,128]{2,1,0:T(8,128)(2,1)S(1)}, u32[]{:S(2)}, u32[]{:S(2)}) collective-permute-start(bf16[24,16,128]{2,1,0:T(8,128)(2,1)} %correct.1), channel_id=1, source_target_pairs={{0,6},{1,7},{2,4},{3,5},{4,2},{5,3},{6,0},{7,1},{8,14},{9,15},{10,... | collective-permute-start | bytes 294920 | tf_op jit(solution)/shard_map/ppermute | solution.py:706
  41.2 11.4 %collective-permute-start.11 = (bf16[24,16,128]{2,1,0:T(8,128)(2,1)}, bf16[24,16,128]{2,1,0:T(8,128)(2,1)S(1)}, u32[]{:S(2)}, u32[]{:S(2)}) collective-permute-start(bf16[24,16,128]{2,1,0:T(8,128)(2,1)} %correct.1), channel_id=1, source_target_pairs={{0,4},{1,5},{2,6},{3,7},{4,0},{5,1},{6,2},{7,3},{8,12},{9,13},{10,... | collective-permute-start | bytes 294920 | tf_op jit(solution)/shard_map/ppermute | solution.py:706
  44.7 7.8 %collective-permute-start.10 = (bf16[24,16,128]{2,1,0:T(8,128)(2,1)}, bf16[24,16,128]{2,1,0:T(8,128)(2,1)S(1)}, u32[]{:S(2)}, u32[]{:S(2)}) collective-permute-start(bf16[24,16,128]{2,1,0:T(8,128)(2,1)} %correct.1), channel_id=1, source_target_pairs={{0,2},{1,3},{2,0},{3,1},{4,6},{5,7},{6,4},{7,5},{8,10},{9,11},{10,... | collective-permute-start | bytes 294920 | tf_op jit(solution)/shard_map/ppermute | solution.py:706
  48.0 14.2 %copy-start.17 = (s32[768]{0:T(1024)}, s32[768]{0:T(1024)S(1)}, u32[]{:S(2)}) copy-start(s32[768]{0:T(1024)S(1)} %add.327.row_ref) | copy-start | bytes 9220
  48.1 14.1 %copy-start.16 = (s32[768]{0:T(1024)}, s32[768]{0:T(1024)S(1)}, u32[]{:S(2)}) copy-start(s32[768]{0:T(1024)S(1)} %add.324.col_ref) | copy-start | bytes 9220
  53.5 8.7 %copy-start = (bf16[96,16,128]{2,1,0:T(8,128)(2,1)}, bf16[96,16,128]{2,1,0:T(8,128)(2,1)S(1)}, u32[]{:S(2)}) copy-start(bf16[96,16,128]{2,1,0:T(8,128)(2,1)S(1)} %pad_maximum_fusion.1) | copy-start | bytes 1179652
  53.5 8.7 %collective-permute-start.16 = (bf16[96,16,128]{2,1,0:T(8,128)(2,1)S(1)}, bf16[96,16,128]{2,1,0:T(8,128)(2,1)S(1)}, u32[]{:S(2)}, u32[]{:S(2)}) collective-permute-start(bf16[96,16,128]{2,1,0:T(8,128)(2,1)S(1)} %pad_maximum_fusion.1), channel_id=1, source_target_pairs={{0,1},{1,0},{2,3},{3,2},{4,5},{5,4},{6,7},{7,6},{8,9},{9,8},{10,11... | collective-permute-start | bytes 1179656 | tf_op jit(solution)/shard_map/ppermute | solution.py:706
  54.5 20.6 %collective-permute-start.15 = (bf16[96,16,128]{2,1,0:T(8,128)(2,1)S(1)}, bf16[96,16,128]{2,1,0:T(8,128)(2,1)S(1)}, u32[]{:S(2)}, u32[]{:S(2)}) collective-permute-start(bf16[96,16,128]{2,1,0:T(8,128)(2,1)S(1)} %pad_maximum_fusion.1), channel_id=1, source_target_pairs={{0,24},{8,16},{16,8},{24,0},{1,25},{9,17},{17,9},{25,1},{2,26},{10... | collective-permute-start | bytes 1179656 | tf_op jit(solution)/shard_map/ppermute | solution.py:706
  56.7 18.4 %collective-permute-start.14 = (bf16[96,16,128]{2,1,0:T(8,128)(2,1)S(1)}, bf16[96,16,128]{2,1,0:T(8,128)(2,1)S(1)}, u32[]{:S(2)}, u32[]{:S(2)}) collective-permute-start(bf16[96,16,128]{2,1,0:T(8,128)(2,1)S(1)} %pad_maximum_fusion.1), channel_id=1, source_target_pairs={{0,16},{8,24},{16,0},{24,8},{1,17},{9,25},{17,1},{25,9},{2,18},{10... | collective-permute-start | bytes 1179656 | tf_op jit(solution)/shard_map/ppermute | solution.py:706
  56.9 18.2 %collective-permute-start.13 = (bf16[96,16,128]{2,1,0:T(8,128)(2,1)S(1)}, bf16[96,16,128]{2,1,0:T(8,128)(2,1)S(1)}, u32[]{:S(2)}, u32[]{:S(2)}) collective-permute-start(bf16[96,16,128]{2,1,0:T(8,128)(2,1)S(1)} %pad_maximum_fusion.1), channel_id=1, source_target_pairs={{0,8},{8,0},{16,24},{24,16},{1,9},{9,1},{17,25},{25,17},{2,10},{10... | collective-permute-start | bytes 1179656 | tf_op jit(solution)/shard_map/ppermute | solution.py:706
  62.2 0.8 copy-start.1
  75.1 6.8 %copy-start.3 = (bf16[96,16,128]{2,1,0:T(8,128)(2,1)}, bf16[96,16,128]{2,1,0:T(8,128)(2,1)S(1)}, u32[]{:S(2)}) copy-start(bf16[96,16,128]{2,1,0:T(8,128)(2,1)S(1)} %collective-permute-done.15) | copy-start | bytes 1179652
  75.2 6.8 %copy-start.4 = (bf16[96,16,128]{2,1,0:T(8,128)(2,1)}, bf16[96,16,128]{2,1,0:T(8,128)(2,1)S(1)}, u32[]{:S(2)}) copy-start(bf16[96,16,128]{2,1,0:T(8,128)(2,1)S(1)} %collective-permute-done.14) | copy-start | bytes 1179652
  75.2 6.8 %copy-start.5 = (bf16[96,16,128]{2,1,0:T(8,128)(2,1)}, bf16[96,16,128]{2,1,0:T(8,128)(2,1)S(1)}, u32[]{:S(2)}) copy-start(bf16[96,16,128]{2,1,0:T(8,128)(2,1)S(1)} %collective-permute-done.13) | copy-start | bytes 1179652
  75.2 5.7 %collective-permute-start.17 = (bf16[96,16,128]{2,1,0:T(8,128)(2,1)S(1)}, bf16[96,16,128]{2,1,0:T(8,128)(2,1)S(1)}, u32[]{:S(2)}, u32[]{:S(2)}) collective-permute-start(bf16[96,16,128]{2,1,0:T(8,128)(2,1)S(1)} %collective-permute-done.13), channel_id=1, source_target_pairs={{0,1},{1,0},{2,3},{3,2},{4,5},{5,4},{6,7},{7,6},{8,9},{9,8},{10,11... | collective-permute-start | bytes 1179656 | tf_op jit(solution)/shard_map/ppermute | solution.py:706
  79.5 1.9 %collective-permute-start.18 = (bf16[96,16,128]{2,1,0:T(8,128)(2,1)S(1)}, bf16[96,16,128]{2,1,0:T(8,128)(2,1)S(1)}, u32[]{:S(2)}, u32[]{:S(2)}) collective-permute-start(bf16[96,16,128]{2,1,0:T(8,128)(2,1)S(1)} %collective-permute-done.14), channel_id=1, source_target_pairs={{0,1},{1,0},{2,3},{3,2},{4,5},{5,4},{6,7},{7,6},{8,9},{9,8},{10,11... | collective-permute-start | bytes 1179656 | tf_op jit(solution)/shard_map/ppermute | solution.py:706
  79.6 2.4 %collective-permute-start.19 = (bf16[96,16,128]{2,1,0:T(8,128)(2,1)S(1)}, bf16[96,16,128]{2,1,0:T(8,128)(2,1)S(1)}, u32[]{:S(2)}, u32[]{:S(2)}) collective-permute-start(bf16[96,16,128]{2,1,0:T(8,128)(2,1)S(1)} %collective-permute-done.15), channel_id=1, source_target_pairs={{0,1},{1,0},{2,3},{3,2},{4,5},{5,4},{6,7},{7,6},{8,9},{9,8},{10,11... | collective-permute-start | bytes 1179656 | tf_op jit(solution)/shard_map/ppermute | solution.py:706
  80.9 1.1 copy-start.6
  81.4 0.8 copy-start.7
  82.0 0.8 copy-start.8

commit v10 on v9

--- a/solution.py
+++ b/solution.py
@@ -231,6 +231,7 @@
         inside = lane < offset + SUB - LANES
         if not over:
             inside = (lane >= offset) & (lane < offset + SUB)
+        added = []
         for h in range(2):
             for part in range(2):
                 from_lane = (2 * h + part) * SUB
@@ -242,9 +243,11 @@
                     for wrapped in range(2):
                         keep = jnp.logical_and(inside, late if wrapped == 0 else ~late)
                         start = (base + SUB * wrapped + first_row) * lanes
-                        start = start + 2 * (tile + over) + part
-                        at = pl.ds(start, 8, stride=lanes)
-                        total_ref[at, :] = total_ref[at, :] + jnp.where(keep, values, 0.0)
+                        at = pl.ds(start + 2 * (tile + over) + part, 8, stride=lanes)
+                        added.append((at, jnp.where(keep, values, 0.0)))
+        sums = [total_ref[at, :] + values for at, values in added]
+        for (at, _), value in zip(added, sums):
+            total_ref[at, :] = value
 
     place(0)
 

time: 119 us -> 119 us (level)
  the two profiles are of different devices: /device:TPU:17 before, /device:TPU:0 now
where the time goes in v10:
time: 119 us; the launch traced here: 118 us
  Pallas kernels  69.5 us (58%)
  starting transfers between devices  22.1 us (19%)
  other arithmetic  12.6 us (11%)
  local copies, waits for them, and re-layouts  9.18 us (8%)
  waiting for transfers between devices  3.71 us (3%)
    pallas_call x1, Pallas kernels, image_rows_of(): pl.pallas_call(functools.partial(image_kernel, pieces=len(uv), chunks=chu...  35 us
    ppermute x20, starting transfers between devices, from_partner(): return lax.ppermute(value, axis, [(i, i ^ mask) for i in range(count)])  22.1 us
    pallas_call x3, Pallas kernels, sky_sums(): pl.pallas_call(sky_kernel, grid=(1,), in_specs=[pl.BlockSpec((count, 2, v...  13.8 us
    pallas_call x1, Pallas kernels, uv_tile_own(): pl.pallas_call(functools.partial(tile_kernel, pieces=len(uv), tile_rows=t...  11.7 us
    pallas_call x1, Pallas kernels, corrected_subgrids(): pl.pallas_call(functools.partial(correct_kernel, pieces=len(tables), skie...  6.66 us
    unnamed x56, local copies, waits for them, and re-layouts  6.02 us
    ppermute x20, waiting for transfers between devices, from_partner(): return lax.ppermute(value, axis, [(i, i ^ mask) for i in range(count)])  3.71 us
    another operation x1, other arithmetic  3.47 us
  transfers between devices with their start and end apart: 20, of which 6 were waited for; matrix products, arithmetic and copies ran while one was open for 13% of the time, Pallas kernels for 24%

profile of v10, /device:TPU:0, one launch (start us, length us, event | category | flops | bytes accessed | tf_op | source)
XLA Modules:
  0.0 118.2 jit_solution(7703097702096778332)
XLA Ops:
  0.6 0.8 and_select_fusion.15
  1.4 0.1 convert_element_type.85
  1.5 1.0 reshape.669
  2.6 0.2 copy.42
  2.8 0.2 reshape.670
  3.0 5.1 %collective-permute-start.2 = (bf16[17,16,128]{2,1,0:T(8,128)(2,1)S(1)}, bf16[17,16,128]{2,1,0:T(8,128)(2,1)S(1)}, u32[]{:S(2)}, u32[]{:S(2)}) collective-permute-start(bf16[17,16,128]{2,1,0:T(8,128)(2,1)S(1)} %pad_maximum_fusion.2), channel_id=1, source_target_pairs={{0,6},{1,7},{2,4},{3,5},{4,2},{5,3},{6,0},{7,1},{8,14},{9,15},{10,... | collective-permute-start | bytes 208904 | tf_op jit(solution)/shard_map/ppermute | solution.py:709
  8.1 0.6 collective-permute-start
  8.9 4.6 %sky_sums.3.refs_8_ = f32[8,16,128]{2,1,0:T(8,128)} custom-call(bf16[24,2,2048]{2,1,0:T(2,128)(2,1)} %vis_ref.5, f32[48,128]{1,0:T(8,128)} %bitcast.135, f32[1,16]{1,0:T(1,128)} %bitcast.146), custom_call_target="tpu_custom_call" | custom-call | bytes 20000000 | tf_op jit(solution)/shard_map/sky_sums/pallas_call | solution.py:119
  13.5 0.6 add_add_fusion
  14.2 2.7 %collective-permute-start.5 = (bf16[68,16,128]{2,1,0:T(8,128)(2,1)S(1)}, bf16[68,16,128]{2,1,0:T(8,128)(2,1)S(1)}, u32[]{:S(2)}, u32[]{:S(2)}) collective-permute-start(bf16[68,16,128]{2,1,0:T(8,128)(2,1)S(1)} %constant_dynamic-update-slice_fusion.refs_0_), channel_id=1, source_target_pairs={{0,24},{8,16},{16,8},{24,0},{1,25},{9,17},{17,9},{25,1},{2,26},{10... | collective-permute-start | bytes 835592 | tf_op jit(solution)/shard_map/ppermute | solution.py:709
  16.9 0.5 collective-permute-start.4
  17.4 0.4 collective-permute-start.3
  17.8 0.7 fusion.16
  18.5 0.7 and_select_fusion.3
  19.2 0.7 broadcast_multiply_fusion
  19.8 4.6 %sky_sums.5.refs_10_ = f32[8,16,128]{2,1,0:T(8,128)} custom-call(bf16[24,2,2048]{2,1,0:T(2,128)(2,1)} %vis_ref.5, f32[48,128]{1,0:T(8,128)} %bitcast.136, f32[1,16]{1,0:T(1,128)} %bitcast.147), custom_call_target="tpu_custom_call" | custom-call | bytes 20000000 | tf_op jit(solution)/shard_map/sky_sums/pallas_call | solution.py:119
  24.5 4.6 %sky_sums.4.refs_9_ = f32[8,16,128]{2,1,0:T(8,128)} custom-call(bf16[24,2,2048]{2,1,0:T(2,128)(2,1)} %vis_ref.5, f32[48,128]{1,0:T(8,128)} %bitcast.137, f32[1,16]{1,0:T(1,128)} %bitcast.148), custom_call_target="tpu_custom_call" | custom-call | bytes 20000000 | tf_op jit(solution)/shard_map/sky_sums/pallas_call | solution.py:119
  29.1 0.1 copy.22
  29.2 0.6 reshape.674.stations_ref
  29.8 1.5 %fusion.8.refs_11_ = f32[24,16,128]{2,1,0:T(8,128)} fusion(f32[16,128]{1,0:T(8,128)S(1)} %get-tuple-element.83, f32[128]{0:T(128)S(1)} %fusion.19, s32[16,128]{1,0:T(8,128)S(1)} %fusion.10, s32[24]{0:T(128)S(1)} %and_select_fusion.3, f32[16,128]{1,0:T(8,128)S(1)} %get-tuple-element.82, f32[24]{0:T(128)S(1)} %broadcast_multiply_fusion), kind=kLoop, calls=%fused_computation.24 | loop fusion | flops 884736 | bytes 221888 | tf_op jit(solution)/shard_map/mul | solution.py:704
  31.3 0.1 collective-permute-start.9
  31.4 0.5 collective-permute-start.8
  31.9 0.1 collective-permute-start.6
  32.0 0.4 collective-permute-start.7
  32.5 1.3 %collective-permute-done.6.refs_1_ = bf16[68,16,128]{2,1,0:T(8,128)(2,1)S(1)} collective-permute-done((bf16[68,16,128]{2,1,0:T(8,128)(2,1)S(1)}, bf16[68,16,128]{2,1,0:T(8,128)(2,1)S(1)}, u32[]{:S(2)}, u32[]{:S(2)}) %collective-permute-start.6) | collective-permute-done | bytes 278560 | tf_op jit(solution)/shard_map/ppermute | solution.py:709
  33.8 0.4 collective-permute-done.7.refs_3_
  34.2 0.3 copy-done.14
  34.5 0.4 copy-done.15
  34.9 0.1 copy-done.13
  35.0 0.7 copy-done.12
  35.7 6.7 %correct.1 = bf16[24,16,128]{2,1,0:T(8,128)(2,1)} custom-call(s32[48]{0:T(128)} %reshape.674.stations_ref, bf16[68,16,128]{2,1,0:T(8,128)(2,1)} %copy-done.2, bf16[68,16,128]{2,1,0:T(8,128)(2,1)} %copy-done.14, bf16[68,16,128]{2,1,0:T(8,128)(2,1)} %copy-done.11, bf16[68,16,128]{2,1,0:T(8,128)(2,1)} %copy-done.15, bf16[68,16,128]{2,1,0:T(8,128)(2,1)} %copy-done.10, ...), custom_call_target="tpu_custom_call" | custom-call | bytes 16000000 | tf_op jit(solution)/shard_map/correct/pallas_call | solution.py:194
  42.3 3.7 %collective-permute-start.12 = (bf16[24,16,128]{2,1,0:T(8,128)(2,1)}, bf16[24,16,128]{2,1,0:T(8,128)(2,1)S(1)}, u32[]{:S(2)}, u32[]{:S(2)}) collective-permute-start(bf16[24,16,128]{2,1,0:T(8,128)(2,1)} %correct.1), channel_id=1, source_target_pairs={{0,6},{1,7},{2,4},{3,5},{4,2},{5,3},{6,0},{7,1},{8,14},{9,15},{10,... | collective-permute-start | bytes 294920 | tf_op jit(solution)/shard_map/ppermute | solution.py:709
  46.1 0.6 collective-permute-start.10
  46.7 0.7 slice_bitcast_fusion.6
  47.5 0.7 slice_bitcast_fusion.4
  48.2 0.7 slice_bitcast_fusion.2
  48.9 0.7 slice_bitcast_fusion
  49.7 0.1 concatenate.41
  49.8 0.1 slice_add_fusion
  49.9 0.1 add.327.row_ref
  50.0 0.1 add.324.col_ref
  50.1 3.5 %cosine_convert_fusion = (bf16[1,256,768]{2,1,0:T(8,128)(2,1)S(1)}, bf16[1,256,768]{2,1,0:T(8,128)(2,1)S(1)}) fusion(s32[768]{0:T(1024)S(1)} %add.324.col_ref, s32[256]{0:T(256)S(1)} %iota_add_fusion.1), kind=kLoop, calls=%fused_computation.10 | loop fusion | flops 3145728 | bytes 790528 | tf_op jit(solution)/shard_map/convert
  53.6 1.0 pad_maximum_fusion.refs_11_
  54.6 0.9 pad_maximum_fusion.1
  55.5 0.1 collective-permute-start.16
  55.6 2.7 %collective-permute-start.15 = (bf16[96,16,128]{2,1,0:T(8,128)(2,1)S(1)}, bf16[96,16,128]{2,1,0:T(8,128)(2,1)S(1)}, u32[]{:S(2)}, u32[]{:S(2)}) collective-permute-start(bf16[96,16,128]{2,1,0:T(8,128)(2,1)S(1)} %pad_maximum_fusion.1), channel_id=1, source_target_pairs={{0,24},{8,16},{16,8},{24,0},{1,25},{9,17},{17,9},{25,1},{2,26},{10... | collective-permute-start | bytes 1179656 | tf_op jit(solution)/shard_map/ppermute | solution.py:709
  58.3 0.5 collective-permute-start.14
  58.8 0.4 collective-permute-start.13
  59.2 0.1 fusion.25
  59.2 0.6 reshape.685.corner_ref
  59.8 2.3 %lookups.1 = (bf16[768,256]{1,0:T(8,128)(2,1)}, bf16[768,256]{1,0:T(8,128)(2,1)}, f32[768,128]{1,0:T(8,128)}) custom-call(s32[1,768]{1,0:T(1,128)} %reshape.685.corner_ref, bf16[256,256]{1,0:T(8,128)(2,1)} %constant.325.clone.unit_ref, bf16[32,128]{1,0:T(8,128)(2,1)} %constant.326.clone.count_ref), custom_call_target="tpu_custom_call" | custom-call | bytes 8000000 | tf_op jit(solution)/shard_map/lookups/pallas_call | solution.py:394
  62.2 2.0 %subtract_convert_fusion.refs_12_ = bf16[1024,128]{1,0:T(8,128)(2,1)} fusion(f32[1024,128]{1,0:T(8,128)} %constant.328.clone, f32[1024,128]{1,0:T(8,128)} %constant.327.clone, f32[128]{0:T(128)S(1)} %fusion.25, f32[128]{0:T(128)S(1)} %fusion.26), kind=kLoop, calls=%fused_computation.11 | loop fusion | flops 524288 | bytes 1311744 | tf_op jit(solution)/shard_map/convert_element_type | solution.py:579
  64.2 0.7 copy-done.1
  64.9 11.7 %uv_tile.1.refs_14_ = f32[32768,128]{1,0:T(8,128)} custom-call(s32[3]{0:T(128)} %get-tuple-element.54.info_ref, s32[768]{0:T(1024)} %copy-done.17, s32[768]{0:T(1024)} %copy-done.16, bf16[1536,128]{1,0:T(8,128)(2,1)} %bitcast.116, bf16[1536,128]{1,0:T(8,128)(2,1)} %bitcast.118), custom_call_target="tpu_custom_call" | custom-call | bytes 41943040 | tf_op jit(solution)/shard_map/uv_tile/pallas_call | solution.py:312
  76.6 0.1 collective-permute-done.13
  76.7 3.2 %collective-permute-start.17 = (bf16[96,16,128]{2,1,0:T(8,128)(2,1)S(1)}, bf16[96,16,128]{2,1,0:T(8,128)(2,1)S(1)}, u32[]{:S(2)}, u32[]{:S(2)}) collective-permute-start(bf16[96,16,128]{2,1,0:T(8,128)(2,1)S(1)} %collective-permute-done.13), channel_id=1, source_target_pairs={{0,1},{1,0},{2,3},{3,2},{4,5},{5,4},{6,7},{7,6},{8,9},{9,8},{10,11... | collective-permute-start | bytes 1179656 | tf_op jit(solution)/shard_map/ppermute | solution.py:709
  79.9 0.1 collective-permute-start.18
  80.0 0.4 collective-permute-start.19
  80.4 0.8 collective-permute-done.17
  81.3 0.6 collective-permute-done.18
  81.9 0.6 collective-permute-done.19
  82.4 0.2 copy-done.7
  82.6 0.6 copy-done.8
  83.2 35.0 %image.1 = (f32[32768,128]{1,0:T(8,128)}, f32[32768,128]{1,0:T(8,128)}) custom-call(s32[3]{0:T(128)} %get-tuple-element.50.info_ref, s32[768]{0:T(1024)} %copy-done.17, s32[768]{0:T(1024)} %copy-done.16, bf16[1536,128]{1,0:T(8,128)(2,1)} %bitcast.117, bf16[1536,128]{1,0:T(8,128)(2,1)} %bitcast.119, ...), custom_call_target="tpu_custom_call", output_to_operand_aliasing={{1}: (17, {})} | custom-call | tf_op jit(solution)/shard_map/image/pallas_call | solution.py:625
  (74 shorter events, 0.4 us)
Async XLA Ops:
  3.0 11.2 %collective-permute-start.2 = (bf16[17,16,128]{2,1,0:T(8,128)(2,1)S(1)}, bf16[17,16,128]{2,1,0:T(8,128)(2,1)S(1)}, u32[]{:S(2)}, u32[]{:S(2)}) collective-permute-start(bf16[17,16,128]{2,1,0:T(8,128)(2,1)S(1)} %pad_maximum_fusion.2), channel_id=1, source_target_pairs={{0,6},{1,7},{2,4},{3,5},{4,2},{5,3},{6,0},{7,1},{8,14},{9,15},{10,... | collective-permute-start | bytes 208904 | tf_op jit(solution)/shard_map/ppermute | solution.py:709
  8.1 6.0 %collective-permute-start.1 = (bf16[17,16,128]{2,1,0:T(8,128)(2,1)S(1)}, bf16[17,16,128]{2,1,0:T(8,128)(2,1)S(1)}, u32[]{:S(2)}, u32[]{:S(2)}) collective-permute-start(bf16[17,16,128]{2,1,0:T(8,128)(2,1)S(1)} %pad_maximum_fusion.2), channel_id=1, source_target_pairs={{0,4},{1,5},{2,6},{3,7},{4,0},{5,1},{6,2},{7,3},{8,12},{9,13},{10,... | collective-permute-start | bytes 208904 | tf_op jit(solution)/shard_map/ppermute | solution.py:709
  8.1 6.0 %collective-permute-start = (bf16[17,16,128]{2,1,0:T(8,128)(2,1)S(1)}, bf16[17,16,128]{2,1,0:T(8,128)(2,1)S(1)}, u32[]{:S(2)}, u32[]{:S(2)}) collective-permute-start(bf16[17,16,128]{2,1,0:T(8,128)(2,1)S(1)} %pad_maximum_fusion.2), channel_id=1, source_target_pairs={{0,2},{1,3},{2,0},{3,1},{4,6},{5,7},{6,4},{7,5},{8,10},{9,11},{10,... | collective-permute-start | bytes 208904 | tf_op jit(solution)/shard_map/ppermute | solution.py:709
  14.2 19.9 %copy-start.2 = (bf16[68,16,128]{2,1,0:T(8,128)(2,1)}, bf16[68,16,128]{2,1,0:T(8,128)(2,1)S(1)}, u32[]{:S(2)}) copy-start(bf16[68,16,128]{2,1,0:T(8,128)(2,1)S(1)} %constant_dynamic-update-slice_fusion.refs_0_) | copy-start | bytes 835588
  14.2 17.1 %collective-permute-start.5 = (bf16[68,16,128]{2,1,0:T(8,128)(2,1)S(1)}, bf16[68,16,128]{2,1,0:T(8,128)(2,1)S(1)}, u32[]{:S(2)}, u32[]{:S(2)}) collective-permute-start(bf16[68,16,128]{2,1,0:T(8,128)(2,1)S(1)} %constant_dynamic-update-slice_fusion.refs_0_), channel_id=1, source_target_pairs={{0,24},{8,16},{16,8},{24,0},{1,25},{9,17},{17,9},{25,1},{2,26},{10... | collective-permute-start | bytes 835592 | tf_op jit(solution)/shard_map/ppermute | solution.py:709
  16.9 14.4 %collective-permute-start.4 = (bf16[68,16,128]{2,1,0:T(8,128)(2,1)S(1)}, bf16[68,16,128]{2,1,0:T(8,128)(2,1)S(1)}, u32[]{:S(2)}, u32[]{:S(2)}) collective-permute-start(bf16[68,16,128]{2,1,0:T(8,128)(2,1)S(1)} %constant_dynamic-update-slice_fusion.refs_0_), channel_id=1, source_target_pairs={{0,16},{8,24},{16,0},{24,8},{1,17},{9,25},{17,1},{25,9},{2,18},{10... | collective-permute-start | bytes 835592 | tf_op jit(solution)/shard_map/ppermute | solution.py:709
  17.4 13.9 %collective-permute-start.3 = (bf16[68,16,128]{2,1,0:T(8,128)(2,1)S(1)}, bf16[68,16,128]{2,1,0:T(8,128)(2,1)S(1)}, u32[]{:S(2)}, u32[]{:S(2)}) collective-permute-start(bf16[68,16,128]{2,1,0:T(8,128)(2,1)S(1)} %constant_dynamic-update-slice_fusion.refs_0_), channel_id=1, source_target_pairs={{0,8},{8,0},{16,24},{24,16},{1,9},{9,1},{17,25},{25,17},{2,10},{10... | collective-permute-start | bytes 835592 | tf_op jit(solution)/shard_map/ppermute | solution.py:709
  31.3 2.9 %copy-start.9 = (bf16[68,16,128]{2,1,0:T(8,128)(2,1)}, bf16[68,16,128]{2,1,0:T(8,128)(2,1)S(1)}, u32[]{:S(2)}) copy-start(bf16[68,16,128]{2,1,0:T(8,128)(2,1)S(1)} %collective-permute-done.5.refs_6_) | copy-start | bytes 835588
  31.3 2.9 %copy-start.10 = (bf16[68,16,128]{2,1,0:T(8,128)(2,1)}, bf16[68,16,128]{2,1,0:T(8,128)(2,1)S(1)}, u32[]{:S(2)}) copy-start(bf16[68,16,128]{2,1,0:T(8,128)(2,1)S(1)} %collective-permute-done.4.refs_4_) | copy-start | bytes 835588
  31.3 2.9 %copy-start.11 = (bf16[68,16,128]{2,1,0:T(8,128)(2,1)}, bf16[68,16,128]{2,1,0:T(8,128)(2,1)S(1)}, u32[]{:S(2)}) copy-start(bf16[68,16,128]{2,1,0:T(8,128)(2,1)S(1)} %collective-permute-done.3.refs_2_) | copy-start | bytes 835588
  31.3 2.8 %collective-permute-start.9 = (bf16[68,16,128]{2,1,0:T(8,128)(2,1)S(1)}, bf16[68,16,128]{2,1,0:T(8,128)(2,1)S(1)}, u32[]{:S(2)}, u32[]{:S(2)}) collective-permute-start(bf16[68,16,128]{2,1,0:T(8,128)(2,1)S(1)} %collective-permute-done.5.refs_6_), channel_id=1, source_target_pairs={{0,1},{1,0},{2,3},{3,2},{4,5},{5,4},{6,7},{7,6},{8,9},{9,8},{10,11... | collective-permute-start | bytes 835592 | tf_op jit(solution)/shard_map/ppermute | solution.py:709
  31.4 2.7 %collective-permute-start.8 = (bf16[68,16,128]{2,1,0:T(8,128)(2,1)S(1)}, bf16[68,16,128]{2,1,0:T(8,128)(2,1)S(1)}, u32[]{:S(2)}, u32[]{:S(2)}) collective-permute-start(bf16[68,16,128]{2,1,0:T(8,128)(2,1)S(1)} %collective-permute-done.4.refs_4_), channel_id=1, source_target_pairs={{0,1},{1,0},{2,3},{3,2},{4,5},{5,4},{6,7},{7,6},{8,9},{9,8},{10,11... | collective-permute-start | bytes 835592 | tf_op jit(solution)/shard_map/ppermute | solution.py:709
  31.9 1.8 %collective-permute-start.6 = (bf16[68,16,128]{2,1,0:T(8,128)(2,1)S(1)}, bf16[68,16,128]{2,1,0:T(8,128)(2,1)S(1)}, u32[]{:S(2)}, u32[]{:S(2)}) collective-permute-start(bf16[68,16,128]{2,1,0:T(8,128)(2,1)S(1)} %constant_dynamic-update-slice_fusion.refs_0_), channel_id=1, source_target_pairs={{0,1},{1,0},{2,3},{3,2},{4,5},{5,4},{6,7},{7,6},{8,9},{9,8},{10,11... | collective-permute-start | bytes 835592 | tf_op jit(solution)/shard_map/ppermute | solution.py:709
  32.0 2.2 %collective-permute-start.7 = (bf16[68,16,128]{2,1,0:T(8,128)(2,1)S(1)}, bf16[68,16,128]{2,1,0:T(8,128)(2,1)S(1)}, u32[]{:S(2)}, u32[]{:S(2)}) collective-permute-start(bf16[68,16,128]{2,1,0:T(8,128)(2,1)S(1)} %collective-permute-done.3.refs_2_), channel_id=1, source_target_pairs={{0,1},{1,0},{2,3},{3,2},{4,5},{5,4},{6,7},{7,6},{8,9},{9,8},{10,11... | collective-permute-start | bytes 835592 | tf_op jit(solution)/shard_map/ppermute | solution.py:709
  33.8 0.7 copy-start.14
  34.2 0.7 copy-start.15
  34.2 0.8 copy-start.13
  35.0 0.7 copy-start.12
  42.3 12.2 %collective-permute-start.12 = (bf16[24,16,128]{2,1,0:T(8,128)(2,1)}, bf16[24,16,128]{2,1,0:T(8,128)(2,1)S(1)}, u32[]{:S(2)}, u32[]{:S(2)}) collective-permute-start(bf16[24,16,128]{2,1,0:T(8,128)(2,1)} %correct.1), channel_id=1, source_target_pairs={{0,6},{1,7},{2,4},{3,5},{4,2},{5,3},{6,0},{7,1},{8,14},{9,15},{10,... | collective-permute-start | bytes 294920 | tf_op jit(solution)/shard_map/ppermute | solution.py:709
  46.1 8.5 %collective-permute-start.11 = (bf16[24,16,128]{2,1,0:T(8,128)(2,1)}, bf16[24,16,128]{2,1,0:T(8,128)(2,1)S(1)}, u32[]{:S(2)}, u32[]{:S(2)}) collective-permute-start(bf16[24,16,128]{2,1,0:T(8,128)(2,1)} %correct.1), channel_id=1, source_target_pairs={{0,4},{1,5},{2,6},{3,7},{4,0},{5,1},{6,2},{7,3},{8,12},{9,13},{10,... | collective-permute-start | bytes 294920 | tf_op jit(solution)/shard_map/ppermute | solution.py:709
  46.1 8.5 %collective-permute-start.10 = (bf16[24,16,128]{2,1,0:T(8,128)(2,1)}, bf16[24,16,128]{2,1,0:T(8,128)(2,1)S(1)}, u32[]{:S(2)}, u32[]{:S(2)}) collective-permute-start(bf16[24,16,128]{2,1,0:T(8,128)(2,1)} %correct.1), channel_id=1, source_target_pairs={{0,2},{1,3},{2,0},{3,1},{4,6},{5,7},{6,4},{7,5},{8,10},{9,11},{10,... | collective-permute-start | bytes 294920 | tf_op jit(solution)/shard_map/ppermute | solution.py:709
  50.0 14.1 %copy-start.17 = (s32[768]{0:T(1024)}, s32[768]{0:T(1024)S(1)}, u32[]{:S(2)}) copy-start(s32[768]{0:T(1024)S(1)} %add.327.row_ref) | copy-start | bytes 9220
  50.1 14.0 %copy-start.16 = (s32[768]{0:T(1024)}, s32[768]{0:T(1024)S(1)}, u32[]{:S(2)}) copy-start(s32[768]{0:T(1024)S(1)} %add.324.col_ref) | copy-start | bytes 9220
  55.5 8.6 %copy-start = (bf16[96,16,128]{2,1,0:T(8,128)(2,1)}, bf16[96,16,128]{2,1,0:T(8,128)(2,1)S(1)}, u32[]{:S(2)}) copy-start(bf16[96,16,128]{2,1,0:T(8,128)(2,1)S(1)} %pad_maximum_fusion.1) | copy-start | bytes 1179652
  55.5 8.6 %collective-permute-start.16 = (bf16[96,16,128]{2,1,0:T(8,128)(2,1)S(1)}, bf16[96,16,128]{2,1,0:T(8,128)(2,1)S(1)}, u32[]{:S(2)}, u32[]{:S(2)}) collective-permute-start(bf16[96,16,128]{2,1,0:T(8,128)(2,1)S(1)} %pad_maximum_fusion.1), channel_id=1, source_target_pairs={{0,1},{1,0},{2,3},{3,2},{4,5},{5,4},{6,7},{7,6},{8,9},{9,8},{10,11... | collective-permute-start | bytes 1179656 | tf_op jit(solution)/shard_map/ppermute | solution.py:709
  55.6 21.0 %collective-permute-start.15 = (bf16[96,16,128]{2,1,0:T(8,128)(2,1)S(1)}, bf16[96,16,128]{2,1,0:T(8,128)(2,1)S(1)}, u32[]{:S(2)}, u32[]{:S(2)}) collective-permute-start(bf16[96,16,128]{2,1,0:T(8,128)(2,1)S(1)} %pad_maximum_fusion.1), channel_id=1, source_target_pairs={{0,24},{8,16},{16,8},{24,0},{1,25},{9,17},{17,9},{25,1},{2,26},{10... | collective-permute-start | bytes 1179656 | tf_op jit(solution)/shard_map/ppermute | solution.py:709
  58.3 18.4 %collective-permute-start.14 = (bf16[96,16,128]{2,1,0:T(8,128)(2,1)S(1)}, bf16[96,16,128]{2,1,0:T(8,128)(2,1)S(1)}, u32[]{:S(2)}, u32[]{:S(2)}) collective-permute-start(bf16[96,16,128]{2,1,0:T(8,128)(2,1)S(1)} %pad_maximum_fusion.1), channel_id=1, source_target_pairs={{0,16},{8,24},{16,0},{24,8},{1,17},{9,25},{17,1},{25,9},{2,18},{10... | collective-permute-start | bytes 1179656 | tf_op jit(solution)/shard_map/ppermute | solution.py:709
  58.8 17.9 %collective-permute-start.13 = (bf16[96,16,128]{2,1,0:T(8,128)(2,1)S(1)}, bf16[96,16,128]{2,1,0:T(8,128)(2,1)S(1)}, u32[]{:S(2)}, u32[]{:S(2)}) collective-permute-start(bf16[96,16,128]{2,1,0:T(8,128)(2,1)S(1)} %pad_maximum_fusion.1), channel_id=1, source_target_pairs={{0,8},{8,0},{16,24},{24,16},{1,9},{9,1},{17,25},{25,17},{2,10},{10... | collective-permute-start | bytes 1179656 | tf_op jit(solution)/shard_map/ppermute | solution.py:709
  64.1 0.8 copy-start.1
  76.6 5.8 %copy-start.3 = (bf16[96,16,128]{2,1,0:T(8,128)(2,1)}, bf16[96,16,128]{2,1,0:T(8,128)(2,1)S(1)}, u32[]{:S(2)}) copy-start(bf16[96,16,128]{2,1,0:T(8,128)(2,1)S(1)} %collective-permute-done.15) | copy-start | bytes 1179652
  76.6 5.8 %copy-start.4 = (bf16[96,16,128]{2,1,0:T(8,128)(2,1)}, bf16[96,16,128]{2,1,0:T(8,128)(2,1)S(1)}, u32[]{:S(2)}) copy-start(bf16[96,16,128]{2,1,0:T(8,128)(2,1)S(1)} %collective-permute-done.14) | copy-start | bytes 1179652
  76.7 5.7 %copy-start.5 = (bf16[96,16,128]{2,1,0:T(8,128)(2,1)}, bf16[96,16,128]{2,1,0:T(8,128)(2,1)S(1)}, u32[]{:S(2)}) copy-start(bf16[96,16,128]{2,1,0:T(8,128)(2,1)S(1)} %collective-permute-done.13) | copy-start | bytes 1179652
  76.7 4.6 %collective-permute-start.17 = (bf16[96,16,128]{2,1,0:T(8,128)(2,1)S(1)}, bf16[96,16,128]{2,1,0:T(8,128)(2,1)S(1)}, u32[]{:S(2)}, u32[]{:S(2)}) collective-permute-start(bf16[96,16,128]{2,1,0:T(8,128)(2,1)S(1)} %collective-permute-done.13), channel_id=1, source_target_pairs={{0,1},{1,0},{2,3},{3,2},{4,5},{5,4},{6,7},{7,6},{8,9},{9,8},{10,11... | collective-permute-start | bytes 1179656 | tf_op jit(solution)/shard_map/ppermute | solution.py:709
  79.9 1.9 %collective-permute-start.18 = (bf16[96,16,128]{2,1,0:T(8,128)(2,1)S(1)}, bf16[96,16,128]{2,1,0:T(8,128)(2,1)S(1)}, u32[]{:S(2)}, u32[]{:S(2)}) collective-permute-start(bf16[96,16,128]{2,1,0:T(8,128)(2,1)S(1)} %collective-permute-done.14), channel_id=1, source_target_pairs={{0,1},{1,0},{2,3},{3,2},{4,5},{5,4},{6,7},{7,6},{8,9},{9,8},{10,11... | collective-permute-start | bytes 1179656 | tf_op jit(solution)/shard_map/ppermute | solution.py:709
  80.0 2.4 %collective-permute-start.19 = (bf16[96,16,128]{2,1,0:T(8,128)(2,1)S(1)}, bf16[96,16,128]{2,1,0:T(8,128)(2,1)S(1)}, u32[]{:S(2)}, u32[]{:S(2)}) collective-permute-start(bf16[96,16,128]{2,1,0:T(8,128)(2,1)S(1)} %collective-permute-done.15), channel_id=1, source_target_pairs={{0,1},{1,0},{2,3},{3,2},{4,5},{5,4},{6,7},{7,6},{8,9},{9,8},{10,11... | collective-permute-start | bytes 1179656 | tf_op jit(solution)/shard_map/ppermute | solution.py:709
  81.3 1.1 copy-start.6
  81.9 0.8 copy-start.7
  82.4 0.8 copy-start.8
